TPU v7x, 32 devices: a whole 2x2x4 slice. The times are simulated.
32 devices in a mesh: row: 4 (over x, core), long: 8 (over z, y).
Axes of the slice: x: 2, y: 2, z: 4, core: 2. Of those that a mesh axis runs over, the one named last changes fastest.
Arguments:
- slip: float32 [32, 16, 768], P('long'), may hold values from -6 to 6
- vertices: float32 [3, 4488], P(None, 'long'), may hold values from -2.5 to 258.5
- triangles: int32 [3, 8192], P(None, 'long'), may hold values from 0 to 4487, as said below
- elem_map: int32 [32, 256], P('long'), may hold values from 0 to 1023, as said below
- near_pairs: int32 [2, 640], P(None, ('row', 'long')), may hold values from 0 to 31, as said below
- near_count: int32 [32], P(('row', 'long')), may hold values from 1 to 20, as said below
- far_pairs: int32 [2, 512], P(None, ('row', 'long')), may hold values from 0 to 31, as said below
- far_coef: bfloat16 [512, 1024], P(('row', 'long')), may hold values from -1 to 1
- basis: bfloat16 [32, 32, 768], P('long'), may hold values from -0.21875 to 0.21875
Outputs:
- traction: float32 [32, 16, 768], P('long')
Inputs may be any that keep to these rules, and one draw needn't show every extreme that they name: `triangles`: each element's three vertices belong to its owner's block of 561 vertices (owner = element // 1024). `elem_map`: the 4 clusters of one owner name each of its 1024 elements exactly once. `near_pairs`: in device block b the first cluster is owned by long index b % 8 and the second is the first plus 0 to 2; dead slots hold pairs of the same kind. `near_count`: some device has all 20 slots live. `far_pairs`: the second cluster of a far pair is owned by a long index more than 1 away from the first cluster's owner in both directions around the axis.
All inputs are finite; a program needn't handle non-finite values.
Results may differ from a plain program's by a relative error of at most 0.0041.
Values may be sent and summed in bfloat16 or wider, within the bound.
No kernel may reach another device: no remote copies, remote signals or barrier semaphores. Data moves between devices by JAX's collectives and lax.ppermute only.
A program may use at most 64 MiB of HBM per device.

v0:
```python
import jax
import jax.numpy as jnp
from jax import lax
from jax.sharding import PartitionSpec as P

NEARC = 2
REACH = 1


soften = 0.25


def shifted(block, axis, distance):
    devices = range(lax.axis_size(axis))
    route = [(i - distance, i) for i in devices if i - distance in devices]
    return lax.ppermute(block, axis, route)


def element_geometry(vertices, triangles):
    corner_one = vertices[:, triangles[0]]
    corner_two = vertices[:, triangles[1]]
    corner_three = vertices[:, triangles[2]]
    centre = (corner_one + corner_two + corner_three) / 3.0
    edge_one = corner_two - corner_one
    edge_two = corner_three - corner_one
    normal = jnp.stack(
        [
            edge_one[1] * edge_two[2] - edge_one[2] * edge_two[1],
            edge_one[2] * edge_two[0] - edge_one[0] * edge_two[2],
            edge_one[0] * edge_two[1] - edge_one[1] * edge_two[0],
        ]
    )
    element_area = 0.5 * jnp.sqrt(jnp.sum(normal * normal, axis=0))
    return jnp.concatenate([centre, element_area[None]], axis=0)


def near_block(geom_left, geom_right):
    offsets = [geom_left[axis_id][:, None] - geom_right[axis_id][None, :] for axis_id in range(3)]
    radius_sq = offsets[0] * offsets[0] + offsets[1] * offsets[1] + offsets[2] * offsets[2]
    inverse = lax.rsqrt(radius_sq + soften)
    cubed = inverse * inverse * inverse
    weight = geom_left[3][:, None] * geom_right[3][None, :]
    blocks = []
    for row_id in range(3):
        pieces = []
        for col_id in range(3):
            term = offsets[row_id] * offsets[col_id] * cubed
            if row_id == col_id:
                term = term + inverse
            pieces.append(weight * term)
        blocks.append(jnp.concatenate(pieces, axis=1))
    return jnp.concatenate(blocks, axis=0).astype(jnp.bfloat16)


def shards(slip, vertices, triangles, elem_map, near_pairs, near_count, far_pairs, far_coef, basis):
    clusters = slip.shape[0]
    rhs_count = slip.shape[1]
    unknowns = slip.shape[2]
    rank_size = basis.shape[1]
    long_index = lax.axis_index("long")
    cluster_base = long_index * clusters
    geometry = element_geometry(vertices, triangles - long_index * vertices.shape[1])
    own_geom = jnp.transpose(geometry[:, elem_map], (1, 0, 2))
    slip_half = slip.astype(jnp.bfloat16)
    reach_steps = list(range(1, REACH + 1))
    sent_counts = [min(clusters, NEARC - (reach_step - 1) * clusters) for reach_step in reach_steps]
    window_length = clusters + sum(sent_counts)
    geom_parts = [own_geom]
    for reach_step, moved_count in zip(reach_steps, sent_counts):
        geom_parts.append(shifted(own_geom[:moved_count], "long", -reach_step))
    geom_window = jnp.concatenate(geom_parts, axis=0)

    def apply_pair(window_slip, cluster_a, cluster_b, running):
        local_a = cluster_a - cluster_base
        local_b = cluster_b - cluster_base
        block = near_block(geom_window[local_a], geom_window[local_b])
        into_a = lax.dot_general(
            window_slip[local_b],
            block,
            (((1,), (1,)), ((), ())),
            preferred_element_type=jnp.float32,
        )
        into_b = jnp.dot(window_slip[local_a], block, preferred_element_type=jnp.float32)
        other = (cluster_a != cluster_b).astype(jnp.float32)
        running = running.at[local_a].add(into_a)
        return running.at[local_b].add(other * into_b)

    parts = [slip_half]
    for window_reach_step, window_moved_count in zip(reach_steps, sent_counts):
        parts.append(shifted(slip_half[:window_moved_count], "long", -window_reach_step))
    window_slip = jnp.concatenate(parts, axis=0)
    empty_window = jnp.zeros((window_length, rhs_count, unknowns), jnp.float32)

    def visit_slot(turn_id, running):
        return apply_pair(window_slip, near_pairs[0, turn_id], near_pairs[1, turn_id], running)

    window_sum = lax.fori_loop(0, near_count[0], visit_slot, empty_window)
    summed = lax.psum(window_sum, "row")
    near_field = summed[:clusters]
    for reach_step, moved_count in zip(reach_steps, sent_counts):
        begin = clusters + (reach_step - 1) * clusters
        arriving = shifted(summed[begin : begin + moved_count], "long", reach_step)
        near_field = near_field.at[:moved_count].add(arriving)
    coeffs = jnp.einsum(
        "cna,cka->cnk", slip_half, basis, preferred_element_type=jnp.float32
    ).astype(jnp.bfloat16)
    all_coeffs = lax.all_gather(
        coeffs.reshape(clusters, rhs_count * rank_size), "long", axis=0, tiled=True
    )
    total_clusters = all_coeffs.shape[0]
    coupling = far_coef.reshape(-1, rank_size, rank_size)
    coeff_first = all_coeffs[far_pairs[0]].reshape(-1, rhs_count, rank_size)
    coeff_second = all_coeffs[far_pairs[1]].reshape(-1, rhs_count, rank_size)
    to_first = jnp.einsum(
        "fnm,fkm->fnk", coeff_second, coupling, preferred_element_type=jnp.float32
    )
    to_second = jnp.einsum(
        "fnk,fkm->fnm", coeff_first, coupling, preferred_element_type=jnp.float32
    )
    cluster_ids = jnp.arange(total_clusters, dtype=jnp.int32)
    pick_first = (cluster_ids[:, None] == far_pairs[0][None, :]).astype(jnp.float32)
    pick_second = (cluster_ids[:, None] == far_pairs[1][None, :]).astype(jnp.float32)
    pair_total = to_first.shape[0]
    far_terms = jnp.dot(
        pick_first, to_first.reshape(pair_total, -1), precision=lax.Precision.HIGHEST
    )
    far_terms = far_terms + jnp.dot(
        pick_second, to_second.reshape(pair_total, -1), precision=lax.Precision.HIGHEST
    )
    row_terms = lax.psum(far_terms, "row")
    far_own = lax.psum_scatter(row_terms, "long", scatter_dimension=0, tiled=True)
    far_round = far_own.astype(jnp.bfloat16).reshape(clusters, rhs_count, rank_size)
    far_field = jnp.einsum("cnk,cka->cna", far_round, basis, preferred_element_type=jnp.float32)
    return near_field + far_field


def solution(mesh):
    placed = (
        P("long", None, None),
        P(None, "long"),
        P(None, "long"),
        P("long", None),
        P(None, ("row", "long")),
        P(("row", "long")),
        P(None, ("row", "long")),
        P(("row", "long"), None),
        P("long", None, None),
    )
    return jax.shard_map(
        shards, mesh=mesh, in_specs=placed, out_specs=P("long", None, None), check_vma=False
    )
```

profile of v0, /device:TPU:0, one launch (start us, length us, event | category | flops | bytes accessed | tf_op | source)
XLA Modules:
  0.0 323.7 jit_solution(710277702606147703)
XLA Ops:
  6.5 1.0 convert_element_type.15
  7.5 1.3 collective-permute-start
  8.8 0.7 fusion.38
  9.5 0.7 broadcast_subtract_fusion
  10.3 0.8 copy.32
  11.2 2.8 gather_fusion.2
  14.2 2.8 gather_fusion.1
  17.2 2.8 gather_fusion
  20.6 2.8 gather_fusion.3
  23.6 1.3 collective-permute-start.1
  25.2 35.3 %all-gather = bf16[8,4,512]{2,1,0:T(4,128)(2,1)S(1)} all-gather(bf16[1,4,512]{2,1,0:T(4,128)(2,1)S(1)} %reshape.348), channel_id=1, replica_groups=mesh['row'=4,'long'=8] {'long'}, dimensions={0}, use_global_device_ids=true | all-gather | bytes 36864 | tf_op jit(solution)/shard_map/all_gather | solution.py:107
  63.0 42.9 %while.13 = (s32[]{:T(128)}, f32[6,16,768]{2,1,0:T(8,128)S(1)}, s32[]{:T(128)}, s32[2,20]{1,0:T(2,128)S(1)}, s32[]{:T(128)}, /*index=5*/bf16[6,16,768]{2,1,0:T(8...) while((s32[]{:T(128)}, f32[6,16,768]{2,1,0:T(8,128)S(1)}, ...), condition=%wide.region_4.0_spmd, body=%wide.region_1.0_spmd.sunk | while | flops 50786352 | bytes 5382565 | solution.py:97
  63.7 0.7 constant_dynamic-slice_fusion.13
  66.8 0.7 and_reduce_fusion.3
  68.1 1.0 fusion.67
  69.1 0.9 fusion.68
  70.7 0.7 constant_dynamic-slice_fusion.13
  73.9 0.7 and_reduce_fusion.3
  75.1 1.0 fusion.67
  76.1 0.9 fusion.68
  77.7 0.7 constant_dynamic-slice_fusion.13
  80.9 0.7 and_reduce_fusion.3
  82.2 1.0 fusion.67
  83.1 0.9 fusion.68
  84.8 0.7 constant_dynamic-slice_fusion.13
  88.0 0.7 and_reduce_fusion.3
  89.2 1.0 fusion.67
  90.2 0.9 fusion.68
  91.8 0.7 constant_dynamic-slice_fusion.13
  95.0 0.7 and_reduce_fusion.3
  96.2 1.0 fusion.67
  97.2 0.9 fusion.68
  98.8 0.7 constant_dynamic-slice_fusion.13
  102.0 0.7 and_reduce_fusion.3
  103.3 1.0 fusion.67
  104.2 0.9 fusion.68
  105.9 0.7 copy-done.1
  106.7 0.8 convolution_add_fusion.1
  107.5 0.6 dynamic-slice.28
  108.7 126.9 %all-reduce.4.cloned.1.call-done = f32[6,16,768]{2,1,0:T(8,128)} async-done(((f32[6,16,768]{2,1,0:T(8,128)}), f32[6,16,768]{2,1,0:T(8,128)}) %all-reduce.4.cloned.1.call-update) | async-done | bytes 294928 | tf_op jit(solution)/shard_map/psum | solution.py:98
  235.7 0.9 slice.189
  236.6 3.4 %collective-permute-start.2 = (f32[2,16,768]{2,1,0:T(8,128)S(1)}, f32[2,16,768]{2,1,0:T(8,128)S(1)}, u32[]{:S(2)}, u32[]{:S(2)}) collective-permute-start(f32[2,16,768]{2,1,0:T(8,128)S(1)} %slice.189), channel_id=1, source_target_pairs={{0,1},{1,2},{2,3},{3,4},{4,5},{5,6},{6,7},{8,9},{9,10},{10,11},{11... | collective-permute-start | bytes 294920 | tf_op jit(solution)/shard_map/ppermute | solution.py:16
  239.9 67.6 %all-reduce.6.cloned.1.call-done = f32[32,512]{1,0:T(8,128)} async-done(((f32[32,512]{1,0:T(8,128)}), f32[32,512]{1,0:T(8,128)}) %all-reduce.6.cloned.1.call-update) | async-done | bytes 65552
  307.6 0.7 constant_dynamic-slice_fusion.10
  308.3 5.7 %psum.16 = bf16[4,512]{1,0:T(4,128)(2,1)S(1)} all-reduce(f32[4,512]{1,0:T(4,128)S(1)} %constant_dynamic-slice_fusion.10), channel_id=1, replica_groups=mesh['row'=4,'long'=8] {'row'}, use_global_device_ids=true, to_apply=%region_6.0 | all-reduce | flops 2048 | bytes 12288 | tf_op jit(solution)/shard_map/psum | solution.py:130
  314.1 0.9 slice.187
  315.1 0.9 fusion.32
  316.0 0.8 convolution_add_fusion
  (76 shorter events, 6.8 us)
Async XLA Ops:
  6.5 18.4 %copy-start = (bf16[4,32,768]{2,1,0:T(8,128)(2,1)S(1)}, bf16[4,32,768]{2,1,0:T(8,128)(2,1)}, u32[]{:S(2)}) copy-start(bf16[4,32,768]{2,1,0:T(8,128)(2,1)} %param.25) | copy-start | bytes 589828
  6.5 229.1 %all-reduce.4.cloned.1.call-start = ((), (), s32[]{:S(2)}) async-start(), calls=%async_computation | async-start | bytes 589824 | tf_op jit(solution)/shard_map/psum | solution.py:98
  7.5 55.4 %collective-permute-start = (bf16[2,16,768]{2,1,0:T(8,128)(2,1)S(1)}, bf16[2,16,768]{2,1,0:T(8,128)(2,1)S(1)}, u32[]{:S(2)}, u32[]{:S(2)}) collective-permute-start(bf16[2,16,768]{2,1,0:T(8,128)(2,1)S(1)} %slice.176), channel_id=1, source_target_pairs={{1,0},{2,1},{3,2},{4,3},{5,4},{6,5},{7,6},{9,8},{10,9},{11,10},{12... | collective-permute-start | bytes 147464 | tf_op jit(solution)/shard_map/ppermute | solution.py:16
  17.2 7.7 %copy-start.5 = (s32[2,16]{1,0:T(2,128)S(1)}, s32[2,16]{1,0:T(2,128)}, u32[]{:S(2)}) copy-start(s32[2,16]{1,0:T(2,128)} %param.23) | copy-start | bytes 388
  20.2 41.8 %copy-start.2 = (bf16[16,1024]{1,0:T(8,128)(2,1)S(1)}, bf16[16,1024]{1,0:T(8,128)(2,1)}, u32[]{:S(2)}) copy-start(bf16[16,1024]{1,0:T(8,128)(2,1)} %param.24) | copy-start | bytes 98308
  23.6 39.3 %collective-permute-start.1 = (f32[2,4,256]{2,1,0:T(4,128)S(1)}, f32[2,4,256]{2,1,0:T(4,128)S(1)}, u32[]{:S(2)}, u32[]{:S(2)}) collective-permute-start(f32[2,4,256]{2,1,0:T(4,128)S(1)} %slice.186), channel_id=1, source_target_pairs={{1,0},{2,1},{3,2},{4,3},{5,4},{6,5},{7,6},{9,8},{10,9},{11,10},{12... | collective-permute-start | bytes 24584 | tf_op jit(solution)/shard_map/ppermute | solution.py:16
  60.6 2.4 copy-start.3
  60.6 2.4 copy-start.4
  63.0 44.5 %copy-start.6 = (u32[32]{0:T(128)S(1)}, u32[32]{0:T(128)}, u32[]{:S(2)}) copy-start(u32[32]{0:T(128)} %constant.115) | copy-start | bytes 388
  105.9 0.7 copy-start.1
  106.6 201.0 %all-reduce.6.cloned.1.call-start = ((), (), s32[]{:S(2)}) async-start(), calls=%async_computation.1 | async-start | bytes 131072
  236.6 78.5 %collective-permute-start.2 = (f32[2,16,768]{2,1,0:T(8,128)S(1)}, f32[2,16,768]{2,1,0:T(8,128)S(1)}, u32[]{:S(2)}, u32[]{:S(2)}) collective-permute-start(f32[2,16,768]{2,1,0:T(8,128)S(1)} %slice.189), channel_id=1, source_target_pairs={{0,1},{1,2},{2,3},{3,4},{4,5},{5,6},{6,7},{8,9},{9,10},{10,11},{11... | collective-permute-start | bytes 294920 | tf_op jit(solution)/shard_map/ppermute | solution.py:16
Sparse Core Ops, SparseCore 0:
  106.7 128.8 all-reduce.3
  239.1 68.4 all-reduce.5
where the time goes:
time: 326 us; the launch traced here: 324 us
  waiting for transfers between devices  195 us (60%)
  blocking collectives  41.1 us (13%)
  local copies, waits for them, and re-layouts  23 us (7%)
  loops' own time  20 us (6%)
  between operations  14.4 us (4%)
  matrix products  13.8 us (4%)
  other arithmetic  10.7 us (3%)
  starting transfers between devices  6 us (2%)
    psum x1, waiting for transfers between devices, shards(): summed = lax.psum(window_sum, 'row')  127 us
    unnamed x3, waiting for transfers between devices  67.7 us
    all_gather x1, blocking collectives, shards(): lax.all_gather(coeffs.reshape(clusters, rhs_count * rank_size), 'long', a...  35.3 us
    another operation x1, loops' own time, shards(): window_sum = lax.fori_loop(0, near_count[0], visit_slot, empty_window)  20 us
    another operation x12, other arithmetic  6.81 us
  transfers between devices with their start and end apart: 5, of which 2 were waited for; matrix products, arithmetic and copies ran while one was open for 7% of the time, Pallas kernels for 0%

commit v1 on v0

v1 whole, which is shorter than its diff:
```python
import functools

import jax
import jax.numpy as jnp
from jax import lax
from jax.experimental import pallas as pl
from jax.experimental.pallas import tpu as pltpu
from jax.sharding import PartitionSpec as P

NEARC = 2
LANES = 128
ROWS = 16
PIECES = 3

soften = 0.25

VMEM = pl.BlockSpec(memory_space=pltpu.VMEM)
SMEM = pl.BlockSpec(memory_space=pltpu.SMEM)


def shifted(block, axis, distance):
    devices = range(lax.axis_size(axis))
    route = [(i - distance, i) for i in devices if i - distance in devices]
    return lax.ppermute(block, axis, route)


def lane_gather(table, index):
    length = table.shape[1]
    lane = index & (LANES - 1)
    chunk = index // LANES
    found = jnp.zeros(index.shape, table.dtype)
    for piece_id in range(-(-length // LANES)):
        piece = table[:, piece_id * LANES : min(length, (piece_id + 1) * LANES)]
        missing = LANES - piece.shape[1]
        if missing:
            piece = jnp.concatenate([piece, jnp.zeros((1, missing), table.dtype)], axis=1)
        picked = jnp.take_along_axis(jnp.broadcast_to(piece, index.shape), lane, axis=1)
        found = jnp.where(chunk == piece_id, picked, found)
    return found


def split_three(value):
    high = value.astype(jnp.bfloat16).astype(jnp.float32)
    rest = value - high
    middle = rest.astype(jnp.bfloat16).astype(jnp.float32)
    return [high, middle, rest - middle]


def prepare_kernel(
    slip_ref, basis_ref, vertices_ref, triangles_ref, map_ref, pairs_ref, count_ref, place_ref,
    pay_ref, xs_ref, to_next_ref, to_prev_ref, geom_ref,
):
    clusters, rhs_count, unknowns = slip_ref.shape
    rank_size = basis_ref.shape[1]
    row_index = place_ref[0]
    long_index = place_ref[1]
    xs_ref[...] = slip_ref[...].astype(jnp.bfloat16)

    mine = row_index % clusters
    wide = jnp.concatenate([basis_ref[mine]] * (LANES // rank_size), axis=0)
    coeffs = lax.dot_general(
        xs_ref[mine], wide, (((1,), (1,)), ((), ())), preferred_element_type=jnp.float32
    )
    first = pairs_ref[0:1, :]
    kind = (first - long_index * clusters) * (NEARC + 1) + pairs_ref[1:2, :] - first
    slots = lax.broadcasted_iota(jnp.int32, (rhs_count, kind.shape[1]), 1)
    kinds = lax.broadcasted_iota(jnp.int32, (rhs_count, kind.shape[1]), 0)
    hits = jnp.where((slots < count_ref[0]) & (kinds == kind), 1.0, 0.0)
    counts = jnp.sum(hits, axis=1, keepdims=True)
    lane_id = lax.broadcasted_iota(jnp.int32, (rhs_count, LANES), 1)
    pay = jnp.where(lane_id < LANES - rank_size, coeffs, counts).astype(jnp.bfloat16)
    for target in range(pay_ref.shape[0]):
        pay_ref[target] = pay

    half = map_ref.shape[1] // LANES
    slot_map = map_ref[...]
    index = jnp.concatenate(
        [slot_map[:, part * LANES : (part + 1) * LANES] for part in range(half)], axis=0
    )
    vertex_base = long_index * vertices_ref.shape[1]
    corners = []
    for corner_id in range(3):
        vertex = lane_gather(triangles_ref[corner_id : corner_id + 1, :], index) - vertex_base
        corners.append(
            [lane_gather(vertices_ref[axis_id : axis_id + 1, :], vertex) for axis_id in range(3)]
        )
    one, two, three = corners
    centre = [(one[a] + two[a] + three[a]) / 3.0 for a in range(3)]
    edge_one = [two[a] - one[a] for a in range(3)]
    edge_two = [three[a] - one[a] for a in range(3)]
    normal = [
        edge_one[1] * edge_two[2] - edge_one[2] * edge_two[1],
        edge_one[2] * edge_two[0] - edge_one[0] * edge_two[2],
        edge_one[0] * edge_two[1] - edge_one[1] * edge_two[0],
    ]
    area = 0.5 * jnp.sqrt(normal[0] * normal[0] + normal[1] * normal[1] + normal[2] * normal[2])
    geometry = []
    for part_id, value in enumerate(centre + [area]):
        whole = jnp.concatenate(
            [value[part * clusters : (part + 1) * clusters] for part in range(half)], axis=1
        )
        geom_ref[part_id] = whole
        geometry.extend(split_three(whole))

    size = map_ref.shape[1]
    for out_ref, start in ((to_next_ref, clusters - NEARC), (to_prev_ref, 0)):
        for turn in range(NEARC):
            cluster = start + turn
            rows = [piece[cluster : cluster + 1, :] for piece in geometry]
            rows.append(jnp.zeros((ROWS - len(rows), size), jnp.float32))
            out_ref[turn, 0:rhs_count, :] = xs_ref[cluster]
            out_ref[turn, rhs_count : rhs_count + ROWS, 0:size] = jnp.concatenate(
                rows, axis=0
            ).astype(jnp.bfloat16)
            out_ref[turn, rhs_count : rhs_count + ROWS, size:unknowns] = jnp.zeros(
                (ROWS, unknowns - size), jnp.bfloat16
            )


def near_kernel(xs_ref, geom_ref, prev_ref, next_ref, out_ref, cols_ref, block_ref):
    clusters, rhs_count, unknowns = xs_ref.shape
    size = geom_ref.shape[2]
    window = clusters + 2 * NEARC
    step_rows = ROWS

    def halo_geometry(ref, turn):
        pieces = ref[turn, rhs_count : rhs_count + ROWS, 0:size].astype(jnp.float32)
        return [
            (pieces[3 * p + 2 : 3 * p + 3] + pieces[3 * p + 1 : 3 * p + 2]) + pieces[3 * p : 3 * p + 1]
            for p in range(4)
        ]

    rows = []
    for place in range(window):
        if place < NEARC:
            rows += halo_geometry(prev_ref, place)
        elif place < NEARC + clusters:
            rows += [geom_ref[p, place - NEARC : place - NEARC + 1, :] for p in range(4)]
        else:
            rows += halo_geometry(next_ref, place - NEARC - clusters)
    if len(rows) < LANES:
        rows.append(jnp.zeros((LANES - len(rows), size), jnp.float32))
    cols_ref[...] = jnp.concatenate(rows, axis=0).T

    def slip_of(place):
        if place < NEARC:
            return prev_ref[place, 0:rhs_count, :]
        if place < NEARC + clusters:
            return xs_ref[place - NEARC]
        return next_ref[place - NEARC - clusters, 0:rhs_count, :]

    parts = [(0, 0), (1, 1), (2, 2), (0, 1), (0, 2), (1, 2)]
    for place in range(window):
        targets = [a for a in range(clusters) if abs(a - (place - NEARC)) <= NEARC]

        def fill(step, carry):
            begin = pl.multiple_of(step * step_rows, step_rows)
            here = pl.ds(begin, step_rows)
            column = cols_ref[here, :]
            left = [
                jnp.broadcast_to(column[:, 4 * place + p : 4 * place + p + 1], (step_rows, size))
                for p in range(4)
            ]
            for target in targets:
                right = [geom_ref[p, target : target + 1, :] for p in range(4)]
                offset = [left[p] - right[p] for p in range(3)]
                radius_sq = offset[0] * offset[0] + offset[1] * offset[1] + offset[2] * offset[2]
                inverse = lax.rsqrt(radius_sq + soften)
                weight = left[3] * right[3]
                flat = weight * inverse
                cubed = flat * (inverse * inverse)
                scaled = [offset[p] * cubed for p in range(3)]
                for part_id, (i, j) in enumerate(parts):
                    term = offset[i] * scaled[j]
                    if i == j:
                        term = term + flat
                    block_ref[target, part_id, here, :] = term.astype(jnp.bfloat16)
            return carry

        lax.fori_loop(0, size // step_rows, fill, 0)
        slip = slip_of(place)
        pieces = [slip[:, p * size : (p + 1) * size] for p in range(3)]
        for target in targets:
            sums = [
                jnp.dot(pieces[p], block_ref[target, p], preferred_element_type=jnp.float32)
                for p in range(3)
            ]
            for part_id in range(3, 6):
                i, j = parts[part_id]
                both = jnp.dot(
                    jnp.concatenate([pieces[j], pieces[i]], axis=0),
                    block_ref[target, part_id],
                    preferred_element_type=jnp.float32,
                )
                sums[i] = sums[i] + both[0:rhs_count]
                sums[j] = sums[j] + both[rhs_count : 2 * rhs_count]
            for p in range(3):
                out_ref[target, place - target, :, p * size : (p + 1) * size] = sums[p]


def far_kernel(pairs_ref, coeff_ref, coupling_ref, out_ref, total_ref, *, clusters):
    long_count = total_ref.shape[0]
    rhs_count = coeff_ref.shape[1]
    rank_size = coupling_ref.shape[1]
    groups = LANES // rank_size
    group_id = lax.broadcasted_iota(jnp.int32, (rhs_count, LANES), 1) // rank_size
    total_ref[...] = jnp.zeros(total_ref.shape, jnp.float32)
    results = []
    for pair_id in range(pairs_ref.shape[1]):
        first = pairs_ref[0, pair_id]
        second = pairs_ref[1, pair_id]
        coupling = coupling_ref[pair_id]
        coeff_first = coeff_ref[(first % clusters) * long_count + first // clusters]
        coeff_second = coeff_ref[(second % clusters) * long_count + second // clusters]
        to_first = lax.dot_general(
            coeff_second[:, 0:rank_size],
            jnp.concatenate([coupling] * groups, axis=0),
            (((1,), (1,)), ((), ())),
            preferred_element_type=jnp.float32,
        )
        to_second = jnp.dot(
            coeff_first[:, 0:rank_size],
            jnp.concatenate([coupling] * groups, axis=1),
            preferred_element_type=jnp.float32,
        )
        results.append((first, to_first))
        results.append((second, to_second))
    for cluster, value in results:
        owner = cluster // clusters
        total_ref[owner] += jnp.where(group_id == cluster % clusters, value, 0.0)
    sent = total_ref[...].astype(jnp.bfloat16)
    for copy_id in range(out_ref.shape[0] // long_count):
        out_ref[copy_id * long_count : (copy_id + 1) * long_count] = sent


def finish_kernel(near_ref, pay_ref, far_ref, basis_ref, place_ref, out_ref, *, long_count):
    clusters, rank_size, unknowns = basis_ref.shape
    rhs_count = near_ref.shape[2]
    rows = pay_ref.shape[0] // long_count
    long_index = place_ref[1]
    before = jnp.maximum(long_index - 1, 0)
    own = jnp.zeros(pay_ref.shape[1:], jnp.float32)
    other = jnp.zeros(pay_ref.shape[1:], jnp.float32)
    for row in range(rows):
        own = own + pay_ref[row * long_count + long_index].astype(jnp.float32)
        other = other + pay_ref[row * long_count + before].astype(jnp.float32)
    total = jnp.sum(far_ref[...].astype(jnp.float32), axis=0)
    group_id = lax.broadcasted_iota(jnp.int32, total.shape, 1) // rank_size
    flat_basis = basis_ref[...].reshape(clusters * rank_size, unknowns)
    for cluster in range(clusters):
        picked = jnp.where(group_id == cluster, total, 0.0).astype(jnp.bfloat16)
        result = jnp.dot(picked, flat_basis, preferred_element_type=jnp.float32)
        for turn in range(2 * NEARC + 1):
            reach = turn - NEARC
            if reach >= 0:
                kind, source = cluster * (NEARC + 1) + reach, own
            elif cluster + reach >= 0:
                kind, source = (cluster + reach) * (NEARC + 1) - reach, own
            else:
                kind, source = (cluster + reach + clusters) * (NEARC + 1) - reach, other
            count = source[kind : kind + 1, LANES - 1 : LANES]
            result = result + count * near_ref[cluster, turn]
        out_ref[cluster] = result


def shards(slip, vertices, triangles, elem_map, near_pairs, near_count, far_pairs, far_coef, basis):
    clusters, rhs_count, unknowns = slip.shape
    rank_size = basis.shape[1]
    size = elem_map.shape[1]
    row_count = lax.axis_size("row")
    long_count = lax.axis_size("long")
    devices = row_count * long_count
    place = jnp.stack([lax.axis_index("row"), lax.axis_index("long")]).astype(jnp.int32)
    coupling = far_coef.reshape(-1, rank_size, rank_size)

    halo = jax.ShapeDtypeStruct((NEARC, rhs_count + ROWS, unknowns), jnp.bfloat16)
    pay, xs, to_next, to_prev, geometry = pl.pallas_call(
        prepare_kernel,
        out_shape=[
            jax.ShapeDtypeStruct((devices, rhs_count, LANES), jnp.bfloat16),
            jax.ShapeDtypeStruct(slip.shape, jnp.bfloat16),
            halo,
            halo,
            jax.ShapeDtypeStruct((4, clusters, size), jnp.float32),
        ],
        in_specs=[VMEM] * 6 + [SMEM] * 2,
        out_specs=[VMEM] * 5,
        compiler_params=pltpu.CompilerParams(vmem_limit_bytes=16 << 20),
        name="prepare",
    )(slip, basis, vertices, triangles, elem_map, near_pairs, near_count, place)

    everyone = lax.all_to_all(pay, ("row", "long"), 0, 0, tiled=True)
    from_prev = shifted(to_next, "long", 1)
    from_next = shifted(to_prev, "long", -1)

    near = pl.pallas_call(
        near_kernel,
        out_shape=jax.ShapeDtypeStruct((clusters, 2 * NEARC + 1, rhs_count, unknowns), jnp.float32),
        in_specs=[VMEM] * 4,
        out_specs=VMEM,
        scratch_shapes=[
            pltpu.VMEM((size, LANES), jnp.float32),
            pltpu.VMEM((clusters, 6, size, size), jnp.bfloat16),
        ],
        compiler_params=pltpu.CompilerParams(vmem_limit_bytes=24 << 20),
        cost_estimate=pl.CostEstimate(flops=40_000_000, bytes_accessed=2_000_000, transcendentals=1_300_000),
        name="near",
    )(xs, geometry, from_prev, from_next)

    far = pl.pallas_call(
        functools.partial(far_kernel, clusters=clusters),
        out_shape=jax.ShapeDtypeStruct((devices, rhs_count, clusters * rank_size), jnp.bfloat16),
        in_specs=[SMEM, VMEM, VMEM],
        out_specs=VMEM,
        scratch_shapes=[pltpu.VMEM((long_count, rhs_count, clusters * rank_size), jnp.float32)],
        compiler_params=pltpu.CompilerParams(vmem_limit_bytes=16 << 20),
        name="far",
    )(far_pairs, everyone, coupling)
    far_terms = lax.all_to_all(far, ("row", "long"), 0, 0, tiled=True)

    return pl.pallas_call(
        functools.partial(finish_kernel, long_count=long_count),
        out_shape=jax.ShapeDtypeStruct(slip.shape, jnp.float32),
        in_specs=[VMEM] * 4 + [SMEM],
        out_specs=VMEM,
        compiler_params=pltpu.CompilerParams(vmem_limit_bytes=16 << 20),
        name="finish",
    )(near, everyone, far_terms, basis, place)


def solution(mesh):
    placed = (
        P("long", None, None),
        P(None, "long"),
        P(None, "long"),
        P("long", None),
        P(None, ("row", "long")),
        P(("row", "long")),
        P(None, ("row", "long")),
        P(("row", "long"), None),
        P("long", None, None),
    )
    return jax.shard_map(
        shards, mesh=mesh, in_specs=placed, out_specs=P("long", None, None), check_vma=False
    )
```

time: 326 us -> 55.9 us (0.17)
  waiting for transfers between devices: 195 us -> 12.8 us
  blocking collectives: 41.1 us -> 0 us
  Pallas kernels: 0 us -> 23.1 us
  loops' own time: 20 us -> 0 us
  local copies, waits for them, and re-layouts: 23 us -> 4.01 us
  matrix products: 13.8 us -> 0 us
  between operations: 14.4 us -> 0.74 us
  other arithmetic: 10.7 us -> 0.08 us
  starting transfers between devices: 6 us -> 14.7 us
    psum x1 -> x0, waiting for transfers between devices: 127 us -> none  [shards(): summed = lax.psum(window_sum, 'row')]
    unnamed x3 -> x0, waiting for transfers between devices: 67.7 us -> none
    all_gather x1 -> x0, blocking collectives: 35.3 us -> none  [shards(): lax.all_gather(coeffs.reshape(clusters, rhs_count * rank_size), 'long', a...]
    pallas_call x0 -> x4, Pallas kernels: none -> 23.1 us  [the longest x1 18.5 us: shards(): pl.pallas_call(near_kernel, out_shape=jax.ShapeDtypeStruct((clusters, 2 *...]
    another operation x1 -> x0, loops' own time: 20 us -> none  [shards(): window_sum = lax.fori_loop(0, near_count[0], visit_slot, empty_window)]
    dot_general x18 -> x0, matrix products: 13.8 us -> none  [the longest x6 5.89 us: apply_pair(): lax.dot_general(window_slip[local_b], block, (((1,), (1,)), ((), ())), pr...]
    gather x10 -> x0, local copies, waits for them, and re-layouts: 13.2 us -> none  [the longest x2 3 us: element_geometry(): corner_one = vertices[:, triangles[0]]]
    all_to_all x0 -> x2, starting transfers between devices: none -> 9.87 us  [the longest x1 7.3 us: shards(): everyone = lax.all_to_all(pay, ('row', 'long'), 0, 0, tiled=True)]
  transfers between devices with their start and end apart: 5 -> 4, of which waited for: 2 -> 3; matrix products, arithmetic and copies ran while one was open for 7% -> 0% of each run, Pallas kernels for 0% -> 33%
where the time goes in v1:
time: 55.9 us; the launch traced here: 55.4 us
  Pallas kernels  23.1 us (41%)
  starting transfers between devices  14.7 us (26%)
  waiting for transfers between devices  12.8 us (23%)
  local copies, waits for them, and re-layouts  4.01 us (7%)
  between operations  0.74 us (1%)
    pallas_call x1, Pallas kernels, shards(): pl.pallas_call(near_kernel, out_shape=jax.ShapeDtypeStruct((clusters, 2 *...  18.5 us
    all_to_all x1, waiting for transfers between devices, shards(): everyone = lax.all_to_all(pay, ('row', 'long'), 0, 0, tiled=True)  7.56 us
    all_to_all x1, starting transfers between devices, shards(): everyone = lax.all_to_all(pay, ('row', 'long'), 0, 0, tiled=True)  7.3 us
    ppermute x2, waiting for transfers between devices, shifted(): return lax.ppermute(block, axis, route)  5.21 us
    ppermute x2, starting transfers between devices, shifted(): return lax.ppermute(block, axis, route)  4.85 us
    unnamed x18, local copies, waits for them, and re-layouts  3.86 us
    all_to_all x1, starting transfers between devices, shards(): far_terms = lax.all_to_all(far, ('row', 'long'), 0, 0, tiled=True)  2.58 us
    pallas_call x1, Pallas kernels, shards(): pl.pallas_call(functools.partial(far_kernel, clusters=clusters), out_shap...  1.76 us
  transfers between devices with their start and end apart: 4, of which 3 were waited for; matrix products, arithmetic and copies ran while one was open for 0% of the time, Pallas kernels for 33%

profile of v1, /device:TPU:0, one launch (start us, length us, event | category | flops | bytes accessed | tf_op | source)
XLA Modules:
  0.0 55.4 jit_solution(13004661465316348402)
XLA Ops:
  0.0 0.0 copy-start.3
  0.7 0.0 copy-start.7
  0.7 0.1 pad_add_fusion.place_ref
  0.7 0.0 copy-done.3
  0.8 0.6 %copy-done.7 = s32[2,20]{1,0:T(2,128)S(1)} copy-done((s32[2,20]{1,0:T(2,128)S(1)}, s32[2,20]{1,0:T(2,128)}, u32[]{:S(2)}) %copy-start.7) | copy-done | bytes 184
  1.3 0.0 copy-start
  1.3 0.9 %copy-done = bf16[4,32,768]{2,1,0:T(8,128)(2,1)S(1)} copy-done((bf16[4,32,768]{2,1,0:T(8,128)(2,1)S(1)}, bf16[4,32,768]{2,1,0:T(8,128)(2,1)}, u32[]{:S(2)}) %copy-start) | copy-done | bytes 196632
  2.3 0.0 copy-start.2
  2.3 0.9 %copy-done.2 = f32[4,16,768]{2,1,0:T(8,128)S(1)} copy-done((f32[4,16,768]{2,1,0:T(8,128)S(1)}, f32[4,16,768]{2,1,0:T(8,128)}, u32[]{:S(2)}) %copy-start.2) | copy-done | bytes 196632
  3.2 0.0 copy-start.4
  3.2 0.7 %copy-done.4 = f32[3,561]{1,0:T(4,128)S(1)} copy-done((f32[3,561]{1,0:T(4,128)S(1)}, f32[3,561]{1,0:T(4,128)}, u32[]{:S(2)}) %copy-start.4) | copy-done | bytes 6756
  3.9 0.0 copy-start.5
  3.9 0.7 %copy-done.5 = s32[4,256]{1,0:T(4,128)S(1)} copy-done((s32[4,256]{1,0:T(4,128)S(1)}, s32[4,256]{1,0:T(4,128)}, u32[]{:S(2)}) %copy-start.5) | copy-done | bytes 4120
  4.6 1.4 %prepare.1 = (bf16[32,16,128]{2,1,0:T(8,128)(2,1)}, bf16[4,16,768]{2,1,0:T(8,128)(2,1)S(1)}, bf16[2,32,768]{2,1,0:T(8,128)(2,1)S(1)}, bf16[2,32,768]{2,1,0:T(8,128)(2,1)S(1)}, f32[4,4,256]{2,1,0:T(4,128)S(1)}) custom-call(f32[4,16,768]{2,1,0:T(8,128)S(1)} %copy-done.2, bf16[4,32,768]{2,1,0:T(8,128)(2,1)S(1)} %copy-done, f32[3,561]{1,0:T(4,128)S(1)} %copy-done.4, ...), custom_call_target="tpu_custom_call" | custom-call | tf_op jit(solution)/shard_map/prepare/pallas_call | solution.py:277
  6.0 0.0 copy-start.8
  6.0 7.3 %all-to-all-start = ((bf16[32,16,128]{2,1,0:T(8,128)(2,1)}), bf16[32,16,128]{2,1,0:T(8,128)(2,1)S(1)}, u32[]{:S(2)}, u32[]{:S(2)}) async-start(bf16[32,16,128]{2,1,0:T(8,128)(2,1)} %get-tuple-element.14), calls=%async_computation | async-start | bytes 262144 | tf_op jit(solution)/shard_map/all_to_all | solution.py:292
  13.3 0.0 copy-done.8
  13.3 0.0 copy-start.6
  13.3 0.1 reshape.3.coupling_ref
  13.5 7.6 %all-to-all-done.coeff_ref.pay_ref = bf16[32,16,128]{2,1,0:T(8,128)(2,1)S(1)} async-done(((bf16[32,16,128]{2,1,0:T(8,128)(2,1)}), bf16[32,16,128]{2,1,0:T(8,128)(2,1)S(1)}, u32[]{:S(2)}, u32[]{:S(2)}) %all-to-all-start) | async-done | bytes 131104 | tf_op jit(solution)/shard_map/all_to_all | solution.py:292
  21.0 0.0 copy-done.6
  21.0 1.8 %far.1 = bf16[32,16,128]{2,1,0:T(8,128)(2,1)} custom-call(s32[2,16]{1,0:T(2,128)S(1)} %copy-done.6, bf16[32,16,128]{2,1,0:T(8,128)(2,1)S(1)} %all-to-all-done.coeff_ref.pay_ref, bf16[16,32,32]{2,1,0:T(8,128)(2,1)S(1)} %reshape.3.coupling_ref), custom_call_target="tpu_custom_call" | custom-call | tf_op jit(solution)/shard_map/far/pallas_call | solution.py:310
  22.8 2.6 %all-to-all-start.1 = ((bf16[32,16,128]{2,1,0:T(8,128)(2,1)}), bf16[32,16,128]{2,1,0:T(8,128)(2,1)S(1)}, u32[]{:S(2)}, u32[]{:S(2)}) async-start(bf16[32,16,128]{2,1,0:T(8,128)(2,1)} %far.1), calls=%async_computation.1 | async-start | bytes 262144 | tf_op jit(solution)/shard_map/all_to_all | solution.py:319
  25.4 3.6 %collective-permute-start = (bf16[2,32,768]{2,1,0:T(8,128)(2,1)S(1)}, bf16[2,32,768]{2,1,0:T(8,128)(2,1)S(1)}, u32[]{:S(2)}, u32[]{:S(2)}) collective-permute-start(bf16[2,32,768]{2,1,0:T(8,128)(2,1)S(1)} %get-tuple-element.12), channel_id=1, source_target_pairs={{0,1},{1,2},{2,3},{3,4},{4,5},{5,6},{6,7},{8,9},{9,10},{10,11},{11... | collective-permute-start | bytes 294920 | tf_op jit(solution)/shard_map/ppermute | solution.py:24
  29.0 1.3 %collective-permute-start.1 = (bf16[2,32,768]{2,1,0:T(8,128)(2,1)S(1)}, bf16[2,32,768]{2,1,0:T(8,128)(2,1)S(1)}, u32[]{:S(2)}, u32[]{:S(2)}) collective-permute-start(bf16[2,32,768]{2,1,0:T(8,128)(2,1)S(1)} %get-tuple-element.13), channel_id=1, source_target_pairs={{1,0},{2,1},{3,2},{4,3},{5,4},{6,5},{7,6},{9,8},{10,9},{11,10},{12... | collective-permute-start | bytes 294920 | tf_op jit(solution)/shard_map/ppermute | solution.py:24
  30.3 1.6 %collective-permute-done.prev_ref = bf16[2,32,768]{2,1,0:T(8,128)(2,1)S(1)} collective-permute-done((bf16[2,32,768]{2,1,0:T(8,128)(2,1)S(1)}, bf16[2,32,768]{2,1,0:T(8,128)(2,1)S(1)}, u32[]{:S(2)}, u32[]{:S(2)}) %collective-permute-start) | collective-permute-done | bytes 98336 | tf_op jit(solution)/shard_map/ppermute | solution.py:24
  31.9 3.6 %collective-permute-done.1.next_ref = bf16[2,32,768]{2,1,0:T(8,128)(2,1)S(1)} collective-permute-done((bf16[2,32,768]{2,1,0:T(8,128)(2,1)S(1)}, bf16[2,32,768]{2,1,0:T(8,128)(2,1)S(1)}, u32[]{:S(2)}, u32[]{:S(2)}) %collective-permute-start.1) | collective-permute-done | bytes 98336 | tf_op jit(solution)/shard_map/ppermute | solution.py:24
  35.5 0.0 copy-start.1
  35.5 18.5 %near.1.near_ref = f32[4,5,16,768]{3,2,1,0:T(8,128)S(1)} custom-call(bf16[4,16,768]{2,1,0:T(8,128)(2,1)S(1)} %get-tuple-element.10.xs_ref, f32[4,4,256]{2,1,0:T(4,128)S(1)} %get-tuple-element.11.geom_ref, bf16[2,32,768]{2,1,0:T(8,128)(2,1)S(1)} %collective-permute-done.prev_ref, bf16[2,32,768]{2,1,0:T(8,128)(2,1)S(1)} %collective-permute-done.1.next_ref), custom_call_target="tpu_custom_call" | custom-call | flops 40000000 | bytes 2000000 | tf_op jit(solution)/shard_map/near/pallas_call | solution.py:296
  53.9 0.0 all-to-all-done.1.far_ref
  53.9 0.0 copy-done.1
  54.0 1.5 %finish.1 = f32[4,16,768]{2,1,0:T(8,128)} custom-call(f32[4,5,16,768]{3,2,1,0:T(8,128)S(1)} %near.1.near_ref, bf16[32,16,128]{2,1,0:T(8,128)(2,1)S(1)} %all-to-all-done.coeff_ref.pay_ref, bf16[32,16,128]{2,1,0:T(8,128)(2,1)S(1)} %all-to-all-done.1.far_ref, bf16[4,32,768]{2,1,0:T(8,128)(2,1)S(1)} %copy-done.1, s32[2]{0:T(128)S(1)} %pad_add_fusion.place_ref), custom_call_target="tpu_custom_call" | custom-call | tf_op jit(solution)/shard_map/finish/pallas_call | solution.py:321
Async XLA Ops:
  0.0 0.7 %copy-start.3 = (s32[3,1024]{1,0:T(4,128)S(1)}, s32[3,1024]{1,0:T(4,128)}, u32[]{:S(2)}) copy-start(s32[3,1024]{1,0:T(4,128)} %triangles_ref.1) | copy-start | bytes 36868
  0.7 0.7 %copy-start.7 = (s32[2,20]{1,0:T(2,128)S(1)}, s32[2,20]{1,0:T(2,128)}, u32[]{:S(2)}) copy-start(s32[2,20]{1,0:T(2,128)} %pairs_ref.2) | copy-start | bytes 484
  1.3 0.9 %copy-start = (bf16[4,32,768]{2,1,0:T(8,128)(2,1)S(1)}, bf16[4,32,768]{2,1,0:T(8,128)(2,1)}, u32[]{:S(2)}) copy-start(bf16[4,32,768]{2,1,0:T(8,128)(2,1)} %basis_ref.3) | copy-start | bytes 589828
  2.3 0.9 %copy-start.2 = (f32[4,16,768]{2,1,0:T(8,128)S(1)}, f32[4,16,768]{2,1,0:T(8,128)}, u32[]{:S(2)}) copy-start(f32[4,16,768]{2,1,0:T(8,128)} %slip_ref.1) | copy-start | bytes 589828
  3.2 0.7 %copy-start.4 = (f32[3,561]{1,0:T(4,128)S(1)}, f32[3,561]{1,0:T(4,128)}, u32[]{:S(2)}) copy-start(f32[3,561]{1,0:T(4,128)} %vertices_ref.1) | copy-start | bytes 20200
  3.9 0.7 %copy-start.5 = (s32[4,256]{1,0:T(4,128)S(1)}, s32[4,256]{1,0:T(4,128)}, u32[]{:S(2)}) copy-start(s32[4,256]{1,0:T(4,128)} %map_ref.1) | copy-start | bytes 12292
  6.0 7.3 %copy-start.8 = (bf16[16,1024]{1,0:T(8,128)(2,1)S(1)}, bf16[16,1024]{1,0:T(8,128)(2,1)}, u32[]{:S(2)}) copy-start(bf16[16,1024]{1,0:T(8,128)(2,1)} %param.16) | copy-start | bytes 98308
  6.0 15.0 %all-to-all-start = ((bf16[32,16,128]{2,1,0:T(8,128)(2,1)}), bf16[32,16,128]{2,1,0:T(8,128)(2,1)S(1)}, u32[]{:S(2)}, u32[]{:S(2)}) async-start(bf16[32,16,128]{2,1,0:T(8,128)(2,1)} %get-tuple-element.14), calls=%async_computation | async-start | bytes 262144 | tf_op jit(solution)/shard_map/all_to_all | solution.py:292
  13.3 7.7 %copy-start.6 = (s32[2,16]{1,0:T(2,128)S(1)}, s32[2,16]{1,0:T(2,128)}, u32[]{:S(2)}) copy-start(s32[2,16]{1,0:T(2,128)} %pairs_ref.3) | copy-start | bytes 388
  22.8 31.1 %all-to-all-start.1 = ((bf16[32,16,128]{2,1,0:T(8,128)(2,1)}), bf16[32,16,128]{2,1,0:T(8,128)(2,1)S(1)}, u32[]{:S(2)}, u32[]{:S(2)}) async-start(bf16[32,16,128]{2,1,0:T(8,128)(2,1)} %far.1), calls=%async_computation.1 | async-start | bytes 262144 | tf_op jit(solution)/shard_map/all_to_all | solution.py:319
  25.4 6.5 %collective-permute-start = (bf16[2,32,768]{2,1,0:T(8,128)(2,1)S(1)}, bf16[2,32,768]{2,1,0:T(8,128)(2,1)S(1)}, u32[]{:S(2)}, u32[]{:S(2)}) collective-permute-start(bf16[2,32,768]{2,1,0:T(8,128)(2,1)S(1)} %get-tuple-element.12), channel_id=1, source_target_pairs={{0,1},{1,2},{2,3},{3,4},{4,5},{5,6},{6,7},{8,9},{9,10},{10,11},{11... | collective-permute-start | bytes 294920 | tf_op jit(solution)/shard_map/ppermute | solution.py:24
  29.0 6.5 %collective-permute-start.1 = (bf16[2,32,768]{2,1,0:T(8,128)(2,1)S(1)}, bf16[2,32,768]{2,1,0:T(8,128)(2,1)S(1)}, u32[]{:S(2)}, u32[]{:S(2)}) collective-permute-start(bf16[2,32,768]{2,1,0:T(8,128)(2,1)S(1)} %get-tuple-element.13), channel_id=1, source_target_pairs={{1,0},{2,1},{3,2},{4,3},{5,4},{6,5},{7,6},{9,8},{10,9},{11,10},{12... | collective-permute-start | bytes 294920 | tf_op jit(solution)/shard_map/ppermute | solution.py:24
  35.5 18.5 %copy-start.1 = (bf16[4,32,768]{2,1,0:T(8,128)(2,1)S(1)}, bf16[4,32,768]{2,1,0:T(8,128)(2,1)}, u32[]{:S(2)}) copy-start(bf16[4,32,768]{2,1,0:T(8,128)(2,1)} %basis_ref.3) | copy-start | bytes 589828

commit v2 on v1

v2 whole, which is shorter than its diff:
```python
import functools

import jax
import jax.numpy as jnp
from jax import lax
from jax.experimental import pallas as pl
from jax.experimental.pallas import tpu as pltpu
from jax.sharding import PartitionSpec as P

NEARC = 2
LANES = 128
ROWS = 16
PIECES = 3

soften = 0.25

VMEM = pl.BlockSpec(memory_space=pltpu.VMEM)
SMEM = pl.BlockSpec(memory_space=pltpu.SMEM)
HBM = pl.BlockSpec(memory_space=pltpu.HBM)


def lane_gather(table, index):
    length = table.shape[1]
    lane = index & (LANES - 1)
    chunk = index // LANES
    found = jnp.zeros(index.shape, table.dtype)
    for piece_id in range(-(-length // LANES)):
        piece = table[:, piece_id * LANES : min(length, (piece_id + 1) * LANES)]
        missing = LANES - piece.shape[1]
        if missing:
            piece = jnp.concatenate([piece, jnp.zeros((1, missing), table.dtype)], axis=1)
        picked = jnp.take_along_axis(jnp.broadcast_to(piece, index.shape), lane, axis=1)
        found = jnp.where(chunk == piece_id, picked, found)
    return found


def split_three(value):
    high = value.astype(jnp.bfloat16).astype(jnp.float32)
    rest = value - high
    middle = rest.astype(jnp.bfloat16).astype(jnp.float32)
    return [high, middle, rest - middle]


def prepare_kernel(
    slip_hbm, basis_hbm, vertices_hbm, triangles_hbm, map_hbm, pairs_hbm, count_ref,
    pay_ref, xs_ref, halo_ref, geom_ref,
    slip_ref, basis_ref, vertices_ref, triangles_ref, map_ref, pairs_ref, sems,
):
    sources = (slip_hbm, basis_hbm, vertices_hbm, triangles_hbm, map_hbm, pairs_hbm)
    targets = (slip_ref, basis_ref, vertices_ref, triangles_ref, map_ref, pairs_ref)
    copies = [
        pltpu.make_async_copy(source, target, sems.at[place])
        for place, (source, target) in enumerate(zip(sources, targets))
    ]
    for copy in copies:
        copy.start()
    clusters, rhs_count, unknowns = slip_ref.shape
    rank_size = basis_ref.shape[1]
    row_index = lax.axis_index("row")
    long_index = lax.axis_index("long")
    mine = row_index % clusters
    for copy in copies:
        copy.wait()

    size = map_ref.shape[1]
    half = size // LANES
    slot_map = map_ref[...]
    index = jnp.concatenate(
        [slot_map[:, part * LANES : (part + 1) * LANES] for part in range(half)], axis=0
    )
    vertex_base = long_index * vertices_ref.shape[1]
    corners = []
    for corner_id in range(3):
        vertex = lane_gather(triangles_ref[corner_id : corner_id + 1, :], index) - vertex_base
        corners.append(
            [lane_gather(vertices_ref[axis_id : axis_id + 1, :], vertex) for axis_id in range(3)]
        )
    one, two, three = corners
    centre = [(one[a] + two[a] + three[a]) / 3.0 for a in range(3)]
    edge_one = [two[a] - one[a] for a in range(3)]
    edge_two = [three[a] - one[a] for a in range(3)]
    normal = [
        edge_one[1] * edge_two[2] - edge_one[2] * edge_two[1],
        edge_one[2] * edge_two[0] - edge_one[0] * edge_two[2],
        edge_one[0] * edge_two[1] - edge_one[1] * edge_two[0],
    ]
    area = 0.5 * jnp.sqrt(normal[0] * normal[0] + normal[1] * normal[1] + normal[2] * normal[2])
    geometry = []
    for value in centre + [area]:
        geometry.append(
            jnp.concatenate(
                [value[part * clusters : (part + 1) * clusters] for part in range(half)], axis=1
            )
        )
    for cluster in range(clusters):
        geom_ref[cluster] = jnp.concatenate(
            [whole[cluster : cluster + 1, :] for whole in geometry], axis=0
        )

    xs_ref[...] = slip_ref[...].astype(jnp.bfloat16)
    wide = jnp.concatenate([basis_ref[mine]] * (LANES // rank_size), axis=0)
    coeffs = lax.dot_general(
        xs_ref[mine], wide, (((1,), (1,)), ((), ())), preferred_element_type=jnp.float32
    )
    first = pairs_ref[0:1, :]
    kind = (first - long_index * clusters) * (NEARC + 1) + pairs_ref[1:2, :] - first
    slots = lax.broadcasted_iota(jnp.int32, (rhs_count, kind.shape[1]), 1)
    kinds = lax.broadcasted_iota(jnp.int32, (rhs_count, kind.shape[1]), 0)
    hits = jnp.where((slots < count_ref[0]) & (kinds == kind), 1.0, 0.0)
    counts = jnp.sum(hits, axis=1, keepdims=True)
    lane_id = lax.broadcasted_iota(jnp.int32, (rhs_count, LANES), 1)
    pay = jnp.where(lane_id < LANES - rank_size, coeffs, counts).astype(jnp.bfloat16)
    for target in range(pay_ref.shape[0]):
        pay_ref[target] = pay

    upward = mine < NEARC
    start = jnp.where(upward, clusters - NEARC, 0)
    pieces = [piece for whole in geometry for piece in split_three(whole)]
    for turn in range(NEARC):
        last = clusters - NEARC + turn
        rows = [
            jnp.where(upward, piece[last : last + 1, :], piece[turn : turn + 1, :])
            for piece in pieces
        ]
        rows.append(jnp.zeros((ROWS - len(rows), size), jnp.float32))
        halo_ref[turn, 0:rhs_count, :] = xs_ref[start + turn]
        halo_ref[turn, rhs_count : rhs_count + ROWS, 0:size] = jnp.concatenate(
            rows, axis=0
        ).astype(jnp.bfloat16)
        halo_ref[turn, rhs_count : rhs_count + ROWS, size:unknowns] = jnp.zeros(
            (ROWS, unknowns - size), jnp.bfloat16
        )


def near_kernel(xs_ref, geom_ref, halo_ref, out_ref, slip_ref, place_ref, cols_ref, block_ref):
    clusters, rhs_count, unknowns = xs_ref.shape
    size = geom_ref.shape[2]
    slots = clusters + NEARC
    mine = lax.axis_index("row") % clusters
    reaches = 2 * NEARC + 1
    where_at = [(mine - NEARC + turn + slots) % slots for turn in range(reaches)]

    slip_ref[0:clusters] = xs_ref[...]
    place_ref[0:clusters] = geom_ref[...]
    for turn in range(NEARC):
        slip_ref[clusters + turn] = halo_ref[turn, 0:rhs_count, :]
        pieces = halo_ref[turn, rhs_count : rhs_count + ROWS, 0:size].astype(jnp.float32)
        place_ref[clusters + turn] = jnp.concatenate(
            [
                (pieces[3 * p + 2 : 3 * p + 3] + pieces[3 * p + 1 : 3 * p + 2])
                + pieces[3 * p : 3 * p + 1]
                for p in range(4)
            ],
            axis=0,
        )
    rows = [place_ref[at] for at in where_at]
    rows.append(jnp.zeros((LANES - 4 * reaches, size), jnp.float32))
    cols_ref[...] = jnp.concatenate(rows, axis=0).T
    parts = [(0, 0), (1, 1), (2, 2), (0, 1), (0, 2), (1, 2)]

    def fill(step, carry):
        here = pl.ds(pl.multiple_of(step * ROWS, ROWS), ROWS)
        column = cols_ref[here, :]
        right = [place_ref[mine, p : p + 1, :] for p in range(4)]
        for turn in range(reaches):
            left = [
                jnp.broadcast_to(column[:, 4 * turn + p : 4 * turn + p + 1], (ROWS, size))
                for p in range(4)
            ]
            offset = [left[p] - right[p] for p in range(3)]
            radius_sq = offset[0] * offset[0] + offset[1] * offset[1] + offset[2] * offset[2]
            inverse = lax.rsqrt(radius_sq + soften)
            flat = (left[3] * right[3]) * inverse
            cubed = flat * (inverse * inverse)
            scaled = [offset[p] * cubed for p in range(3)]
            for part_id, (i, j) in enumerate(parts):
                term = offset[i] * scaled[j]
                if i == j:
                    term = term + flat
                block_ref[turn, part_id, here, :] = term.astype(jnp.bfloat16)
        return carry

    lax.fori_loop(0, size // ROWS, fill, 0)
    for turn in range(reaches):
        slip = slip_ref[where_at[turn]]
        pieces = [slip[:, p * size : (p + 1) * size] for p in range(3)]
        sums = [
            jnp.dot(pieces[p], block_ref[turn, p], preferred_element_type=jnp.float32)
            for p in range(3)
        ]
        for part_id in range(3, 6):
            i, j = parts[part_id]
            both = jnp.dot(
                jnp.concatenate([pieces[j], pieces[i]], axis=0),
                block_ref[turn, part_id],
                preferred_element_type=jnp.float32,
            )
            sums[i] = sums[i] + both[0:rhs_count]
            sums[j] = sums[j] + both[rhs_count : 2 * rhs_count]
        for p in range(3):
            out_ref[turn, :, p * size : (p + 1) * size] = sums[p]


def far_kernel(pairs_ref, coeff_ref, coupling_ref, near_ref, out_ref, own_ref, total_ref, *, clusters):
    long_count = total_ref.shape[0]
    rhs_count = coeff_ref.shape[1]
    rank_size = coupling_ref.shape[1]
    groups = LANES // rank_size
    group_id = lax.broadcasted_iota(jnp.int32, (rhs_count, LANES), 1) // rank_size
    total_ref[...] = jnp.zeros(total_ref.shape, jnp.float32)
    results = []
    for pair_id in range(pairs_ref.shape[1]):
        first = pairs_ref[0, pair_id]
        second = pairs_ref[1, pair_id]
        coupling = coupling_ref[pair_id]
        coeff_first = coeff_ref[(first % clusters) * long_count + first // clusters]
        coeff_second = coeff_ref[(second % clusters) * long_count + second // clusters]
        to_first = lax.dot_general(
            coeff_second[:, 0:rank_size],
            jnp.concatenate([coupling] * groups, axis=0),
            (((1,), (1,)), ((), ())),
            preferred_element_type=jnp.float32,
        )
        to_second = jnp.dot(
            coeff_first[:, 0:rank_size],
            jnp.concatenate([coupling] * groups, axis=1),
            preferred_element_type=jnp.float32,
        )
        results.append((first, to_first))
        results.append((second, to_second))
    for cluster, value in results:
        owner = cluster // clusters
        total_ref[owner] += jnp.where(group_id == cluster % clusters, value, 0.0)
    sent = total_ref[...].astype(jnp.bfloat16)
    for copy_id in range(out_ref.shape[0] // long_count):
        out_ref[copy_id * long_count : (copy_id + 1) * long_count] = sent

    long_index = lax.axis_index("long")
    mine = lax.axis_index("row") % clusters
    before = jnp.maximum(long_index - 1, 0)
    own = jnp.zeros(coeff_ref.shape[1:], jnp.float32)
    other = jnp.zeros(coeff_ref.shape[1:], jnp.float32)
    for row in range(coeff_ref.shape[0] // long_count):
        own = own + coeff_ref[row * long_count + long_index].astype(jnp.float32)
        other = other + coeff_ref[row * long_count + before].astype(jnp.float32)
    kinds = lax.broadcasted_iota(jnp.int32, own.shape, 0)
    result = jnp.zeros(own_ref.shape[1:], jnp.float32)
    for turn in range(near_ref.shape[0]):
        reach = turn - NEARC
        lower = mine + min(reach, 0)
        inside = lower >= 0
        kind = jnp.where(inside, lower, lower + clusters) * (NEARC + 1) + abs(reach)
        source = jnp.where(kinds == kind, jnp.where(inside, own, other), 0.0)
        count = jnp.sum(source, axis=0, keepdims=True)[:, LANES - 1 : LANES]
        result = result + count * near_ref[turn]
    result = result.astype(own_ref.dtype)
    for target in range(own_ref.shape[0]):
        own_ref[target] = result


def finish_kernel(near_ref, far_ref, basis_ref, out_ref):
    clusters, rank_size, unknowns = basis_ref.shape
    total = jnp.sum(far_ref[...].astype(jnp.float32), axis=0)
    group_id = lax.broadcasted_iota(jnp.int32, total.shape, 1) // rank_size
    flat_basis = basis_ref[...].reshape(clusters * rank_size, unknowns)
    for cluster in range(clusters):
        picked = jnp.where(group_id == cluster, total, 0.0).astype(jnp.bfloat16)
        result = jnp.dot(picked, flat_basis, preferred_element_type=jnp.float32)
        out_ref[cluster] = result + near_ref[cluster].astype(jnp.float32)


def shards(slip, vertices, triangles, elem_map, near_pairs, near_count, far_pairs, far_coef, basis):
    clusters, rhs_count, unknowns = slip.shape
    rank_size = basis.shape[1]
    size = elem_map.shape[1]
    row_count = lax.axis_size("row")
    long_count = lax.axis_size("long")
    devices = row_count * long_count
    coupling = far_coef.reshape(-1, rank_size, rank_size)
    reaches = 2 * NEARC + 1

    pay, xs, to_neighbour, geometry = pl.pallas_call(
        prepare_kernel,
        out_shape=[
            jax.ShapeDtypeStruct((devices, rhs_count, LANES), jnp.bfloat16),
            jax.ShapeDtypeStruct(slip.shape, jnp.bfloat16),
            jax.ShapeDtypeStruct((NEARC, rhs_count + ROWS, unknowns), jnp.bfloat16),
            jax.ShapeDtypeStruct((clusters, 4, size), jnp.float32),
        ],
        in_specs=[HBM] * 6 + [SMEM],
        out_specs=[VMEM] * 4,
        scratch_shapes=[
            pltpu.VMEM(slip.shape, slip.dtype),
            pltpu.VMEM(basis.shape, basis.dtype),
            pltpu.VMEM(vertices.shape, vertices.dtype),
            pltpu.VMEM(triangles.shape, triangles.dtype),
            pltpu.VMEM(elem_map.shape, elem_map.dtype),
            pltpu.VMEM(near_pairs.shape, near_pairs.dtype),
            pltpu.SemaphoreType.DMA((6,)),
        ],
        compiler_params=pltpu.CompilerParams(vmem_limit_bytes=16 << 20),
        name="prepare",
    )(
        *[
            pltpu.with_memory_space_constraint(array, pltpu.HBM)
            for array in (slip, basis, vertices, triangles, elem_map, near_pairs)
        ],
        near_count,
    )

    everyone = lax.all_to_all(pay, ("row", "long"), 0, 0, tiled=True)
    route = []
    for row in range(row_count):
        step = 1 if row % clusters < NEARC else -1
        for owner in range(long_count):
            if 0 <= owner - step < long_count:
                route.append((row * long_count + owner - step, row * long_count + owner))
    halo = lax.ppermute(to_neighbour, ("row", "long"), route)

    near = pl.pallas_call(
        near_kernel,
        out_shape=jax.ShapeDtypeStruct((reaches, rhs_count, unknowns), jnp.float32),
        in_specs=[VMEM] * 3,
        out_specs=VMEM,
        scratch_shapes=[
            pltpu.VMEM((clusters + NEARC, rhs_count, unknowns), jnp.bfloat16),
            pltpu.VMEM((clusters + NEARC, 4, size), jnp.float32),
            pltpu.VMEM((size, LANES), jnp.float32),
            pltpu.VMEM((reaches, 6, size, size), jnp.bfloat16),
        ],
        compiler_params=pltpu.CompilerParams(vmem_limit_bytes=24 << 20),
        cost_estimate=pl.CostEstimate(
            flops=500_000_000, bytes_accessed=1_000_000, transcendentals=330_000
        ),
        name="near",
    )(xs, geometry, halo)

    far, own = pl.pallas_call(
        functools.partial(far_kernel, clusters=clusters),
        out_shape=[
            jax.ShapeDtypeStruct((devices, rhs_count, clusters * rank_size), jnp.bfloat16),
            jax.ShapeDtypeStruct((row_count, rhs_count, unknowns), jnp.float32),
        ],
        in_specs=[SMEM, VMEM, VMEM, VMEM],
        out_specs=[VMEM] * 2,
        scratch_shapes=[pltpu.VMEM((long_count, rhs_count, clusters * rank_size), jnp.float32)],
        compiler_params=pltpu.CompilerParams(vmem_limit_bytes=16 << 20),
        name="far",
    )(far_pairs, everyone, coupling, near)
    far_terms = lax.all_to_all(far, ("row", "long"), 0, 0, tiled=True)
    near_rows = lax.all_to_all(own, "row", 0, 0, tiled=True)

    return pl.pallas_call(
        finish_kernel,
        out_shape=jax.ShapeDtypeStruct(slip.shape, jnp.float32),
        in_specs=[VMEM] * 3,
        out_specs=VMEM,
        compiler_params=pltpu.CompilerParams(vmem_limit_bytes=16 << 20),
        name="finish",
    )(near_rows, far_terms, basis)


def solution(mesh):
    placed = (
        P("long", None, None),
        P(None, "long"),
        P(None, "long"),
        P("long", None),
        P(None, ("row", "long")),
        P(("row", "long")),
        P(None, ("row", "long")),
        P(("row", "long"), None),
        P("long", None, None),
    )
    return jax.shard_map(
        shards, mesh=mesh, in_specs=placed, out_specs=P("long", None, None), check_vma=False
    )
```

time: 55.9 us -> 42.7 us (0.76)
  blocking collectives: 0 us -> 20.4 us
  Pallas kernels: 23.1 us -> 7.34 us
  waiting for transfers between devices: 12.8 us -> 2.77 us
  local copies, waits for them, and re-layouts: 4.01 us -> 0.16 us
  starting transfers between devices: 14.7 us -> 11 us
    all_to_all x0 -> x2, blocking collectives: none -> 20.4 us  [the longest x1 11.5 us: shards(): far_terms = lax.all_to_all(far, ('row', 'long'), 0, 0, tiled=True)]
    pallas_call x2, Pallas kernels: 19.9 us -> 4.22 us  [the longest x1 3.29 us: shards(): pl.pallas_call(near_kernel, out_shape=jax.ShapeDtypeStruct((reaches, rhs_...]
    all_to_all x1, waiting for transfers between devices: 7.56 us -> 0.03 us  [shards(): everyone = lax.all_to_all(pay, ('row', 'long'), 0, 0, tiled=True)]
    unnamed x18 -> x6, local copies, waits for them, and re-layouts: 3.86 us -> 0.01 us
    all_to_all x1 -> x0, starting transfers between devices: 2.58 us -> none  [shards(): far_terms = lax.all_to_all(far, ('row', 'long'), 0, 0, tiled=True)]
    ppermute x2 -> x1, waiting for transfers between devices: 5.21 us -> 2.74 us  [shards(): halo = lax.ppermute(to_neighbour, ('row', 'long'), route)]
    ppermute x2 -> x1, starting transfers between devices: 4.85 us -> 3.68 us  [shards(): halo = lax.ppermute(to_neighbour, ('row', 'long'), route)]
    pallas_call x1, Pallas kernels: 1.76 us -> 1.11 us  [shards(): pl.pallas_call(functools.partial(far_kernel, clusters=clusters), out_shap...]
  transfers between devices with their start and end apart: 4 -> 2, of which waited for: 3 -> 1; matrix products, arithmetic and copies ran while one was open for 0% -> 0% of each run, Pallas kernels for 33% -> 8%
where the time goes in v2:
time: 42.7 us; the launch traced here: 42.4 us
  blocking collectives  20.4 us (48%)
  starting transfers between devices  11 us (26%)
  Pallas kernels  7.34 us (17%)
  waiting for transfers between devices  2.77 us (6%)
  between operations  0.73 us (2%)
    all_to_all x1, blocking collectives, shards(): far_terms = lax.all_to_all(far, ('row', 'long'), 0, 0, tiled=True)  11.5 us
    all_to_all x1, blocking collectives, shards(): near_rows = lax.all_to_all(own, 'row', 0, 0, tiled=True)  8.91 us
    all_to_all x1, starting transfers between devices, shards(): everyone = lax.all_to_all(pay, ('row', 'long'), 0, 0, tiled=True)  7.3 us
    ppermute x1, starting transfers between devices, shards(): halo = lax.ppermute(to_neighbour, ('row', 'long'), route)  3.68 us
    pallas_call x1, Pallas kernels, shards(): pl.pallas_call(near_kernel, out_shape=jax.ShapeDtypeStruct((reaches, rhs_...  3.29 us
    ppermute x1, waiting for transfers between devices, shards(): halo = lax.ppermute(to_neighbour, ('row', 'long'), route)  2.74 us
    pallas_call x1, Pallas kernels, shards(): pl.pallas_call(prepare_kernel, out_shape=[jax.ShapeDtypeStruct((devices,...  2 us
    pallas_call x1, Pallas kernels, shards(): pl.pallas_call(functools.partial(far_kernel, clusters=clusters), out_shap...  1.11 us
  transfers between devices with their start and end apart: 2, of which 1 were waited for; matrix products, arithmetic and copies ran while one was open for 0% of the time, Pallas kernels for 8%

profile of v2, /device:TPU:0, one launch (start us, length us, event | category | flops | bytes accessed | tf_op | source)
XLA Modules:
  0.0 42.4 jit_solution(11135405925553553082)
XLA Ops:
  0.7 2.0 %prepare.1 = (bf16[32,16,128]{2,1,0:T(8,128)(2,1)}, bf16[4,16,768]{2,1,0:T(8,128)(2,1)S(1)}, bf16[2,32,768]{2,1,0:T(8,128)(2,1)S(1)}, f32[4,4,256]{2,1,0:T(4,128)S(1)}) custom-call(f32[4,16,768]{2,1,0:T(8,128)} %slip_hbm.1, bf16[4,32,768]{2,1,0:T(8,128)(2,1)} %basis_ref.1, f32[3,561]{1,0:T(4,128)} %vertices_hbm.1, s32[3,1024]{1,0:T(4,128)} %triangles_hbm.1, ...), custom_call_target="tpu_custom_call" | custom-call | tf_op jit(solution)/shard_map/prepare/pallas_call | solution.py:282
  2.7 0.0 copy-start.2
  2.7 7.3 %all-to-all-start = ((bf16[32,16,128]{2,1,0:T(8,128)(2,1)}), bf16[32,16,128]{2,1,0:T(8,128)(2,1)S(1)}, u32[]{:S(2)}, u32[]{:S(2)}) async-start(bf16[32,16,128]{2,1,0:T(8,128)(2,1)} %get-tuple-element.11), calls=%async_computation | async-start | bytes 262144 | tf_op jit(solution)/shard_map/all_to_all | solution.py:311
  10.0 3.7 %collective-permute-start = (bf16[2,32,768]{2,1,0:T(8,128)(2,1)S(1)}, bf16[2,32,768]{2,1,0:T(8,128)(2,1)S(1)}, u32[]{:S(2)}, u32[]{:S(2)}) collective-permute-start(bf16[2,32,768]{2,1,0:T(8,128)(2,1)S(1)} %get-tuple-element.14), channel_id=1, source_target_pairs={{0,1},{1,2},{2,3},{3,4},{4,5},{5,6},{6,7},{8,9},{9,10},{10,11},{11... | collective-permute-start | bytes 294920 | tf_op jit(solution)/shard_map/ppermute | solution.py:318
  13.7 0.0 copy-done.2
  13.7 0.1 reshape.3.coupling_ref
  13.8 2.7 %collective-permute-done.halo_ref = bf16[2,32,768]{2,1,0:T(8,128)(2,1)S(1)} collective-permute-done((bf16[2,32,768]{2,1,0:T(8,128)(2,1)S(1)}, bf16[2,32,768]{2,1,0:T(8,128)(2,1)S(1)}, u32[]{:S(2)}, u32[]{:S(2)}) %collective-permute-start) | collective-permute-done | bytes 98336 | tf_op jit(solution)/shard_map/ppermute | solution.py:318
  16.6 0.0 copy-start.1
  16.6 3.3 %near.1.near_ref = f32[5,16,768]{2,1,0:T(8,128)S(1)} custom-call(bf16[4,16,768]{2,1,0:T(8,128)(2,1)S(1)} %get-tuple-element.12.xs_ref, f32[4,4,256]{2,1,0:T(4,128)S(1)} %get-tuple-element.13.geom_ref, bf16[2,32,768]{2,1,0:T(8,128)(2,1)S(1)} %collective-permute-done.halo_ref), custom_call_target="tpu_custom_call" | custom-call | flops 500000000 | bytes 1000000 | tf_op jit(solution)/shard_map/near/pallas_call | solution.py:320
  19.9 0.0 all-to-all-done.coeff_ref
  19.9 0.0 copy-done.1
  19.9 1.1 %far.1 = (bf16[32,16,128]{2,1,0:T(8,128)(2,1)S(1)}, f32[4,16,768]{2,1,0:T(8,128)S(1)}) custom-call(s32[2,16]{1,0:T(2,128)S(1)} %copy-done.1, bf16[32,16,128]{2,1,0:T(8,128)(2,1)S(1)} %all-to-all-done.coeff_ref, bf16[16,32,32]{2,1,0:T(8,128)(2,1)S(1)} %reshape.3.coupling_ref, f32[5,16,768]{2,1,0:T(8,128)S(1)} %near.1.near_ref), custom_call_target="tpu_custom_call" | custom-call | tf_op jit(solution)/shard_map/far/pallas_call | solution.py:338
  21.0 8.9 %all_to_all.15.near_ref = f32[4,16,768]{2,1,0:T(8,128)S(1)} all-to-all(f32[4,16,768]{2,1,0:T(8,128)S(1)} %get-tuple-element.15), channel_id=1, replica_groups=mesh['row'=4,'long'=8] {'row'}, dimensions={0} | all-to-all | bytes 393216 | tf_op jit(solution)/shard_map/all_to_all | solution.py:351
  30.0 0.0 copy-start
  30.0 11.5 %all_to_all.16.far_ref = bf16[32,16,128]{2,1,0:T(8,128)(2,1)S(1)} all-to-all(bf16[32,16,128]{2,1,0:T(8,128)(2,1)S(1)} %get-tuple-element.16), channel_id=1, replica_groups=mesh['row'=4,'long'=8] {'row','long'}, dimensions={0} | all-to-all | bytes 262144 | tf_op jit(solution)/shard_map/all_to_all | solution.py:350
  41.5 0.0 copy-done
  41.5 0.9 %finish.1 = f32[4,16,768]{2,1,0:T(8,128)} custom-call(f32[4,16,768]{2,1,0:T(8,128)S(1)} %all_to_all.15.near_ref, bf16[32,16,128]{2,1,0:T(8,128)(2,1)S(1)} %all_to_all.16.far_ref, bf16[4,32,768]{2,1,0:T(8,128)(2,1)S(1)} %copy-done), custom_call_target="tpu_custom_call" | custom-call | tf_op jit(solution)/shard_map/finish/pallas_call | solution.py:353
Async XLA Ops:
  2.7 11.0 %copy-start.2 = (bf16[16,1024]{1,0:T(8,128)(2,1)S(1)}, bf16[16,1024]{1,0:T(8,128)(2,1)}, u32[]{:S(2)}) copy-start(bf16[16,1024]{1,0:T(8,128)(2,1)} %param.16) | copy-start | bytes 98308
  2.7 17.2 %all-to-all-start = ((bf16[32,16,128]{2,1,0:T(8,128)(2,1)}), bf16[32,16,128]{2,1,0:T(8,128)(2,1)S(1)}, u32[]{:S(2)}, u32[]{:S(2)}) async-start(bf16[32,16,128]{2,1,0:T(8,128)(2,1)} %get-tuple-element.11), calls=%async_computation | async-start | bytes 262144 | tf_op jit(solution)/shard_map/all_to_all | solution.py:311
  10.0 6.6 %collective-permute-start = (bf16[2,32,768]{2,1,0:T(8,128)(2,1)S(1)}, bf16[2,32,768]{2,1,0:T(8,128)(2,1)S(1)}, u32[]{:S(2)}, u32[]{:S(2)}) collective-permute-start(bf16[2,32,768]{2,1,0:T(8,128)(2,1)S(1)} %get-tuple-element.14), channel_id=1, source_target_pairs={{0,1},{1,2},{2,3},{3,4},{4,5},{5,6},{6,7},{8,9},{9,10},{10,11},{11... | collective-permute-start | bytes 294920 | tf_op jit(solution)/shard_map/ppermute | solution.py:318
  16.6 3.3 %copy-start.1 = (s32[2,16]{1,0:T(2,128)S(1)}, s32[2,16]{1,0:T(2,128)}, u32[]{:S(2)}) copy-start(s32[2,16]{1,0:T(2,128)} %pairs_ref.1) | copy-start | bytes 388
  30.0 11.5 %copy-start = (bf16[4,32,768]{2,1,0:T(8,128)(2,1)S(1)}, bf16[4,32,768]{2,1,0:T(8,128)(2,1)}, u32[]{:S(2)}) copy-start(bf16[4,32,768]{2,1,0:T(8,128)(2,1)} %basis_ref.1) | copy-start | bytes 589828

commit v3 on v2

v3 whole, which is shorter than its diff:
```python
import functools

import jax
import jax.numpy as jnp
from jax import lax
from jax.experimental import pallas as pl
from jax.experimental.pallas import tpu as pltpu
from jax.sharding import PartitionSpec as P

NEARC = 2
LANES = 128
ROWS = 16
COUNT_ROWS = 8

soften = 0.25

VMEM = pl.BlockSpec(memory_space=pltpu.VMEM)
SMEM = pl.BlockSpec(memory_space=pltpu.SMEM)
HBM = pl.BlockSpec(memory_space=pltpu.HBM)


def lane_gather(table, index):
    length = table.shape[1]
    lane = index & (LANES - 1)
    chunk = index // LANES
    found = jnp.zeros(index.shape, table.dtype)
    for piece_id in range(-(-length // LANES)):
        piece = table[:, piece_id * LANES : min(length, (piece_id + 1) * LANES)]
        missing = LANES - piece.shape[1]
        if missing:
            piece = jnp.concatenate([piece, jnp.zeros((1, missing), table.dtype)], axis=1)
        picked = jnp.take_along_axis(jnp.broadcast_to(piece, index.shape), lane, axis=1)
        found = jnp.where(chunk == piece_id, picked, found)
    return found


def split_three(value):
    high = value.astype(jnp.bfloat16).astype(jnp.float32)
    rest = value - high
    middle = rest.astype(jnp.bfloat16).astype(jnp.float32)
    return [high, middle, rest - middle]


def prepare_kernel(
    slip_hbm, basis_hbm, vertices_hbm, triangles_hbm, map_hbm,
    pay_ref, xs_ref, halo_ref, geom_ref,
    slip_ref, basis_ref, vertices_ref, triangles_ref, map_ref, sems,
):
    sources = (slip_hbm, basis_hbm, vertices_hbm, triangles_hbm, map_hbm)
    targets = (slip_ref, basis_ref, vertices_ref, triangles_ref, map_ref)
    copies = [
        pltpu.make_async_copy(source, target, sems.at[place])
        for place, (source, target) in enumerate(zip(sources, targets))
    ]
    for copy in copies:
        copy.start()
    clusters, rhs_count, unknowns = slip_ref.shape
    long_index = lax.axis_index("long")
    for copy in copies:
        copy.wait()

    size = map_ref.shape[1]
    half = size // LANES
    slot_map = map_ref[...]
    index = jnp.concatenate(
        [slot_map[:, part * LANES : (part + 1) * LANES] for part in range(half)], axis=0
    )
    vertex_base = long_index * vertices_ref.shape[1]
    corners = []
    for corner_id in range(3):
        vertex = lane_gather(triangles_ref[corner_id : corner_id + 1, :], index) - vertex_base
        corners.append(
            [lane_gather(vertices_ref[axis_id : axis_id + 1, :], vertex) for axis_id in range(3)]
        )
    one, two, three = corners
    centre = [(one[a] + two[a] + three[a]) / 3.0 for a in range(3)]
    edge_one = [two[a] - one[a] for a in range(3)]
    edge_two = [three[a] - one[a] for a in range(3)]
    normal = [
        edge_one[1] * edge_two[2] - edge_one[2] * edge_two[1],
        edge_one[2] * edge_two[0] - edge_one[0] * edge_two[2],
        edge_one[0] * edge_two[1] - edge_one[1] * edge_two[0],
    ]
    area = 0.5 * jnp.sqrt(normal[0] * normal[0] + normal[1] * normal[1] + normal[2] * normal[2])
    geometry = []
    for value in centre + [area]:
        geometry.append(
            jnp.concatenate(
                [value[part * clusters : (part + 1) * clusters] for part in range(half)], axis=1
            )
        )
    for cluster in range(clusters):
        geom_ref[cluster] = jnp.concatenate(
            [whole[cluster : cluster + 1, :] for whole in geometry], axis=0
        )

    xs_ref[...] = slip_ref[...].astype(jnp.bfloat16)
    coeffs = jnp.concatenate(
        [
            lax.dot_general(
                xs_ref[cluster],
                basis_ref[cluster],
                (((1,), (1,)), ((), ())),
                preferred_element_type=jnp.float32,
            )
            for cluster in range(clusters)
        ],
        axis=1,
    ).astype(jnp.bfloat16)
    for target in range(pay_ref.shape[0]):
        pay_ref[target] = coeffs

    upward = lax.axis_index("row") % 2 == 0
    start = jnp.where(upward, clusters - NEARC, 0)
    pieces = [piece for whole in geometry for piece in split_three(whole)]
    for turn in range(NEARC):
        last = clusters - NEARC + turn
        rows = [
            jnp.where(upward, piece[last : last + 1, :], piece[turn : turn + 1, :])
            for piece in pieces
        ]
        rows.append(jnp.zeros((ROWS - len(rows), size), jnp.float32))
        halo_ref[turn, 0:rhs_count, :] = xs_ref[start + turn]
        halo_ref[turn, rhs_count : rhs_count + ROWS, 0:size] = jnp.concatenate(
            rows, axis=0
        ).astype(jnp.bfloat16)
        halo_ref[turn, rhs_count : rhs_count + ROWS, size:unknowns] = jnp.zeros(
            (ROWS, unknowns - size), jnp.bfloat16
        )


def near_kernel(
    xs_ref, geom_ref, halo_ref, out_ref, slip_ref, place_ref, cols_ref, even_ref, odd_ref
):
    clusters, rhs_count, unknowns = xs_ref.shape
    size = geom_ref.shape[2]
    slots = clusters + NEARC
    begin = (lax.axis_index("row") % 2) * NEARC

    def slot_of(place):
        return (begin - NEARC + place + slots) % slots

    slip_ref[0:clusters] = xs_ref[...]
    place_ref[0:clusters] = geom_ref[...]
    for turn in range(NEARC):
        slip_ref[clusters + turn] = halo_ref[turn, 0:rhs_count, :]
        pieces = halo_ref[turn, rhs_count : rhs_count + ROWS, 0:size].astype(jnp.float32)
        place_ref[clusters + turn] = jnp.concatenate(
            [
                (pieces[3 * p + 2 : 3 * p + 3] + pieces[3 * p + 1 : 3 * p + 2])
                + pieces[3 * p : 3 * p + 1]
                for p in range(4)
            ],
            axis=0,
        )
    for place in range(slots):
        rows = jnp.concatenate([place_ref[slot_of(place)], jnp.zeros((4, size), jnp.float32)], axis=0)
        cols_ref[place] = rows.T
    right = [[place_ref[begin + u, p : p + 1, :] for p in range(4)] for u in range(NEARC)]
    parts = [(0, 0), (1, 1), (2, 2), (0, 1), (0, 2), (1, 2)]

    def fill(place, targets, block_ref):
        for step in range(size // ROWS):
            here = pl.ds(step * ROWS, ROWS)
            column = cols_ref[place, here, :]
            left = [jnp.broadcast_to(column[:, p : p + 1], (ROWS, size)) for p in range(4)]
            for u in targets:
                offset = [left[p] - right[u][p] for p in range(3)]
                radius_sq = offset[0] * offset[0] + offset[1] * offset[1] + offset[2] * offset[2]
                inverse = lax.rsqrt(radius_sq + soften)
                flat = (left[3] * right[u][3]) * inverse
                cubed = flat * (inverse * inverse)
                scaled = [offset[p] * cubed for p in range(3)]
                for part_id, (i, j) in enumerate(parts):
                    term = offset[i] * scaled[j]
                    if i == j:
                        term = term + flat
                    block_ref[u, part_id, here, :] = term.astype(jnp.bfloat16)

    def apply(place, targets, block_ref):
        slip = slip_ref[slot_of(place)]
        pieces = [slip[:, p * size : (p + 1) * size] for p in range(3)]
        for u in targets:
            sums = [
                jnp.dot(pieces[p], block_ref[u, p], preferred_element_type=jnp.float32)
                for p in range(3)
            ]
            for part_id in range(3, 6):
                i, j = parts[part_id]
                both = jnp.dot(
                    jnp.concatenate([pieces[j], pieces[i]], axis=0),
                    block_ref[u, part_id],
                    preferred_element_type=jnp.float32,
                )
                sums[i] = sums[i] + both[0:rhs_count]
                sums[j] = sums[j] + both[rhs_count : 2 * rhs_count]
            for p in range(3):
                out_ref[place, u, :, p * size : (p + 1) * size] = sums[p].astype(jnp.bfloat16)

    every = list(range(NEARC))
    fill(0, [0], even_ref)
    even_ref[1] = jnp.zeros(even_ref.shape[1:], jnp.bfloat16)

    def two_places(turn, carry):
        place = 2 * turn
        fill(place + 1, every, odd_ref)
        apply(place, every, even_ref)
        fill(place + 2, every, even_ref)
        apply(place + 1, every, odd_ref)
        return carry

    lax.fori_loop(0, (slots - 2) // 2, two_places, 0)
    fill(slots - 1, [NEARC - 1], odd_ref)
    apply(slots - 2, every, even_ref)
    apply(slots - 1, [NEARC - 1], odd_ref)
    out_ref[slots - 1, 0] = jnp.zeros(out_ref.shape[2:], jnp.bfloat16)


def far_kernel(
    pairs_ref, count_ref, coeff_ref, coupling_ref, near_pairs_ref, out_ref, total_ref, *, clusters
):
    long_count = total_ref.shape[0]
    rhs_count = coeff_ref.shape[1]
    rank_size = coupling_ref.shape[1]
    groups = LANES // rank_size
    lane_id = lax.broadcasted_iota(jnp.int32, (rhs_count, LANES), 1)
    group_id = lane_id // rank_size
    total_ref[...] = jnp.zeros(total_ref.shape, jnp.float32)

    def coeff_of(cluster):
        whole = coeff_ref[cluster // clusters].astype(jnp.float32)
        turned = pltpu.roll(whole, (LANES - rank_size * (cluster % clusters)) % LANES, 1)
        return turned[:, 0:rank_size].astype(jnp.bfloat16)

    results = []
    for pair_id in range(pairs_ref.shape[1]):
        first = pairs_ref[0, pair_id]
        second = pairs_ref[1, pair_id]
        coupling = coupling_ref[pair_id]
        to_first = lax.dot_general(
            coeff_of(second),
            jnp.concatenate([coupling] * groups, axis=0),
            (((1,), (1,)), ((), ())),
            preferred_element_type=jnp.float32,
        )
        to_second = jnp.dot(
            coeff_of(first),
            jnp.concatenate([coupling] * groups, axis=1),
            preferred_element_type=jnp.float32,
        )
        results.append((first, to_first))
        results.append((second, to_second))
    for cluster, value in results:
        owner = cluster // clusters
        total_ref[owner] += jnp.where(group_id == cluster % clusters, value, 0.0)

    long_index = lax.axis_index("long")
    first = near_pairs_ref[0:1, :]
    kind = (first - long_index * clusters) * (NEARC + 1) + near_pairs_ref[1:2, :] - first
    kinds = lax.broadcasted_iota(jnp.int32, (COUNT_ROWS, kind.shape[1]), 0)
    live = lax.broadcasted_iota(jnp.int32, kinds.shape, 1) < count_ref[0]
    low = jnp.sum(jnp.where(live & (kinds == kind), 1.0, 0.0), axis=1, keepdims=True)
    high = jnp.sum(jnp.where(live & (kinds + COUNT_ROWS == kind), 1.0, 0.0), axis=1, keepdims=True)
    group = lax.broadcasted_iota(jnp.int32, (COUNT_ROWS, LANES), 1) // (LANES // 4)
    counts = jnp.where(group % 2 == 0, low, high)
    for owner in range(long_count):
        use = jnp.where(
            group < 2, (long_index == owner).astype(jnp.int32), (long_index + 1 == owner).astype(jnp.int32)
        )
        sent = jnp.concatenate([total_ref[owner], jnp.where(use > 0, counts, 0.0)], axis=0).astype(
            jnp.bfloat16
        )
        for copy_id in range(out_ref.shape[0] // long_count):
            out_ref[copy_id * long_count + owner] = sent


def finish_kernel(own_ref, other_ref, far_ref, basis_ref, out_ref):
    clusters, rank_size, unknowns = basis_ref.shape
    rhs_count = out_ref.shape[1]
    whole = jnp.sum(far_ref[...].astype(jnp.float32), axis=0)
    total = whole[0:rhs_count]
    counts = whole[rhs_count : rhs_count + COUNT_ROWS]
    group_id = lax.broadcasted_iota(jnp.int32, total.shape, 1) // rank_size
    flat_basis = basis_ref[...].reshape(clusters * rank_size, unknowns)
    even = lax.axis_index("row") % 2 == 0
    for cluster in range(clusters):
        picked = jnp.where(group_id == cluster, total, 0.0).astype(jnp.bfloat16)
        result = jnp.dot(picked, flat_basis, preferred_element_type=jnp.float32)
        u = cluster % NEARC
        for turn in range(2 * NEARC + 1):
            reach = turn - NEARC
            lower = cluster + min(reach, 0)
            source = 0 if lower >= 0 else 2
            kind = (lower if lower >= 0 else lower + clusters) * (NEARC + 1) + abs(reach)
            lane = (source + kind // COUNT_ROWS) * (LANES // 4)
            count = counts[kind % COUNT_ROWS : kind % COUNT_ROWS + 1, lane : lane + 1]
            mine, theirs = own_ref[u + turn, u], other_ref[u + turn, u]
            here = even if cluster < NEARC else jnp.logical_not(even)
            result = result + count * jnp.where(here, mine, theirs).astype(jnp.float32)
        out_ref[cluster] = result


def shards(slip, vertices, triangles, elem_map, near_pairs, near_count, far_pairs, far_coef, basis):
    clusters, rhs_count, unknowns = slip.shape
    rank_size = basis.shape[1]
    size = elem_map.shape[1]
    row_count = lax.axis_size("row")
    long_count = lax.axis_size("long")
    devices = row_count * long_count
    coupling = far_coef.reshape(-1, rank_size, rank_size)
    slots = clusters + NEARC

    pay, xs, to_neighbour, geometry = pl.pallas_call(
        prepare_kernel,
        out_shape=[
            jax.ShapeDtypeStruct((long_count, rhs_count, clusters * rank_size), jnp.bfloat16),
            jax.ShapeDtypeStruct(slip.shape, jnp.bfloat16),
            jax.ShapeDtypeStruct((NEARC, rhs_count + ROWS, unknowns), jnp.bfloat16),
            jax.ShapeDtypeStruct((clusters, 4, size), jnp.float32),
        ],
        in_specs=[HBM] * 5,
        out_specs=[VMEM] * 4,
        scratch_shapes=[
            pltpu.VMEM(slip.shape, slip.dtype),
            pltpu.VMEM(basis.shape, basis.dtype),
            pltpu.VMEM(vertices.shape, vertices.dtype),
            pltpu.VMEM(triangles.shape, triangles.dtype),
            pltpu.VMEM(elem_map.shape, elem_map.dtype),
            pltpu.SemaphoreType.DMA((5,)),
        ],
        compiler_params=pltpu.CompilerParams(vmem_limit_bytes=16 << 20),
        name="prepare",
    )(
        *[
            pltpu.with_memory_space_constraint(array, pltpu.HBM)
            for array in (slip, basis, vertices, triangles, elem_map)
        ]
    )

    coeffs = lax.all_to_all(pay, "long", 0, 0, tiled=True)
    route = []
    for row in range(row_count):
        step = 1 if row % 2 == 0 else -1
        for owner in range(long_count):
            if 0 <= owner - step < long_count:
                route.append((row * long_count + owner - step, row * long_count + owner))
    halo = lax.ppermute(to_neighbour, ("row", "long"), route)

    far = pl.pallas_call(
        functools.partial(far_kernel, clusters=clusters),
        out_shape=jax.ShapeDtypeStruct((devices, rhs_count + COUNT_ROWS, LANES), jnp.bfloat16),
        in_specs=[SMEM, SMEM, VMEM, VMEM, VMEM],
        out_specs=VMEM,
        scratch_shapes=[pltpu.VMEM((long_count, rhs_count, LANES), jnp.float32)],
        compiler_params=pltpu.CompilerParams(vmem_limit_bytes=16 << 20),
        name="far",
    )(far_pairs, near_count, coeffs, coupling, near_pairs)
    far_terms = lax.all_to_all(far, ("row", "long"), 0, 0, tiled=True)

    near = pl.pallas_call(
        near_kernel,
        out_shape=jax.ShapeDtypeStruct((slots, NEARC, rhs_count, unknowns), jnp.bfloat16),
        in_specs=[VMEM] * 3,
        out_specs=VMEM,
        scratch_shapes=[
            pltpu.VMEM((slots, rhs_count, unknowns), jnp.bfloat16),
            pltpu.VMEM((slots, 4, size), jnp.float32),
            pltpu.VMEM((slots, size, 8), jnp.float32),
            pltpu.VMEM((NEARC, 6, size, size), jnp.bfloat16),
            pltpu.VMEM((NEARC, 6, size, size), jnp.bfloat16),
        ],
        compiler_params=pltpu.CompilerParams(vmem_limit_bytes=24 << 20),
        cost_estimate=pl.CostEstimate(
            flops=1_000_000_000, bytes_accessed=1_000_000, transcendentals=660_000
        ),
        name="near",
    )(xs, geometry, halo)
    partner = [(row, row ^ 1) for row in range(row_count)]
    other = lax.ppermute(near, "row", partner)

    return pl.pallas_call(
        finish_kernel,
        out_shape=jax.ShapeDtypeStruct(slip.shape, jnp.float32),
        in_specs=[VMEM] * 4,
        out_specs=VMEM,
        compiler_params=pltpu.CompilerParams(vmem_limit_bytes=16 << 20),
        name="finish",
    )(near, other, far_terms, basis)


def solution(mesh):
    placed = (
        P("long", None, None),
        P(None, "long"),
        P(None, "long"),
        P("long", None),
        P(None, ("row", "long")),
        P(("row", "long")),
        P(None, ("row", "long")),
        P(("row", "long"), None),
        P("long", None, None),
    )
    return jax.shard_map(
        shards, mesh=mesh, in_specs=placed, out_specs=P("long", None, None), check_vma=False
    )
```

time: 42.7 us -> 32.6 us (0.76)
  blocking collectives: 20.4 us -> 0 us
  waiting for transfers between devices: 2.77 us -> 10.5 us
  starting transfers between devices: 11 us -> 12.5 us
  Pallas kernels: 7.34 us -> 8.39 us
    all_to_all x2 -> x0, blocking collectives: 20.4 us -> none  [the longest x1 11.5 us: shards(): far_terms = lax.all_to_all(far, ('row', 'long'), 0, 0, tiled=True)]
    all_to_all x1 -> x2, waiting for transfers between devices: 0.03 us -> 9.05 us  [the longest x1 5.84 us: shards(): coeffs = lax.all_to_all(pay, 'long', 0, 0, tiled=True)]
    ppermute x1, waiting for transfers between devices: 2.74 us -> 0.01 us  [shards(): halo = lax.ppermute(to_neighbour, ('row', 'long'), route)]
    ppermute x0 -> x1, waiting for transfers between devices: none -> 1.47 us  [shards(): other = lax.ppermute(near, 'row', partner)]
    ppermute x1, starting transfers between devices: 3.68 us -> 4.88 us  [shards(): halo = lax.ppermute(to_neighbour, ('row', 'long'), route)]
    pallas_call x1, Pallas kernels: 1.11 us -> 1.78 us  [shards(): pl.pallas_call(functools.partial(far_kernel, clusters=clusters), out_shap...]
    all_to_all x1 -> x2, starting transfers between devices: 7.3 us -> 7.47 us  [the longest x1 4.89 us: shards(): coeffs = lax.all_to_all(pay, 'long', 0, 0, tiled=True)]
  transfers between devices with their start and end apart: 2 -> 4, of which waited for: 1 -> 3; matrix products, arithmetic and copies ran while one was open for 0% -> 0% of each run, Pallas kernels for 8% -> 17%
where the time goes in v3:
time: 32.6 us; the launch traced here: 32.3 us
  starting transfers between devices  12.5 us (38%)
  waiting for transfers between devices  10.5 us (32%)
  Pallas kernels  8.39 us (26%)
  between operations  0.74 us (2%)
    all_to_all x1, waiting for transfers between devices, shards(): coeffs = lax.all_to_all(pay, 'long', 0, 0, tiled=True)  5.84 us
    all_to_all x1, starting transfers between devices, shards(): coeffs = lax.all_to_all(pay, 'long', 0, 0, tiled=True)  4.89 us
    ppermute x1, starting transfers between devices, shards(): halo = lax.ppermute(to_neighbour, ('row', 'long'), route)  4.88 us
    pallas_call x1, Pallas kernels, shards(): pl.pallas_call(near_kernel, out_shape=jax.ShapeDtypeStruct((slots, NEARC,...  3.71 us
    all_to_all x1, waiting for transfers between devices, shards(): far_terms = lax.all_to_all(far, ('row', 'long'), 0, 0, tiled=True)  3.2 us
    all_to_all x1, starting transfers between devices, shards(): far_terms = lax.all_to_all(far, ('row', 'long'), 0, 0, tiled=True)  2.58 us
    pallas_call x1, Pallas kernels, shards(): pl.pallas_call(prepare_kernel, out_shape=[jax.ShapeDtypeStruct((long_coun...  1.96 us
    pallas_call x1, Pallas kernels, shards(): pl.pallas_call(functools.partial(far_kernel, clusters=clusters), out_shap...  1.78 us
  transfers between devices with their start and end apart: 4, of which 3 were waited for; matrix products, arithmetic and copies ran while one was open for 0% of the time, Pallas kernels for 17%

profile of v3, /device:TPU:0, one launch (start us, length us, event | category | flops | bytes accessed | tf_op | source)
XLA Modules:
  0.0 32.3 jit_solution(11681973488052773785)
XLA Ops:
  0.0 2.0 %prepare.1 = (bf16[8,16,128]{2,1,0:T(8,128)(2,1)}, bf16[4,16,768]{2,1,0:T(8,128)(2,1)S(1)}, bf16[2,32,768]{2,1,0:T(8,128)(2,1)S(1)}, f32[4,4,256]{2,1,0:T(4,128)S(1)}) custom-call(f32[4,16,768]{2,1,0:T(8,128)} %slip_hbm.1, bf16[4,32,768]{2,1,0:T(8,128)(2,1)} %basis_ref.1, f32[3,561]{1,0:T(4,128)} %vertices_hbm.1, s32[3,1024]{1,0:T(4,128)} %triangles_hbm.1, ...), custom_call_target="tpu_custom_call" | custom-call | tf_op jit(solution)/shard_map/prepare/pallas_call | solution.py:313
  2.0 4.9 %collective-permute-start = (bf16[2,32,768]{2,1,0:T(8,128)(2,1)S(1)}, bf16[2,32,768]{2,1,0:T(8,128)(2,1)S(1)}, u32[]{:S(2)}, u32[]{:S(2)}) collective-permute-start(bf16[2,32,768]{2,1,0:T(8,128)(2,1)S(1)} %get-tuple-element.11), channel_id=1, source_target_pairs={{0,1},{1,2},{2,3},{3,4},{4,5},{5,6},{6,7},{9,8},{10,9},{11,10},{12... | collective-permute-start | bytes 294920 | tf_op jit(solution)/shard_map/ppermute | solution.py:347
  6.9 0.0 copy-start.3
  6.9 4.9 %all-to-all-start = ((bf16[8,16,128]{2,1,0:T(8,128)(2,1)}), bf16[8,16,128]{2,1,0:T(8,128)(2,1)S(1)}, u32[]{:S(2)}, u32[]{:S(2)}) async-start(bf16[8,16,128]{2,1,0:T(8,128)(2,1)} %get-tuple-element.12), calls=%async_computation | async-start | bytes 65536 | tf_op jit(solution)/shard_map/all_to_all | solution.py:340
  12.4 0.0 copy-done.3
  12.4 0.0 copy-start.1
  12.4 0.0 copy-start.2
  12.4 0.1 reshape.3.coupling_ref
  12.6 5.8 %all-to-all-done.coeff_ref = bf16[8,16,128]{2,1,0:T(8,128)(2,1)S(1)} async-done(((bf16[8,16,128]{2,1,0:T(8,128)(2,1)}), bf16[8,16,128]{2,1,0:T(8,128)(2,1)S(1)}, u32[]{:S(2)}, u32[]{:S(2)}) %all-to-all-start) | async-done | bytes 32800 | tf_op jit(solution)/shard_map/all_to_all | solution.py:340
  18.4 0.0 copy-done.1
  18.4 0.0 copy-done.2
  18.4 1.8 %far.1 = bf16[32,24,128]{2,1,0:T(8,128)(2,1)} custom-call(s32[2,16]{1,0:T(2,128)S(1)} %copy-done.1, s32[1]{0:T(128)S(6)} %copy.10.count_ref, bf16[8,16,128]{2,1,0:T(8,128)(2,1)S(1)} %all-to-all-done.coeff_ref, bf16[16,32,32]{2,1,0:T(8,128)(2,1)S(1)} %reshape.3.coupling_ref, s32[2,20]{1,0:T(2,128)S(1)} %copy-done.2), custom_call_target="tpu_custom_call" | custom-call | tf_op jit(solution)/shard_map/far/pallas_call | solution.py:349
  20.2 2.6 %all-to-all-start.1 = ((bf16[32,24,128]{2,1,0:T(8,128)(2,1)}), bf16[32,24,128]{2,1,0:T(8,128)(2,1)S(1)}, u32[]{:S(2)}, u32[]{:S(2)}) async-start(bf16[32,24,128]{2,1,0:T(8,128)(2,1)} %far.1), calls=%async_computation.1 | async-start | bytes 393216 | tf_op jit(solution)/shard_map/all_to_all | solution.py:358
  22.8 0.0 collective-permute-done.halo_ref
  22.8 0.0 copy-start
  22.8 3.7 %near.1.own_ref = bf16[6,2,16,768]{3,2,1,0:T(8,128)(2,1)S(1)} custom-call(bf16[4,16,768]{2,1,0:T(8,128)(2,1)S(1)} %get-tuple-element.9.xs_ref, f32[4,4,256]{2,1,0:T(4,128)S(1)} %get-tuple-element.10.geom_ref, bf16[2,32,768]{2,1,0:T(8,128)(2,1)S(1)} %collective-permute-done.halo_ref), custom_call_target="tpu_custom_call" | custom-call | flops 1000000000 | bytes 1000000 | tf_op jit(solution)/shard_map/near/pallas_call | solution.py:360
  26.5 0.1 collective-permute-start.1
  26.7 1.5 %collective-permute-done.1.other_ref = bf16[6,2,16,768]{3,2,1,0:T(8,128)(2,1)S(1)} collective-permute-done((bf16[6,2,16,768]{3,2,1,0:T(8,128)(2,1)S(1)}, bf16[6,2,16,768]{3,2,1,0:T(8,128)(2,1)S(1)}, u32[]{:S(2)}, u32[]{:S(2)}) %collective-permute-start.1) | collective-permute-done | bytes 294944 | tf_op jit(solution)/shard_map/ppermute | solution.py:379
  28.2 3.2 %all-to-all-done.1.far_ref = bf16[32,24,128]{2,1,0:T(8,128)(2,1)S(1)} async-done(((bf16[32,24,128]{2,1,0:T(8,128)(2,1)}), bf16[32,24,128]{2,1,0:T(8,128)(2,1)S(1)}, u32[]{:S(2)}, u32[]{:S(2)}) %all-to-all-start.1) | async-done | bytes 196640 | tf_op jit(solution)/shard_map/all_to_all | solution.py:358
  31.4 0.0 copy-done
  31.4 0.9 %finish.1 = f32[4,16,768]{2,1,0:T(8,128)} custom-call(bf16[6,2,16,768]{3,2,1,0:T(8,128)(2,1)S(1)} %near.1.own_ref, bf16[6,2,16,768]{3,2,1,0:T(8,128)(2,1)S(1)} %collective-permute-done.1.other_ref, bf16[32,24,128]{2,1,0:T(8,128)(2,1)S(1)} %all-to-all-done.1.far_ref, bf16[4,32,768]{2,1,0:T(8,128)(2,1)S(1)} %copy-done), custom_call_target="tpu_custom_call" | custom-call | tf_op jit(solution)/shard_map/finish/pallas_call | solution.py:381
Async XLA Ops:
  2.0 20.8 %collective-permute-start = (bf16[2,32,768]{2,1,0:T(8,128)(2,1)S(1)}, bf16[2,32,768]{2,1,0:T(8,128)(2,1)S(1)}, u32[]{:S(2)}, u32[]{:S(2)}) collective-permute-start(bf16[2,32,768]{2,1,0:T(8,128)(2,1)S(1)} %get-tuple-element.11), channel_id=1, source_target_pairs={{0,1},{1,2},{2,3},{3,4},{4,5},{5,6},{6,7},{9,8},{10,9},{11,10},{12... | collective-permute-start | bytes 294920 | tf_op jit(solution)/shard_map/ppermute | solution.py:347
  6.9 5.6 %copy-start.3 = (bf16[16,1024]{1,0:T(8,128)(2,1)S(1)}, bf16[16,1024]{1,0:T(8,128)(2,1)}, u32[]{:S(2)}) copy-start(bf16[16,1024]{1,0:T(8,128)(2,1)} %param.16) | copy-start | bytes 98308
  6.9 11.6 %all-to-all-start = ((bf16[8,16,128]{2,1,0:T(8,128)(2,1)}), bf16[8,16,128]{2,1,0:T(8,128)(2,1)S(1)}, u32[]{:S(2)}, u32[]{:S(2)}) async-start(bf16[8,16,128]{2,1,0:T(8,128)(2,1)} %get-tuple-element.12), calls=%async_computation | async-start | bytes 65536 | tf_op jit(solution)/shard_map/all_to_all | solution.py:340
  12.4 6.0 %copy-start.1 = (s32[2,16]{1,0:T(2,128)S(1)}, s32[2,16]{1,0:T(2,128)}, u32[]{:S(2)}) copy-start(s32[2,16]{1,0:T(2,128)} %pairs_ref.1) | copy-start | bytes 388
  12.4 6.0 %copy-start.2 = (s32[2,20]{1,0:T(2,128)S(1)}, s32[2,20]{1,0:T(2,128)}, u32[]{:S(2)}) copy-start(s32[2,20]{1,0:T(2,128)} %near_pairs_ref.1) | copy-start | bytes 484
  20.2 11.1 %all-to-all-start.1 = ((bf16[32,24,128]{2,1,0:T(8,128)(2,1)}), bf16[32,24,128]{2,1,0:T(8,128)(2,1)S(1)}, u32[]{:S(2)}, u32[]{:S(2)}) async-start(bf16[32,24,128]{2,1,0:T(8,128)(2,1)} %far.1), calls=%async_computation.1 | async-start | bytes 393216 | tf_op jit(solution)/shard_map/all_to_all | solution.py:358
  22.8 8.5 %copy-start = (bf16[4,32,768]{2,1,0:T(8,128)(2,1)S(1)}, bf16[4,32,768]{2,1,0:T(8,128)(2,1)}, u32[]{:S(2)}) copy-start(bf16[4,32,768]{2,1,0:T(8,128)(2,1)} %basis_ref.1) | copy-start | bytes 589828
  26.5 1.6 %collective-permute-start.1 = (bf16[6,2,16,768]{3,2,1,0:T(8,128)(2,1)S(1)}, bf16[6,2,16,768]{3,2,1,0:T(8,128)(2,1)S(1)}, u32[]{:S(2)}, u32[]{:S(2)}) collective-permute-start(bf16[6,2,16,768]{3,2,1,0:T(8,128)(2,1)S(1)} %near.1.own_ref), channel_id=1, source_target_pairs={{0,8},{8,0},{16,24},{24,16},{1,9},{9,1},{17,25},{25,17},{2,10},{10... | collective-permute-start | bytes 884744 | tf_op jit(solution)/shard_map/ppermute | solution.py:379

commit v4 on v3

--- a/solution.py
+++ b/solution.py
@@ -41,23 +41,35 @@
     return [high, middle, rest - middle]
 
 
-def prepare_kernel(
-    slip_hbm, basis_hbm, vertices_hbm, triangles_hbm, map_hbm,
-    pay_ref, xs_ref, halo_ref, geom_ref,
-    slip_ref, basis_ref, vertices_ref, triangles_ref, map_ref, sems,
-):
-    sources = (slip_hbm, basis_hbm, vertices_hbm, triangles_hbm, map_hbm)
-    targets = (slip_ref, basis_ref, vertices_ref, triangles_ref, map_ref)
+def coeffs_kernel(slip_hbm, basis_hbm, pay_ref, xs_ref, slip_ref, basis_ref, sems):
     copies = [
-        pltpu.make_async_copy(source, target, sems.at[place])
-        for place, (source, target) in enumerate(zip(sources, targets))
+        pltpu.make_async_copy(slip_hbm, slip_ref, sems.at[0]),
+        pltpu.make_async_copy(basis_hbm, basis_ref, sems.at[1]),
     ]
     for copy in copies:
         copy.start()
-    clusters, rhs_count, unknowns = slip_ref.shape
-    long_index = lax.axis_index("long")
     for copy in copies:
         copy.wait()
+    xs_ref[...] = slip_ref[...].astype(jnp.bfloat16)
+    coeffs = jnp.concatenate(
+        [
+            lax.dot_general(
+                xs_ref[cluster],
+                basis_ref[cluster],
+                (((1,), (1,)), ((), ())),
+                preferred_element_type=jnp.float32,
+            )
+            for cluster in range(slip_ref.shape[0])
+        ],
+        axis=1,
+    ).astype(jnp.bfloat16)
+    for target in range(pay_ref.shape[0]):
+        pay_ref[target] = coeffs
+
+
+def geometry_kernel(xs_ref, vertices_ref, triangles_ref, map_ref, halo_ref, geom_ref):
+    clusters, rhs_count, unknowns = xs_ref.shape
+    long_index = lax.axis_index("long")
 
     size = map_ref.shape[1]
     half = size // LANES
@@ -93,22 +105,6 @@
         geom_ref[cluster] = jnp.concatenate(
             [whole[cluster : cluster + 1, :] for whole in geometry], axis=0
         )
-
-    xs_ref[...] = slip_ref[...].astype(jnp.bfloat16)
-    coeffs = jnp.concatenate(
-        [
-            lax.dot_general(
-                xs_ref[cluster],
-                basis_ref[cluster],
-                (((1,), (1,)), ((), ())),
-                preferred_element_type=jnp.float32,
-            )
-            for cluster in range(clusters)
-        ],
-        axis=1,
-    ).astype(jnp.bfloat16)
-    for target in range(pay_ref.shape[0]):
-        pay_ref[target] = coeffs
 
     upward = lax.axis_index("row") % 2 == 0
     start = jnp.where(upward, clusters - NEARC, 0)
@@ -310,34 +306,38 @@
     coupling = far_coef.reshape(-1, rank_size, rank_size)
     slots = clusters + NEARC
 
-    pay, xs, to_neighbour, geometry = pl.pallas_call(
-        prepare_kernel,
+    pay, xs = pl.pallas_call(
+        coeffs_kernel,
         out_shape=[
             jax.ShapeDtypeStruct((long_count, rhs_count, clusters * rank_size), jnp.bfloat16),
             jax.ShapeDtypeStruct(slip.shape, jnp.bfloat16),
+        ],
+        in_specs=[HBM] * 2,
+        out_specs=[VMEM] * 2,
+        scratch_shapes=[
+            pltpu.VMEM(slip.shape, slip.dtype),
+            pltpu.VMEM(basis.shape, basis.dtype),
+            pltpu.SemaphoreType.DMA((2,)),
+        ],
+        compiler_params=pltpu.CompilerParams(vmem_limit_bytes=16 << 20),
+        name="coeffs",
+    )(*[pltpu.with_memory_space_constraint(array, pltpu.HBM) for array in (slip, basis)])
+
+    coeffs = lax.all_to_all(pay, "long", 0, 0, tiled=True)
+    to_neighbour, geometry = pl.pallas_call(
+        geometry_kernel,
+        out_shape=[
             jax.ShapeDtypeStruct((NEARC, rhs_count + ROWS, unknowns), jnp.bfloat16),
             jax.ShapeDtypeStruct((clusters, 4, size), jnp.float32),
         ],
-        in_specs=[HBM] * 5,
-        out_specs=[VMEM] * 4,
-        scratch_shapes=[
-            pltpu.VMEM(slip.shape, slip.dtype),
-            pltpu.VMEM(basis.shape, basis.dtype),
-            pltpu.VMEM(vertices.shape, vertices.dtype),
-            pltpu.VMEM(triangles.shape, triangles.dtype),
-            pltpu.VMEM(elem_map.shape, elem_map.dtype),
-            pltpu.SemaphoreType.DMA((5,)),
-        ],
+        in_specs=[VMEM] * 4,
+        out_specs=[VMEM] * 2,
         compiler_params=pltpu.CompilerParams(vmem_limit_bytes=16 << 20),
-        name="prepare",
-    )(
-        *[
-            pltpu.with_memory_space_constraint(array, pltpu.HBM)
-            for array in (slip, basis, vertices, triangles, elem_map)
-        ]
-    )
-
-    coeffs = lax.all_to_all(pay, "long", 0, 0, tiled=True)
+        cost_estimate=pl.CostEstimate(
+            flops=2_000_000, bytes_accessed=1_000_000, transcendentals=1_000
+        ),
+        name="geometry",
+    )(xs, vertices, triangles, elem_map)
     route = []
     for row in range(row_count):
         step = 1 if row % 2 == 0 else -1

time: 32.6 us -> 32.9 us (level)
    pallas_call x1 -> x2, Pallas kernels: 1.96 us -> 2.2 us  [the longest x1 1.94 us: shards(): pl.pallas_call(coeffs_kernel, out_shape=[jax.ShapeDtypeStruct((long_count...]
where the time goes in v4:
time: 32.9 us; the launch traced here: 32.6 us
  starting transfers between devices  12.5 us (38%)
  waiting for transfers between devices  10.5 us (32%)
  Pallas kernels  8.63 us (26%)
  between operations  0.77 us (2%)
    all_to_all x1, waiting for transfers between devices, shards(): coeffs = lax.all_to_all(pay, 'long', 0, 0, tiled=True)  5.84 us
    all_to_all x1, starting transfers between devices, shards(): coeffs = lax.all_to_all(pay, 'long', 0, 0, tiled=True)  4.89 us
    ppermute x1, starting transfers between devices, shards(): halo = lax.ppermute(to_neighbour, ('row', 'long'), route)  4.88 us
    pallas_call x1, Pallas kernels, shards(): pl.pallas_call(near_kernel, out_shape=jax.ShapeDtypeStruct((slots, NEARC,...  3.71 us
    all_to_all x1, waiting for transfers between devices, shards(): far_terms = lax.all_to_all(far, ('row', 'long'), 0, 0, tiled=True)  3.2 us
    all_to_all x1, starting transfers between devices, shards(): far_terms = lax.all_to_all(far, ('row', 'long'), 0, 0, tiled=True)  2.58 us
    pallas_call x1, Pallas kernels, shards(): pl.pallas_call(coeffs_kernel, out_shape=[jax.ShapeDtypeStruct((long_count...  1.94 us
    pallas_call x1, Pallas kernels, shards(): pl.pallas_call(functools.partial(far_kernel, clusters=clusters), out_shap...  1.78 us
  transfers between devices with their start and end apart: 4, of which 3 were waited for; matrix products, arithmetic and copies ran while one was open for 0% of the time, Pallas kernels for 17%

profile of v4, /device:TPU:0, one launch (start us, length us, event | category | flops | bytes accessed | tf_op | source)
XLA Modules:
  0.0 32.6 jit_solution(8618455064954504626)
XLA Ops:
  0.0 0.0 copy-start.1
  0.0 0.0 copy-start.2
  0.0 0.0 copy-start.3
  0.0 1.9 %coeffs.1 = (bf16[8,16,128]{2,1,0:T(8,128)(2,1)}, bf16[4,16,768]{2,1,0:T(8,128)(2,1)S(1)}) custom-call(f32[4,16,768]{2,1,0:T(8,128)} %slip_hbm.1, bf16[4,32,768]{2,1,0:T(8,128)(2,1)} %basis_ref.1), custom_call_target="tpu_custom_call" | custom-call | tf_op jit(solution)/shard_map/coeffs/pallas_call | solution.py:309
  2.0 0.0 copy-done.1
  2.0 0.0 copy-done.2
  2.0 0.0 copy-done.3
  2.0 0.3 geometry.1
  2.2 4.9 %collective-permute-start = (bf16[2,32,768]{2,1,0:T(8,128)(2,1)S(1)}, bf16[2,32,768]{2,1,0:T(8,128)(2,1)S(1)}, u32[]{:S(2)}, u32[]{:S(2)}) collective-permute-start(bf16[2,32,768]{2,1,0:T(8,128)(2,1)S(1)} %get-tuple-element.11), channel_id=1, source_target_pairs={{0,1},{1,2},{2,3},{3,4},{4,5},{5,6},{6,7},{9,8},{10,9},{11,10},{12... | collective-permute-start | bytes 294920 | tf_op jit(solution)/shard_map/ppermute | solution.py:347
  7.1 0.0 copy-start.6
  7.1 4.9 %all-to-all-start = ((bf16[8,16,128]{2,1,0:T(8,128)(2,1)}), bf16[8,16,128]{2,1,0:T(8,128)(2,1)S(1)}, u32[]{:S(2)}, u32[]{:S(2)}) async-start(bf16[8,16,128]{2,1,0:T(8,128)(2,1)} %get-tuple-element.12), calls=%async_computation | async-start | bytes 65536 | tf_op jit(solution)/shard_map/all_to_all | solution.py:326
  12.7 0.0 copy-done.6
  12.7 0.0 copy-start.4
  12.7 0.0 copy-start.5
  12.7 0.1 reshape.3.coupling_ref
  12.9 5.8 %all-to-all-done.coeff_ref = bf16[8,16,128]{2,1,0:T(8,128)(2,1)S(1)} async-done(((bf16[8,16,128]{2,1,0:T(8,128)(2,1)}), bf16[8,16,128]{2,1,0:T(8,128)(2,1)S(1)}, u32[]{:S(2)}, u32[]{:S(2)}) %all-to-all-start) | async-done | bytes 32800 | tf_op jit(solution)/shard_map/all_to_all | solution.py:326
  18.7 0.0 copy-done.4
  18.7 0.0 copy-done.5
  18.7 1.8 %far.1 = bf16[32,24,128]{2,1,0:T(8,128)(2,1)} custom-call(s32[2,16]{1,0:T(2,128)S(1)} %copy-done.4, s32[1]{0:T(128)S(6)} %copy.10.count_ref, bf16[8,16,128]{2,1,0:T(8,128)(2,1)S(1)} %all-to-all-done.coeff_ref, bf16[16,32,32]{2,1,0:T(8,128)(2,1)S(1)} %reshape.3.coupling_ref, s32[2,20]{1,0:T(2,128)S(1)} %copy-done.5), custom_call_target="tpu_custom_call" | custom-call | tf_op jit(solution)/shard_map/far/pallas_call | solution.py:349
  20.5 2.6 %all-to-all-start.1 = ((bf16[32,24,128]{2,1,0:T(8,128)(2,1)}), bf16[32,24,128]{2,1,0:T(8,128)(2,1)S(1)}, u32[]{:S(2)}, u32[]{:S(2)}) async-start(bf16[32,24,128]{2,1,0:T(8,128)(2,1)} %far.1), calls=%async_computation.1 | async-start | bytes 393216 | tf_op jit(solution)/shard_map/all_to_all | solution.py:358
  23.1 0.0 collective-permute-done.halo_ref
  23.1 0.0 copy-start
  23.1 3.7 %near.1.own_ref = bf16[6,2,16,768]{3,2,1,0:T(8,128)(2,1)S(1)} custom-call(bf16[4,16,768]{2,1,0:T(8,128)(2,1)S(1)} %get-tuple-element.9.xs_ref, f32[4,4,256]{2,1,0:T(4,128)S(1)} %get-tuple-element.10.geom_ref, bf16[2,32,768]{2,1,0:T(8,128)(2,1)S(1)} %collective-permute-done.halo_ref), custom_call_target="tpu_custom_call" | custom-call | flops 1000000000 | bytes 1000000 | tf_op jit(solution)/shard_map/near/pallas_call | solution.py:360
  26.8 0.1 collective-permute-start.1
  27.0 1.5 %collective-permute-done.1.other_ref = bf16[6,2,16,768]{3,2,1,0:T(8,128)(2,1)S(1)} collective-permute-done((bf16[6,2,16,768]{3,2,1,0:T(8,128)(2,1)S(1)}, bf16[6,2,16,768]{3,2,1,0:T(8,128)(2,1)S(1)}, u32[]{:S(2)}, u32[]{:S(2)}) %collective-permute-start.1) | collective-permute-done | bytes 294944 | tf_op jit(solution)/shard_map/ppermute | solution.py:379
  28.4 3.2 %all-to-all-done.1.far_ref = bf16[32,24,128]{2,1,0:T(8,128)(2,1)S(1)} async-done(((bf16[32,24,128]{2,1,0:T(8,128)(2,1)}), bf16[32,24,128]{2,1,0:T(8,128)(2,1)S(1)}, u32[]{:S(2)}, u32[]{:S(2)}) %all-to-all-start.1) | async-done | bytes 196640 | tf_op jit(solution)/shard_map/all_to_all | solution.py:358
  31.6 0.0 copy-done
  31.6 0.9 %finish.1 = f32[4,16,768]{2,1,0:T(8,128)} custom-call(bf16[6,2,16,768]{3,2,1,0:T(8,128)(2,1)S(1)} %near.1.own_ref, bf16[6,2,16,768]{3,2,1,0:T(8,128)(2,1)S(1)} %collective-permute-done.1.other_ref, bf16[32,24,128]{2,1,0:T(8,128)(2,1)S(1)} %all-to-all-done.1.far_ref, bf16[4,32,768]{2,1,0:T(8,128)(2,1)S(1)} %copy-done), custom_call_target="tpu_custom_call" | custom-call | tf_op jit(solution)/shard_map/finish/pallas_call | solution.py:381
Async XLA Ops:
  0.0 2.0 %copy-start.1 = (s32[3,1024]{1,0:T(4,128)S(1)}, s32[3,1024]{1,0:T(4,128)}, u32[]{:S(2)}) copy-start(s32[3,1024]{1,0:T(4,128)} %triangles_ref.1) | copy-start | bytes 36868
  0.0 2.0 %copy-start.2 = (f32[3,561]{1,0:T(4,128)S(1)}, f32[3,561]{1,0:T(4,128)}, u32[]{:S(2)}) copy-start(f32[3,561]{1,0:T(4,128)} %vertices_ref.1) | copy-start | bytes 20200
  0.0 2.0 %copy-start.3 = (s32[4,256]{1,0:T(4,128)S(1)}, s32[4,256]{1,0:T(4,128)}, u32[]{:S(2)}) copy-start(s32[4,256]{1,0:T(4,128)} %map_ref.1) | copy-start | bytes 12292
  2.2 20.9 %collective-permute-start = (bf16[2,32,768]{2,1,0:T(8,128)(2,1)S(1)}, bf16[2,32,768]{2,1,0:T(8,128)(2,1)S(1)}, u32[]{:S(2)}, u32[]{:S(2)}) collective-permute-start(bf16[2,32,768]{2,1,0:T(8,128)(2,1)S(1)} %get-tuple-element.11), channel_id=1, source_target_pairs={{0,1},{1,2},{2,3},{3,4},{4,5},{5,6},{6,7},{9,8},{10,9},{11,10},{12... | collective-permute-start | bytes 294920 | tf_op jit(solution)/shard_map/ppermute | solution.py:347
  7.1 5.6 %copy-start.6 = (bf16[16,1024]{1,0:T(8,128)(2,1)S(1)}, bf16[16,1024]{1,0:T(8,128)(2,1)}, u32[]{:S(2)}) copy-start(bf16[16,1024]{1,0:T(8,128)(2,1)} %param.16) | copy-start | bytes 98308
  7.1 11.6 %all-to-all-start = ((bf16[8,16,128]{2,1,0:T(8,128)(2,1)}), bf16[8,16,128]{2,1,0:T(8,128)(2,1)S(1)}, u32[]{:S(2)}, u32[]{:S(2)}) async-start(bf16[8,16,128]{2,1,0:T(8,128)(2,1)} %get-tuple-element.12), calls=%async_computation | async-start | bytes 65536 | tf_op jit(solution)/shard_map/all_to_all | solution.py:326
  12.7 6.0 %copy-start.4 = (s32[2,16]{1,0:T(2,128)S(1)}, s32[2,16]{1,0:T(2,128)}, u32[]{:S(2)}) copy-start(s32[2,16]{1,0:T(2,128)} %pairs_ref.1) | copy-start | bytes 388
  12.7 6.0 %copy-start.5 = (s32[2,20]{1,0:T(2,128)S(1)}, s32[2,20]{1,0:T(2,128)}, u32[]{:S(2)}) copy-start(s32[2,20]{1,0:T(2,128)} %near_pairs_ref.1) | copy-start | bytes 484
  20.5 11.1 %all-to-all-start.1 = ((bf16[32,24,128]{2,1,0:T(8,128)(2,1)}), bf16[32,24,128]{2,1,0:T(8,128)(2,1)S(1)}, u32[]{:S(2)}, u32[]{:S(2)}) async-start(bf16[32,24,128]{2,1,0:T(8,128)(2,1)} %far.1), calls=%async_computation.1 | async-start | bytes 393216 | tf_op jit(solution)/shard_map/all_to_all | solution.py:358
  23.1 8.5 %copy-start = (bf16[4,32,768]{2,1,0:T(8,128)(2,1)S(1)}, bf16[4,32,768]{2,1,0:T(8,128)(2,1)}, u32[]{:S(2)}) copy-start(bf16[4,32,768]{2,1,0:T(8,128)(2,1)} %basis_ref.1) | copy-start | bytes 589828
  26.8 1.6 %collective-permute-start.1 = (bf16[6,2,16,768]{3,2,1,0:T(8,128)(2,1)S(1)}, bf16[6,2,16,768]{3,2,1,0:T(8,128)(2,1)S(1)}, u32[]{:S(2)}, u32[]{:S(2)}) collective-permute-start(bf16[6,2,16,768]{3,2,1,0:T(8,128)(2,1)S(1)} %near.1.own_ref), channel_id=1, source_target_pairs={{0,8},{8,0},{16,24},{24,16},{1,9},{9,1},{17,25},{25,17},{2,10},{10... | collective-permute-start | bytes 884744 | tf_op jit(solution)/shard_map/ppermute | solution.py:379

commit v5 on v4

--- a/solution.py
+++ b/solution.py
@@ -10,13 +10,13 @@
 NEARC = 2
 LANES = 128
 ROWS = 16
-COUNT_ROWS = 8
 
 soften = 0.25
 
 VMEM = pl.BlockSpec(memory_space=pltpu.VMEM)
 SMEM = pl.BlockSpec(memory_space=pltpu.SMEM)
 HBM = pl.BlockSpec(memory_space=pltpu.HBM)
+ANY = pl.BlockSpec(memory_space=pl.ANY)
 
 
 def lane_gather(table, index):
@@ -41,34 +41,49 @@
     return [high, middle, rest - middle]
 
 
-def coeffs_kernel(slip_hbm, basis_hbm, pay_ref, xs_ref, slip_ref, basis_ref, sems):
+def coeffs_kernel(
+    slip_hbm, basis_hbm, pairs_hbm, count_ref, pay_ref, slip_ref, basis_ref, pairs_ref, sems
+):
+    clusters = slip_hbm.shape[0]
+    rhs_count = slip_ref.shape[0]
+    rank_size = basis_ref.shape[0]
+    mine = lax.axis_index("row") % clusters
     copies = [
-        pltpu.make_async_copy(slip_hbm, slip_ref, sems.at[0]),
-        pltpu.make_async_copy(basis_hbm, basis_ref, sems.at[1]),
+        pltpu.make_async_copy(slip_hbm.at[mine], slip_ref, sems.at[0]),
+        pltpu.make_async_copy(basis_hbm.at[mine], basis_ref, sems.at[1]),
+        pltpu.make_async_copy(pairs_hbm, pairs_ref, sems.at[2]),
     ]
     for copy in copies:
         copy.start()
     for copy in copies:
         copy.wait()
-    xs_ref[...] = slip_ref[...].astype(jnp.bfloat16)
-    coeffs = jnp.concatenate(
-        [
-            lax.dot_general(
-                xs_ref[cluster],
-                basis_ref[cluster],
-                (((1,), (1,)), ((), ())),
-                preferred_element_type=jnp.float32,
-            )
-            for cluster in range(slip_ref.shape[0])
-        ],
-        axis=1,
+    half = rhs_count // 2
+    wide = jnp.concatenate([basis_ref[...]] * (LANES // rank_size), axis=0)
+    coeffs = lax.dot_general(
+        slip_ref[...].astype(jnp.bfloat16),
+        wide,
+        (((1,), (1,)), ((), ())),
+        preferred_element_type=jnp.float32,
+    )
+    first = pairs_ref[0:1, :]
+    kind = (first - lax.axis_index("long") * clusters) * (NEARC + 1) + pairs_ref[1:2, :] - first
+    kinds = lax.broadcasted_iota(jnp.int32, (half, kind.shape[1]), 0)
+    live = lax.broadcasted_iota(jnp.int32, kinds.shape, 1) < count_ref[0]
+    low = jnp.sum(jnp.where(live & (kinds == kind), 1.0, 0.0), axis=1, keepdims=True)
+    high = jnp.sum(jnp.where(live & (kinds + half == kind), 1.0, 0.0), axis=1, keepdims=True)
+    group = lax.broadcasted_iota(jnp.int32, (half, LANES), 1) // rank_size
+    pay = jnp.where(
+        group == 0, coeffs[0:half], jnp.where(group == 1, coeffs[half:], jnp.where(group == 2, low, high))
     ).astype(jnp.bfloat16)
     for target in range(pay_ref.shape[0]):
-        pay_ref[target] = coeffs
-
-
-def geometry_kernel(xs_ref, vertices_ref, triangles_ref, map_ref, halo_ref, geom_ref):
-    clusters, rhs_count, unknowns = xs_ref.shape
+        pay_ref[target] = pay
+
+
+def geometry_kernel(
+    slip_ref, vertices_ref, triangles_ref, map_ref, after_ref, xs_ref, halo_ref, geom_ref
+):
+    clusters, rhs_count, unknowns = slip_ref.shape
+    xs_ref[...] = slip_ref[...].astype(jnp.bfloat16)
     long_index = lax.axis_index("long")
 
     size = map_ref.shape[1]
@@ -125,23 +140,23 @@
         )
 
 
-def near_kernel(
-    xs_ref, geom_ref, halo_ref, out_ref, slip_ref, place_ref, cols_ref, even_ref, odd_ref
-):
+def window_kernel(xs_ref, geom_ref, halo_ref, slip_ref, place_ref):
     clusters, rhs_count, unknowns = xs_ref.shape
     size = geom_ref.shape[2]
     slots = clusters + NEARC
-    begin = (lax.axis_index("row") % 2) * NEARC
-
-    def slot_of(place):
-        return (begin - NEARC + place + slots) % slots
-
-    slip_ref[0:clusters] = xs_ref[...]
-    place_ref[0:clusters] = geom_ref[...]
+    odd = lax.axis_index("row") % 2
+
+    def place_of(cluster):
+        return (cluster + NEARC * (1 - odd) + slots) % slots
+
+    for cluster in range(clusters):
+        slip_ref[place_of(cluster)] = xs_ref[cluster]
+        place_ref[place_of(cluster)] = geom_ref[cluster]
     for turn in range(NEARC):
-        slip_ref[clusters + turn] = halo_ref[turn, 0:rhs_count, :]
+        at = place_of(clusters + turn)
+        slip_ref[at] = halo_ref[turn, 0:rhs_count, :]
         pieces = halo_ref[turn, rhs_count : rhs_count + ROWS, 0:size].astype(jnp.float32)
-        place_ref[clusters + turn] = jnp.concatenate(
+        place_ref[at] = jnp.concatenate(
             [
                 (pieces[3 * p + 2 : 3 * p + 3] + pieces[3 * p + 1 : 3 * p + 2])
                 + pieces[3 * p : 3 * p + 1]
@@ -149,10 +164,15 @@
             ],
             axis=0,
         )
+
+
+def near_kernel(slip_ref, place_ref, after_ref, out_ref, cols_ref, even_ref, odd_ref):
+    slots, rhs_count, unknowns = slip_ref.shape
+    size = place_ref.shape[2]
     for place in range(slots):
-        rows = jnp.concatenate([place_ref[slot_of(place)], jnp.zeros((4, size), jnp.float32)], axis=0)
+        rows = jnp.concatenate([place_ref[place], jnp.zeros((4, size), jnp.float32)], axis=0)
         cols_ref[place] = rows.T
-    right = [[place_ref[begin + u, p : p + 1, :] for p in range(4)] for u in range(NEARC)]
+    right = [[place_ref[NEARC + u, p : p + 1, :] for p in range(4)] for u in range(NEARC)]
     parts = [(0, 0), (1, 1), (2, 2), (0, 1), (0, 2), (1, 2)]
 
     def fill(place, targets, block_ref):
@@ -174,7 +194,7 @@
                     block_ref[u, part_id, here, :] = term.astype(jnp.bfloat16)
 
     def apply(place, targets, block_ref):
-        slip = slip_ref[slot_of(place)]
+        slip = slip_ref[place]
         pieces = [slip[:, p * size : (p + 1) * size] for p in range(3)]
         for u in targets:
             sums = [
@@ -212,21 +232,19 @@
     out_ref[slots - 1, 0] = jnp.zeros(out_ref.shape[2:], jnp.bfloat16)
 
 
-def far_kernel(
-    pairs_ref, count_ref, coeff_ref, coupling_ref, near_pairs_ref, out_ref, total_ref, *, clusters
-):
-    long_count = total_ref.shape[0]
-    rhs_count = coeff_ref.shape[1]
+def far_kernel(pairs_ref, coeff_ref, coupling_ref, after_ref, out_ref, total_ref, *, clusters):
+    long_count, rhs_count, _ = total_ref.shape
     rank_size = coupling_ref.shape[1]
     groups = LANES // rank_size
-    lane_id = lax.broadcasted_iota(jnp.int32, (rhs_count, LANES), 1)
-    group_id = lane_id // rank_size
+    group_id = lax.broadcasted_iota(jnp.int32, (rhs_count, LANES), 1) // rank_size
     total_ref[...] = jnp.zeros(total_ref.shape, jnp.float32)
 
     def coeff_of(cluster):
-        whole = coeff_ref[cluster // clusters].astype(jnp.float32)
-        turned = pltpu.roll(whole, (LANES - rank_size * (cluster % clusters)) % LANES, 1)
-        return turned[:, 0:rank_size].astype(jnp.bfloat16)
+        whole = coeff_ref[(cluster % clusters) * long_count + cluster // clusters]
+        whole = whole.astype(jnp.float32)
+        return jnp.concatenate(
+            [whole[:, 0:rank_size], whole[:, rank_size : 2 * rank_size]], axis=0
+        ).astype(jnp.bfloat16)
 
     results = []
     for pair_id in range(pairs_ref.shape[1]):
@@ -250,32 +268,21 @@
         owner = cluster // clusters
         total_ref[owner] += jnp.where(group_id == cluster % clusters, value, 0.0)
 
+    sent = total_ref[...].astype(jnp.bfloat16)
+    for copy_id in range(out_ref.shape[0] // long_count):
+        out_ref[copy_id * long_count : (copy_id + 1) * long_count] = sent
+
+
+def finish_kernel(own_ref, other_ref, pay_ref, far_ref, basis_ref, out_ref, *, long_count):
+    clusters, rank_size, unknowns = basis_ref.shape
     long_index = lax.axis_index("long")
-    first = near_pairs_ref[0:1, :]
-    kind = (first - long_index * clusters) * (NEARC + 1) + near_pairs_ref[1:2, :] - first
-    kinds = lax.broadcasted_iota(jnp.int32, (COUNT_ROWS, kind.shape[1]), 0)
-    live = lax.broadcasted_iota(jnp.int32, kinds.shape, 1) < count_ref[0]
-    low = jnp.sum(jnp.where(live & (kinds == kind), 1.0, 0.0), axis=1, keepdims=True)
-    high = jnp.sum(jnp.where(live & (kinds + COUNT_ROWS == kind), 1.0, 0.0), axis=1, keepdims=True)
-    group = lax.broadcasted_iota(jnp.int32, (COUNT_ROWS, LANES), 1) // (LANES // 4)
-    counts = jnp.where(group % 2 == 0, low, high)
-    for owner in range(long_count):
-        use = jnp.where(
-            group < 2, (long_index == owner).astype(jnp.int32), (long_index + 1 == owner).astype(jnp.int32)
-        )
-        sent = jnp.concatenate([total_ref[owner], jnp.where(use > 0, counts, 0.0)], axis=0).astype(
-            jnp.bfloat16
-        )
-        for copy_id in range(out_ref.shape[0] // long_count):
-            out_ref[copy_id * long_count + owner] = sent
-
-
-def finish_kernel(own_ref, other_ref, far_ref, basis_ref, out_ref):
-    clusters, rank_size, unknowns = basis_ref.shape
-    rhs_count = out_ref.shape[1]
-    whole = jnp.sum(far_ref[...].astype(jnp.float32), axis=0)
-    total = whole[0:rhs_count]
-    counts = whole[rhs_count : rhs_count + COUNT_ROWS]
+    before = jnp.maximum(long_index - 1, 0)
+    half = pay_ref.shape[1]
+    counts = [jnp.zeros(pay_ref.shape[1:], jnp.float32) for _ in range(2)]
+    for row in range(pay_ref.shape[0] // long_count):
+        for source, owner in enumerate((long_index, before)):
+            counts[source] += pay_ref[row * long_count + owner].astype(jnp.float32)
+    total = jnp.sum(far_ref[...].astype(jnp.float32), axis=0)
     group_id = lax.broadcasted_iota(jnp.int32, total.shape, 1) // rank_size
     flat_basis = basis_ref[...].reshape(clusters * rank_size, unknowns)
     even = lax.axis_index("row") % 2 == 0
@@ -286,10 +293,10 @@
         for turn in range(2 * NEARC + 1):
             reach = turn - NEARC
             lower = cluster + min(reach, 0)
-            source = 0 if lower >= 0 else 2
+            source = 0 if lower >= 0 else 1
             kind = (lower if lower >= 0 else lower + clusters) * (NEARC + 1) + abs(reach)
-            lane = (source + kind // COUNT_ROWS) * (LANES // 4)
-            count = counts[kind % COUNT_ROWS : kind % COUNT_ROWS + 1, lane : lane + 1]
+            lane = (2 + kind // half) * rank_size
+            count = counts[source][kind % half : kind % half + 1, lane : lane + 1]
             mine, theirs = own_ref[u + turn, u], other_ref[u + turn, u]
             here = even if cluster < NEARC else jnp.logical_not(even)
             result = result + count * jnp.where(here, mine, theirs).astype(jnp.float32)
@@ -306,38 +313,43 @@
     coupling = far_coef.reshape(-1, rank_size, rank_size)
     slots = clusters + NEARC
 
-    pay, xs = pl.pallas_call(
+    pay = pl.pallas_call(
         coeffs_kernel,
-        out_shape=[
-            jax.ShapeDtypeStruct((long_count, rhs_count, clusters * rank_size), jnp.bfloat16),
-            jax.ShapeDtypeStruct(slip.shape, jnp.bfloat16),
-        ],
-        in_specs=[HBM] * 2,
-        out_specs=[VMEM] * 2,
+        out_shape=jax.ShapeDtypeStruct((devices, rhs_count // 2, LANES), jnp.bfloat16),
+        in_specs=[HBM] * 3 + [SMEM],
+        out_specs=VMEM,
         scratch_shapes=[
-            pltpu.VMEM(slip.shape, slip.dtype),
-            pltpu.VMEM(basis.shape, basis.dtype),
-            pltpu.SemaphoreType.DMA((2,)),
+            pltpu.VMEM(slip.shape[1:], slip.dtype),
+            pltpu.VMEM(basis.shape[1:], basis.dtype),
+            pltpu.VMEM(near_pairs.shape, near_pairs.dtype),
+            pltpu.SemaphoreType.DMA((3,)),
         ],
         compiler_params=pltpu.CompilerParams(vmem_limit_bytes=16 << 20),
         name="coeffs",
-    )(*[pltpu.with_memory_space_constraint(array, pltpu.HBM) for array in (slip, basis)])
-
-    coeffs = lax.all_to_all(pay, "long", 0, 0, tiled=True)
-    to_neighbour, geometry = pl.pallas_call(
+    )(
+        *[
+            pltpu.with_memory_space_constraint(array, pltpu.HBM)
+            for array in (slip, basis, near_pairs)
+        ],
+        near_count,
+    )
+    everyone = lax.all_to_all(pay, ("row", "long"), 0, 0, tiled=True)
+
+    xs, to_neighbour, geometry = pl.pallas_call(
         geometry_kernel,
         out_shape=[
+            jax.ShapeDtypeStruct(slip.shape, jnp.bfloat16),
             jax.ShapeDtypeStruct((NEARC, rhs_count + ROWS, unknowns), jnp.bfloat16),
             jax.ShapeDtypeStruct((clusters, 4, size), jnp.float32),
         ],
-        in_specs=[VMEM] * 4,
-        out_specs=[VMEM] * 2,
+        in_specs=[VMEM] * 4 + [ANY],
+        out_specs=[VMEM] * 3,
         compiler_params=pltpu.CompilerParams(vmem_limit_bytes=16 << 20),
         cost_estimate=pl.CostEstimate(
             flops=2_000_000, bytes_accessed=1_000_000, transcendentals=1_000
         ),
         name="geometry",
-    )(xs, vertices, triangles, elem_map)
+    )(slip, vertices, triangles, elem_map, pay)
     route = []
     for row in range(row_count):
         step = 1 if row % 2 == 0 else -1
@@ -346,25 +358,38 @@
                 route.append((row * long_count + owner - step, row * long_count + owner))
     halo = lax.ppermute(to_neighbour, ("row", "long"), route)
 
+    window, places = pl.pallas_call(
+        window_kernel,
+        out_shape=[
+            jax.ShapeDtypeStruct((slots, rhs_count, unknowns), jnp.bfloat16),
+            jax.ShapeDtypeStruct((slots, 4, size), jnp.float32),
+        ],
+        in_specs=[VMEM] * 3,
+        out_specs=[VMEM] * 2,
+        compiler_params=pltpu.CompilerParams(vmem_limit_bytes=16 << 20),
+        cost_estimate=pl.CostEstimate(
+            flops=500_000_000, bytes_accessed=1_000_000, transcendentals=300_000
+        ),
+        name="window",
+    )(xs, geometry, halo)
+
     far = pl.pallas_call(
         functools.partial(far_kernel, clusters=clusters),
-        out_shape=jax.ShapeDtypeStruct((devices, rhs_count + COUNT_ROWS, LANES), jnp.bfloat16),
-        in_specs=[SMEM, SMEM, VMEM, VMEM, VMEM],
+        out_shape=jax.ShapeDtypeStruct((devices, rhs_count, clusters * rank_size), jnp.bfloat16),
+        in_specs=[SMEM, VMEM, VMEM, ANY],
         out_specs=VMEM,
-        scratch_shapes=[pltpu.VMEM((long_count, rhs_count, LANES), jnp.float32)],
+        scratch_shapes=[pltpu.VMEM((long_count, rhs_count, clusters * rank_size), jnp.float32)],
         compiler_params=pltpu.CompilerParams(vmem_limit_bytes=16 << 20),
         name="far",
-    )(far_pairs, near_count, coeffs, coupling, near_pairs)
+    )(far_pairs, everyone, coupling, places)
     far_terms = lax.all_to_all(far, ("row", "long"), 0, 0, tiled=True)
 
     near = pl.pallas_call(
         near_kernel,
         out_shape=jax.ShapeDtypeStruct((slots, NEARC, rhs_count, unknowns), jnp.bfloat16),
-        in_specs=[VMEM] * 3,
+        in_specs=[VMEM] * 2 + [ANY],
         out_specs=VMEM,
         scratch_shapes=[
-            pltpu.VMEM((slots, rhs_count, unknowns), jnp.bfloat16),
-            pltpu.VMEM((slots, 4, size), jnp.float32),
             pltpu.VMEM((slots, size, 8), jnp.float32),
             pltpu.VMEM((NEARC, 6, size, size), jnp.bfloat16),
             pltpu.VMEM((NEARC, 6, size, size), jnp.bfloat16),
@@ -374,18 +399,18 @@
             flops=1_000_000_000, bytes_accessed=1_000_000, transcendentals=660_000
         ),
         name="near",
-    )(xs, geometry, halo)
+    )(window, places, far)
     partner = [(row, row ^ 1) for row in range(row_count)]
     other = lax.ppermute(near, "row", partner)
 
     return pl.pallas_call(
-        finish_kernel,
+        functools.partial(finish_kernel, long_count=long_count),
         out_shape=jax.ShapeDtypeStruct(slip.shape, jnp.float32),
-        in_specs=[VMEM] * 4,
+        in_specs=[VMEM] * 5,
         out_specs=VMEM,
         compiler_params=pltpu.CompilerParams(vmem_limit_bytes=16 << 20),
         name="finish",
-    )(near, other, far_terms, basis)
+    )(near, other, everyone, far_terms, basis)
 
 
 def solution(mesh):

time: 32.9 us -> 35.4 us (1.076)
  blocking collectives: 0 us -> 9.43 us
  waiting for transfers between devices: 10.5 us -> 7.04 us
  starting transfers between devices: 12.5 us -> 9.93 us
  Pallas kernels: 8.63 us -> 7.77 us
    all_to_all x0 -> x1, blocking collectives: none -> 9.43 us  [shards(): far_terms = lax.all_to_all(far, ('row', 'long'), 0, 0, tiled=True)]
    all_to_all x2 -> x1, starting transfers between devices: 7.47 us -> 4.9 us  [shards(): everyone = lax.all_to_all(pay, ('row', 'long'), 0, 0, tiled=True)]
    all_to_all x2 -> x1, waiting for transfers between devices: 9.05 us -> 7.04 us  [shards(): everyone = lax.all_to_all(pay, ('row', 'long'), 0, 0, tiled=True)]
    ppermute x1, waiting for transfers between devices: 1.47 us -> 0.01 us  [shards(): other = lax.ppermute(near, 'row', partner)]
    pallas_call x1, Pallas kernels: 1.78 us -> 1.08 us  [shards(): pl.pallas_call(functools.partial(far_kernel, clusters=clusters), out_shap...]
    pallas_call x3 -> x4, Pallas kernels: 3.14 us -> 3.02 us  [the longest x1 1.77 us: shards(): pl.pallas_call(coeffs_kernel, out_shape=jax.ShapeDtypeStruct((devices, rh...]
  transfers between devices with their start and end apart: 4 -> 3, of which waited for: 3 -> 1; matrix products, arithmetic and copies ran while one was open for 0% -> 0% of each run, Pallas kernels for 17% -> 0%
where the time goes in v5:
time: 35.4 us; the launch traced here: 35.2 us
  starting transfers between devices  9.93 us (28%)
  blocking collectives  9.43 us (27%)
  Pallas kernels  7.77 us (22%)
  waiting for transfers between devices  7.04 us (20%)
  between operations  0.81 us (2%)
    all_to_all x1, blocking collectives, shards(): far_terms = lax.all_to_all(far, ('row', 'long'), 0, 0, tiled=True)  9.43 us
    all_to_all x1, waiting for transfers between devices, shards(): everyone = lax.all_to_all(pay, ('row', 'long'), 0, 0, tiled=True)  7.04 us
    all_to_all x1, starting transfers between devices, shards(): everyone = lax.all_to_all(pay, ('row', 'long'), 0, 0, tiled=True)  4.9 us
    ppermute x1, starting transfers between devices, shards(): halo = lax.ppermute(to_neighbour, ('row', 'long'), route)  4.88 us
    pallas_call x1, Pallas kernels, shards(): pl.pallas_call(near_kernel, out_shape=jax.ShapeDtypeStruct((slots, NEARC,...  3.67 us
    pallas_call x1, Pallas kernels, shards(): pl.pallas_call(coeffs_kernel, out_shape=jax.ShapeDtypeStruct((devices, rh...  1.77 us
    pallas_call x1, Pallas kernels, shards(): pl.pallas_call(functools.partial(far_kernel, clusters=clusters), out_shap...  1.08 us
    pallas_call x1, Pallas kernels, shards(): pl.pallas_call(functools.partial(finish_kernel, long_count=long_count), o...  0.95 us
  transfers between devices with their start and end apart: 3, of which 1 were waited for; matrix products, arithmetic and copies ran while one was open for 0% of the time, Pallas kernels for 0%

profile of v5, /device:TPU:0, one launch (start us, length us, event | category | flops | bytes accessed | tf_op | source)
XLA Modules:
  0.0 35.2 jit_solution(16292634301129158655)
XLA Ops:
  0.7 0.0 copy-start.1
  0.7 0.0 copy-start.2
  0.7 0.0 copy-start.3
  0.7 0.0 copy-start.4
  0.7 1.8 %coeffs.1.after_ref = bf16[32,8,128]{2,1,0:T(8,128)(2,1)} custom-call(f32[4,16,768]{2,1,0:T(8,128)} %slip_ref.1, bf16[4,32,768]{2,1,0:T(8,128)(2,1)} %basis_ref.1, s32[2,20]{1,0:T(2,128)} %pairs_hbm.1, s32[1]{0:T(128)S(6)} %copy.10.count_ref), custom_call_target="tpu_custom_call" | custom-call | tf_op jit(solution)/shard_map/coeffs/pallas_call | solution.py:316
  2.5 0.0 copy-done.1
  2.5 0.0 copy-done.2
  2.5 0.0 copy-done.3
  2.5 0.0 copy-done.4
  2.5 0.3 geometry.1
  2.8 0.0 copy-start.6
  2.8 4.9 %collective-permute-start = (bf16[2,32,768]{2,1,0:T(8,128)(2,1)S(1)}, bf16[2,32,768]{2,1,0:T(8,128)(2,1)S(1)}, u32[]{:S(2)}, u32[]{:S(2)}) collective-permute-start(bf16[2,32,768]{2,1,0:T(8,128)(2,1)S(1)} %get-tuple-element.12), channel_id=1, source_target_pairs={{0,1},{1,2},{2,3},{3,4},{4,5},{5,6},{6,7},{9,8},{10,9},{11,10},{12... | collective-permute-start | bytes 294920 | tf_op jit(solution)/shard_map/ppermute | solution.py:359
  7.7 4.9 %all-to-all-start = ((bf16[32,8,128]{2,1,0:T(8,128)(2,1)}), bf16[32,8,128]{2,1,0:T(8,128)(2,1)S(1)}, u32[]{:S(2)}, u32[]{:S(2)}) async-start(bf16[32,8,128]{2,1,0:T(8,128)(2,1)} %coeffs.1.after_ref), calls=%async_computation | async-start | bytes 131072 | tf_op jit(solution)/shard_map/all_to_all | solution.py:336
  12.6 0.0 copy-done.6
  12.6 0.1 reshape.3.coupling_ref
  12.7 0.0 collective-permute-done.halo_ref
  12.8 0.0 copy-start.5
  12.8 7.0 %all-to-all-done.coeff_ref.pay_ref = bf16[32,8,128]{2,1,0:T(8,128)(2,1)S(1)} async-done(((bf16[32,8,128]{2,1,0:T(8,128)(2,1)}), bf16[32,8,128]{2,1,0:T(8,128)(2,1)S(1)}, u32[]{:S(2)}, u32[]{:S(2)}) %all-to-all-start) | async-done | bytes 65568 | tf_op jit(solution)/shard_map/all_to_all | solution.py:336
  19.9 0.0 copy-done.5
  19.9 1.1 %far.1.after_ref = bf16[32,16,128]{2,1,0:T(8,128)(2,1)S(1)} custom-call(s32[2,16]{1,0:T(2,128)S(1)} %copy-done.5, bf16[32,8,128]{2,1,0:T(8,128)(2,1)S(1)} %all-to-all-done.coeff_ref.pay_ref, bf16[16,32,32]{2,1,0:T(8,128)(2,1)S(1)} %reshape.3.coupling_ref, f32[6,4,256]{2,1,0:T(4,128)S(1)} %get-tuple-element.14.after_ref.place_ref), custom_call_target="tpu_custom_call" | custom-call | tf_op jit(solution)/shard_map/far/pallas_call | solution.py:376
  21.0 3.7 %near.1.own_ref = bf16[6,2,16,768]{3,2,1,0:T(8,128)(2,1)S(1)} custom-call(bf16[6,16,768]{2,1,0:T(8,128)(2,1)S(1)} %get-tuple-element.13.slip_ref, f32[6,4,256]{2,1,0:T(4,128)S(1)} %get-tuple-element.14.after_ref.place_ref, bf16[32,16,128]{2,1,0:T(8,128)(2,1)S(1)} %far.1.after_ref), custom_call_target="tpu_custom_call" | custom-call | flops 1000000000 | bytes 1000000 | tf_op jit(solution)/shard_map/near/pallas_call | solution.py:387
  24.6 0.0 copy-start
  24.6 0.2 collective-permute-start.1
  24.8 9.4 %all_to_all.10.far_ref = bf16[32,16,128]{2,1,0:T(8,128)(2,1)S(1)} all-to-all(bf16[32,16,128]{2,1,0:T(8,128)(2,1)S(1)} %far.1.after_ref), channel_id=1, replica_groups=mesh['row'=4,'long'=8] {'row','long'}, dimensions={0} | all-to-all | bytes 262144 | tf_op jit(solution)/shard_map/all_to_all | solution.py:385
  34.2 0.0 collective-permute-done.1.other_ref
  34.2 0.0 copy-done
  34.2 0.9 %finish.1 = f32[4,16,768]{2,1,0:T(8,128)} custom-call(bf16[6,2,16,768]{3,2,1,0:T(8,128)(2,1)S(1)} %near.1.own_ref, bf16[6,2,16,768]{3,2,1,0:T(8,128)(2,1)S(1)} %collective-permute-done.1.other_ref, bf16[32,8,128]{2,1,0:T(8,128)(2,1)S(1)} %all-to-all-done.coeff_ref.pay_ref, bf16[32,16,128]{2,1,0:T(8,128)(2,1)S(1)} %all_to_all.10.far_ref, ...), custom_call_target="tpu_custom_call" | custom-call | tf_op jit(solution)/shard_map/finish/pallas_call | solution.py:406
  (1 shorter events, 0.0 us)
Async XLA Ops:
  0.7 1.8 %copy-start.1 = (f32[4,16,768]{2,1,0:T(8,128)S(1)}, f32[4,16,768]{2,1,0:T(8,128)}, u32[]{:S(2)}) copy-start(f32[4,16,768]{2,1,0:T(8,128)} %slip_ref.1) | copy-start | bytes 589828
  0.7 1.8 %copy-start.2 = (s32[3,1024]{1,0:T(4,128)S(1)}, s32[3,1024]{1,0:T(4,128)}, u32[]{:S(2)}) copy-start(s32[3,1024]{1,0:T(4,128)} %triangles_ref.1) | copy-start | bytes 36868
  0.7 1.8 %copy-start.3 = (f32[3,561]{1,0:T(4,128)S(1)}, f32[3,561]{1,0:T(4,128)}, u32[]{:S(2)}) copy-start(f32[3,561]{1,0:T(4,128)} %vertices_ref.1) | copy-start | bytes 20200
  0.7 1.8 %copy-start.4 = (s32[4,256]{1,0:T(4,128)S(1)}, s32[4,256]{1,0:T(4,128)}, u32[]{:S(2)}) copy-start(s32[4,256]{1,0:T(4,128)} %map_ref.1) | copy-start | bytes 12292
  2.8 9.8 %copy-start.6 = (bf16[16,1024]{1,0:T(8,128)(2,1)S(1)}, bf16[16,1024]{1,0:T(8,128)(2,1)}, u32[]{:S(2)}) copy-start(bf16[16,1024]{1,0:T(8,128)(2,1)} %param.16) | copy-start | bytes 98308
  2.8 10.0 %collective-permute-start = (bf16[2,32,768]{2,1,0:T(8,128)(2,1)S(1)}, bf16[2,32,768]{2,1,0:T(8,128)(2,1)S(1)}, u32[]{:S(2)}, u32[]{:S(2)}) collective-permute-start(bf16[2,32,768]{2,1,0:T(8,128)(2,1)S(1)} %get-tuple-element.12), channel_id=1, source_target_pairs={{0,1},{1,2},{2,3},{3,4},{4,5},{5,6},{6,7},{9,8},{10,9},{11,10},{12... | collective-permute-start | bytes 294920 | tf_op jit(solution)/shard_map/ppermute | solution.py:359
  7.7 12.2 %all-to-all-start = ((bf16[32,8,128]{2,1,0:T(8,128)(2,1)}), bf16[32,8,128]{2,1,0:T(8,128)(2,1)S(1)}, u32[]{:S(2)}, u32[]{:S(2)}) async-start(bf16[32,8,128]{2,1,0:T(8,128)(2,1)} %coeffs.1.after_ref), calls=%async_computation | async-start | bytes 131072 | tf_op jit(solution)/shard_map/all_to_all | solution.py:336
  12.8 7.1 %copy-start.5 = (s32[2,16]{1,0:T(2,128)S(1)}, s32[2,16]{1,0:T(2,128)}, u32[]{:S(2)}) copy-start(s32[2,16]{1,0:T(2,128)} %pairs_ref.1) | copy-start | bytes 388
  24.6 9.6 %copy-start = (bf16[4,32,768]{2,1,0:T(8,128)(2,1)S(1)}, bf16[4,32,768]{2,1,0:T(8,128)(2,1)}, u32[]{:S(2)}) copy-start(bf16[4,32,768]{2,1,0:T(8,128)(2,1)} %basis_ref.1) | copy-start | bytes 589828
  24.6 9.6 %collective-permute-start.1 = (bf16[6,2,16,768]{3,2,1,0:T(8,128)(2,1)S(1)}, bf16[6,2,16,768]{3,2,1,0:T(8,128)(2,1)S(1)}, u32[]{:S(2)}, u32[]{:S(2)}) collective-permute-start(bf16[6,2,16,768]{3,2,1,0:T(8,128)(2,1)S(1)} %near.1.own_ref), channel_id=1, source_target_pairs={{0,8},{8,0},{16,24},{24,16},{1,9},{9,1},{17,25},{25,17},{2,10},{10... | collective-permute-start | bytes 884744 | tf_op jit(solution)/shard_map/ppermute | solution.py:404

commit v6 on v5

--- a/solution.py
+++ b/solution.py
@@ -57,7 +57,6 @@
         copy.start()
     for copy in copies:
         copy.wait()
-    half = rhs_count // 2
     wide = jnp.concatenate([basis_ref[...]] * (LANES // rank_size), axis=0)
     coeffs = lax.dot_general(
         slip_ref[...].astype(jnp.bfloat16),
@@ -67,14 +66,11 @@
     )
     first = pairs_ref[0:1, :]
     kind = (first - lax.axis_index("long") * clusters) * (NEARC + 1) + pairs_ref[1:2, :] - first
-    kinds = lax.broadcasted_iota(jnp.int32, (half, kind.shape[1]), 0)
+    kinds = lax.broadcasted_iota(jnp.int32, (rhs_count, kind.shape[1]), 0)
     live = lax.broadcasted_iota(jnp.int32, kinds.shape, 1) < count_ref[0]
-    low = jnp.sum(jnp.where(live & (kinds == kind), 1.0, 0.0), axis=1, keepdims=True)
-    high = jnp.sum(jnp.where(live & (kinds + half == kind), 1.0, 0.0), axis=1, keepdims=True)
-    group = lax.broadcasted_iota(jnp.int32, (half, LANES), 1) // rank_size
-    pay = jnp.where(
-        group == 0, coeffs[0:half], jnp.where(group == 1, coeffs[half:], jnp.where(group == 2, low, high))
-    ).astype(jnp.bfloat16)
+    counts = jnp.sum(jnp.where(live & (kinds == kind), 1.0, 0.0), axis=1, keepdims=True)
+    lane_id = lax.broadcasted_iota(jnp.int32, coeffs.shape, 1)
+    pay = jnp.where(lane_id < rank_size, coeffs, counts).astype(jnp.bfloat16)
     for target in range(pay_ref.shape[0]):
         pay_ref[target] = pay
 
@@ -130,13 +126,10 @@
             jnp.where(upward, piece[last : last + 1, :], piece[turn : turn + 1, :])
             for piece in pieces
         ]
-        rows.append(jnp.zeros((ROWS - len(rows), size), jnp.float32))
-        halo_ref[turn, 0:rhs_count, :] = xs_ref[start + turn]
-        halo_ref[turn, rhs_count : rhs_count + ROWS, 0:size] = jnp.concatenate(
-            rows, axis=0
-        ).astype(jnp.bfloat16)
-        halo_ref[turn, rhs_count : rhs_count + ROWS, size:unknowns] = jnp.zeros(
-            (ROWS, unknowns - size), jnp.bfloat16
+        rows.append(jnp.zeros((rhs_count - len(rows), size), jnp.float32))
+        halo_ref[turn, :, 0:unknowns] = xs_ref[start + turn]
+        halo_ref[turn, :, unknowns : unknowns + size] = jnp.concatenate(rows, axis=0).astype(
+            jnp.bfloat16
         )
 
 
@@ -154,8 +147,8 @@
         place_ref[place_of(cluster)] = geom_ref[cluster]
     for turn in range(NEARC):
         at = place_of(clusters + turn)
-        slip_ref[at] = halo_ref[turn, 0:rhs_count, :]
-        pieces = halo_ref[turn, rhs_count : rhs_count + ROWS, 0:size].astype(jnp.float32)
+        slip_ref[at] = halo_ref[turn, :, 0:unknowns]
+        pieces = halo_ref[turn, :, unknowns : unknowns + size].astype(jnp.float32)
         place_ref[at] = jnp.concatenate(
             [
                 (pieces[3 * p + 2 : 3 * p + 3] + pieces[3 * p + 1 : 3 * p + 2])
@@ -166,7 +159,7 @@
         )
 
 
-def near_kernel(slip_ref, place_ref, after_ref, out_ref, cols_ref, even_ref, odd_ref):
+def near_kernel(slip_ref, place_ref, out_ref, cols_ref, even_ref, odd_ref):
     slots, rhs_count, unknowns = slip_ref.shape
     size = place_ref.shape[2]
     for place in range(slots):
@@ -240,11 +233,8 @@
     total_ref[...] = jnp.zeros(total_ref.shape, jnp.float32)
 
     def coeff_of(cluster):
-        whole = coeff_ref[(cluster % clusters) * long_count + cluster // clusters]
-        whole = whole.astype(jnp.float32)
-        return jnp.concatenate(
-            [whole[:, 0:rank_size], whole[:, rank_size : 2 * rank_size]], axis=0
-        ).astype(jnp.bfloat16)
+        at = (cluster % clusters) * long_count + cluster // clusters
+        return coeff_ref[at][:, 0:rank_size]
 
     results = []
     for pair_id in range(pairs_ref.shape[1]):
@@ -277,7 +267,6 @@
     clusters, rank_size, unknowns = basis_ref.shape
     long_index = lax.axis_index("long")
     before = jnp.maximum(long_index - 1, 0)
-    half = pay_ref.shape[1]
     counts = [jnp.zeros(pay_ref.shape[1:], jnp.float32) for _ in range(2)]
     for row in range(pay_ref.shape[0] // long_count):
         for source, owner in enumerate((long_index, before)):
@@ -295,8 +284,7 @@
             lower = cluster + min(reach, 0)
             source = 0 if lower >= 0 else 1
             kind = (lower if lower >= 0 else lower + clusters) * (NEARC + 1) + abs(reach)
-            lane = (2 + kind // half) * rank_size
-            count = counts[source][kind % half : kind % half + 1, lane : lane + 1]
+            count = counts[source][kind : kind + 1, LANES - 1 : LANES]
             mine, theirs = own_ref[u + turn, u], other_ref[u + turn, u]
             here = even if cluster < NEARC else jnp.logical_not(even)
             result = result + count * jnp.where(here, mine, theirs).astype(jnp.float32)
@@ -315,7 +303,7 @@
 
     pay = pl.pallas_call(
         coeffs_kernel,
-        out_shape=jax.ShapeDtypeStruct((devices, rhs_count // 2, LANES), jnp.bfloat16),
+        out_shape=jax.ShapeDtypeStruct((devices, rhs_count, LANES), jnp.bfloat16),
         in_specs=[HBM] * 3 + [SMEM],
         out_specs=VMEM,
         scratch_shapes=[
@@ -339,7 +327,7 @@
         geometry_kernel,
         out_shape=[
             jax.ShapeDtypeStruct(slip.shape, jnp.bfloat16),
-            jax.ShapeDtypeStruct((NEARC, rhs_count + ROWS, unknowns), jnp.bfloat16),
+            jax.ShapeDtypeStruct((NEARC, rhs_count, unknowns + size), jnp.bfloat16),
             jax.ShapeDtypeStruct((clusters, 4, size), jnp.float32),
         ],
         in_specs=[VMEM] * 4 + [ANY],
@@ -367,9 +355,7 @@
         in_specs=[VMEM] * 3,
         out_specs=[VMEM] * 2,
         compiler_params=pltpu.CompilerParams(vmem_limit_bytes=16 << 20),
-        cost_estimate=pl.CostEstimate(
-            flops=500_000_000, bytes_accessed=1_000_000, transcendentals=300_000
-        ),
+        cost_estimate=pl.CostEstimate(flops=1000, bytes_accessed=1000, transcendentals=0),
         name="window",
     )(xs, geometry, halo)
 
@@ -387,7 +373,7 @@
     near = pl.pallas_call(
         near_kernel,
         out_shape=jax.ShapeDtypeStruct((slots, NEARC, rhs_count, unknowns), jnp.bfloat16),
-        in_specs=[VMEM] * 2 + [ANY],
+        in_specs=[VMEM] * 2,
         out_specs=VMEM,
         scratch_shapes=[
             pltpu.VMEM((slots, size, 8), jnp.float32),
@@ -399,7 +385,7 @@
             flops=1_000_000_000, bytes_accessed=1_000_000, transcendentals=660_000
         ),
         name="near",
-    )(window, places, far)
+    )(window, places)
     partner = [(row, row ^ 1) for row in range(row_count)]
     other = lax.ppermute(near, "row", partner)
 

time: 35.4 us -> 37.2 us (1.051)
  blocking collectives: 9.43 us -> 0 us
  starting transfers between devices: 9.93 us -> 16.6 us
  waiting for transfers between devices: 7.04 us -> 10.5 us
  Pallas kernels: 7.77 us -> 8.38 us
  local copies, waits for them, and re-layouts: 0.18 us -> 0.65 us
    all_to_all x1 -> x0, blocking collectives: 9.43 us -> none  [shards(): far_terms = lax.all_to_all(far, ('row', 'long'), 0, 0, tiled=True)]
    all_to_all x0 -> x1, waiting for transfers between devices: none -> 7.73 us  [shards(): far_terms = lax.all_to_all(far, ('row', 'long'), 0, 0, tiled=True)]
    all_to_all x1, waiting for transfers between devices: 7.04 us -> 0.01 us  [shards(): everyone = lax.all_to_all(pay, ('row', 'long'), 0, 0, tiled=True)]
    all_to_all x0 -> x1, starting transfers between devices: none -> 5.55 us  [shards(): far_terms = lax.all_to_all(far, ('row', 'long'), 0, 0, tiled=True)]
    ppermute x1, waiting for transfers between devices: 0.01 us -> 2.76 us  [shards(): halo = lax.ppermute(to_neighbour, ('row', 'long'), route)]
    all_to_all x1, starting transfers between devices: 4.9 us -> 7.3 us  [shards(): everyone = lax.all_to_all(pay, ('row', 'long'), 0, 0, tiled=True)]
    ppermute x1, starting transfers between devices: 4.88 us -> 3.68 us  [shards(): halo = lax.ppermute(to_neighbour, ('row', 'long'), route)]
    pallas_call x1, Pallas kernels: 1.08 us -> 1.76 us  [shards(): pl.pallas_call(functools.partial(far_kernel, clusters=clusters), out_shap...]
  transfers between devices with their start and end apart: 3 -> 4, of which waited for: 1 -> 2; matrix products, arithmetic and copies ran while one was open for 0% -> 0% of each run, Pallas kernels for 0% -> 16%
where the time goes in v6:
time: 37.2 us; the launch traced here: 36.9 us
  starting transfers between devices  16.6 us (45%)
  waiting for transfers between devices  10.5 us (28%)
  Pallas kernels  8.38 us (23%)
  between operations  0.81 us (2%)
  local copies, waits for them, and re-layouts  0.65 us (2%)
    all_to_all x1, waiting for transfers between devices, shards(): far_terms = lax.all_to_all(far, ('row', 'long'), 0, 0, tiled=True)  7.73 us
    all_to_all x1, starting transfers between devices, shards(): everyone = lax.all_to_all(pay, ('row', 'long'), 0, 0, tiled=True)  7.3 us
    all_to_all x1, starting transfers between devices, shards(): far_terms = lax.all_to_all(far, ('row', 'long'), 0, 0, tiled=True)  5.55 us
    ppermute x1, starting transfers between devices, shards(): halo = lax.ppermute(to_neighbour, ('row', 'long'), route)  3.68 us
    pallas_call x1, Pallas kernels, shards(): pl.pallas_call(near_kernel, out_shape=jax.ShapeDtypeStruct((slots, NEARC,...  3.67 us
    ppermute x1, waiting for transfers between devices, shards(): halo = lax.ppermute(to_neighbour, ('row', 'long'), route)  2.76 us
    pallas_call x1, Pallas kernels, shards(): pl.pallas_call(functools.partial(far_kernel, clusters=clusters), out_shap...  1.76 us
    pallas_call x1, Pallas kernels, shards(): pl.pallas_call(coeffs_kernel, out_shape=jax.ShapeDtypeStruct((devices, rh...  1.71 us
  transfers between devices with their start and end apart: 4, of which 2 were waited for; matrix products, arithmetic and copies ran while one was open for 0% of the time, Pallas kernels for 16%

profile of v6, /device:TPU:0, one launch (start us, length us, event | category | flops | bytes accessed | tf_op | source)
XLA Modules:
  0.0 36.9 jit_solution(8755760072702294973)
XLA Ops:
  0.7 1.7 %coeffs.1.after_ref = bf16[32,16,128]{2,1,0:T(8,128)(2,1)} custom-call(f32[4,16,768]{2,1,0:T(8,128)} %slip_ref.1, bf16[4,32,768]{2,1,0:T(8,128)(2,1)} %basis_ref.1, s32[2,20]{1,0:T(2,128)} %pairs_hbm.1, s32[1]{0:T(128)S(6)} %copy.10.count_ref), custom_call_target="tpu_custom_call" | custom-call | tf_op jit(solution)/shard_map/coeffs/pallas_call | solution.py:304
  2.4 0.0 copy-start.1
  2.4 0.0 copy-start.2
  2.4 0.0 copy-start.3
  2.4 0.0 copy-start.4
  2.4 7.3 %all-to-all-start = ((bf16[32,16,128]{2,1,0:T(8,128)(2,1)}), bf16[32,16,128]{2,1,0:T(8,128)(2,1)S(1)}, u32[]{:S(2)}, u32[]{:S(2)}) async-start(bf16[32,16,128]{2,1,0:T(8,128)(2,1)} %coeffs.1.after_ref), calls=%async_computation | async-start | bytes 262144 | tf_op jit(solution)/shard_map/all_to_all | solution.py:324
  9.7 0.0 copy-done.1
  9.7 0.0 copy-done.2
  9.8 0.0 copy-done.3
  9.8 0.0 copy-done.4
  9.8 0.3 geometry.1
  10.0 3.7 %collective-permute-start = (bf16[2,16,1024]{2,1,0:T(8,128)(2,1)S(1)}, bf16[2,16,1024]{2,1,0:T(8,128)(2,1)S(1)}, u32[]{:S(2)}, u32[]{:S(2)}) collective-permute-start(bf16[2,16,1024]{2,1,0:T(8,128)(2,1)S(1)} %get-tuple-element.12), channel_id=1, source_target_pairs={{0,1},{1,2},{2,3},{3,4},{4,5},{5,6},{6,7},{9,8},{10,9},{11,10},{12... | collective-permute-start | bytes 196616 | tf_op jit(solution)/shard_map/ppermute | solution.py:347
  13.7 2.8 %collective-permute-done.halo_ref = bf16[2,16,1024]{2,1,0:T(8,128)(2,1)S(1)} collective-permute-done((bf16[2,16,1024]{2,1,0:T(8,128)(2,1)S(1)}, bf16[2,16,1024]{2,1,0:T(8,128)(2,1)S(1)}, u32[]{:S(2)}, u32[]{:S(2)}) %collective-permute-start) | collective-permute-done | bytes 65568 | tf_op jit(solution)/shard_map/ppermute | solution.py:347
  16.5 0.0 copy-start.6
  16.5 3.7 %near.1.own_ref = bf16[6,2,16,768]{3,2,1,0:T(8,128)(2,1)S(1)} custom-call(bf16[6,16,768]{2,1,0:T(8,128)(2,1)S(1)} %get-tuple-element.13.slip_ref, f32[6,4,256]{2,1,0:T(4,128)S(1)} %get-tuple-element.14.place_ref.after_ref), custom_call_target="tpu_custom_call" | custom-call | flops 1000000000 | bytes 1000000 | tf_op jit(solution)/shard_map/near/pallas_call | solution.py:373
  20.2 0.0 copy-start.5
  20.2 0.0 collective-permute-start.1
  20.3 0.0 copy-done.6
  20.3 0.1 reshape.3.coupling_ref
  20.4 0.0 all-to-all-done.coeff_ref.pay_ref
  20.4 0.5 %copy-done.5 = s32[2,16]{1,0:T(2,128)S(1)} copy-done((s32[2,16]{1,0:T(2,128)S(1)}, s32[2,16]{1,0:T(2,128)}, u32[]{:S(2)}) %copy-start.5) | copy-done | bytes 152
  20.9 1.8 %far.1 = bf16[32,16,128]{2,1,0:T(8,128)(2,1)} custom-call(s32[2,16]{1,0:T(2,128)S(1)} %copy-done.5, bf16[32,16,128]{2,1,0:T(8,128)(2,1)S(1)} %all-to-all-done.coeff_ref.pay_ref, bf16[16,32,32]{2,1,0:T(8,128)(2,1)S(1)} %reshape.3.coupling_ref, f32[6,4,256]{2,1,0:T(4,128)S(1)} %get-tuple-element.14.place_ref.after_ref), custom_call_target="tpu_custom_call" | custom-call | tf_op jit(solution)/shard_map/far/pallas_call | solution.py:362
  22.7 0.0 copy-start
  22.7 5.5 %all-to-all-start.1 = ((bf16[32,16,128]{2,1,0:T(8,128)(2,1)}), bf16[32,16,128]{2,1,0:T(8,128)(2,1)S(1)}, u32[]{:S(2)}, u32[]{:S(2)}) async-start(bf16[32,16,128]{2,1,0:T(8,128)(2,1)} %far.1), calls=%async_computation.1 | async-start | bytes 262144 | tf_op jit(solution)/shard_map/all_to_all | solution.py:371
  28.2 0.0 collective-permute-done.1.other_ref
  28.2 7.7 %all-to-all-done.1.far_ref = bf16[32,16,128]{2,1,0:T(8,128)(2,1)S(1)} async-done(((bf16[32,16,128]{2,1,0:T(8,128)(2,1)}), bf16[32,16,128]{2,1,0:T(8,128)(2,1)S(1)}, u32[]{:S(2)}, u32[]{:S(2)}) %all-to-all-start.1) | async-done | bytes 131104 | tf_op jit(solution)/shard_map/all_to_all | solution.py:371
  36.0 0.0 copy-done
  36.0 0.9 %finish.1 = f32[4,16,768]{2,1,0:T(8,128)} custom-call(bf16[6,2,16,768]{3,2,1,0:T(8,128)(2,1)S(1)} %near.1.own_ref, bf16[6,2,16,768]{3,2,1,0:T(8,128)(2,1)S(1)} %collective-permute-done.1.other_ref, bf16[32,16,128]{2,1,0:T(8,128)(2,1)S(1)} %all-to-all-done.coeff_ref.pay_ref, bf16[32,16,128]{2,1,0:T(8,128)(2,1)S(1)} %all-to-all-done.1.far_ref, ...), custom_call_target="tpu_custom_call" | custom-call | tf_op jit(solution)/shard_map/finish/pallas_call | solution.py:392
  (1 shorter events, 0.0 us)
Async XLA Ops:
  2.4 7.4 %copy-start.1 = (f32[4,16,768]{2,1,0:T(8,128)S(1)}, f32[4,16,768]{2,1,0:T(8,128)}, u32[]{:S(2)}) copy-start(f32[4,16,768]{2,1,0:T(8,128)} %slip_ref.1) | copy-start | bytes 589828
  2.4 7.4 %copy-start.2 = (s32[3,1024]{1,0:T(4,128)S(1)}, s32[3,1024]{1,0:T(4,128)}, u32[]{:S(2)}) copy-start(s32[3,1024]{1,0:T(4,128)} %triangles_ref.1) | copy-start | bytes 36868
  2.4 7.4 %copy-start.3 = (f32[3,561]{1,0:T(4,128)S(1)}, f32[3,561]{1,0:T(4,128)}, u32[]{:S(2)}) copy-start(f32[3,561]{1,0:T(4,128)} %vertices_ref.1) | copy-start | bytes 20200
  2.4 7.4 %copy-start.4 = (s32[4,256]{1,0:T(4,128)S(1)}, s32[4,256]{1,0:T(4,128)}, u32[]{:S(2)}) copy-start(s32[4,256]{1,0:T(4,128)} %map_ref.1) | copy-start | bytes 12292
  2.4 18.0 %all-to-all-start = ((bf16[32,16,128]{2,1,0:T(8,128)(2,1)}), bf16[32,16,128]{2,1,0:T(8,128)(2,1)S(1)}, u32[]{:S(2)}, u32[]{:S(2)}) async-start(bf16[32,16,128]{2,1,0:T(8,128)(2,1)} %coeffs.1.after_ref), calls=%async_computation | async-start | bytes 262144 | tf_op jit(solution)/shard_map/all_to_all | solution.py:324
  10.0 6.4 %collective-permute-start = (bf16[2,16,1024]{2,1,0:T(8,128)(2,1)S(1)}, bf16[2,16,1024]{2,1,0:T(8,128)(2,1)S(1)}, u32[]{:S(2)}, u32[]{:S(2)}) collective-permute-start(bf16[2,16,1024]{2,1,0:T(8,128)(2,1)S(1)} %get-tuple-element.12), channel_id=1, source_target_pairs={{0,1},{1,2},{2,3},{3,4},{4,5},{5,6},{6,7},{9,8},{10,9},{11,10},{12... | collective-permute-start | bytes 196616 | tf_op jit(solution)/shard_map/ppermute | solution.py:347
  16.5 3.7 %copy-start.6 = (bf16[16,1024]{1,0:T(8,128)(2,1)S(1)}, bf16[16,1024]{1,0:T(8,128)(2,1)}, u32[]{:S(2)}) copy-start(bf16[16,1024]{1,0:T(8,128)(2,1)} %param.16) | copy-start | bytes 98308
  20.2 0.7 %copy-start.5 = (s32[2,16]{1,0:T(2,128)S(1)}, s32[2,16]{1,0:T(2,128)}, u32[]{:S(2)}) copy-start(s32[2,16]{1,0:T(2,128)} %pairs_ref.1) | copy-start | bytes 388
  20.2 8.0 %collective-permute-start.1 = (bf16[6,2,16,768]{3,2,1,0:T(8,128)(2,1)S(1)}, bf16[6,2,16,768]{3,2,1,0:T(8,128)(2,1)S(1)}, u32[]{:S(2)}, u32[]{:S(2)}) collective-permute-start(bf16[6,2,16,768]{3,2,1,0:T(8,128)(2,1)S(1)} %near.1.own_ref), channel_id=1, source_target_pairs={{0,8},{8,0},{16,24},{24,16},{1,9},{9,1},{17,25},{25,17},{2,10},{10... | collective-permute-start | bytes 884744 | tf_op jit(solution)/shard_map/ppermute | solution.py:390
  22.7 13.3 %copy-start = (bf16[4,32,768]{2,1,0:T(8,128)(2,1)S(1)}, bf16[4,32,768]{2,1,0:T(8,128)(2,1)}, u32[]{:S(2)}) copy-start(bf16[4,32,768]{2,1,0:T(8,128)(2,1)} %basis_ref.1) | copy-start | bytes 589828
  22.7 13.3 %all-to-all-start.1 = ((bf16[32,16,128]{2,1,0:T(8,128)(2,1)}), bf16[32,16,128]{2,1,0:T(8,128)(2,1)S(1)}, u32[]{:S(2)}, u32[]{:S(2)}) async-start(bf16[32,16,128]{2,1,0:T(8,128)(2,1)} %far.1), calls=%async_computation.1 | async-start | bytes 262144 | tf_op jit(solution)/shard_map/all_to_all | solution.py:371

commit v7 on v6

--- a/solution.py
+++ b/solution.py
@@ -159,7 +159,7 @@
         )
 
 
-def near_kernel(slip_ref, place_ref, out_ref, cols_ref, even_ref, odd_ref):
+def near_kernel(slip_ref, place_ref, after_ref, out_ref, cols_ref, even_ref, odd_ref):
     slots, rhs_count, unknowns = slip_ref.shape
     size = place_ref.shape[2]
     for place in range(slots):
@@ -225,7 +225,10 @@
     out_ref[slots - 1, 0] = jnp.zeros(out_ref.shape[2:], jnp.bfloat16)
 
 
-def far_kernel(pairs_ref, coeff_ref, coupling_ref, after_ref, out_ref, total_ref, *, clusters):
+def far_kernel(
+    pairs_ref, coeff_ref, coupling_ref, after_ref, out_ref, done_ref, total_ref, *, clusters
+):
+    done_ref[...] = jnp.zeros(done_ref.shape, jnp.float32)
     long_count, rhs_count, _ = total_ref.shape
     rank_size = coupling_ref.shape[1]
     groups = LANES // rank_size
@@ -263,21 +266,17 @@
         out_ref[copy_id * long_count : (copy_id + 1) * long_count] = sent
 
 
-def finish_kernel(own_ref, other_ref, pay_ref, far_ref, basis_ref, out_ref, *, long_count):
-    clusters, rank_size, unknowns = basis_ref.shape
+def weigh_kernel(own_ref, other_ref, pay_ref, out_ref, *, long_count):
+    clusters = out_ref.shape[0]
     long_index = lax.axis_index("long")
     before = jnp.maximum(long_index - 1, 0)
     counts = [jnp.zeros(pay_ref.shape[1:], jnp.float32) for _ in range(2)]
     for row in range(pay_ref.shape[0] // long_count):
         for source, owner in enumerate((long_index, before)):
             counts[source] += pay_ref[row * long_count + owner].astype(jnp.float32)
-    total = jnp.sum(far_ref[...].astype(jnp.float32), axis=0)
-    group_id = lax.broadcasted_iota(jnp.int32, total.shape, 1) // rank_size
-    flat_basis = basis_ref[...].reshape(clusters * rank_size, unknowns)
     even = lax.axis_index("row") % 2 == 0
     for cluster in range(clusters):
-        picked = jnp.where(group_id == cluster, total, 0.0).astype(jnp.bfloat16)
-        result = jnp.dot(picked, flat_basis, preferred_element_type=jnp.float32)
+        result = jnp.zeros(out_ref.shape[1:], jnp.float32)
         u = cluster % NEARC
         for turn in range(2 * NEARC + 1):
             reach = turn - NEARC
@@ -289,6 +288,17 @@
             here = even if cluster < NEARC else jnp.logical_not(even)
             result = result + count * jnp.where(here, mine, theirs).astype(jnp.float32)
         out_ref[cluster] = result
+
+
+def finish_kernel(near_ref, far_ref, basis_ref, out_ref):
+    clusters, rank_size, unknowns = basis_ref.shape
+    total = jnp.sum(far_ref[...].astype(jnp.float32), axis=0)
+    group_id = lax.broadcasted_iota(jnp.int32, total.shape, 1) // rank_size
+    flat_basis = basis_ref[...].reshape(clusters * rank_size, unknowns)
+    for cluster in range(clusters):
+        picked = jnp.where(group_id == cluster, total, 0.0).astype(jnp.bfloat16)
+        result = jnp.dot(picked, flat_basis, preferred_element_type=jnp.float32)
+        out_ref[cluster] = result + near_ref[cluster]
 
 
 def shards(slip, vertices, triangles, elem_map, near_pairs, near_count, far_pairs, far_coef, basis):
@@ -359,11 +369,14 @@
         name="window",
     )(xs, geometry, halo)
 
-    far = pl.pallas_call(
+    far, far_done = pl.pallas_call(
         functools.partial(far_kernel, clusters=clusters),
-        out_shape=jax.ShapeDtypeStruct((devices, rhs_count, clusters * rank_size), jnp.bfloat16),
+        out_shape=[
+            jax.ShapeDtypeStruct((devices, rhs_count, clusters * rank_size), jnp.bfloat16),
+            jax.ShapeDtypeStruct((8, LANES), jnp.float32),
+        ],
         in_specs=[SMEM, VMEM, VMEM, ANY],
-        out_specs=VMEM,
+        out_specs=[VMEM] * 2,
         scratch_shapes=[pltpu.VMEM((long_count, rhs_count, clusters * rank_size), jnp.float32)],
         compiler_params=pltpu.CompilerParams(vmem_limit_bytes=16 << 20),
         name="far",
@@ -373,7 +386,7 @@
     near = pl.pallas_call(
         near_kernel,
         out_shape=jax.ShapeDtypeStruct((slots, NEARC, rhs_count, unknowns), jnp.bfloat16),
-        in_specs=[VMEM] * 2,
+        in_specs=[VMEM] * 2 + [ANY],
         out_specs=VMEM,
         scratch_shapes=[
             pltpu.VMEM((slots, size, 8), jnp.float32),
@@ -385,18 +398,30 @@
             flops=1_000_000_000, bytes_accessed=1_000_000, transcendentals=660_000
         ),
         name="near",
-    )(window, places)
+    )(window, places, far_done)
     partner = [(row, row ^ 1) for row in range(row_count)]
     other = lax.ppermute(near, "row", partner)
 
+    near_field = pl.pallas_call(
+        functools.partial(weigh_kernel, long_count=long_count),
+        out_shape=jax.ShapeDtypeStruct(slip.shape, jnp.float32),
+        in_specs=[VMEM] * 3,
+        out_specs=VMEM,
+        compiler_params=pltpu.CompilerParams(vmem_limit_bytes=16 << 20),
+        cost_estimate=pl.CostEstimate(
+            flops=500_000_000, bytes_accessed=1_000_000, transcendentals=0
+        ),
+        name="weigh",
+    )(near, other, everyone)
+
     return pl.pallas_call(
-        functools.partial(finish_kernel, long_count=long_count),
+        finish_kernel,
         out_shape=jax.ShapeDtypeStruct(slip.shape, jnp.float32),
-        in_specs=[VMEM] * 5,
+        in_specs=[VMEM] * 3,
         out_specs=VMEM,
         compiler_params=pltpu.CompilerParams(vmem_limit_bytes=16 << 20),
         name="finish",
-    )(near, other, everyone, far_terms, basis)
+    )(near_field, far_terms, basis)
 
 
 def solution(mesh):

time: 37.2 us -> 37.3 us (level)
  waiting for transfers between devices: 10.5 us -> 11 us
  local copies, waits for them, and re-layouts: 0.65 us -> 0.19 us
    all_to_all x1, waiting for transfers between devices: 0.01 us -> 0.92 us  [shards(): everyone = lax.all_to_all(pay, ('row', 'long'), 0, 0, tiled=True)]
    unnamed x14, local copies, waits for them, and re-layouts: 0.5 us -> 0.04 us
    pallas_call x1 -> x2, Pallas kernels: 0.94 us -> 1.14 us  [the longest x1 0.93 us: shards(): pl.pallas_call(finish_kernel, out_shape=jax.ShapeDtypeStruct(slip.shape,...]
  transfers between devices with their start and end apart: 4 -> 4, of which waited for: 2 -> 3; matrix products, arithmetic and copies ran while one was open for 0% -> 0% of each run, Pallas kernels for 16% -> 1%
where the time goes in v7:
time: 37.3 us; the launch traced here: 37 us
  starting transfers between devices  16.4 us (44%)
  waiting for transfers between devices  11 us (29%)
  Pallas kernels  8.58 us (23%)
  between operations  0.82 us (2%)
    all_to_all x1, waiting for transfers between devices, shards(): far_terms = lax.all_to_all(far, ('row', 'long'), 0, 0, tiled=True)  7.49 us
    all_to_all x1, starting transfers between devices, shards(): everyone = lax.all_to_all(pay, ('row', 'long'), 0, 0, tiled=True)  7.3 us
    all_to_all x1, starting transfers between devices, shards(): far_terms = lax.all_to_all(far, ('row', 'long'), 0, 0, tiled=True)  5.3 us
    ppermute x1, starting transfers between devices, shards(): halo = lax.ppermute(to_neighbour, ('row', 'long'), route)  3.68 us
    pallas_call x1, Pallas kernels, shards(): pl.pallas_call(near_kernel, out_shape=jax.ShapeDtypeStruct((slots, NEARC,...  3.67 us
    ppermute x1, waiting for transfers between devices, shards(): halo = lax.ppermute(to_neighbour, ('row', 'long'), route)  2.6 us
    pallas_call x1, Pallas kernels, shards(): pl.pallas_call(functools.partial(far_kernel, clusters=clusters), out_shap...  1.76 us
    pallas_call x1, Pallas kernels, shards(): pl.pallas_call(coeffs_kernel, out_shape=jax.ShapeDtypeStruct((devices, rh...  1.71 us
  transfers between devices with their start and end apart: 4, of which 3 were waited for; matrix products, arithmetic and copies ran while one was open for 0% of the time, Pallas kernels for 1%

profile of v7, /device:TPU:0, one launch (start us, length us, event | category | flops | bytes accessed | tf_op | source)
XLA Modules:
  0.0 37.0 jit_solution(3498037280527058504)
XLA Ops:
  0.7 1.7 %coeffs.1.after_ref = bf16[32,16,128]{2,1,0:T(8,128)(2,1)} custom-call(f32[4,16,768]{2,1,0:T(8,128)} %slip_ref.1, bf16[4,32,768]{2,1,0:T(8,128)(2,1)} %basis_ref.1, s32[2,20]{1,0:T(2,128)} %pairs_hbm.1, s32[1]{0:T(128)S(6)} %copy.10.count_ref), custom_call_target="tpu_custom_call" | custom-call | tf_op jit(solution)/shard_map/coeffs/pallas_call | solution.py:314
  2.4 0.0 copy-start
  2.4 0.0 copy-start.2
  2.4 0.0 copy-start.3
  2.4 0.0 copy-start.4
  2.4 7.3 %all-to-all-start = ((bf16[32,16,128]{2,1,0:T(8,128)(2,1)}), bf16[32,16,128]{2,1,0:T(8,128)(2,1)S(1)}, u32[]{:S(2)}, u32[]{:S(2)}) async-start(bf16[32,16,128]{2,1,0:T(8,128)(2,1)} %coeffs.1.after_ref), calls=%async_computation | async-start | bytes 262144 | tf_op jit(solution)/shard_map/all_to_all | solution.py:334
  9.7 0.0 copy-done
  9.7 0.0 copy-done.2
  9.8 0.0 copy-done.3
  9.8 0.0 copy-done.4
  9.8 0.0 copy-start.6
  9.8 0.3 geometry.1
  10.1 3.7 %collective-permute-start = (bf16[2,16,1024]{2,1,0:T(8,128)(2,1)S(1)}, bf16[2,16,1024]{2,1,0:T(8,128)(2,1)S(1)}, u32[]{:S(2)}, u32[]{:S(2)}) collective-permute-start(bf16[2,16,1024]{2,1,0:T(8,128)(2,1)S(1)} %get-tuple-element.14), channel_id=1, source_target_pairs={{0,1},{1,2},{2,3},{3,4},{4,5},{5,6},{6,7},{9,8},{10,9},{11,10},{12... | collective-permute-start | bytes 196616 | tf_op jit(solution)/shard_map/ppermute | solution.py:357
  13.7 0.0 copy-done.6
  13.7 0.1 reshape.3.coupling_ref
  13.9 2.6 %collective-permute-done.halo_ref = bf16[2,16,1024]{2,1,0:T(8,128)(2,1)S(1)} collective-permute-done((bf16[2,16,1024]{2,1,0:T(8,128)(2,1)S(1)}, bf16[2,16,1024]{2,1,0:T(8,128)(2,1)S(1)}, u32[]{:S(2)}, u32[]{:S(2)}) %collective-permute-start) | collective-permute-done | bytes 65568 | tf_op jit(solution)/shard_map/ppermute | solution.py:357
  16.5 0.0 copy-start.5
  16.6 0.9 %all-to-all-done.coeff_ref.pay_ref = bf16[32,16,128]{2,1,0:T(8,128)(2,1)S(1)} async-done(((bf16[32,16,128]{2,1,0:T(8,128)(2,1)}), bf16[32,16,128]{2,1,0:T(8,128)(2,1)S(1)}, u32[]{:S(2)}, u32[]{:S(2)}) %all-to-all-start) | async-done | bytes 131104 | tf_op jit(solution)/shard_map/all_to_all | solution.py:334
  17.5 0.0 copy-done.5
  17.5 1.8 %far.1 = (bf16[32,16,128]{2,1,0:T(8,128)(2,1)}, f32[8,128]{1,0:T(8,128)S(1)}) custom-call(s32[2,16]{1,0:T(2,128)S(1)} %copy-done.5, bf16[32,16,128]{2,1,0:T(8,128)(2,1)S(1)} %all-to-all-done.coeff_ref.pay_ref, bf16[16,32,32]{2,1,0:T(8,128)(2,1)S(1)} %reshape.3.coupling_ref, f32[6,4,256]{2,1,0:T(4,128)S(1)} %get-tuple-element.16.after_ref.place_ref), custom_call_target="tpu_custom_call" | custom-call | tf_op jit(solution)/shard_map/far/pallas_call | solution.py:372
  19.2 3.7 %near.1.own_ref = bf16[6,2,16,768]{3,2,1,0:T(8,128)(2,1)S(1)} custom-call(bf16[6,16,768]{2,1,0:T(8,128)(2,1)S(1)} %get-tuple-element.15.slip_ref, f32[6,4,256]{2,1,0:T(4,128)S(1)} %get-tuple-element.16.after_ref.place_ref, f32[8,128]{1,0:T(8,128)S(1)} %get-tuple-element.17.after_ref), custom_call_target="tpu_custom_call" | custom-call | flops 1000000000 | bytes 1000000 | tf_op jit(solution)/shard_map/near/pallas_call | solution.py:386
  22.9 0.1 collective-permute-start.1
  23.0 5.3 %all-to-all-start.1 = ((bf16[32,16,128]{2,1,0:T(8,128)(2,1)}), bf16[32,16,128]{2,1,0:T(8,128)(2,1)S(1)}, u32[]{:S(2)}, u32[]{:S(2)}) async-start(bf16[32,16,128]{2,1,0:T(8,128)(2,1)} %get-tuple-element.18), calls=%async_computation.1 | async-start | bytes 262144 | tf_op jit(solution)/shard_map/all_to_all | solution.py:384
  28.3 0.0 copy-start.1
  28.4 0.0 collective-permute-done.1.other_ref
  28.4 0.2 weigh.1.near_ref
  28.6 7.5 %all-to-all-done.1.far_ref = bf16[32,16,128]{2,1,0:T(8,128)(2,1)S(1)} async-done(((bf16[32,16,128]{2,1,0:T(8,128)(2,1)}), bf16[32,16,128]{2,1,0:T(8,128)(2,1)S(1)}, u32[]{:S(2)}, u32[]{:S(2)}) %all-to-all-start.1) | async-done | bytes 131104 | tf_op jit(solution)/shard_map/all_to_all | solution.py:384
  36.1 0.0 copy-done.1
  36.1 0.9 %finish.1 = f32[4,16,768]{2,1,0:T(8,128)} custom-call(f32[4,16,768]{2,1,0:T(8,128)S(1)} %weigh.1.near_ref, bf16[32,16,128]{2,1,0:T(8,128)(2,1)S(1)} %all-to-all-done.1.far_ref, bf16[4,32,768]{2,1,0:T(8,128)(2,1)S(1)} %copy-done.1), custom_call_target="tpu_custom_call" | custom-call | tf_op jit(solution)/shard_map/finish/pallas_call | solution.py:417
  (1 shorter events, 0.0 us)
Async XLA Ops:
  2.4 7.4 %copy-start = (f32[4,16,768]{2,1,0:T(8,128)S(1)}, f32[4,16,768]{2,1,0:T(8,128)}, u32[]{:S(2)}) copy-start(f32[4,16,768]{2,1,0:T(8,128)} %slip_ref.1) | copy-start | bytes 589828
  2.4 7.4 %copy-start.2 = (s32[3,1024]{1,0:T(4,128)S(1)}, s32[3,1024]{1,0:T(4,128)}, u32[]{:S(2)}) copy-start(s32[3,1024]{1,0:T(4,128)} %triangles_ref.1) | copy-start | bytes 36868
  2.4 7.4 %copy-start.3 = (f32[3,561]{1,0:T(4,128)S(1)}, f32[3,561]{1,0:T(4,128)}, u32[]{:S(2)}) copy-start(f32[3,561]{1,0:T(4,128)} %vertices_ref.1) | copy-start | bytes 20200
  2.4 7.4 %copy-start.4 = (s32[4,256]{1,0:T(4,128)S(1)}, s32[4,256]{1,0:T(4,128)}, u32[]{:S(2)}) copy-start(s32[4,256]{1,0:T(4,128)} %map_ref.1) | copy-start | bytes 12292
  2.4 15.1 %all-to-all-start = ((bf16[32,16,128]{2,1,0:T(8,128)(2,1)}), bf16[32,16,128]{2,1,0:T(8,128)(2,1)S(1)}, u32[]{:S(2)}, u32[]{:S(2)}) async-start(bf16[32,16,128]{2,1,0:T(8,128)(2,1)} %coeffs.1.after_ref), calls=%async_computation | async-start | bytes 262144 | tf_op jit(solution)/shard_map/all_to_all | solution.py:334
  9.8 4.0 %copy-start.6 = (bf16[16,1024]{1,0:T(8,128)(2,1)S(1)}, bf16[16,1024]{1,0:T(8,128)(2,1)}, u32[]{:S(2)}) copy-start(bf16[16,1024]{1,0:T(8,128)(2,1)} %param.16) | copy-start | bytes 98308
  10.1 6.4 %collective-permute-start = (bf16[2,16,1024]{2,1,0:T(8,128)(2,1)S(1)}, bf16[2,16,1024]{2,1,0:T(8,128)(2,1)S(1)}, u32[]{:S(2)}, u32[]{:S(2)}) collective-permute-start(bf16[2,16,1024]{2,1,0:T(8,128)(2,1)S(1)} %get-tuple-element.14), channel_id=1, source_target_pairs={{0,1},{1,2},{2,3},{3,4},{4,5},{5,6},{6,7},{9,8},{10,9},{11,10},{12... | collective-permute-start | bytes 196616 | tf_op jit(solution)/shard_map/ppermute | solution.py:357
  16.5 0.9 %copy-start.5 = (s32[2,16]{1,0:T(2,128)S(1)}, s32[2,16]{1,0:T(2,128)}, u32[]{:S(2)}) copy-start(s32[2,16]{1,0:T(2,128)} %pairs_ref.1) | copy-start | bytes 388
  22.9 5.5 %collective-permute-start.1 = (bf16[6,2,16,768]{3,2,1,0:T(8,128)(2,1)S(1)}, bf16[6,2,16,768]{3,2,1,0:T(8,128)(2,1)S(1)}, u32[]{:S(2)}, u32[]{:S(2)}) collective-permute-start(bf16[6,2,16,768]{3,2,1,0:T(8,128)(2,1)S(1)} %near.1.own_ref), channel_id=1, source_target_pairs={{0,8},{8,0},{16,24},{24,16},{1,9},{9,1},{17,25},{25,17},{2,10},{10... | collective-permute-start | bytes 884744 | tf_op jit(solution)/shard_map/ppermute | solution.py:403
  23.0 13.0 %all-to-all-start.1 = ((bf16[32,16,128]{2,1,0:T(8,128)(2,1)}), bf16[32,16,128]{2,1,0:T(8,128)(2,1)S(1)}, u32[]{:S(2)}, u32[]{:S(2)}) async-start(bf16[32,16,128]{2,1,0:T(8,128)(2,1)} %get-tuple-element.18), calls=%async_computation.1 | async-start | bytes 262144 | tf_op jit(solution)/shard_map/all_to_all | solution.py:384
  28.3 7.7 %copy-start.1 = (bf16[4,32,768]{2,1,0:T(8,128)(2,1)S(1)}, bf16[4,32,768]{2,1,0:T(8,128)(2,1)}, u32[]{:S(2)}) copy-start(bf16[4,32,768]{2,1,0:T(8,128)(2,1)} %basis_ref.1) | copy-start | bytes 589828

commit v8 on v6

--- a/solution.py
+++ b/solution.py
@@ -159,9 +159,32 @@
         )
 
 
-def near_kernel(slip_ref, place_ref, out_ref, cols_ref, even_ref, odd_ref):
+def near_kernel(
+    slip_ref, place_ref, pay_ref, after_ref, out_ref, cols_ref, even_ref, odd_ref, *, long_count, clusters
+):
     slots, rhs_count, unknowns = slip_ref.shape
     size = place_ref.shape[2]
+    long_index = lax.axis_index("long")
+    before = jnp.maximum(long_index - 1, 0)
+    totals = [jnp.zeros(pay_ref.shape[1:], jnp.float32) for _ in range(2)]
+    for row in range(pay_ref.shape[0] // long_count):
+        for source, owner in enumerate((long_index, before)):
+            totals[source] += pay_ref[row * long_count + owner].astype(jnp.float32)
+    even = lax.axis_index("row") % 2 == 0
+    kinds = lax.broadcasted_iota(jnp.int32, (rhs_count, LANES), 0)
+
+    def count_of(place, u):
+        both = []
+        for cluster in (u, clusters - NEARC + u):
+            reach = place - u - NEARC
+            lower = cluster + jnp.minimum(reach, 0)
+            inside = lower >= 0
+            kind = jnp.where(inside, lower, lower + clusters) * (NEARC + 1) + jnp.abs(reach)
+            source = jnp.where(inside, totals[0], totals[1])
+            both.append(jnp.sum(jnp.where(kinds == kind, source, 0.0), axis=0, keepdims=True))
+        return jnp.where(even, both[0], both[1])[:, LANES - 1 : LANES]
+
+    out_ref[...] = jnp.zeros(out_ref.shape, jnp.float32)
     for place in range(slots):
         rows = jnp.concatenate([place_ref[place], jnp.zeros((4, size), jnp.float32)], axis=0)
         cols_ref[place] = rows.T
@@ -190,6 +213,7 @@
         slip = slip_ref[place]
         pieces = [slip[:, p * size : (p + 1) * size] for p in range(3)]
         for u in targets:
+            count = count_of(place, u)
             sums = [
                 jnp.dot(pieces[p], block_ref[u, p], preferred_element_type=jnp.float32)
                 for p in range(3)
@@ -204,11 +228,12 @@
                 sums[i] = sums[i] + both[0:rhs_count]
                 sums[j] = sums[j] + both[rhs_count : 2 * rhs_count]
             for p in range(3):
-                out_ref[place, u, :, p * size : (p + 1) * size] = sums[p].astype(jnp.bfloat16)
+                out_ref[u, :, p * size : (p + 1) * size] += count * sums[p]
 
     every = list(range(NEARC))
     fill(0, [0], even_ref)
-    even_ref[1] = jnp.zeros(even_ref.shape[1:], jnp.bfloat16)
+    for u in range(1, NEARC):
+        even_ref[u] = jnp.zeros(even_ref.shape[1:], jnp.bfloat16)
 
     def two_places(turn, carry):
         place = 2 * turn
@@ -222,10 +247,12 @@
     fill(slots - 1, [NEARC - 1], odd_ref)
     apply(slots - 2, every, even_ref)
     apply(slots - 1, [NEARC - 1], odd_ref)
-    out_ref[slots - 1, 0] = jnp.zeros(out_ref.shape[2:], jnp.bfloat16)
-
-
-def far_kernel(pairs_ref, coeff_ref, coupling_ref, after_ref, out_ref, total_ref, *, clusters):
+
+
+def far_kernel(
+    pairs_ref, coeff_ref, coupling_ref, out_ref, done_ref, total_ref, *, clusters
+):
+    done_ref[...] = jnp.zeros(done_ref.shape, jnp.float32)
     long_count, rhs_count, _ = total_ref.shape
     rank_size = coupling_ref.shape[1]
     groups = LANES // rank_size
@@ -263,32 +290,19 @@
         out_ref[copy_id * long_count : (copy_id + 1) * long_count] = sent
 
 
-def finish_kernel(own_ref, other_ref, pay_ref, far_ref, basis_ref, out_ref, *, long_count):
+def finish_kernel(own_ref, other_ref, far_ref, basis_ref, out_ref):
     clusters, rank_size, unknowns = basis_ref.shape
-    long_index = lax.axis_index("long")
-    before = jnp.maximum(long_index - 1, 0)
-    counts = [jnp.zeros(pay_ref.shape[1:], jnp.float32) for _ in range(2)]
-    for row in range(pay_ref.shape[0] // long_count):
-        for source, owner in enumerate((long_index, before)):
-            counts[source] += pay_ref[row * long_count + owner].astype(jnp.float32)
     total = jnp.sum(far_ref[...].astype(jnp.float32), axis=0)
     group_id = lax.broadcasted_iota(jnp.int32, total.shape, 1) // rank_size
     flat_basis = basis_ref[...].reshape(clusters * rank_size, unknowns)
     even = lax.axis_index("row") % 2 == 0
     for cluster in range(clusters):
+        u = cluster % NEARC
+        here = even if cluster < NEARC else jnp.logical_not(even)
+        near = jnp.where(here, own_ref[u], other_ref[u])
         picked = jnp.where(group_id == cluster, total, 0.0).astype(jnp.bfloat16)
         result = jnp.dot(picked, flat_basis, preferred_element_type=jnp.float32)
-        u = cluster % NEARC
-        for turn in range(2 * NEARC + 1):
-            reach = turn - NEARC
-            lower = cluster + min(reach, 0)
-            source = 0 if lower >= 0 else 1
-            kind = (lower if lower >= 0 else lower + clusters) * (NEARC + 1) + abs(reach)
-            count = counts[source][kind : kind + 1, LANES - 1 : LANES]
-            mine, theirs = own_ref[u + turn, u], other_ref[u + turn, u]
-            here = even if cluster < NEARC else jnp.logical_not(even)
-            result = result + count * jnp.where(here, mine, theirs).astype(jnp.float32)
-        out_ref[cluster] = result
+        out_ref[cluster] = result + near
 
 
 def shards(slip, vertices, triangles, elem_map, near_pairs, near_count, far_pairs, far_coef, basis):
@@ -359,21 +373,24 @@
         name="window",
     )(xs, geometry, halo)
 
-    far = pl.pallas_call(
+    far, far_done = pl.pallas_call(
         functools.partial(far_kernel, clusters=clusters),
-        out_shape=jax.ShapeDtypeStruct((devices, rhs_count, clusters * rank_size), jnp.bfloat16),
-        in_specs=[SMEM, VMEM, VMEM, ANY],
-        out_specs=VMEM,
+        out_shape=[
+            jax.ShapeDtypeStruct((devices, rhs_count, clusters * rank_size), jnp.bfloat16),
+            jax.ShapeDtypeStruct((8, LANES), jnp.float32),
+        ],
+        in_specs=[SMEM, VMEM, VMEM],
+        out_specs=[VMEM] * 2,
         scratch_shapes=[pltpu.VMEM((long_count, rhs_count, clusters * rank_size), jnp.float32)],
         compiler_params=pltpu.CompilerParams(vmem_limit_bytes=16 << 20),
         name="far",
-    )(far_pairs, everyone, coupling, places)
+    )(far_pairs, everyone, coupling)
     far_terms = lax.all_to_all(far, ("row", "long"), 0, 0, tiled=True)
 
     near = pl.pallas_call(
-        near_kernel,
-        out_shape=jax.ShapeDtypeStruct((slots, NEARC, rhs_count, unknowns), jnp.bfloat16),
-        in_specs=[VMEM] * 2,
+        functools.partial(near_kernel, long_count=long_count, clusters=clusters),
+        out_shape=jax.ShapeDtypeStruct((NEARC, rhs_count, unknowns), jnp.float32),
+        in_specs=[VMEM] * 3 + [ANY],
         out_specs=VMEM,
         scratch_shapes=[
             pltpu.VMEM((slots, size, 8), jnp.float32),
@@ -385,18 +402,18 @@
             flops=1_000_000_000, bytes_accessed=1_000_000, transcendentals=660_000
         ),
         name="near",
-    )(window, places)
+    )(window, places, everyone, far_done)
     partner = [(row, row ^ 1) for row in range(row_count)]
     other = lax.ppermute(near, "row", partner)
 
     return pl.pallas_call(
-        functools.partial(finish_kernel, long_count=long_count),
+        finish_kernel,
         out_shape=jax.ShapeDtypeStruct(slip.shape, jnp.float32),
-        in_specs=[VMEM] * 5,
+        in_specs=[VMEM] * 4,
         out_specs=VMEM,
         compiler_params=pltpu.CompilerParams(vmem_limit_bytes=16 << 20),
         name="finish",
-    )(near, other, everyone, far_terms, basis)
+    )(near, other, far_terms, basis)
 
 
 def solution(mesh):

time: 37.2 us -> 30.8 us (0.83)
  waiting for transfers between devices: 10.5 us -> 7.21 us
  starting transfers between devices: 16.6 us -> 13.8 us
  local copies, waits for them, and re-layouts: 0.65 us -> 0.19 us
    all_to_all x1, waiting for transfers between devices: 7.73 us -> 2.58 us  [shards(): far_terms = lax.all_to_all(far, ('row', 'long'), 0, 0, tiled=True)]
    all_to_all x1, waiting for transfers between devices: 0.01 us -> 3.56 us  [shards(): everyone = lax.all_to_all(pay, ('row', 'long'), 0, 0, tiled=True)]
    all_to_all x1, starting transfers between devices: 5.55 us -> 2.58 us  [shards(): far_terms = lax.all_to_all(far, ('row', 'long'), 0, 0, tiled=True)]
    ppermute x1, waiting for transfers between devices: 2.76 us -> 0.01 us  [shards(): halo = lax.ppermute(to_neighbour, ('row', 'long'), route)]
    ppermute x1, waiting for transfers between devices: 0.01 us -> 1.07 us  [shards(): other = lax.ppermute(near, 'row', partner)]
    unnamed x14, local copies, waits for them, and re-layouts: 0.5 us -> 0.04 us
  transfers between devices with their start and end apart: 4 -> 4, of which waited for: 2 -> 3; matrix products, arithmetic and copies ran while one was open for 0% -> 0% of each run, Pallas kernels for 16% -> 19%
where the time goes in v8:
time: 30.8 us; the launch traced here: 30.5 us
  starting transfers between devices  13.8 us (45%)
  Pallas kernels  8.44 us (27%)
  waiting for transfers between devices  7.21 us (23%)
  between operations  0.81 us (3%)
    all_to_all x1, starting transfers between devices, shards(): everyone = lax.all_to_all(pay, ('row', 'long'), 0, 0, tiled=True)  7.3 us
    pallas_call x1, Pallas kernels, shards(): pl.pallas_call(functools.partial(near_kernel, long_count=long_count, clus...  3.73 us
    ppermute x1, starting transfers between devices, shards(): halo = lax.ppermute(to_neighbour, ('row', 'long'), route)  3.68 us
    all_to_all x1, waiting for transfers between devices, shards(): everyone = lax.all_to_all(pay, ('row', 'long'), 0, 0, tiled=True)  3.56 us
    all_to_all x1, waiting for transfers between devices, shards(): far_terms = lax.all_to_all(far, ('row', 'long'), 0, 0, tiled=True)  2.58 us
    all_to_all x1, starting transfers between devices, shards(): far_terms = lax.all_to_all(far, ('row', 'long'), 0, 0, tiled=True)  2.58 us
    pallas_call x1, Pallas kernels, shards(): pl.pallas_call(functools.partial(far_kernel, clusters=clusters), out_shap...  1.76 us
    pallas_call x1, Pallas kernels, shards(): pl.pallas_call(coeffs_kernel, out_shape=jax.ShapeDtypeStruct((devices, rh...  1.71 us
  transfers between devices with their start and end apart: 4, of which 3 were waited for; matrix products, arithmetic and copies ran while one was open for 0% of the time, Pallas kernels for 19%

profile of v8, /device:TPU:0, one launch (start us, length us, event | category | flops | bytes accessed | tf_op | source)
XLA Modules:
  0.0 30.5 jit_solution(17080599378551282387)
XLA Ops:
  0.7 1.7 %coeffs.1.after_ref = bf16[32,16,128]{2,1,0:T(8,128)(2,1)} custom-call(f32[4,16,768]{2,1,0:T(8,128)} %slip_ref.1, bf16[4,32,768]{2,1,0:T(8,128)(2,1)} %basis_ref.1, s32[2,20]{1,0:T(2,128)} %pairs_hbm.1, s32[1]{0:T(128)S(6)} %copy.10.count_ref), custom_call_target="tpu_custom_call" | custom-call | tf_op jit(solution)/shard_map/coeffs/pallas_call | solution.py:318
  2.4 0.0 copy-start
  2.4 0.0 copy-start.2
  2.4 0.0 copy-start.3
  2.4 0.0 copy-start.4
  2.4 7.3 %all-to-all-start = ((bf16[32,16,128]{2,1,0:T(8,128)(2,1)}), bf16[32,16,128]{2,1,0:T(8,128)(2,1)S(1)}, u32[]{:S(2)}, u32[]{:S(2)}) async-start(bf16[32,16,128]{2,1,0:T(8,128)(2,1)} %coeffs.1.after_ref), calls=%async_computation | async-start | bytes 262144 | tf_op jit(solution)/shard_map/all_to_all | solution.py:338
  9.7 0.0 copy-done
  9.7 0.0 copy-done.2
  9.8 0.0 copy-done.3
  9.8 0.0 copy-done.4
  9.8 0.0 copy-start.6
  9.8 0.3 geometry.1
  10.1 0.0 copy-start.5
  10.1 3.7 %collective-permute-start = (bf16[2,16,1024]{2,1,0:T(8,128)(2,1)S(1)}, bf16[2,16,1024]{2,1,0:T(8,128)(2,1)S(1)}, u32[]{:S(2)}, u32[]{:S(2)}) collective-permute-start(bf16[2,16,1024]{2,1,0:T(8,128)(2,1)S(1)} %get-tuple-element.14), channel_id=1, source_target_pairs={{0,1},{1,2},{2,3},{3,4},{4,5},{5,6},{6,7},{9,8},{10,9},{11,10},{12... | collective-permute-start | bytes 196616 | tf_op jit(solution)/shard_map/ppermute | solution.py:361
  13.7 0.0 copy-done.6
  13.8 0.1 reshape.3.coupling_ref
  13.9 3.6 %all-to-all-done.coeff_ref.pay_ref = bf16[32,16,128]{2,1,0:T(8,128)(2,1)S(1)} async-done(((bf16[32,16,128]{2,1,0:T(8,128)(2,1)}), bf16[32,16,128]{2,1,0:T(8,128)(2,1)S(1)}, u32[]{:S(2)}, u32[]{:S(2)}) %all-to-all-start) | async-done | bytes 131104 | tf_op jit(solution)/shard_map/all_to_all | solution.py:338
  17.5 0.0 copy-done.5
  17.5 1.8 %far.1 = (bf16[32,16,128]{2,1,0:T(8,128)(2,1)}, f32[8,128]{1,0:T(8,128)S(1)}) custom-call(s32[2,16]{1,0:T(2,128)S(1)} %copy-done.5, bf16[32,16,128]{2,1,0:T(8,128)(2,1)S(1)} %all-to-all-done.coeff_ref.pay_ref, bf16[16,32,32]{2,1,0:T(8,128)(2,1)S(1)} %reshape.3.coupling_ref), custom_call_target="tpu_custom_call" | custom-call | tf_op jit(solution)/shard_map/far/pallas_call | solution.py:376
  19.2 2.6 %all-to-all-start.1 = ((bf16[32,16,128]{2,1,0:T(8,128)(2,1)}), bf16[32,16,128]{2,1,0:T(8,128)(2,1)S(1)}, u32[]{:S(2)}, u32[]{:S(2)}) async-start(bf16[32,16,128]{2,1,0:T(8,128)(2,1)} %get-tuple-element.18), calls=%async_computation.1 | async-start | bytes 262144 | tf_op jit(solution)/shard_map/all_to_all | solution.py:388
  21.8 0.0 collective-permute-done.halo_ref
  21.9 0.0 copy-start.1
  21.9 3.7 %near.1.own_ref = f32[2,16,768]{2,1,0:T(8,128)S(1)} custom-call(bf16[6,16,768]{2,1,0:T(8,128)(2,1)S(1)} %get-tuple-element.15.slip_ref, f32[6,4,256]{2,1,0:T(4,128)S(1)} %get-tuple-element.16.place_ref, bf16[32,16,128]{2,1,0:T(8,128)(2,1)S(1)} %all-to-all-done.coeff_ref.pay_ref, f32[8,128]{1,0:T(8,128)S(1)} %get-tuple-element.17.after_ref), custom_call_target="tpu_custom_call" | custom-call | flops 1000000000 | bytes 1000000 | tf_op jit(solution)/shard_map/near/pallas_call | solution.py:390
  25.6 0.3 collective-permute-start.1
  25.9 1.1 %collective-permute-done.1.other_ref = f32[2,16,768]{2,1,0:T(8,128)S(1)} collective-permute-done((f32[2,16,768]{2,1,0:T(8,128)S(1)}, f32[2,16,768]{2,1,0:T(8,128)S(1)}, u32[]{:S(2)}, u32[]{:S(2)}) %collective-permute-start.1) | collective-permute-done | bytes 98336 | tf_op jit(solution)/shard_map/ppermute | solution.py:407
  27.0 2.6 %all-to-all-done.1.far_ref = bf16[32,16,128]{2,1,0:T(8,128)(2,1)S(1)} async-done(((bf16[32,16,128]{2,1,0:T(8,128)(2,1)}), bf16[32,16,128]{2,1,0:T(8,128)(2,1)S(1)}, u32[]{:S(2)}, u32[]{:S(2)}) %all-to-all-start.1) | async-done | bytes 131104 | tf_op jit(solution)/shard_map/all_to_all | solution.py:388
  29.6 0.0 copy-done.1
  29.6 0.9 %finish.1 = f32[4,16,768]{2,1,0:T(8,128)} custom-call(f32[2,16,768]{2,1,0:T(8,128)S(1)} %near.1.own_ref, f32[2,16,768]{2,1,0:T(8,128)S(1)} %collective-permute-done.1.other_ref, bf16[32,16,128]{2,1,0:T(8,128)(2,1)S(1)} %all-to-all-done.1.far_ref, bf16[4,32,768]{2,1,0:T(8,128)(2,1)S(1)} %copy-done.1), custom_call_target="tpu_custom_call" | custom-call | tf_op jit(solution)/shard_map/finish/pallas_call | solution.py:409
  (1 shorter events, 0.0 us)
Async XLA Ops:
  2.4 7.4 %copy-start = (f32[4,16,768]{2,1,0:T(8,128)S(1)}, f32[4,16,768]{2,1,0:T(8,128)}, u32[]{:S(2)}) copy-start(f32[4,16,768]{2,1,0:T(8,128)} %slip_ref.1) | copy-start | bytes 589828
  2.4 7.4 %copy-start.2 = (s32[3,1024]{1,0:T(4,128)S(1)}, s32[3,1024]{1,0:T(4,128)}, u32[]{:S(2)}) copy-start(s32[3,1024]{1,0:T(4,128)} %triangles_ref.1) | copy-start | bytes 36868
  2.4 7.4 %copy-start.3 = (f32[3,561]{1,0:T(4,128)S(1)}, f32[3,561]{1,0:T(4,128)}, u32[]{:S(2)}) copy-start(f32[3,561]{1,0:T(4,128)} %vertices_ref.1) | copy-start | bytes 20200
  2.4 7.4 %copy-start.4 = (s32[4,256]{1,0:T(4,128)S(1)}, s32[4,256]{1,0:T(4,128)}, u32[]{:S(2)}) copy-start(s32[4,256]{1,0:T(4,128)} %map_ref.1) | copy-start | bytes 12292
  2.4 15.1 %all-to-all-start = ((bf16[32,16,128]{2,1,0:T(8,128)(2,1)}), bf16[32,16,128]{2,1,0:T(8,128)(2,1)S(1)}, u32[]{:S(2)}, u32[]{:S(2)}) async-start(bf16[32,16,128]{2,1,0:T(8,128)(2,1)} %coeffs.1.after_ref), calls=%async_computation | async-start | bytes 262144 | tf_op jit(solution)/shard_map/all_to_all | solution.py:338
  9.8 4.0 %copy-start.6 = (bf16[16,1024]{1,0:T(8,128)(2,1)S(1)}, bf16[16,1024]{1,0:T(8,128)(2,1)}, u32[]{:S(2)}) copy-start(bf16[16,1024]{1,0:T(8,128)(2,1)} %param.16) | copy-start | bytes 98308
  10.1 7.4 %copy-start.5 = (s32[2,16]{1,0:T(2,128)S(1)}, s32[2,16]{1,0:T(2,128)}, u32[]{:S(2)}) copy-start(s32[2,16]{1,0:T(2,128)} %pairs_ref.1) | copy-start | bytes 388
  10.1 11.8 %collective-permute-start = (bf16[2,16,1024]{2,1,0:T(8,128)(2,1)S(1)}, bf16[2,16,1024]{2,1,0:T(8,128)(2,1)S(1)}, u32[]{:S(2)}, u32[]{:S(2)}) collective-permute-start(bf16[2,16,1024]{2,1,0:T(8,128)(2,1)S(1)} %get-tuple-element.14), channel_id=1, source_target_pairs={{0,1},{1,2},{2,3},{3,4},{4,5},{5,6},{6,7},{9,8},{10,9},{11,10},{12... | collective-permute-start | bytes 196616 | tf_op jit(solution)/shard_map/ppermute | solution.py:361
  19.2 10.3 %all-to-all-start.1 = ((bf16[32,16,128]{2,1,0:T(8,128)(2,1)}), bf16[32,16,128]{2,1,0:T(8,128)(2,1)S(1)}, u32[]{:S(2)}, u32[]{:S(2)}) async-start(bf16[32,16,128]{2,1,0:T(8,128)(2,1)} %get-tuple-element.18), calls=%async_computation.1 | async-start | bytes 262144 | tf_op jit(solution)/shard_map/all_to_all | solution.py:388
  21.9 7.7 %copy-start.1 = (bf16[4,32,768]{2,1,0:T(8,128)(2,1)S(1)}, bf16[4,32,768]{2,1,0:T(8,128)(2,1)}, u32[]{:S(2)}) copy-start(bf16[4,32,768]{2,1,0:T(8,128)(2,1)} %basis_ref.1) | copy-start | bytes 589828
  25.6 1.4 %collective-permute-start.1 = (f32[2,16,768]{2,1,0:T(8,128)S(1)}, f32[2,16,768]{2,1,0:T(8,128)S(1)}, u32[]{:S(2)}, u32[]{:S(2)}) collective-permute-start(f32[2,16,768]{2,1,0:T(8,128)S(1)} %near.1.own_ref), channel_id=1, source_target_pairs={{0,8},{8,0},{16,24},{24,16},{1,9},{9,1},{17,25},{25,17},{2,10},{10... | collective-permute-start | bytes 294920 | tf_op jit(solution)/shard_map/ppermute | solution.py:407

commit v9 on v8

--- a/solution.py
+++ b/solution.py
@@ -57,6 +57,7 @@
         copy.start()
     for copy in copies:
         copy.wait()
+    half = rhs_count // 2
     wide = jnp.concatenate([basis_ref[...]] * (LANES // rank_size), axis=0)
     coeffs = lax.dot_general(
         slip_ref[...].astype(jnp.bfloat16),
@@ -66,11 +67,14 @@
     )
     first = pairs_ref[0:1, :]
     kind = (first - lax.axis_index("long") * clusters) * (NEARC + 1) + pairs_ref[1:2, :] - first
-    kinds = lax.broadcasted_iota(jnp.int32, (rhs_count, kind.shape[1]), 0)
+    kinds = lax.broadcasted_iota(jnp.int32, (half, kind.shape[1]), 0)
     live = lax.broadcasted_iota(jnp.int32, kinds.shape, 1) < count_ref[0]
-    counts = jnp.sum(jnp.where(live & (kinds == kind), 1.0, 0.0), axis=1, keepdims=True)
-    lane_id = lax.broadcasted_iota(jnp.int32, coeffs.shape, 1)
-    pay = jnp.where(lane_id < rank_size, coeffs, counts).astype(jnp.bfloat16)
+    low = jnp.sum(jnp.where(live & (kinds == kind), 1.0, 0.0), axis=1, keepdims=True)
+    high = jnp.sum(jnp.where(live & (kinds + half == kind), 1.0, 0.0), axis=1, keepdims=True)
+    group = lax.broadcasted_iota(jnp.int32, (half, LANES), 1) // rank_size
+    pay = jnp.where(
+        group == 0, coeffs[0:half], jnp.where(group == 1, coeffs[half:], jnp.where(group == 2, low, high))
+    ).astype(jnp.bfloat16)
     for target in range(pay_ref.shape[0]):
         pay_ref[target] = pay
 
@@ -171,7 +175,13 @@
         for source, owner in enumerate((long_index, before)):
             totals[source] += pay_ref[row * long_count + owner].astype(jnp.float32)
     even = lax.axis_index("row") % 2 == 0
-    kinds = lax.broadcasted_iota(jnp.int32, (rhs_count, LANES), 0)
+    half = pay_ref.shape[1]
+    rank_size = pay_ref.shape[2] // 4
+    group = lax.broadcasted_iota(jnp.int32, (half, LANES), 1) // rank_size
+    kinds = lax.broadcasted_iota(jnp.int32, (half, LANES), 0) + jnp.where(group == 3, half, 0)
+    kinds = jnp.where(group < 2, -1, kinds)
+    lane_id = lax.broadcasted_iota(jnp.int32, (half, LANES), 1)
+    kinds = jnp.where(lane_id % rank_size == 0, kinds, -1)
 
     def count_of(place, u):
         both = []
@@ -181,8 +191,9 @@
             inside = lower >= 0
             kind = jnp.where(inside, lower, lower + clusters) * (NEARC + 1) + jnp.abs(reach)
             source = jnp.where(inside, totals[0], totals[1])
-            both.append(jnp.sum(jnp.where(kinds == kind, source, 0.0), axis=0, keepdims=True))
-        return jnp.where(even, both[0], both[1])[:, LANES - 1 : LANES]
+            both.append(jnp.where(kinds == kind, source, 0.0))
+        picked = jnp.sum(jnp.where(even, both[0], both[1]), axis=0, keepdims=True)
+        return jnp.sum(picked, axis=1, keepdims=True)
 
     out_ref[...] = jnp.zeros(out_ref.shape, jnp.float32)
     for place in range(slots):
@@ -260,8 +271,11 @@
     total_ref[...] = jnp.zeros(total_ref.shape, jnp.float32)
 
     def coeff_of(cluster):
-        at = (cluster % clusters) * long_count + cluster // clusters
-        return coeff_ref[at][:, 0:rank_size]
+        whole = coeff_ref[(cluster % clusters) * long_count + cluster // clusters]
+        whole = whole.astype(jnp.float32)
+        return jnp.concatenate(
+            [whole[:, 0:rank_size], whole[:, rank_size : 2 * rank_size]], axis=0
+        ).astype(jnp.bfloat16)
 
     results = []
     for pair_id in range(pairs_ref.shape[1]):
@@ -317,7 +331,7 @@
 
     pay = pl.pallas_call(
         coeffs_kernel,
-        out_shape=jax.ShapeDtypeStruct((devices, rhs_count, LANES), jnp.bfloat16),
+        out_shape=pltpu.VMEM((devices, rhs_count // 2, LANES), jnp.bfloat16),
         in_specs=[HBM] * 3 + [SMEM],
         out_specs=VMEM,
         scratch_shapes=[
@@ -376,7 +390,7 @@
     far, far_done = pl.pallas_call(
         functools.partial(far_kernel, clusters=clusters),
         out_shape=[
-            jax.ShapeDtypeStruct((devices, rhs_count, clusters * rank_size), jnp.bfloat16),
+            pltpu.VMEM((devices, rhs_count, clusters * rank_size), jnp.bfloat16),
             jax.ShapeDtypeStruct((8, LANES), jnp.float32),
         ],
         in_specs=[SMEM, VMEM, VMEM],

time: 30.8 us -> 30.3 us (0.984)
    all_to_all x1, waiting for transfers between devices: 3.56 us -> 3.1 us  [shards(): everyone = lax.all_to_all(pay, ('row', 'long'), 0, 0, tiled=True)]
where the time goes in v9:
time: 30.3 us; the launch traced here: 30 us
  starting transfers between devices  13.7 us (45%)
  Pallas kernels  8.35 us (28%)
  waiting for transfers between devices  6.94 us (23%)
  between operations  0.81 us (3%)
    all_to_all x1, starting transfers between devices, shards(): everyone = lax.all_to_all(pay, ('row', 'long'), 0, 0, tiled=True)  7.3 us
    ppermute x1, starting transfers between devices, shards(): halo = lax.ppermute(to_neighbour, ('row', 'long'), route)  3.68 us
    pallas_call x1, Pallas kernels, shards(): pl.pallas_call(functools.partial(near_kernel, long_count=long_count, clus...  3.66 us
    all_to_all x1, waiting for transfers between devices, shards(): everyone = lax.all_to_all(pay, ('row', 'long'), 0, 0, tiled=True)  3.1 us
    all_to_all x1, waiting for transfers between devices, shards(): far_terms = lax.all_to_all(far, ('row', 'long'), 0, 0, tiled=True)  2.65 us
    all_to_all x1, starting transfers between devices, shards(): far_terms = lax.all_to_all(far, ('row', 'long'), 0, 0, tiled=True)  2.58 us
    pallas_call x1, Pallas kernels, shards(): pl.pallas_call(functools.partial(far_kernel, clusters=clusters), out_shap...  1.74 us
    pallas_call x1, Pallas kernels, shards(): pl.pallas_call(coeffs_kernel, out_shape=pltpu.VMEM((devices, rhs_count //...  1.72 us
  transfers between devices with their start and end apart: 4, of which 3 were waited for; matrix products, arithmetic and copies ran while one was open for 0% of the time, Pallas kernels for 19%

profile of v9, /device:TPU:0, one launch (start us, length us, event | category | flops | bytes accessed | tf_op | source)
XLA Modules:
  0.0 30.0 jit_solution(16988944748088544776)
XLA Ops:
  0.7 0.0 copy-start
  0.7 1.7 %coeffs.1.after_ref = bf16[32,8,128]{2,1,0:T(8,128)(2,1)} custom-call(f32[4,16,768]{2,1,0:T(8,128)} %slip_ref.1, bf16[4,32,768]{2,1,0:T(8,128)(2,1)} %basis_ref.1, s32[2,20]{1,0:T(2,128)} %pairs_hbm.1, s32[1]{0:T(128)S(6)} %copy.10.count_ref), custom_call_target="tpu_custom_call" | custom-call | tf_op jit(solution)/shard_map/coeffs/pallas_call | solution.py:332
  2.4 0.0 copy-start.2
  2.4 0.0 copy-start.3
  2.4 0.0 copy-start.4
  2.4 7.3 %all-to-all-start = ((bf16[32,8,128]{2,1,0:T(8,128)(2,1)}), bf16[32,8,128]{2,1,0:T(8,128)(2,1)S(1)}, u32[]{:S(2)}, u32[]{:S(2)}) async-start(bf16[32,8,128]{2,1,0:T(8,128)(2,1)} %coeffs.1.after_ref), calls=%async_computation | async-start | bytes 131072 | tf_op jit(solution)/shard_map/all_to_all | solution.py:352
  9.7 0.0 copy-done
  9.7 0.0 copy-done.2
  9.8 0.0 copy-done.3
  9.8 0.0 copy-done.4
  9.8 0.0 copy-start.6
  9.8 0.3 geometry.1
  10.1 0.0 copy-start.5
  10.1 3.7 %collective-permute-start = (bf16[2,16,1024]{2,1,0:T(8,128)(2,1)S(1)}, bf16[2,16,1024]{2,1,0:T(8,128)(2,1)S(1)}, u32[]{:S(2)}, u32[]{:S(2)}) collective-permute-start(bf16[2,16,1024]{2,1,0:T(8,128)(2,1)S(1)} %get-tuple-element.14), channel_id=1, source_target_pairs={{0,1},{1,2},{2,3},{3,4},{4,5},{5,6},{6,7},{9,8},{10,9},{11,10},{12... | collective-permute-start | bytes 196616 | tf_op jit(solution)/shard_map/ppermute | solution.py:375
  13.8 0.0 copy-done.6
  13.8 0.1 reshape.3.coupling_ref
  13.9 3.1 %all-to-all-done.coeff_ref.pay_ref = bf16[32,8,128]{2,1,0:T(8,128)(2,1)S(1)} async-done(((bf16[32,8,128]{2,1,0:T(8,128)(2,1)}), bf16[32,8,128]{2,1,0:T(8,128)(2,1)S(1)}, u32[]{:S(2)}, u32[]{:S(2)}) %all-to-all-start) | async-done | bytes 65568 | tf_op jit(solution)/shard_map/all_to_all | solution.py:352
  17.0 0.0 copy-done.5
  17.0 1.7 %far.1 = (bf16[32,16,128]{2,1,0:T(8,128)(2,1)}, f32[8,128]{1,0:T(8,128)S(1)}) custom-call(s32[2,16]{1,0:T(2,128)S(1)} %copy-done.5, bf16[32,8,128]{2,1,0:T(8,128)(2,1)S(1)} %all-to-all-done.coeff_ref.pay_ref, bf16[16,32,32]{2,1,0:T(8,128)(2,1)S(1)} %reshape.3.coupling_ref), custom_call_target="tpu_custom_call" | custom-call | tf_op jit(solution)/shard_map/far/pallas_call | solution.py:390
  18.8 2.6 %all-to-all-start.1 = ((bf16[32,16,128]{2,1,0:T(8,128)(2,1)}), bf16[32,16,128]{2,1,0:T(8,128)(2,1)S(1)}, u32[]{:S(2)}, u32[]{:S(2)}) async-start(bf16[32,16,128]{2,1,0:T(8,128)(2,1)} %get-tuple-element.18), calls=%async_computation.1 | async-start | bytes 262144 | tf_op jit(solution)/shard_map/all_to_all | solution.py:402
  21.3 0.0 collective-permute-done.halo_ref
  21.4 0.0 copy-start.1
  21.4 3.7 %near.1.own_ref = f32[2,16,768]{2,1,0:T(8,128)S(1)} custom-call(bf16[6,16,768]{2,1,0:T(8,128)(2,1)S(1)} %get-tuple-element.15.slip_ref, f32[6,4,256]{2,1,0:T(4,128)S(1)} %get-tuple-element.16.place_ref, bf16[32,8,128]{2,1,0:T(8,128)(2,1)S(1)} %all-to-all-done.coeff_ref.pay_ref, f32[8,128]{1,0:T(8,128)S(1)} %get-tuple-element.17.after_ref), custom_call_target="tpu_custom_call" | custom-call | flops 1000000000 | bytes 1000000 | tf_op jit(solution)/shard_map/near/pallas_call | solution.py:404
  25.1 0.2 collective-permute-start.1
  25.2 1.2 %collective-permute-done.1.other_ref = f32[2,16,768]{2,1,0:T(8,128)S(1)} collective-permute-done((f32[2,16,768]{2,1,0:T(8,128)S(1)}, f32[2,16,768]{2,1,0:T(8,128)S(1)}, u32[]{:S(2)}, u32[]{:S(2)}) %collective-permute-start.1) | collective-permute-done | bytes 98336 | tf_op jit(solution)/shard_map/ppermute | solution.py:421
  26.4 2.7 %all-to-all-done.1.far_ref = bf16[32,16,128]{2,1,0:T(8,128)(2,1)S(1)} async-done(((bf16[32,16,128]{2,1,0:T(8,128)(2,1)}), bf16[32,16,128]{2,1,0:T(8,128)(2,1)S(1)}, u32[]{:S(2)}, u32[]{:S(2)}) %all-to-all-start.1) | async-done | bytes 131104 | tf_op jit(solution)/shard_map/all_to_all | solution.py:402
  29.1 0.0 copy-done.1
  29.1 0.9 %finish.1 = f32[4,16,768]{2,1,0:T(8,128)} custom-call(f32[2,16,768]{2,1,0:T(8,128)S(1)} %near.1.own_ref, f32[2,16,768]{2,1,0:T(8,128)S(1)} %collective-permute-done.1.other_ref, bf16[32,16,128]{2,1,0:T(8,128)(2,1)S(1)} %all-to-all-done.1.far_ref, bf16[4,32,768]{2,1,0:T(8,128)(2,1)S(1)} %copy-done.1), custom_call_target="tpu_custom_call" | custom-call | tf_op jit(solution)/shard_map/finish/pallas_call | solution.py:423
  (1 shorter events, 0.0 us)
Async XLA Ops:
  0.7 9.1 %copy-start = (f32[4,16,768]{2,1,0:T(8,128)S(1)}, f32[4,16,768]{2,1,0:T(8,128)}, u32[]{:S(2)}) copy-start(f32[4,16,768]{2,1,0:T(8,128)} %slip_ref.1) | copy-start | bytes 589828
  2.4 7.4 %copy-start.2 = (s32[3,1024]{1,0:T(4,128)S(1)}, s32[3,1024]{1,0:T(4,128)}, u32[]{:S(2)}) copy-start(s32[3,1024]{1,0:T(4,128)} %triangles_ref.1) | copy-start | bytes 36868
  2.4 7.4 %copy-start.3 = (f32[3,561]{1,0:T(4,128)S(1)}, f32[3,561]{1,0:T(4,128)}, u32[]{:S(2)}) copy-start(f32[3,561]{1,0:T(4,128)} %vertices_ref.1) | copy-start | bytes 20200
  2.4 7.4 %copy-start.4 = (s32[4,256]{1,0:T(4,128)S(1)}, s32[4,256]{1,0:T(4,128)}, u32[]{:S(2)}) copy-start(s32[4,256]{1,0:T(4,128)} %map_ref.1) | copy-start | bytes 12292
  2.4 14.6 %all-to-all-start = ((bf16[32,8,128]{2,1,0:T(8,128)(2,1)}), bf16[32,8,128]{2,1,0:T(8,128)(2,1)S(1)}, u32[]{:S(2)}, u32[]{:S(2)}) async-start(bf16[32,8,128]{2,1,0:T(8,128)(2,1)} %coeffs.1.after_ref), calls=%async_computation | async-start | bytes 131072 | tf_op jit(solution)/shard_map/all_to_all | solution.py:352
  9.8 4.0 %copy-start.6 = (bf16[16,1024]{1,0:T(8,128)(2,1)S(1)}, bf16[16,1024]{1,0:T(8,128)(2,1)}, u32[]{:S(2)}) copy-start(bf16[16,1024]{1,0:T(8,128)(2,1)} %param.16) | copy-start | bytes 98308
  10.1 7.0 %copy-start.5 = (s32[2,16]{1,0:T(2,128)S(1)}, s32[2,16]{1,0:T(2,128)}, u32[]{:S(2)}) copy-start(s32[2,16]{1,0:T(2,128)} %pairs_ref.1) | copy-start | bytes 388
  10.1 11.3 %collective-permute-start = (bf16[2,16,1024]{2,1,0:T(8,128)(2,1)S(1)}, bf16[2,16,1024]{2,1,0:T(8,128)(2,1)S(1)}, u32[]{:S(2)}, u32[]{:S(2)}) collective-permute-start(bf16[2,16,1024]{2,1,0:T(8,128)(2,1)S(1)} %get-tuple-element.14), channel_id=1, source_target_pairs={{0,1},{1,2},{2,3},{3,4},{4,5},{5,6},{6,7},{9,8},{10,9},{11,10},{12... | collective-permute-start | bytes 196616 | tf_op jit(solution)/shard_map/ppermute | solution.py:375
  18.8 10.3 %all-to-all-start.1 = ((bf16[32,16,128]{2,1,0:T(8,128)(2,1)}), bf16[32,16,128]{2,1,0:T(8,128)(2,1)S(1)}, u32[]{:S(2)}, u32[]{:S(2)}) async-start(bf16[32,16,128]{2,1,0:T(8,128)(2,1)} %get-tuple-element.18), calls=%async_computation.1 | async-start | bytes 262144 | tf_op jit(solution)/shard_map/all_to_all | solution.py:402
  21.4 7.7 %copy-start.1 = (bf16[4,32,768]{2,1,0:T(8,128)(2,1)S(1)}, bf16[4,32,768]{2,1,0:T(8,128)(2,1)}, u32[]{:S(2)}) copy-start(bf16[4,32,768]{2,1,0:T(8,128)(2,1)} %basis_ref.1) | copy-start | bytes 589828
  25.1 1.4 %collective-permute-start.1 = (f32[2,16,768]{2,1,0:T(8,128)S(1)}, f32[2,16,768]{2,1,0:T(8,128)S(1)}, u32[]{:S(2)}, u32[]{:S(2)}) collective-permute-start(f32[2,16,768]{2,1,0:T(8,128)S(1)} %near.1.own_ref), channel_id=1, source_target_pairs={{0,8},{8,0},{16,24},{24,16},{1,9},{9,1},{17,25},{25,17},{2,10},{10... | collective-permute-start | bytes 294920 | tf_op jit(solution)/shard_map/ppermute | solution.py:421

commit v10 on v9

--- a/solution.py
+++ b/solution.py
@@ -171,9 +171,10 @@
     long_index = lax.axis_index("long")
     before = jnp.maximum(long_index - 1, 0)
     totals = [jnp.zeros(pay_ref.shape[1:], jnp.float32) for _ in range(2)]
-    for row in range(pay_ref.shape[0] // long_count):
+    row_count = pay_ref.shape[0] // long_count
+    for row in range(row_count):
         for source, owner in enumerate((long_index, before)):
-            totals[source] += pay_ref[row * long_count + owner].astype(jnp.float32)
+            totals[source] += pay_ref[owner * row_count + row].astype(jnp.float32)
     even = lax.axis_index("row") % 2 == 0
     half = pay_ref.shape[1]
     rank_size = pay_ref.shape[2] // 4
@@ -266,12 +267,13 @@
     done_ref[...] = jnp.zeros(done_ref.shape, jnp.float32)
     long_count, rhs_count, _ = total_ref.shape
     rank_size = coupling_ref.shape[1]
+    row_count = out_ref.shape[0] // long_count
     groups = LANES // rank_size
     group_id = lax.broadcasted_iota(jnp.int32, (rhs_count, LANES), 1) // rank_size
     total_ref[...] = jnp.zeros(total_ref.shape, jnp.float32)
 
     def coeff_of(cluster):
-        whole = coeff_ref[(cluster % clusters) * long_count + cluster // clusters]
+        whole = coeff_ref[(cluster // clusters) * row_count + cluster % clusters]
         whole = whole.astype(jnp.float32)
         return jnp.concatenate(
             [whole[:, 0:rank_size], whole[:, rank_size : 2 * rank_size]], axis=0
@@ -299,9 +301,10 @@
         owner = cluster // clusters
         total_ref[owner] += jnp.where(group_id == cluster % clusters, value, 0.0)
 
-    sent = total_ref[...].astype(jnp.bfloat16)
-    for copy_id in range(out_ref.shape[0] // long_count):
-        out_ref[copy_id * long_count : (copy_id + 1) * long_count] = sent
+    for owner in range(long_count):
+        sent = total_ref[owner].astype(jnp.bfloat16)
+        for row in range(row_count):
+            out_ref[owner * row_count + row] = sent
 
 
 def finish_kernel(own_ref, other_ref, far_ref, basis_ref, out_ref):
@@ -331,7 +334,7 @@
 
     pay = pl.pallas_call(
         coeffs_kernel,
-        out_shape=pltpu.VMEM((devices, rhs_count // 2, LANES), jnp.bfloat16),
+        out_shape=jax.ShapeDtypeStruct((devices, rhs_count // 2, LANES), jnp.bfloat16),
         in_specs=[HBM] * 3 + [SMEM],
         out_specs=VMEM,
         scratch_shapes=[
@@ -349,7 +352,7 @@
         ],
         near_count,
     )
-    everyone = lax.all_to_all(pay, ("row", "long"), 0, 0, tiled=True)
+    everyone = lax.all_to_all(pay, ("long", "row"), 0, 0, tiled=True)
 
     xs, to_neighbour, geometry = pl.pallas_call(
         geometry_kernel,
@@ -390,7 +393,7 @@
     far, far_done = pl.pallas_call(
         functools.partial(far_kernel, clusters=clusters),
         out_shape=[
-            pltpu.VMEM((devices, rhs_count, clusters * rank_size), jnp.bfloat16),
+            jax.ShapeDtypeStruct((devices, rhs_count, clusters * rank_size), jnp.bfloat16),
             jax.ShapeDtypeStruct((8, LANES), jnp.float32),
         ],
         in_specs=[SMEM, VMEM, VMEM],
@@ -399,7 +402,7 @@
         compiler_params=pltpu.CompilerParams(vmem_limit_bytes=16 << 20),
         name="far",
     )(far_pairs, everyone, coupling)
-    far_terms = lax.all_to_all(far, ("row", "long"), 0, 0, tiled=True)
+    far_terms = lax.all_to_all(far, ("long", "row"), 0, 0, tiled=True)
 
     near = pl.pallas_call(
         functools.partial(near_kernel, long_count=long_count, clusters=clusters),

time: 30.3 us -> 30.9 us (1.020)
  waiting for transfers between devices: 6.94 us -> 7.56 us
    all_to_all x2, waiting for transfers between devices: 5.75 us -> 6.37 us  [the longest x1 3.23 us: shards(): everyone = lax.all_to_all(pay, ('long', 'row'), 0, 0, tiled=True)]
where the time goes in v10:
time: 30.9 us; the launch traced here: 30.6 us
  starting transfers between devices  13.7 us (44%)
  Pallas kernels  8.35 us (27%)
  waiting for transfers between devices  7.56 us (24%)
  between operations  0.81 us (3%)
    all_to_all x1, starting transfers between devices, shards(): everyone = lax.all_to_all(pay, ('long', 'row'), 0, 0, tiled=True)  7.3 us
    ppermute x1, starting transfers between devices, shards(): halo = lax.ppermute(to_neighbour, ('row', 'long'), route)  3.68 us
    pallas_call x1, Pallas kernels, shards(): pl.pallas_call(functools.partial(near_kernel, long_count=long_count, clus...  3.66 us
    all_to_all x1, waiting for transfers between devices, shards(): everyone = lax.all_to_all(pay, ('long', 'row'), 0, 0, tiled=True)  3.23 us
    all_to_all x1, waiting for transfers between devices, shards(): far_terms = lax.all_to_all(far, ('long', 'row'), 0, 0, tiled=True)  3.14 us
    all_to_all x1, starting transfers between devices, shards(): far_terms = lax.all_to_all(far, ('long', 'row'), 0, 0, tiled=True)  2.58 us
    pallas_call x1, Pallas kernels, shards(): pl.pallas_call(functools.partial(far_kernel, clusters=clusters), out_shap...  1.74 us
    pallas_call x1, Pallas kernels, shards(): pl.pallas_call(coeffs_kernel, out_shape=jax.ShapeDtypeStruct((devices, rh...  1.72 us
  transfers between devices with their start and end apart: 4, of which 3 were waited for; matrix products, arithmetic and copies ran while one was open for 0% of the time, Pallas kernels for 19%

profile of v10, /device:TPU:0, one launch (start us, length us, event | category | flops | bytes accessed | tf_op | source)
XLA Modules:
  0.0 30.6 jit_solution(7898176684674917816)
XLA Ops:
  0.7 0.0 copy-start
  0.7 1.7 %coeffs.1.after_ref = bf16[32,8,128]{2,1,0:T(8,128)(2,1)} custom-call(f32[4,16,768]{2,1,0:T(8,128)} %slip_ref.1, bf16[4,32,768]{2,1,0:T(8,128)(2,1)} %basis_ref.1, s32[2,20]{1,0:T(2,128)} %pairs_hbm.1, s32[1]{0:T(128)S(6)} %copy.10.count_ref), custom_call_target="tpu_custom_call" | custom-call | tf_op jit(solution)/shard_map/coeffs/pallas_call | solution.py:335
  2.4 0.0 copy-start.2
  2.4 0.0 copy-start.3
  2.4 0.0 copy-start.4
  2.4 7.3 %all-to-all-start = ((bf16[32,8,128]{2,1,0:T(8,128)(2,1)}), bf16[32,8,128]{2,1,0:T(8,128)(2,1)S(1)}, u32[]{:S(2)}, u32[]{:S(2)}) async-start(bf16[32,8,128]{2,1,0:T(8,128)(2,1)} %coeffs.1.after_ref), calls=%async_computation | async-start | bytes 131072 | tf_op jit(solution)/shard_map/all_to_all | solution.py:355
  9.7 0.0 copy-done
  9.7 0.0 copy-done.2
  9.8 0.0 copy-done.3
  9.8 0.0 copy-done.4
  9.8 0.0 copy-start.6
  9.8 0.3 geometry.1
  10.1 0.0 copy-start.5
  10.1 3.7 %collective-permute-start = (bf16[2,16,1024]{2,1,0:T(8,128)(2,1)S(1)}, bf16[2,16,1024]{2,1,0:T(8,128)(2,1)S(1)}, u32[]{:S(2)}, u32[]{:S(2)}) collective-permute-start(bf16[2,16,1024]{2,1,0:T(8,128)(2,1)S(1)} %get-tuple-element.14), channel_id=1, source_target_pairs={{0,1},{1,2},{2,3},{3,4},{4,5},{5,6},{6,7},{9,8},{10,9},{11,10},{12... | collective-permute-start | bytes 196616 | tf_op jit(solution)/shard_map/ppermute | solution.py:378
  13.8 0.0 copy-done.6
  13.8 0.1 reshape.3.coupling_ref
  13.9 3.2 %all-to-all-done.coeff_ref.pay_ref = bf16[32,8,128]{2,1,0:T(8,128)(2,1)S(1)} async-done(((bf16[32,8,128]{2,1,0:T(8,128)(2,1)}), bf16[32,8,128]{2,1,0:T(8,128)(2,1)S(1)}, u32[]{:S(2)}, u32[]{:S(2)}) %all-to-all-start) | async-done | bytes 65568 | tf_op jit(solution)/shard_map/all_to_all | solution.py:355
  17.1 0.0 copy-done.5
  17.1 1.7 %far.1 = (bf16[32,16,128]{2,1,0:T(8,128)(2,1)}, f32[8,128]{1,0:T(8,128)S(1)}) custom-call(s32[2,16]{1,0:T(2,128)S(1)} %copy-done.5, bf16[32,8,128]{2,1,0:T(8,128)(2,1)S(1)} %all-to-all-done.coeff_ref.pay_ref, bf16[16,32,32]{2,1,0:T(8,128)(2,1)S(1)} %reshape.3.coupling_ref), custom_call_target="tpu_custom_call" | custom-call | tf_op jit(solution)/shard_map/far/pallas_call | solution.py:393
  18.9 2.6 %all-to-all-start.1 = ((bf16[32,16,128]{2,1,0:T(8,128)(2,1)}), bf16[32,16,128]{2,1,0:T(8,128)(2,1)S(1)}, u32[]{:S(2)}, u32[]{:S(2)}) async-start(bf16[32,16,128]{2,1,0:T(8,128)(2,1)} %get-tuple-element.18), calls=%async_computation.1 | async-start | bytes 262144 | tf_op jit(solution)/shard_map/all_to_all | solution.py:405
  21.5 0.0 collective-permute-done.halo_ref
  21.5 0.0 copy-start.1
  21.5 3.7 %near.1.own_ref = f32[2,16,768]{2,1,0:T(8,128)S(1)} custom-call(bf16[6,16,768]{2,1,0:T(8,128)(2,1)S(1)} %get-tuple-element.15.slip_ref, f32[6,4,256]{2,1,0:T(4,128)S(1)} %get-tuple-element.16.place_ref, bf16[32,8,128]{2,1,0:T(8,128)(2,1)S(1)} %all-to-all-done.coeff_ref.pay_ref, f32[8,128]{1,0:T(8,128)S(1)} %get-tuple-element.17.after_ref), custom_call_target="tpu_custom_call" | custom-call | flops 1000000000 | bytes 1000000 | tf_op jit(solution)/shard_map/near/pallas_call | solution.py:407
  25.2 0.2 collective-permute-start.1
  25.4 1.2 %collective-permute-done.1.other_ref = f32[2,16,768]{2,1,0:T(8,128)S(1)} collective-permute-done((f32[2,16,768]{2,1,0:T(8,128)S(1)}, f32[2,16,768]{2,1,0:T(8,128)S(1)}, u32[]{:S(2)}, u32[]{:S(2)}) %collective-permute-start.1) | collective-permute-done | bytes 98336 | tf_op jit(solution)/shard_map/ppermute | solution.py:424
  26.6 3.1 %all-to-all-done.1.far_ref = bf16[32,16,128]{2,1,0:T(8,128)(2,1)S(1)} async-done(((bf16[32,16,128]{2,1,0:T(8,128)(2,1)}), bf16[32,16,128]{2,1,0:T(8,128)(2,1)S(1)}, u32[]{:S(2)}, u32[]{:S(2)}) %all-to-all-start.1) | async-done | bytes 131104 | tf_op jit(solution)/shard_map/all_to_all | solution.py:405
  29.7 0.0 copy-done.1
  29.7 0.9 %finish.1 = f32[4,16,768]{2,1,0:T(8,128)} custom-call(f32[2,16,768]{2,1,0:T(8,128)S(1)} %near.1.own_ref, f32[2,16,768]{2,1,0:T(8,128)S(1)} %collective-permute-done.1.other_ref, bf16[32,16,128]{2,1,0:T(8,128)(2,1)S(1)} %all-to-all-done.1.far_ref, bf16[4,32,768]{2,1,0:T(8,128)(2,1)S(1)} %copy-done.1), custom_call_target="tpu_custom_call" | custom-call | tf_op jit(solution)/shard_map/finish/pallas_call | solution.py:426
  (1 shorter events, 0.0 us)
Async XLA Ops:
  0.7 9.1 %copy-start = (f32[4,16,768]{2,1,0:T(8,128)S(1)}, f32[4,16,768]{2,1,0:T(8,128)}, u32[]{:S(2)}) copy-start(f32[4,16,768]{2,1,0:T(8,128)} %slip_ref.1) | copy-start | bytes 589828
  2.4 7.4 %copy-start.2 = (s32[3,1024]{1,0:T(4,128)S(1)}, s32[3,1024]{1,0:T(4,128)}, u32[]{:S(2)}) copy-start(s32[3,1024]{1,0:T(4,128)} %triangles_ref.1) | copy-start | bytes 36868
  2.4 7.4 %copy-start.3 = (f32[3,561]{1,0:T(4,128)S(1)}, f32[3,561]{1,0:T(4,128)}, u32[]{:S(2)}) copy-start(f32[3,561]{1,0:T(4,128)} %vertices_ref.1) | copy-start | bytes 20200
  2.4 7.4 %copy-start.4 = (s32[4,256]{1,0:T(4,128)S(1)}, s32[4,256]{1,0:T(4,128)}, u32[]{:S(2)}) copy-start(s32[4,256]{1,0:T(4,128)} %map_ref.1) | copy-start | bytes 12292
  2.4 14.7 %all-to-all-start = ((bf16[32,8,128]{2,1,0:T(8,128)(2,1)}), bf16[32,8,128]{2,1,0:T(8,128)(2,1)S(1)}, u32[]{:S(2)}, u32[]{:S(2)}) async-start(bf16[32,8,128]{2,1,0:T(8,128)(2,1)} %coeffs.1.after_ref), calls=%async_computation | async-start | bytes 131072 | tf_op jit(solution)/shard_map/all_to_all | solution.py:355
  9.8 4.0 %copy-start.6 = (bf16[16,1024]{1,0:T(8,128)(2,1)S(1)}, bf16[16,1024]{1,0:T(8,128)(2,1)}, u32[]{:S(2)}) copy-start(bf16[16,1024]{1,0:T(8,128)(2,1)} %param.16) | copy-start | bytes 98308
  10.1 7.1 %copy-start.5 = (s32[2,16]{1,0:T(2,128)S(1)}, s32[2,16]{1,0:T(2,128)}, u32[]{:S(2)}) copy-start(s32[2,16]{1,0:T(2,128)} %pairs_ref.1) | copy-start | bytes 388
  10.1 11.4 %collective-permute-start = (bf16[2,16,1024]{2,1,0:T(8,128)(2,1)S(1)}, bf16[2,16,1024]{2,1,0:T(8,128)(2,1)S(1)}, u32[]{:S(2)}, u32[]{:S(2)}) collective-permute-start(bf16[2,16,1024]{2,1,0:T(8,128)(2,1)S(1)} %get-tuple-element.14), channel_id=1, source_target_pairs={{0,1},{1,2},{2,3},{3,4},{4,5},{5,6},{6,7},{9,8},{10,9},{11,10},{12... | collective-permute-start | bytes 196616 | tf_op jit(solution)/shard_map/ppermute | solution.py:378
  18.9 10.8 %all-to-all-start.1 = ((bf16[32,16,128]{2,1,0:T(8,128)(2,1)}), bf16[32,16,128]{2,1,0:T(8,128)(2,1)S(1)}, u32[]{:S(2)}, u32[]{:S(2)}) async-start(bf16[32,16,128]{2,1,0:T(8,128)(2,1)} %get-tuple-element.18), calls=%async_computation.1 | async-start | bytes 262144 | tf_op jit(solution)/shard_map/all_to_all | solution.py:405
  21.5 8.2 %copy-start.1 = (bf16[4,32,768]{2,1,0:T(8,128)(2,1)S(1)}, bf16[4,32,768]{2,1,0:T(8,128)(2,1)}, u32[]{:S(2)}) copy-start(bf16[4,32,768]{2,1,0:T(8,128)(2,1)} %basis_ref.1) | copy-start | bytes 589828
  25.2 1.4 %collective-permute-start.1 = (f32[2,16,768]{2,1,0:T(8,128)S(1)}, f32[2,16,768]{2,1,0:T(8,128)S(1)}, u32[]{:S(2)}, u32[]{:S(2)}) collective-permute-start(f32[2,16,768]{2,1,0:T(8,128)S(1)} %near.1.own_ref), channel_id=1, source_target_pairs={{0,8},{8,0},{16,24},{24,16},{1,9},{9,1},{17,25},{25,17},{2,10},{10... | collective-permute-start | bytes 294920 | tf_op jit(solution)/shard_map/ppermute | solution.py:424

commit v11 on v9

--- a/solution.py
+++ b/solution.py
@@ -17,6 +17,7 @@
 SMEM = pl.BlockSpec(memory_space=pltpu.SMEM)
 HBM = pl.BlockSpec(memory_space=pltpu.HBM)
 ANY = pl.BlockSpec(memory_space=pl.ANY)
+SMALL = pl.CostEstimate(flops=1000, bytes_accessed=1000, transcendentals=0)
 
 
 def lane_gather(table, index):
@@ -55,26 +56,24 @@
     ]
     for copy in copies:
         copy.start()
-    for copy in copies:
-        copy.wait()
     half = rhs_count // 2
-    wide = jnp.concatenate([basis_ref[...]] * (LANES // rank_size), axis=0)
-    coeffs = lax.dot_general(
-        slip_ref[...].astype(jnp.bfloat16),
-        wide,
-        (((1,), (1,)), ((), ())),
-        preferred_element_type=jnp.float32,
-    )
+    copies[2].wait()
     first = pairs_ref[0:1, :]
     kind = (first - lax.axis_index("long") * clusters) * (NEARC + 1) + pairs_ref[1:2, :] - first
     kinds = lax.broadcasted_iota(jnp.int32, (half, kind.shape[1]), 0)
     live = lax.broadcasted_iota(jnp.int32, kinds.shape, 1) < count_ref[0]
     low = jnp.sum(jnp.where(live & (kinds == kind), 1.0, 0.0), axis=1, keepdims=True)
     high = jnp.sum(jnp.where(live & (kinds + half == kind), 1.0, 0.0), axis=1, keepdims=True)
-    group = lax.broadcasted_iota(jnp.int32, (half, LANES), 1) // rank_size
-    pay = jnp.where(
-        group == 0, coeffs[0:half], jnp.where(group == 1, coeffs[half:], jnp.where(group == 2, low, high))
-    ).astype(jnp.bfloat16)
+    copies[0].wait()
+    copies[1].wait()
+    coeffs = lax.dot_general(
+        slip_ref[...].astype(jnp.bfloat16),
+        basis_ref[...],
+        (((1,), (1,)), ((), ())),
+        preferred_element_type=jnp.float32,
+    )
+    counts = [jnp.broadcast_to(value, (half, rank_size)) for value in (low, high)]
+    pay = jnp.concatenate([coeffs[0:half], coeffs[half:]] + counts, axis=1).astype(jnp.bfloat16)
     for target in range(pay_ref.shape[0]):
         pay_ref[target] = pay
 
@@ -137,23 +136,133 @@
         )
 
 
-def window_kernel(xs_ref, geom_ref, halo_ref, slip_ref, place_ref):
-    clusters, rhs_count, unknowns = xs_ref.shape
-    size = geom_ref.shape[2]
-    slots = clusters + NEARC
+def near_blocks(steps, geometry_of, slip_of, right, add, cols_ref, block_refs):
+    size = cols_ref.shape[1]
+    parts = [(0, 0), (1, 1), (2, 2), (0, 1), (0, 2), (1, 2)]
+    for turn, (place, _) in enumerate(steps):
+        rows = jnp.concatenate([geometry_of(place), jnp.zeros((4, size), jnp.float32)], axis=0)
+        cols_ref[turn] = rows.T
+
+    def fill(turn):
+        block_ref = block_refs[turn % 2]
+        for step in range(size // ROWS):
+            here = pl.ds(step * ROWS, ROWS)
+            column = cols_ref[turn, here, :]
+            left = [jnp.broadcast_to(column[:, p : p + 1], (ROWS, size)) for p in range(4)]
+            for v in steps[turn][1]:
+                offset = [left[p] - right[v][p] for p in range(3)]
+                radius_sq = offset[0] * offset[0] + offset[1] * offset[1] + offset[2] * offset[2]
+                inverse = lax.rsqrt(radius_sq + soften)
+                flat = (left[3] * right[v][3]) * inverse
+                cubed = flat * (inverse * inverse)
+                scaled = [offset[p] * cubed for p in range(3)]
+                for part_id, (i, j) in enumerate(parts):
+                    term = offset[i] * scaled[j]
+                    if i == j:
+                        term = term + flat
+                    block_ref[v, part_id, here, :] = term.astype(jnp.bfloat16)
+
+    def apply(turn):
+        block_ref = block_refs[turn % 2]
+        place, targets = steps[turn]
+        slip = slip_of(place)
+        pieces = [slip[:, p * size : (p + 1) * size] for p in range(3)]
+        for v in targets:
+            sums = [
+                jnp.dot(pieces[p], block_ref[v, p], preferred_element_type=jnp.float32)
+                for p in range(3)
+            ]
+            for part_id in range(3, 6):
+                i, j = parts[part_id]
+                both = jnp.dot(
+                    jnp.concatenate([pieces[j], pieces[i]], axis=0),
+                    block_ref[v, part_id],
+                    preferred_element_type=jnp.float32,
+                )
+                rhs_count = slip.shape[0]
+                sums[i] = sums[i] + both[0:rhs_count]
+                sums[j] = sums[j] + both[rhs_count : 2 * rhs_count]
+            add(place, v, jnp.concatenate(sums, axis=1))
+
+    for turn in range(len(steps)):
+        fill(turn)
+        if turn:
+            apply(turn - 1)
+    apply(len(steps) - 1)
+
+
+def near_counts(pay_ref, long_count):
+    clusters = 2 * NEARC
     odd = lax.axis_index("row") % 2
-
-    def place_of(cluster):
-        return (cluster + NEARC * (1 - odd) + slots) % slots
-
-    for cluster in range(clusters):
-        slip_ref[place_of(cluster)] = xs_ref[cluster]
-        place_ref[place_of(cluster)] = geom_ref[cluster]
-    for turn in range(NEARC):
-        at = place_of(clusters + turn)
-        slip_ref[at] = halo_ref[turn, :, 0:unknowns]
-        pieces = halo_ref[turn, :, unknowns : unknowns + size].astype(jnp.float32)
-        place_ref[at] = jnp.concatenate(
+    long_index = lax.axis_index("long")
+    before = jnp.maximum(long_index - 1, 0)
+    totals = [jnp.zeros(pay_ref.shape[1:], jnp.float32) for _ in range(2)]
+    for row in range(pay_ref.shape[0] // long_count):
+        for source, owner in enumerate((long_index, before)):
+            totals[source] += pay_ref[row * long_count + owner].astype(jnp.float32)
+    half, lanes = pay_ref.shape[1:]
+    lane_id = lax.broadcasted_iota(jnp.int32, (half, lanes), 1)
+    kinds = lax.broadcasted_iota(jnp.int32, (half, lanes), 0)
+    kinds = jnp.where(lane_id == 3 * lanes // 4, kinds + half, kinds)
+    kinds = jnp.where((lane_id == lanes // 2) | (lane_id == 3 * lanes // 4), kinds, -1)
+
+    def count(place, v):
+        picked = []
+        for side in range(2):
+            cluster = NEARC + v if side else NEARC - 1 - v
+            reach = place - NEARC - v if side else NEARC + v - place
+            lower = cluster + min(reach, 0)
+            source = totals[0] if lower >= 0 else totals[1]
+            kind = (lower if lower >= 0 else lower + clusters) * (NEARC + 1) + abs(reach)
+            picked.append(jnp.where(kinds == kind, source, 0.0))
+        chosen = jnp.sum(jnp.where(odd == 1, picked[1], picked[0]), axis=0, keepdims=True)
+        return jnp.sum(chosen, axis=1, keepdims=True)
+
+    return count
+
+
+def own_near_kernel(xs_ref, geom_ref, pay_ref, out_ref, cols_ref, even_ref, odd_ref, *, long_count):
+    clusters = xs_ref.shape[0]
+    odd = lax.axis_index("row") % 2
+    count = near_counts(pay_ref, long_count)
+
+    def cluster_at(place):
+        return jnp.where(odd == 1, place, clusters - 1 - place)
+
+    right = [[geom_ref[cluster_at(NEARC + v), p : p + 1, :] for p in range(4)] for v in range(NEARC)]
+    out_ref[...] = jnp.zeros(out_ref.shape, jnp.float32)
+
+    def add(place, v, value):
+        out_ref[jnp.where(odd == 1, v, NEARC - 1 - v)] += count(place, v) * value
+
+    steps = [
+        (place, [v for v in range(NEARC) if 0 <= place - v <= 2 * NEARC]) for place in range(clusters)
+    ]
+    near_blocks(
+        steps,
+        lambda place: geom_ref[cluster_at(place)],
+        lambda place: xs_ref[cluster_at(place)],
+        right,
+        add,
+        cols_ref,
+        (even_ref, odd_ref),
+    )
+
+
+def halo_near_kernel(
+    begun_ref, halo_ref, geom_ref, pay_ref, out_ref, cols_ref, even_ref, odd_ref, *, long_count, clusters
+):
+    unknowns = out_ref.shape[2]
+    size = unknowns // 3
+    odd = lax.axis_index("row") % 2
+    count = near_counts(pay_ref, long_count)
+
+    def halo_at(place):
+        return jnp.where(odd == 1, place - clusters, clusters + NEARC - 1 - place)
+
+    def geometry_of(place):
+        pieces = halo_ref[halo_at(place), :, unknowns : unknowns + size].astype(jnp.float32)
+        return jnp.concatenate(
             [
                 (pieces[3 * p + 2 : 3 * p + 3] + pieces[3 * p + 1 : 3 * p + 2])
                 + pieces[3 * p : 3 * p + 1]
@@ -162,102 +271,28 @@
             axis=0,
         )
 
-
-def near_kernel(
-    slip_ref, place_ref, pay_ref, after_ref, out_ref, cols_ref, even_ref, odd_ref, *, long_count, clusters
-):
-    slots, rhs_count, unknowns = slip_ref.shape
-    size = place_ref.shape[2]
-    long_index = lax.axis_index("long")
-    before = jnp.maximum(long_index - 1, 0)
-    totals = [jnp.zeros(pay_ref.shape[1:], jnp.float32) for _ in range(2)]
-    for row in range(pay_ref.shape[0] // long_count):
-        for source, owner in enumerate((long_index, before)):
-            totals[source] += pay_ref[row * long_count + owner].astype(jnp.float32)
-    even = lax.axis_index("row") % 2 == 0
-    half = pay_ref.shape[1]
-    rank_size = pay_ref.shape[2] // 4
-    group = lax.broadcasted_iota(jnp.int32, (half, LANES), 1) // rank_size
-    kinds = lax.broadcasted_iota(jnp.int32, (half, LANES), 0) + jnp.where(group == 3, half, 0)
-    kinds = jnp.where(group < 2, -1, kinds)
-    lane_id = lax.broadcasted_iota(jnp.int32, (half, LANES), 1)
-    kinds = jnp.where(lane_id % rank_size == 0, kinds, -1)
-
-    def count_of(place, u):
-        both = []
-        for cluster in (u, clusters - NEARC + u):
-            reach = place - u - NEARC
-            lower = cluster + jnp.minimum(reach, 0)
-            inside = lower >= 0
-            kind = jnp.where(inside, lower, lower + clusters) * (NEARC + 1) + jnp.abs(reach)
-            source = jnp.where(inside, totals[0], totals[1])
-            both.append(jnp.where(kinds == kind, source, 0.0))
-        picked = jnp.sum(jnp.where(even, both[0], both[1]), axis=0, keepdims=True)
-        return jnp.sum(picked, axis=1, keepdims=True)
-
-    out_ref[...] = jnp.zeros(out_ref.shape, jnp.float32)
-    for place in range(slots):
-        rows = jnp.concatenate([place_ref[place], jnp.zeros((4, size), jnp.float32)], axis=0)
-        cols_ref[place] = rows.T
-    right = [[place_ref[NEARC + u, p : p + 1, :] for p in range(4)] for u in range(NEARC)]
-    parts = [(0, 0), (1, 1), (2, 2), (0, 1), (0, 2), (1, 2)]
-
-    def fill(place, targets, block_ref):
-        for step in range(size // ROWS):
-            here = pl.ds(step * ROWS, ROWS)
-            column = cols_ref[place, here, :]
-            left = [jnp.broadcast_to(column[:, p : p + 1], (ROWS, size)) for p in range(4)]
-            for u in targets:
-                offset = [left[p] - right[u][p] for p in range(3)]
-                radius_sq = offset[0] * offset[0] + offset[1] * offset[1] + offset[2] * offset[2]
-                inverse = lax.rsqrt(radius_sq + soften)
-                flat = (left[3] * right[u][3]) * inverse
-                cubed = flat * (inverse * inverse)
-                scaled = [offset[p] * cubed for p in range(3)]
-                for part_id, (i, j) in enumerate(parts):
-                    term = offset[i] * scaled[j]
-                    if i == j:
-                        term = term + flat
-                    block_ref[u, part_id, here, :] = term.astype(jnp.bfloat16)
-
-    def apply(place, targets, block_ref):
-        slip = slip_ref[place]
-        pieces = [slip[:, p * size : (p + 1) * size] for p in range(3)]
-        for u in targets:
-            count = count_of(place, u)
-            sums = [
-                jnp.dot(pieces[p], block_ref[u, p], preferred_element_type=jnp.float32)
-                for p in range(3)
-            ]
-            for part_id in range(3, 6):
-                i, j = parts[part_id]
-                both = jnp.dot(
-                    jnp.concatenate([pieces[j], pieces[i]], axis=0),
-                    block_ref[u, part_id],
-                    preferred_element_type=jnp.float32,
-                )
-                sums[i] = sums[i] + both[0:rhs_count]
-                sums[j] = sums[j] + both[rhs_count : 2 * rhs_count]
-            for p in range(3):
-                out_ref[u, :, p * size : (p + 1) * size] += count * sums[p]
-
-    every = list(range(NEARC))
-    fill(0, [0], even_ref)
-    for u in range(1, NEARC):
-        even_ref[u] = jnp.zeros(even_ref.shape[1:], jnp.bfloat16)
-
-    def two_places(turn, carry):
-        place = 2 * turn
-        fill(place + 1, every, odd_ref)
-        apply(place, every, even_ref)
-        fill(place + 2, every, even_ref)
-        apply(place + 1, every, odd_ref)
-        return carry
-
-    lax.fori_loop(0, (slots - 2) // 2, two_places, 0)
-    fill(slots - 1, [NEARC - 1], odd_ref)
-    apply(slots - 2, every, even_ref)
-    apply(slots - 1, [NEARC - 1], odd_ref)
+    right = []
+    for v in range(NEARC):
+        mine = jnp.where(odd == 1, NEARC + v, NEARC - 1 - v)
+        right.append([geom_ref[mine, p : p + 1, :] for p in range(4)])
+    out_ref[...] = begun_ref[...]
+
+    def add(place, v, value):
+        out_ref[jnp.where(odd == 1, v, NEARC - 1 - v)] += count(place, v) * value
+
+    steps = [
+        (place, [v for v in range(NEARC) if 0 <= place - v <= 2 * NEARC])
+        for place in range(clusters, clusters + NEARC)
+    ]
+    near_blocks(
+        steps,
+        geometry_of,
+        lambda place: halo_ref[halo_at(place), :, 0:unknowns],
+        right,
+        add,
+        cols_ref,
+        (even_ref, odd_ref),
+    )
 
 
 def far_kernel(
@@ -326,12 +361,11 @@
     row_count = lax.axis_size("row")
     long_count = lax.axis_size("long")
     devices = row_count * long_count
-    coupling = far_coef.reshape(-1, rank_size, rank_size)
-    slots = clusters + NEARC
+    blocks = [pltpu.VMEM((NEARC, 6, size, size), jnp.bfloat16)] * 2
 
     pay = pl.pallas_call(
         coeffs_kernel,
-        out_shape=pltpu.VMEM((devices, rhs_count // 2, LANES), jnp.bfloat16),
+        out_shape=jax.ShapeDtypeStruct((devices, rhs_count // 2, LANES), jnp.bfloat16),
         in_specs=[HBM] * 3 + [SMEM],
         out_specs=VMEM,
         scratch_shapes=[
@@ -351,6 +385,23 @@
     )
     everyone = lax.all_to_all(pay, ("row", "long"), 0, 0, tiled=True)
 
+    held, everyone = lax.optimization_barrier((far_coef, everyone))
+    coupling = held.reshape(-1, rank_size, rank_size)
+
+    far, far_done = pl.pallas_call(
+        functools.partial(far_kernel, clusters=clusters),
+        out_shape=[
+            jax.ShapeDtypeStruct((devices, rhs_count, clusters * rank_size), jnp.bfloat16),
+            jax.ShapeDtypeStruct((8, LANES), jnp.float32),
+        ],
+        in_specs=[SMEM, VMEM, VMEM],
+        out_specs=[VMEM] * 2,
+        scratch_shapes=[pltpu.VMEM((long_count, rhs_count, clusters * rank_size), jnp.float32)],
+        compiler_params=pltpu.CompilerParams(vmem_limit_bytes=16 << 20),
+        name="far",
+    )(far_pairs, everyone, coupling)
+    far_terms = lax.all_to_all(far, ("row", "long"), 0, 0, tiled=True)
+
     xs, to_neighbour, geometry = pl.pallas_call(
         geometry_kernel,
         out_shape=[
@@ -361,11 +412,9 @@
         in_specs=[VMEM] * 4 + [ANY],
         out_specs=[VMEM] * 3,
         compiler_params=pltpu.CompilerParams(vmem_limit_bytes=16 << 20),
-        cost_estimate=pl.CostEstimate(
-            flops=2_000_000, bytes_accessed=1_000_000, transcendentals=1_000
-        ),
+        cost_estimate=SMALL,
         name="geometry",
-    )(slip, vertices, triangles, elem_map, pay)
+    )(slip, vertices, triangles, elem_map, far_done)
     route = []
     for row in range(row_count):
         step = 1 if row % 2 == 0 else -1
@@ -374,49 +423,27 @@
                 route.append((row * long_count + owner - step, row * long_count + owner))
     halo = lax.ppermute(to_neighbour, ("row", "long"), route)
 
-    window, places = pl.pallas_call(
-        window_kernel,
-        out_shape=[
-            jax.ShapeDtypeStruct((slots, rhs_count, unknowns), jnp.bfloat16),
-            jax.ShapeDtypeStruct((slots, 4, size), jnp.float32),
-        ],
+    own_near = pl.pallas_call(
+        functools.partial(own_near_kernel, long_count=long_count),
+        out_shape=jax.ShapeDtypeStruct((NEARC, rhs_count, unknowns), jnp.float32),
         in_specs=[VMEM] * 3,
-        out_specs=[VMEM] * 2,
-        compiler_params=pltpu.CompilerParams(vmem_limit_bytes=16 << 20),
-        cost_estimate=pl.CostEstimate(flops=1000, bytes_accessed=1000, transcendentals=0),
-        name="window",
-    )(xs, geometry, halo)
-
-    far, far_done = pl.pallas_call(
-        functools.partial(far_kernel, clusters=clusters),
-        out_shape=[
-            pltpu.VMEM((devices, rhs_count, clusters * rank_size), jnp.bfloat16),
-            jax.ShapeDtypeStruct((8, LANES), jnp.float32),
-        ],
-        in_specs=[SMEM, VMEM, VMEM],
-        out_specs=[VMEM] * 2,
-        scratch_shapes=[pltpu.VMEM((long_count, rhs_count, clusters * rank_size), jnp.float32)],
-        compiler_params=pltpu.CompilerParams(vmem_limit_bytes=16 << 20),
-        name="far",
-    )(far_pairs, everyone, coupling)
-    far_terms = lax.all_to_all(far, ("row", "long"), 0, 0, tiled=True)
+        out_specs=VMEM,
+        scratch_shapes=[pltpu.VMEM((clusters, size, 8), jnp.float32)] + blocks,
+        compiler_params=pltpu.CompilerParams(vmem_limit_bytes=24 << 20),
+        cost_estimate=SMALL,
+        name="own_near",
+    )(xs, geometry, everyone)
 
     near = pl.pallas_call(
-        functools.partial(near_kernel, long_count=long_count, clusters=clusters),
+        functools.partial(halo_near_kernel, long_count=long_count, clusters=clusters),
         out_shape=jax.ShapeDtypeStruct((NEARC, rhs_count, unknowns), jnp.float32),
-        in_specs=[VMEM] * 3 + [ANY],
+        in_specs=[VMEM] * 4,
         out_specs=VMEM,
-        scratch_shapes=[
-            pltpu.VMEM((slots, size, 8), jnp.float32),
-            pltpu.VMEM((NEARC, 6, size, size), jnp.bfloat16),
-            pltpu.VMEM((NEARC, 6, size, size), jnp.bfloat16),
-        ],
+        scratch_shapes=[pltpu.VMEM((NEARC, size, 8), jnp.float32)] + blocks,
         compiler_params=pltpu.CompilerParams(vmem_limit_bytes=24 << 20),
-        cost_estimate=pl.CostEstimate(
-            flops=1_000_000_000, bytes_accessed=1_000_000, transcendentals=660_000
-        ),
-        name="near",
-    )(window, places, everyone, far_done)
+        cost_estimate=SMALL,
+        name="halo_near",
+    )(own_near, halo, geometry, everyone)
     partner = [(row, row ^ 1) for row in range(row_count)]
     other = lax.ppermute(near, "row", partner)
 

time: 30.3 us -> 31.8 us (1.050)
  blocking collectives: 0 us -> 14.4 us
  starting transfers between devices: 13.7 us -> 6.34 us
  waiting for transfers between devices: 6.94 us -> 1.34 us
  local copies, waits for them, and re-layouts: 0.19 us -> 0.7 us
  Pallas kernels: 8.35 us -> 7.9 us
    all_to_all x0 -> x1, blocking collectives: none -> 14.4 us  [shards(): everyone = lax.all_to_all(pay, ('row', 'long'), 0, 0, tiled=True)]
    all_to_all x1 -> x0, starting transfers between devices: 7.3 us -> none  [shards(): everyone = lax.all_to_all(pay, ('row', 'long'), 0, 0, tiled=True)]
    all_to_all x1 -> x0, waiting for transfers between devices: 3.1 us -> none  [shards(): everyone = lax.all_to_all(pay, ('row', 'long'), 0, 0, tiled=True)]
    all_to_all x1, waiting for transfers between devices: 2.65 us -> 0.01 us  [shards(): far_terms = lax.all_to_all(far, ('row', 'long'), 0, 0, tiled=True)]
    unnamed x14, local copies, waits for them, and re-layouts: 0.04 us -> 0.55 us
    pallas_call x3, Pallas kernels: 5.43 us -> 4.98 us  [the longest x1 2.7 us: shards(): pl.pallas_call(functools.partial(own_near_kernel, long_count=long_count),...]
  transfers between devices with their start and end apart: 4 -> 3, of which waited for: 3 -> 1; matrix products, arithmetic and copies ran while one was open for 0% -> 0% of each run, Pallas kernels for 19% -> 13%
where the time goes in v11:
time: 31.8 us; the launch traced here: 31.4 us
  blocking collectives  14.4 us (45%)
  Pallas kernels  7.9 us (25%)
  starting transfers between devices  6.34 us (20%)
  waiting for transfers between devices  1.34 us (4%)
  between operations  0.76 us (2%)
  local copies, waits for them, and re-layouts  0.7 us (2%)
    all_to_all x1, blocking collectives, shards(): everyone = lax.all_to_all(pay, ('row', 'long'), 0, 0, tiled=True)  14.4 us
    ppermute x1, starting transfers between devices, shards(): halo = lax.ppermute(to_neighbour, ('row', 'long'), route)  3.56 us
    all_to_all x1, starting transfers between devices, shards(): far_terms = lax.all_to_all(far, ('row', 'long'), 0, 0, tiled=True)  2.71 us
    pallas_call x1, Pallas kernels, shards(): pl.pallas_call(functools.partial(own_near_kernel, long_count=long_count),...  2.7 us
    pallas_call x1, Pallas kernels, shards(): pl.pallas_call(functools.partial(far_kernel, clusters=clusters), out_shap...  1.74 us
    ppermute x1, waiting for transfers between devices, shards(): other = lax.ppermute(near, 'row', partner)  1.29 us
    pallas_call x1, Pallas kernels, shards(): pl.pallas_call(functools.partial(halo_near_kernel, long_count=long_count,...  1.21 us
    pallas_call x1, Pallas kernels, shards(): pl.pallas_call(coeffs_kernel, out_shape=jax.ShapeDtypeStruct((devices, rh...  1.07 us
  transfers between devices with their start and end apart: 3, of which 1 were waited for; matrix products, arithmetic and copies ran while one was open for 0% of the time, Pallas kernels for 13%

profile of v11, /device:TPU:0, one launch (start us, length us, event | category | flops | bytes accessed | tf_op | source)
XLA Modules:
  0.0 31.4 jit_solution(13285922939303193873)
XLA Ops:
  0.7 1.1 %coeffs.1 = bf16[32,8,128]{2,1,0:T(8,128)(2,1)S(1)} custom-call(f32[4,16,768]{2,1,0:T(8,128)} %slip_ref.1, bf16[4,32,768]{2,1,0:T(8,128)(2,1)} %basis_ref.1, s32[2,20]{1,0:T(2,128)} %pairs_hbm.1, s32[1]{0:T(128)S(6)} %copy.10.count_ref), custom_call_target="tpu_custom_call" | custom-call | tf_op jit(solution)/shard_map/coeffs/pallas_call | solution.py:366
  1.7 0.0 copy-start.6
  1.7 14.4 %all_to_all.10.coeff_ref.pay_ref = bf16[32,8,128]{2,1,0:T(8,128)(2,1)S(1)} all-to-all(bf16[32,8,128]{2,1,0:T(8,128)(2,1)S(1)} %coeffs.1), channel_id=1, replica_groups=mesh['row'=4,'long'=8] {'row','long'}, dimensions={0} | all-to-all | bytes 131072 | tf_op jit(solution)/shard_map/all_to_all | solution.py:386
  16.1 0.0 copy-done.6
  16.1 0.0 copy-start.5
  16.1 0.1 reshape.3.coupling_ref
  16.3 0.5 %copy-done.5 = s32[2,16]{1,0:T(2,128)S(1)} copy-done((s32[2,16]{1,0:T(2,128)S(1)}, s32[2,16]{1,0:T(2,128)}, u32[]{:S(2)}) %copy-start.5) | copy-done | bytes 152
  16.8 0.0 copy-start
  16.8 1.7 %far.1 = (bf16[32,16,128]{2,1,0:T(8,128)(2,1)}, f32[8,128]{1,0:T(8,128)S(1)}) custom-call(s32[2,16]{1,0:T(2,128)S(1)} %copy-done.5, bf16[32,8,128]{2,1,0:T(8,128)(2,1)S(1)} %all_to_all.10.coeff_ref.pay_ref, bf16[16,32,32]{2,1,0:T(8,128)(2,1)S(1)} %reshape.3.coupling_ref), custom_call_target="tpu_custom_call" | custom-call | tf_op jit(solution)/shard_map/far/pallas_call | solution.py:391
  18.5 0.0 copy-start.2
  18.5 0.0 copy-start.3
  18.6 0.0 copy-start.4
  18.6 2.7 %all-to-all-start.1 = ((bf16[32,16,128]{2,1,0:T(8,128)(2,1)}), bf16[32,16,128]{2,1,0:T(8,128)(2,1)S(1)}, u32[]{:S(2)}, u32[]{:S(2)}) async-start(bf16[32,16,128]{2,1,0:T(8,128)(2,1)} %get-tuple-element.18), calls=%async_computation.1 | async-start | bytes 262144 | tf_op jit(solution)/shard_map/all_to_all | solution.py:403
  21.3 0.0 copy-done
  21.3 0.0 copy-done.2
  21.3 0.0 copy-done.3
  21.3 0.0 copy-done.4
  21.3 0.3 geometry.1
  21.6 3.6 %collective-permute-start = (bf16[2,16,1024]{2,1,0:T(8,128)(2,1)S(1)}, bf16[2,16,1024]{2,1,0:T(8,128)(2,1)S(1)}, u32[]{:S(2)}, u32[]{:S(2)}) collective-permute-start(bf16[2,16,1024]{2,1,0:T(8,128)(2,1)S(1)} %get-tuple-element.17), channel_id=1, source_target_pairs={{0,1},{1,2},{2,3},{3,4},{4,5},{5,6},{6,7},{9,8},{10,9},{11,10},{12... | collective-permute-start | bytes 196616 | tf_op jit(solution)/shard_map/ppermute | solution.py:424
  25.1 2.7 %own_near.1.begun_ref = f32[2,16,768]{2,1,0:T(8,128)S(1)} custom-call(bf16[4,16,768]{2,1,0:T(8,128)(2,1)S(1)} %get-tuple-element.15.xs_ref, f32[4,4,256]{2,1,0:T(4,128)S(1)} %get-tuple-element.16.geom_ref, bf16[32,8,128]{2,1,0:T(8,128)(2,1)S(1)} %all_to_all.10.coeff_ref.pay_ref), custom_call_target="tpu_custom_call" | custom-call | flops 1000 | bytes 1000 | tf_op jit(solution)/shard_map/own_near/pallas_call | solution.py:426
  27.8 0.0 copy-start.1
  27.9 0.0 collective-permute-done.halo_ref
  27.9 1.2 %halo_near.1.own_ref = f32[2,16,768]{2,1,0:T(8,128)S(1)} custom-call(f32[2,16,768]{2,1,0:T(8,128)S(1)} %own_near.1.begun_ref, bf16[2,16,1024]{2,1,0:T(8,128)(2,1)S(1)} %collective-permute-done.halo_ref, f32[4,4,256]{2,1,0:T(4,128)S(1)} %get-tuple-element.16.geom_ref, bf16[32,8,128]{2,1,0:T(8,128)(2,1)S(1)} %all_to_all.10.coeff_ref.pay_ref), custom_call_target="tpu_custom_call" | custom-call | flops 1000 | bytes 1000 | tf_op jit(solution)/shard_map/halo_near/pallas_call | solution.py:437
  29.1 0.1 collective-permute-start.1
  29.2 1.3 %collective-permute-done.1.other_ref = f32[2,16,768]{2,1,0:T(8,128)S(1)} collective-permute-done((f32[2,16,768]{2,1,0:T(8,128)S(1)}, f32[2,16,768]{2,1,0:T(8,128)S(1)}, u32[]{:S(2)}, u32[]{:S(2)}) %collective-permute-start.1) | collective-permute-done | bytes 98336 | tf_op jit(solution)/shard_map/ppermute | solution.py:448
  30.5 0.0 all-to-all-done.1.far_ref
  30.5 0.0 copy-done.1
  30.5 0.9 %finish.1 = f32[4,16,768]{2,1,0:T(8,128)} custom-call(f32[2,16,768]{2,1,0:T(8,128)S(1)} %halo_near.1.own_ref, f32[2,16,768]{2,1,0:T(8,128)S(1)} %collective-permute-done.1.other_ref, bf16[32,16,128]{2,1,0:T(8,128)(2,1)S(1)} %all-to-all-done.1.far_ref, bf16[4,32,768]{2,1,0:T(8,128)(2,1)S(1)} %copy-done.1), custom_call_target="tpu_custom_call" | custom-call | tf_op jit(solution)/shard_map/finish/pallas_call | solution.py:450
Async XLA Ops:
  1.7 14.4 %copy-start.6 = (bf16[16,1024]{1,0:T(8,128)(2,1)S(1)}, bf16[16,1024]{1,0:T(8,128)(2,1)}, u32[]{:S(2)}) copy-start(bf16[16,1024]{1,0:T(8,128)(2,1)} %param.16) | copy-start | bytes 98308
  16.1 0.7 %copy-start.5 = (s32[2,16]{1,0:T(2,128)S(1)}, s32[2,16]{1,0:T(2,128)}, u32[]{:S(2)}) copy-start(s32[2,16]{1,0:T(2,128)} %pairs_ref.1) | copy-start | bytes 388
  16.8 4.5 %copy-start = (f32[4,16,768]{2,1,0:T(8,128)S(1)}, f32[4,16,768]{2,1,0:T(8,128)}, u32[]{:S(2)}) copy-start(f32[4,16,768]{2,1,0:T(8,128)} %slip_ref.1) | copy-start | bytes 589828
  18.5 2.7 %copy-start.2 = (s32[3,1024]{1,0:T(4,128)S(1)}, s32[3,1024]{1,0:T(4,128)}, u32[]{:S(2)}) copy-start(s32[3,1024]{1,0:T(4,128)} %triangles_ref.1) | copy-start | bytes 36868
  18.5 2.7 %copy-start.3 = (f32[3,561]{1,0:T(4,128)S(1)}, f32[3,561]{1,0:T(4,128)}, u32[]{:S(2)}) copy-start(f32[3,561]{1,0:T(4,128)} %vertices_ref.1) | copy-start | bytes 20200
  18.6 2.7 %copy-start.4 = (s32[4,256]{1,0:T(4,128)S(1)}, s32[4,256]{1,0:T(4,128)}, u32[]{:S(2)}) copy-start(s32[4,256]{1,0:T(4,128)} %map_ref.1) | copy-start | bytes 12292
  18.6 11.9 %all-to-all-start.1 = ((bf16[32,16,128]{2,1,0:T(8,128)(2,1)}), bf16[32,16,128]{2,1,0:T(8,128)(2,1)S(1)}, u32[]{:S(2)}, u32[]{:S(2)}) async-start(bf16[32,16,128]{2,1,0:T(8,128)(2,1)} %get-tuple-element.18), calls=%async_computation.1 | async-start | bytes 262144 | tf_op jit(solution)/shard_map/all_to_all | solution.py:403
  21.6 6.3 %collective-permute-start = (bf16[2,16,1024]{2,1,0:T(8,128)(2,1)S(1)}, bf16[2,16,1024]{2,1,0:T(8,128)(2,1)S(1)}, u32[]{:S(2)}, u32[]{:S(2)}) collective-permute-start(bf16[2,16,1024]{2,1,0:T(8,128)(2,1)S(1)} %get-tuple-element.17), channel_id=1, source_target_pairs={{0,1},{1,2},{2,3},{3,4},{4,5},{5,6},{6,7},{9,8},{10,9},{11,10},{12... | collective-permute-start | bytes 196616 | tf_op jit(solution)/shard_map/ppermute | solution.py:424
  27.8 2.6 %copy-start.1 = (bf16[4,32,768]{2,1,0:T(8,128)(2,1)S(1)}, bf16[4,32,768]{2,1,0:T(8,128)(2,1)}, u32[]{:S(2)}) copy-start(bf16[4,32,768]{2,1,0:T(8,128)(2,1)} %basis_ref.1) | copy-start | bytes 589828
  29.1 1.4 %collective-permute-start.1 = (f32[2,16,768]{2,1,0:T(8,128)S(1)}, f32[2,16,768]{2,1,0:T(8,128)S(1)}, u32[]{:S(2)}, u32[]{:S(2)}) collective-permute-start(f32[2,16,768]{2,1,0:T(8,128)S(1)} %halo_near.1.own_ref), channel_id=1, source_target_pairs={{0,8},{8,0},{16,24},{24,16},{1,9},{9,1},{17,25},{25,17},{2,10},{10... | collective-permute-start | bytes 294920 | tf_op jit(solution)/shard_map/ppermute | solution.py:448

commit v12 on v9

--- a/solution.py
+++ b/solution.py
@@ -55,26 +55,24 @@
     ]
     for copy in copies:
         copy.start()
-    for copy in copies:
-        copy.wait()
     half = rhs_count // 2
-    wide = jnp.concatenate([basis_ref[...]] * (LANES // rank_size), axis=0)
-    coeffs = lax.dot_general(
-        slip_ref[...].astype(jnp.bfloat16),
-        wide,
-        (((1,), (1,)), ((), ())),
-        preferred_element_type=jnp.float32,
-    )
+    copies[2].wait()
     first = pairs_ref[0:1, :]
     kind = (first - lax.axis_index("long") * clusters) * (NEARC + 1) + pairs_ref[1:2, :] - first
     kinds = lax.broadcasted_iota(jnp.int32, (half, kind.shape[1]), 0)
     live = lax.broadcasted_iota(jnp.int32, kinds.shape, 1) < count_ref[0]
     low = jnp.sum(jnp.where(live & (kinds == kind), 1.0, 0.0), axis=1, keepdims=True)
     high = jnp.sum(jnp.where(live & (kinds + half == kind), 1.0, 0.0), axis=1, keepdims=True)
-    group = lax.broadcasted_iota(jnp.int32, (half, LANES), 1) // rank_size
-    pay = jnp.where(
-        group == 0, coeffs[0:half], jnp.where(group == 1, coeffs[half:], jnp.where(group == 2, low, high))
-    ).astype(jnp.bfloat16)
+    copies[0].wait()
+    copies[1].wait()
+    coeffs = lax.dot_general(
+        slip_ref[...].astype(jnp.bfloat16),
+        basis_ref[...],
+        (((1,), (1,)), ((), ())),
+        preferred_element_type=jnp.float32,
+    )
+    counts = [jnp.broadcast_to(value, (half, rank_size)) for value in (low, high)]
+    pay = jnp.concatenate([coeffs[0:half], coeffs[half:]] + counts, axis=1).astype(jnp.bfloat16)
     for target in range(pay_ref.shape[0]):
         pay_ref[target] = pay
 
@@ -260,46 +258,58 @@
     apply(slots - 1, [NEARC - 1], odd_ref)
 
 
+def coupling_kernel(coupling_ref, after_ref, to_second_ref, to_first_ref):
+    pair_count, rank_size, _ = coupling_ref.shape
+    groups = LANES // rank_size
+    for pair_id in range(pair_count):
+        here = pl.ds(pair_id * rank_size, rank_size)
+        coupling = coupling_ref[pair_id].astype(jnp.float32)
+        for out_ref, value in ((to_second_ref, coupling), (to_first_ref, coupling.T)):
+            out_ref[here, :] = jnp.concatenate([value] * groups, axis=1).astype(jnp.bfloat16)
+
+
 def far_kernel(
-    pairs_ref, coeff_ref, coupling_ref, out_ref, done_ref, total_ref, *, clusters
+    pairs_ref, coeff_ref, to_second_ref, to_first_ref, out_ref, done_ref, *total_refs, clusters
 ):
     done_ref[...] = jnp.zeros(done_ref.shape, jnp.float32)
-    long_count, rhs_count, _ = total_ref.shape
-    rank_size = coupling_ref.shape[1]
-    groups = LANES // rank_size
+    long_count, rhs_count, _ = total_refs[0].shape
+    pair_count = pairs_ref.shape[1]
+    rank_size = LANES // clusters
     group_id = lax.broadcasted_iota(jnp.int32, (rhs_count, LANES), 1) // rank_size
-    total_ref[...] = jnp.zeros(total_ref.shape, jnp.float32)
-
-    def coeff_of(cluster):
+    for total_ref in total_refs:
+        total_ref[...] = jnp.zeros(total_ref.shape, jnp.float32)
+
+    def coeff_of(cluster, group):
         whole = coeff_ref[(cluster % clusters) * long_count + cluster // clusters]
         whole = whole.astype(jnp.float32)
-        return jnp.concatenate(
-            [whole[:, 0:rank_size], whole[:, rank_size : 2 * rank_size]], axis=0
-        ).astype(jnp.bfloat16)
+        low = pltpu.roll(whole, rank_size * group, 1) if group else whole
+        high = pltpu.roll(whole, (rank_size * (group - 1)) % LANES, 1) if group != 1 else whole
+        both = jnp.concatenate([low, high], axis=0)
+        return jnp.where(group_id == group, both, 0.0)
 
     results = []
-    for pair_id in range(pairs_ref.shape[1]):
-        first = pairs_ref[0, pair_id]
-        second = pairs_ref[1, pair_id]
-        coupling = coupling_ref[pair_id]
-        to_first = lax.dot_general(
-            coeff_of(second),
-            jnp.concatenate([coupling] * groups, axis=0),
-            (((1,), (1,)), ((), ())),
-            preferred_element_type=jnp.float32,
-        )
-        to_second = jnp.dot(
-            coeff_of(first),
-            jnp.concatenate([coupling] * groups, axis=1),
-            preferred_element_type=jnp.float32,
-        )
-        results.append((first, to_first))
-        results.append((second, to_second))
-    for cluster, value in results:
-        owner = cluster // clusters
-        total_ref[owner] += jnp.where(group_id == cluster % clusters, value, 0.0)
-
-    sent = total_ref[...].astype(jnp.bfloat16)
+    for begin in range(0, pair_count, clusters):
+        pair_ids = range(begin, min(begin + clusters, pair_count))
+        depth = len(pair_ids) * rank_size
+        here = pl.ds(begin * rank_size, depth)
+        for source, target, matrix_ref in ((0, 1, to_second_ref), (1, 0, to_first_ref)):
+            coeffs = jnp.concatenate(
+                [coeff_of(pairs_ref[source, f], f - begin) for f in pair_ids], axis=0
+            ).astype(jnp.bfloat16)
+            value = jnp.dot(
+                coeffs[:, 0:depth], matrix_ref[here, :], preferred_element_type=jnp.float32
+            )
+            for turn, f in enumerate(pair_ids):
+                results.append(
+                    (pairs_ref[target, f], value[turn * rhs_count : (turn + 1) * rhs_count])
+                )
+    for turn, (cluster, value) in enumerate(results):
+        total_ref = total_refs[turn % len(total_refs)]
+        total_ref[cluster // clusters] += jnp.where(group_id == cluster % clusters, value, 0.0)
+    total = total_refs[0][...]
+    for total_ref in total_refs[1:]:
+        total = total + total_ref[...]
+    sent = total.astype(jnp.bfloat16)
     for copy_id in range(out_ref.shape[0] // long_count):
         out_ref[copy_id * long_count : (copy_id + 1) * long_count] = sent
 
@@ -331,7 +341,7 @@
 
     pay = pl.pallas_call(
         coeffs_kernel,
-        out_shape=pltpu.VMEM((devices, rhs_count // 2, LANES), jnp.bfloat16),
+        out_shape=jax.ShapeDtypeStruct((devices, rhs_count // 2, LANES), jnp.bfloat16),
         in_specs=[HBM] * 3 + [SMEM],
         out_specs=VMEM,
         scratch_shapes=[
@@ -387,18 +397,27 @@
         name="window",
     )(xs, geometry, halo)
 
+    couplings = pl.pallas_call(
+        coupling_kernel,
+        out_shape=[jax.ShapeDtypeStruct((coupling.shape[0] * rank_size, LANES), jnp.bfloat16)] * 2,
+        in_specs=[VMEM, ANY],
+        out_specs=[VMEM] * 2,
+        compiler_params=pltpu.CompilerParams(vmem_limit_bytes=16 << 20),
+        cost_estimate=pl.CostEstimate(flops=1000, bytes_accessed=1000, transcendentals=0),
+        name="coupling",
+    )(coupling, pay)
     far, far_done = pl.pallas_call(
         functools.partial(far_kernel, clusters=clusters),
         out_shape=[
-            pltpu.VMEM((devices, rhs_count, clusters * rank_size), jnp.bfloat16),
+            jax.ShapeDtypeStruct((devices, rhs_count, clusters * rank_size), jnp.bfloat16),
             jax.ShapeDtypeStruct((8, LANES), jnp.float32),
         ],
-        in_specs=[SMEM, VMEM, VMEM],
+        in_specs=[SMEM, VMEM, VMEM, VMEM],
         out_specs=[VMEM] * 2,
-        scratch_shapes=[pltpu.VMEM((long_count, rhs_count, clusters * rank_size), jnp.float32)],
+        scratch_shapes=[pltpu.VMEM((long_count, rhs_count, clusters * rank_size), jnp.float32)] * 4,
         compiler_params=pltpu.CompilerParams(vmem_limit_bytes=16 << 20),
         name="far",
-    )(far_pairs, everyone, coupling)
+    )(far_pairs, everyone, *couplings)
     far_terms = lax.all_to_all(far, ("row", "long"), 0, 0, tiled=True)
 
     near = pl.pallas_call(

time: 30.3 us -> 30.9 us (1.020)
  local copies, waits for them, and re-layouts: 0.19 us -> 0.86 us
  waiting for transfers between devices: 6.94 us -> 6.57 us
    unnamed x14, local copies, waits for them, and re-layouts: 0.04 us -> 0.71 us
    pallas_call x1 -> x2, Pallas kernels: 1.72 us -> 2.1 us  [the longest x1 1.73 us: shards(): pl.pallas_call(coeffs_kernel, out_shape=jax.ShapeDtypeStruct((devices, rh...]
    all_to_all x1, waiting for transfers between devices: 3.1 us -> 2.73 us  [shards(): everyone = lax.all_to_all(pay, ('row', 'long'), 0, 0, tiled=True)]
  transfers between devices with their start and end apart: 4 -> 4, of which waited for: 3 -> 3; matrix products, arithmetic and copies ran while one was open for 0% -> 0% of each run, Pallas kernels for 19% -> 20%
where the time goes in v12:
time: 30.9 us; the launch traced here: 30.6 us
  starting transfers between devices  13.7 us (44%)
  Pallas kernels  8.64 us (28%)
  waiting for transfers between devices  6.57 us (21%)
  local copies, waits for them, and re-layouts  0.86 us (3%)
  between operations  0.81 us (3%)
    all_to_all x1, starting transfers between devices, shards(): everyone = lax.all_to_all(pay, ('row', 'long'), 0, 0, tiled=True)  7.3 us
    ppermute x1, starting transfers between devices, shards(): halo = lax.ppermute(to_neighbour, ('row', 'long'), route)  3.68 us
    pallas_call x1, Pallas kernels, shards(): pl.pallas_call(functools.partial(near_kernel, long_count=long_count, clus...  3.66 us
    all_to_all x1, waiting for transfers between devices, shards(): everyone = lax.all_to_all(pay, ('row', 'long'), 0, 0, tiled=True)  2.73 us
    all_to_all x1, waiting for transfers between devices, shards(): far_terms = lax.all_to_all(far, ('row', 'long'), 0, 0, tiled=True)  2.65 us
    all_to_all x1, starting transfers between devices, shards(): far_terms = lax.all_to_all(far, ('row', 'long'), 0, 0, tiled=True)  2.58 us
    pallas_call x1, Pallas kernels, shards(): pl.pallas_call(coeffs_kernel, out_shape=jax.ShapeDtypeStruct((devices, rh...  1.73 us
    pallas_call x1, Pallas kernels, shards(): pl.pallas_call(functools.partial(far_kernel, clusters=clusters), out_shap...  1.64 us
  transfers between devices with their start and end apart: 4, of which 3 were waited for; matrix products, arithmetic and copies ran while one was open for 0% of the time, Pallas kernels for 20%

profile of v12, /device:TPU:0, one launch (start us, length us, event | category | flops | bytes accessed | tf_op | source)
XLA Modules:
  0.0 30.6 jit_solution(12312698234095194450)
XLA Ops:
  0.7 0.0 copy-start
  0.7 1.7 %coeffs.1.after_ref = bf16[32,8,128]{2,1,0:T(8,128)(2,1)} custom-call(f32[4,16,768]{2,1,0:T(8,128)} %slip_ref.1, bf16[4,32,768]{2,1,0:T(8,128)(2,1)} %basis_ref.1, s32[2,20]{1,0:T(2,128)} %pairs_hbm.1, s32[1]{0:T(128)S(6)} %copy.10.count_ref), custom_call_target="tpu_custom_call" | custom-call | tf_op jit(solution)/shard_map/coeffs/pallas_call | solution.py:342
  2.4 0.0 copy-start.2
  2.4 0.0 copy-start.3
  2.4 0.0 copy-start.4
  2.4 7.3 %all-to-all-start = ((bf16[32,8,128]{2,1,0:T(8,128)(2,1)}), bf16[32,8,128]{2,1,0:T(8,128)(2,1)S(1)}, u32[]{:S(2)}, u32[]{:S(2)}) async-start(bf16[32,8,128]{2,1,0:T(8,128)(2,1)} %coeffs.1.after_ref), calls=%async_computation | async-start | bytes 131072 | tf_op jit(solution)/shard_map/all_to_all | solution.py:362
  9.8 0.0 copy-done
  9.8 0.0 copy-done.2
  9.8 0.0 copy-done.3
  9.8 0.0 copy-done.4
  9.8 0.0 copy-start.6
  9.8 0.3 geometry.1
  10.1 3.7 %collective-permute-start = (bf16[2,16,1024]{2,1,0:T(8,128)(2,1)S(1)}, bf16[2,16,1024]{2,1,0:T(8,128)(2,1)S(1)}, u32[]{:S(2)}, u32[]{:S(2)}) collective-permute-start(bf16[2,16,1024]{2,1,0:T(8,128)(2,1)S(1)} %get-tuple-element.16), channel_id=1, source_target_pairs={{0,1},{1,2},{2,3},{3,4},{4,5},{5,6},{6,7},{9,8},{10,9},{11,10},{12... | collective-permute-start | bytes 196616 | tf_op jit(solution)/shard_map/ppermute | solution.py:385
  13.8 0.0 copy-done.6
  13.8 0.1 reshape.3.coupling_ref
  13.9 0.4 %coupling.1 = (bf16[512,128]{1,0:T(8,128)(2,1)S(1)}, bf16[512,128]{1,0:T(8,128)(2,1)S(1)}) custom-call(bf16[16,32,32]{2,1,0:T(8,128)(2,1)S(1)} %reshape.3.coupling_ref, bf16[32,8,128]{2,1,0:T(8,128)(2,1)} %coeffs.1.after_ref), custom_call_target="tpu_custom_call" | custom-call | flops 1000 | bytes 1000 | tf_op jit(solution)/shard_map/coupling/pallas_call | solution.py:400
  14.3 2.7 %all-to-all-done.coeff_ref.pay_ref = bf16[32,8,128]{2,1,0:T(8,128)(2,1)S(1)} async-done(((bf16[32,8,128]{2,1,0:T(8,128)(2,1)}), bf16[32,8,128]{2,1,0:T(8,128)(2,1)S(1)}, u32[]{:S(2)}, u32[]{:S(2)}) %all-to-all-start) | async-done | bytes 65568 | tf_op jit(solution)/shard_map/all_to_all | solution.py:362
  17.0 0.0 copy-start.5
  17.0 0.7 %copy-done.5 = s32[2,16]{1,0:T(2,128)S(1)} copy-done((s32[2,16]{1,0:T(2,128)S(1)}, s32[2,16]{1,0:T(2,128)}, u32[]{:S(2)}) %copy-start.5) | copy-done | bytes 152
  17.7 1.6 %far.1 = (bf16[32,16,128]{2,1,0:T(8,128)(2,1)}, f32[8,128]{1,0:T(8,128)S(1)}) custom-call(s32[2,16]{1,0:T(2,128)S(1)} %copy-done.5, bf16[32,8,128]{2,1,0:T(8,128)(2,1)S(1)} %all-to-all-done.coeff_ref.pay_ref, bf16[512,128]{1,0:T(8,128)(2,1)S(1)} %get-tuple-element.19.to_second_ref, bf16[512,128]{1,0:T(8,128)(2,1)S(1)} %get-tuple-element.20.to_first_ref), custom_call_target="tpu_custom_call" | custom-call | tf_op jit(solution)/shard_map/far/pallas_call | solution.py:409
  19.3 2.6 %all-to-all-start.1 = ((bf16[32,16,128]{2,1,0:T(8,128)(2,1)}), bf16[32,16,128]{2,1,0:T(8,128)(2,1)S(1)}, u32[]{:S(2)}, u32[]{:S(2)}) async-start(bf16[32,16,128]{2,1,0:T(8,128)(2,1)} %get-tuple-element.22), calls=%async_computation.1 | async-start | bytes 262144 | tf_op jit(solution)/shard_map/all_to_all | solution.py:421
  21.9 0.0 collective-permute-done.halo_ref
  22.0 0.0 copy-start.1
  22.0 3.7 %near.1.own_ref = f32[2,16,768]{2,1,0:T(8,128)S(1)} custom-call(bf16[6,16,768]{2,1,0:T(8,128)(2,1)S(1)} %get-tuple-element.17.slip_ref, f32[6,4,256]{2,1,0:T(4,128)S(1)} %get-tuple-element.18.place_ref, bf16[32,8,128]{2,1,0:T(8,128)(2,1)S(1)} %all-to-all-done.coeff_ref.pay_ref, f32[8,128]{1,0:T(8,128)S(1)} %get-tuple-element.21.after_ref), custom_call_target="tpu_custom_call" | custom-call | flops 1000000000 | bytes 1000000 | tf_op jit(solution)/shard_map/near/pallas_call | solution.py:423
  25.7 0.2 collective-permute-start.1
  25.8 1.2 %collective-permute-done.1.other_ref = f32[2,16,768]{2,1,0:T(8,128)S(1)} collective-permute-done((f32[2,16,768]{2,1,0:T(8,128)S(1)}, f32[2,16,768]{2,1,0:T(8,128)S(1)}, u32[]{:S(2)}, u32[]{:S(2)}) %collective-permute-start.1) | collective-permute-done | bytes 98336 | tf_op jit(solution)/shard_map/ppermute | solution.py:440
  27.0 2.6 %all-to-all-done.1.far_ref = bf16[32,16,128]{2,1,0:T(8,128)(2,1)S(1)} async-done(((bf16[32,16,128]{2,1,0:T(8,128)(2,1)}), bf16[32,16,128]{2,1,0:T(8,128)(2,1)S(1)}, u32[]{:S(2)}, u32[]{:S(2)}) %all-to-all-start.1) | async-done | bytes 131104 | tf_op jit(solution)/shard_map/all_to_all | solution.py:421
  29.7 0.0 copy-done.1
  29.7 0.9 %finish.1 = f32[4,16,768]{2,1,0:T(8,128)} custom-call(f32[2,16,768]{2,1,0:T(8,128)S(1)} %near.1.own_ref, f32[2,16,768]{2,1,0:T(8,128)S(1)} %collective-permute-done.1.other_ref, bf16[32,16,128]{2,1,0:T(8,128)(2,1)S(1)} %all-to-all-done.1.far_ref, bf16[4,32,768]{2,1,0:T(8,128)(2,1)S(1)} %copy-done.1), custom_call_target="tpu_custom_call" | custom-call | tf_op jit(solution)/shard_map/finish/pallas_call | solution.py:442
  (1 shorter events, 0.0 us)
Async XLA Ops:
  0.7 9.1 %copy-start = (f32[4,16,768]{2,1,0:T(8,128)S(1)}, f32[4,16,768]{2,1,0:T(8,128)}, u32[]{:S(2)}) copy-start(f32[4,16,768]{2,1,0:T(8,128)} %slip_ref.1) | copy-start | bytes 589828
  2.4 7.4 %copy-start.2 = (s32[3,1024]{1,0:T(4,128)S(1)}, s32[3,1024]{1,0:T(4,128)}, u32[]{:S(2)}) copy-start(s32[3,1024]{1,0:T(4,128)} %triangles_ref.1) | copy-start | bytes 36868
  2.4 7.4 %copy-start.3 = (f32[3,561]{1,0:T(4,128)S(1)}, f32[3,561]{1,0:T(4,128)}, u32[]{:S(2)}) copy-start(f32[3,561]{1,0:T(4,128)} %vertices_ref.1) | copy-start | bytes 20200
  2.4 7.4 %copy-start.4 = (s32[4,256]{1,0:T(4,128)S(1)}, s32[4,256]{1,0:T(4,128)}, u32[]{:S(2)}) copy-start(s32[4,256]{1,0:T(4,128)} %map_ref.1) | copy-start | bytes 12292
  2.4 14.6 %all-to-all-start = ((bf16[32,8,128]{2,1,0:T(8,128)(2,1)}), bf16[32,8,128]{2,1,0:T(8,128)(2,1)S(1)}, u32[]{:S(2)}, u32[]{:S(2)}) async-start(bf16[32,8,128]{2,1,0:T(8,128)(2,1)} %coeffs.1.after_ref), calls=%async_computation | async-start | bytes 131072 | tf_op jit(solution)/shard_map/all_to_all | solution.py:362
  9.8 4.0 %copy-start.6 = (bf16[16,1024]{1,0:T(8,128)(2,1)S(1)}, bf16[16,1024]{1,0:T(8,128)(2,1)}, u32[]{:S(2)}) copy-start(bf16[16,1024]{1,0:T(8,128)(2,1)} %param.16) | copy-start | bytes 98308
  10.1 11.9 %collective-permute-start = (bf16[2,16,1024]{2,1,0:T(8,128)(2,1)S(1)}, bf16[2,16,1024]{2,1,0:T(8,128)(2,1)S(1)}, u32[]{:S(2)}, u32[]{:S(2)}) collective-permute-start(bf16[2,16,1024]{2,1,0:T(8,128)(2,1)S(1)} %get-tuple-element.16), channel_id=1, source_target_pairs={{0,1},{1,2},{2,3},{3,4},{4,5},{5,6},{6,7},{9,8},{10,9},{11,10},{12... | collective-permute-start | bytes 196616 | tf_op jit(solution)/shard_map/ppermute | solution.py:385
  17.0 0.7 %copy-start.5 = (s32[2,16]{1,0:T(2,128)S(1)}, s32[2,16]{1,0:T(2,128)}, u32[]{:S(2)}) copy-start(s32[2,16]{1,0:T(2,128)} %pairs_ref.1) | copy-start | bytes 388
  19.3 10.3 %all-to-all-start.1 = ((bf16[32,16,128]{2,1,0:T(8,128)(2,1)}), bf16[32,16,128]{2,1,0:T(8,128)(2,1)S(1)}, u32[]{:S(2)}, u32[]{:S(2)}) async-start(bf16[32,16,128]{2,1,0:T(8,128)(2,1)} %get-tuple-element.22), calls=%async_computation.1 | async-start | bytes 262144 | tf_op jit(solution)/shard_map/all_to_all | solution.py:421
  22.0 7.7 %copy-start.1 = (bf16[4,32,768]{2,1,0:T(8,128)(2,1)S(1)}, bf16[4,32,768]{2,1,0:T(8,128)(2,1)}, u32[]{:S(2)}) copy-start(bf16[4,32,768]{2,1,0:T(8,128)(2,1)} %basis_ref.1) | copy-start | bytes 589828
  25.7 1.4 %collective-permute-start.1 = (f32[2,16,768]{2,1,0:T(8,128)S(1)}, f32[2,16,768]{2,1,0:T(8,128)S(1)}, u32[]{:S(2)}, u32[]{:S(2)}) collective-permute-start(f32[2,16,768]{2,1,0:T(8,128)S(1)} %near.1.own_ref), channel_id=1, source_target_pairs={{0,8},{8,0},{16,24},{24,16},{1,9},{9,1},{17,25},{25,17},{2,10},{10... | collective-permute-start | bytes 294920 | tf_op jit(solution)/shard_map/ppermute | solution.py:440

commit v13 on v12

--- a/solution.py
+++ b/solution.py
@@ -42,7 +42,7 @@
 
 
 def coeffs_kernel(
-    slip_hbm, basis_hbm, pairs_hbm, count_ref, pay_ref, slip_ref, basis_ref, pairs_ref, sems
+    slip_hbm, basis_hbm, pairs_hbm, count_ref, pay_hbm, slip_ref, basis_ref, pairs_ref, sent_ref, sems, out_sems
 ):
     clusters = slip_hbm.shape[0]
     rhs_count = slip_ref.shape[0]
@@ -73,8 +73,19 @@
     )
     counts = [jnp.broadcast_to(value, (half, rank_size)) for value in (low, high)]
     pay = jnp.concatenate([coeffs[0:half], coeffs[half:]] + counts, axis=1).astype(jnp.bfloat16)
-    for target in range(pay_ref.shape[0]):
-        pay_ref[target] = pay
+    for target in range(sent_ref.shape[0]):
+        sent_ref[target] = pay
+    parts = pay_hbm.shape[0] // sent_ref.shape[0]
+    sends = [
+        pltpu.make_async_copy(
+            sent_ref, pay_hbm.at[pl.ds(part * sent_ref.shape[0], sent_ref.shape[0])], out_sems.at[part]
+        )
+        for part in range(parts)
+    ]
+    for send in sends:
+        send.start()
+    for send in sends:
+        send.wait()
 
 
 def geometry_kernel(
@@ -258,7 +269,8 @@
     apply(slots - 1, [NEARC - 1], odd_ref)
 
 
-def coupling_kernel(coupling_ref, after_ref, to_second_ref, to_first_ref):
+def coupling_kernel(coupling_ref, pairs_ref, after_ref, to_second_ref, to_first_ref, list_ref):
+    list_ref[...] = pairs_ref[...]
     pair_count, rank_size, _ = coupling_ref.shape
     groups = LANES // rank_size
     for pair_id in range(pair_count):
@@ -269,7 +281,7 @@
 
 
 def far_kernel(
-    pairs_ref, coeff_ref, to_second_ref, to_first_ref, out_ref, done_ref, *total_refs, clusters
+    pairs_ref, coeff_ref, to_second_ref, to_first_ref, out_hbm, done_ref, sent_ref, sems, *total_refs, clusters
 ):
     done_ref[...] = jnp.zeros(done_ref.shape, jnp.float32)
     long_count, rhs_count, _ = total_refs[0].shape
@@ -309,24 +321,39 @@
     total = total_refs[0][...]
     for total_ref in total_refs[1:]:
         total = total + total_ref[...]
-    sent = total.astype(jnp.bfloat16)
-    for copy_id in range(out_ref.shape[0] // long_count):
-        out_ref[copy_id * long_count : (copy_id + 1) * long_count] = sent
-
-
-def finish_kernel(own_ref, other_ref, far_ref, basis_ref, out_ref):
+    sent_ref[...] = total.astype(jnp.bfloat16)
+    copies = [
+        pltpu.make_async_copy(
+            sent_ref, out_hbm.at[pl.ds(copy_id * long_count, long_count)], sems.at[copy_id]
+        )
+        for copy_id in range(out_hbm.shape[0] // long_count)
+    ]
+    for copy in copies:
+        copy.start()
+    for copy in copies:
+        copy.wait()
+
+
+def finish_kernel(own_ref, other_ref, far_ref, basis_ref, out_hbm, sent_ref, sems):
     clusters, rank_size, unknowns = basis_ref.shape
     total = jnp.sum(far_ref[...].astype(jnp.float32), axis=0)
     group_id = lax.broadcasted_iota(jnp.int32, total.shape, 1) // rank_size
     flat_basis = basis_ref[...].reshape(clusters * rank_size, unknowns)
     even = lax.axis_index("row") % 2 == 0
+    copies = []
     for cluster in range(clusters):
         u = cluster % NEARC
         here = even if cluster < NEARC else jnp.logical_not(even)
         near = jnp.where(here, own_ref[u], other_ref[u])
         picked = jnp.where(group_id == cluster, total, 0.0).astype(jnp.bfloat16)
         result = jnp.dot(picked, flat_basis, preferred_element_type=jnp.float32)
-        out_ref[cluster] = result + near
+        sent_ref[cluster] = result + near
+        copies.append(
+            pltpu.make_async_copy(sent_ref.at[cluster], out_hbm.at[cluster], sems.at[cluster])
+        )
+        copies[-1].start()
+    for copy in copies:
+        copy.wait()
 
 
 def shards(slip, vertices, triangles, elem_map, near_pairs, near_count, far_pairs, far_coef, basis):
@@ -343,12 +370,14 @@
         coeffs_kernel,
         out_shape=jax.ShapeDtypeStruct((devices, rhs_count // 2, LANES), jnp.bfloat16),
         in_specs=[HBM] * 3 + [SMEM],
-        out_specs=VMEM,
+        out_specs=HBM,
         scratch_shapes=[
             pltpu.VMEM(slip.shape[1:], slip.dtype),
             pltpu.VMEM(basis.shape[1:], basis.dtype),
             pltpu.VMEM(near_pairs.shape, near_pairs.dtype),
+            pltpu.VMEM((long_count, rhs_count // 2, LANES), jnp.bfloat16),
             pltpu.SemaphoreType.DMA((3,)),
+            pltpu.SemaphoreType.DMA((row_count,)),
         ],
         compiler_params=pltpu.CompilerParams(vmem_limit_bytes=16 << 20),
         name="coeffs",
@@ -397,15 +426,16 @@
         name="window",
     )(xs, geometry, halo)
 
-    couplings = pl.pallas_call(
+    to_second, to_first, pair_list = pl.pallas_call(
         coupling_kernel,
-        out_shape=[jax.ShapeDtypeStruct((coupling.shape[0] * rank_size, LANES), jnp.bfloat16)] * 2,
-        in_specs=[VMEM, ANY],
-        out_specs=[VMEM] * 2,
+        out_shape=[jax.ShapeDtypeStruct((coupling.shape[0] * rank_size, LANES), jnp.bfloat16)] * 2
+        + [jax.ShapeDtypeStruct(far_pairs.shape, far_pairs.dtype)],
+        in_specs=[VMEM, VMEM, ANY],
+        out_specs=[VMEM] * 3,
         compiler_params=pltpu.CompilerParams(vmem_limit_bytes=16 << 20),
         cost_estimate=pl.CostEstimate(flops=1000, bytes_accessed=1000, transcendentals=0),
         name="coupling",
-    )(coupling, pay)
+    )(coupling, far_pairs, pay)
     far, far_done = pl.pallas_call(
         functools.partial(far_kernel, clusters=clusters),
         out_shape=[
@@ -413,11 +443,15 @@
             jax.ShapeDtypeStruct((8, LANES), jnp.float32),
         ],
         in_specs=[SMEM, VMEM, VMEM, VMEM],
-        out_specs=[VMEM] * 2,
-        scratch_shapes=[pltpu.VMEM((long_count, rhs_count, clusters * rank_size), jnp.float32)] * 4,
+        out_specs=[HBM, VMEM],
+        scratch_shapes=[
+            pltpu.VMEM((long_count, rhs_count, clusters * rank_size), jnp.bfloat16),
+            pltpu.SemaphoreType.DMA((row_count,)),
+        ]
+        + [pltpu.VMEM((long_count, rhs_count, clusters * rank_size), jnp.float32)] * 4,
         compiler_params=pltpu.CompilerParams(vmem_limit_bytes=16 << 20),
         name="far",
-    )(far_pairs, everyone, *couplings)
+    )(pair_list, everyone, to_second, to_first)
     far_terms = lax.all_to_all(far, ("row", "long"), 0, 0, tiled=True)
 
     near = pl.pallas_call(
@@ -443,7 +477,11 @@
         finish_kernel,
         out_shape=jax.ShapeDtypeStruct(slip.shape, jnp.float32),
         in_specs=[VMEM] * 4,
-        out_specs=VMEM,
+        out_specs=HBM,
+        scratch_shapes=[
+            pltpu.VMEM(slip.shape, jnp.float32),
+            pltpu.SemaphoreType.DMA((clusters,)),
+        ],
         compiler_params=pltpu.CompilerParams(vmem_limit_bytes=16 << 20),
         name="finish",
     )(near, other, far_terms, basis)

time: 30.9 us -> 30.3 us (0.981)
  local copies, waits for them, and re-layouts: 0.86 us -> 0.19 us
    unnamed x14, local copies, waits for them, and re-layouts: 0.71 us -> 0.04 us
where the time goes in v13:
time: 30.3 us; the launch traced here: 30 us
  starting transfers between devices  13.7 us (45%)
  Pallas kernels  8.65 us (29%)
  waiting for transfers between devices  6.55 us (22%)
  between operations  0.84 us (3%)
    all_to_all x1, starting transfers between devices, shards(): everyone = lax.all_to_all(pay, ('row', 'long'), 0, 0, tiled=True)  7.3 us
    ppermute x1, starting transfers between devices, shards(): halo = lax.ppermute(to_neighbour, ('row', 'long'), route)  3.68 us
    pallas_call x1, Pallas kernels, shards(): pl.pallas_call(functools.partial(near_kernel, long_count=long_count, clus...  3.66 us
    all_to_all x1, waiting for transfers between devices, shards(): everyone = lax.all_to_all(pay, ('row', 'long'), 0, 0, tiled=True)  2.71 us
    all_to_all x1, waiting for transfers between devices, shards(): far_terms = lax.all_to_all(far, ('row', 'long'), 0, 0, tiled=True)  2.65 us
    all_to_all x1, starting transfers between devices, shards(): far_terms = lax.all_to_all(far, ('row', 'long'), 0, 0, tiled=True)  2.59 us
    pallas_call x1, Pallas kernels, shards(): pl.pallas_call(coeffs_kernel, out_shape=jax.ShapeDtypeStruct((devices, rh...  1.76 us
    pallas_call x1, Pallas kernels, shards(): pl.pallas_call(functools.partial(far_kernel, clusters=clusters), out_shap...  1.66 us
  transfers between devices with their start and end apart: 4, of which 3 were waited for; matrix products, arithmetic and copies ran while one was open for 0% of the time, Pallas kernels for 20%

profile of v13, /device:TPU:0, one launch (start us, length us, event | category | flops | bytes accessed | tf_op | source)
XLA Modules:
  0.0 30.0 jit_solution(1364598610794111380)
XLA Ops:
  0.7 0.0 copy-start
  0.7 1.8 %coeffs.1.after_ref = bf16[32,8,128]{2,1,0:T(8,128)(2,1)} custom-call(f32[4,16,768]{2,1,0:T(8,128)} %slip_ref.1, bf16[4,32,768]{2,1,0:T(8,128)(2,1)} %basis_ref.1, s32[2,20]{1,0:T(2,128)} %pairs_hbm.1, s32[1]{0:T(128)S(6)} %copy.10.count_ref), custom_call_target="tpu_custom_call" | custom-call | tf_op jit(solution)/shard_map/coeffs/pallas_call | solution.py:369
  2.4 0.0 copy-start.2
  2.4 0.0 copy-start.3
  2.5 0.0 copy-start.4
  2.5 7.3 %all-to-all-start = ((bf16[32,8,128]{2,1,0:T(8,128)(2,1)}), bf16[32,8,128]{2,1,0:T(8,128)(2,1)S(1)}, u32[]{:S(2)}, u32[]{:S(2)}) async-start(bf16[32,8,128]{2,1,0:T(8,128)(2,1)} %coeffs.1.after_ref), calls=%async_computation | async-start | bytes 131072 | tf_op jit(solution)/shard_map/all_to_all | solution.py:391
  9.8 0.0 copy-done
  9.8 0.0 copy-done.2
  9.8 0.0 copy-done.3
  9.8 0.0 copy-done.4
  9.8 0.0 copy-start.6
  9.8 0.3 geometry.1
  10.1 0.0 copy-start.5
  10.1 3.7 %collective-permute-start = (bf16[2,16,1024]{2,1,0:T(8,128)(2,1)S(1)}, bf16[2,16,1024]{2,1,0:T(8,128)(2,1)S(1)}, u32[]{:S(2)}, u32[]{:S(2)}) collective-permute-start(bf16[2,16,1024]{2,1,0:T(8,128)(2,1)S(1)} %get-tuple-element.17), channel_id=1, source_target_pairs={{0,1},{1,2},{2,3},{3,4},{4,5},{5,6},{6,7},{9,8},{10,9},{11,10},{12... | collective-permute-start | bytes 196616 | tf_op jit(solution)/shard_map/ppermute | solution.py:414
  13.8 0.0 copy-done.6
  13.8 0.1 reshape.3.coupling_ref
  14.0 0.0 copy-done.5
  14.0 0.4 %coupling.1 = (bf16[512,128]{1,0:T(8,128)(2,1)S(1)}, bf16[512,128]{1,0:T(8,128)(2,1)S(1)}, s32[2,16]{1,0:T(2,128)S(1)}) custom-call(bf16[16,32,32]{2,1,0:T(8,128)(2,1)S(1)} %reshape.3.coupling_ref, s32[2,16]{1,0:T(2,128)S(1)} %copy-done.5, bf16[32,8,128]{2,1,0:T(8,128)(2,1)} %coeffs.1.after_ref), custom_call_target="tpu_custom_call" | custom-call | flops 1000 | bytes 1000 | tf_op jit(solution)/shard_map/coupling/pallas_call | solution.py:429
  14.3 2.7 %all-to-all-done.coeff_ref.pay_ref = bf16[32,8,128]{2,1,0:T(8,128)(2,1)S(1)} async-done(((bf16[32,8,128]{2,1,0:T(8,128)(2,1)}), bf16[32,8,128]{2,1,0:T(8,128)(2,1)S(1)}, u32[]{:S(2)}, u32[]{:S(2)}) %all-to-all-start) | async-done | bytes 65568 | tf_op jit(solution)/shard_map/all_to_all | solution.py:391
  17.1 1.7 %far.1 = (bf16[32,16,128]{2,1,0:T(8,128)(2,1)}, f32[8,128]{1,0:T(8,128)S(1)}) custom-call(s32[2,16]{1,0:T(2,128)S(1)} %get-tuple-element.20.pairs_ref, bf16[32,8,128]{2,1,0:T(8,128)(2,1)S(1)} %all-to-all-done.coeff_ref.pay_ref, bf16[512,128]{1,0:T(8,128)(2,1)S(1)} %get-tuple-element.21.to_second_ref, bf16[512,128]{1,0:T(8,128)(2,1)S(1)} %get-tuple-element.22.to_first_ref), custom_call_target="tpu_custom_call" | custom-call | tf_op jit(solution)/shard_map/far/pallas_call | solution.py:439
  18.7 2.6 %all-to-all-start.1 = ((bf16[32,16,128]{2,1,0:T(8,128)(2,1)}), bf16[32,16,128]{2,1,0:T(8,128)(2,1)S(1)}, u32[]{:S(2)}, u32[]{:S(2)}) async-start(bf16[32,16,128]{2,1,0:T(8,128)(2,1)} %get-tuple-element.24), calls=%async_computation.1 | async-start | bytes 262144 | tf_op jit(solution)/shard_map/all_to_all | solution.py:455
  21.3 0.0 collective-permute-done.halo_ref
  21.4 0.0 copy-start.1
  21.4 3.7 %near.1.own_ref = f32[2,16,768]{2,1,0:T(8,128)S(1)} custom-call(bf16[6,16,768]{2,1,0:T(8,128)(2,1)S(1)} %get-tuple-element.18.slip_ref, f32[6,4,256]{2,1,0:T(4,128)S(1)} %get-tuple-element.19.place_ref, bf16[32,8,128]{2,1,0:T(8,128)(2,1)S(1)} %all-to-all-done.coeff_ref.pay_ref, f32[8,128]{1,0:T(8,128)S(1)} %get-tuple-element.23.after_ref), custom_call_target="tpu_custom_call" | custom-call | flops 1000000000 | bytes 1000000 | tf_op jit(solution)/shard_map/near/pallas_call | solution.py:457
  25.1 0.2 collective-permute-start.1
  25.2 1.2 %collective-permute-done.1.other_ref = f32[2,16,768]{2,1,0:T(8,128)S(1)} collective-permute-done((f32[2,16,768]{2,1,0:T(8,128)S(1)}, f32[2,16,768]{2,1,0:T(8,128)S(1)}, u32[]{:S(2)}, u32[]{:S(2)}) %collective-permute-start.1) | collective-permute-done | bytes 98336 | tf_op jit(solution)/shard_map/ppermute | solution.py:474
  26.4 2.7 %all-to-all-done.1.far_ref = bf16[32,16,128]{2,1,0:T(8,128)(2,1)S(1)} async-done(((bf16[32,16,128]{2,1,0:T(8,128)(2,1)}), bf16[32,16,128]{2,1,0:T(8,128)(2,1)S(1)}, u32[]{:S(2)}, u32[]{:S(2)}) %all-to-all-start.1) | async-done | bytes 131104 | tf_op jit(solution)/shard_map/all_to_all | solution.py:455
  29.1 0.0 copy-done.1
  29.1 0.9 %finish.1 = f32[4,16,768]{2,1,0:T(8,128)} custom-call(f32[2,16,768]{2,1,0:T(8,128)S(1)} %near.1.own_ref, f32[2,16,768]{2,1,0:T(8,128)S(1)} %collective-permute-done.1.other_ref, bf16[32,16,128]{2,1,0:T(8,128)(2,1)S(1)} %all-to-all-done.1.far_ref, bf16[4,32,768]{2,1,0:T(8,128)(2,1)S(1)} %copy-done.1), custom_call_target="tpu_custom_call" | custom-call | tf_op jit(solution)/shard_map/finish/pallas_call | solution.py:476
  (1 shorter events, 0.0 us)
Async XLA Ops:
  0.7 9.1 %copy-start = (f32[4,16,768]{2,1,0:T(8,128)S(1)}, f32[4,16,768]{2,1,0:T(8,128)}, u32[]{:S(2)}) copy-start(f32[4,16,768]{2,1,0:T(8,128)} %slip_ref.1) | copy-start | bytes 589828
  2.4 7.4 %copy-start.2 = (s32[3,1024]{1,0:T(4,128)S(1)}, s32[3,1024]{1,0:T(4,128)}, u32[]{:S(2)}) copy-start(s32[3,1024]{1,0:T(4,128)} %triangles_ref.1) | copy-start | bytes 36868
  2.4 7.4 %copy-start.3 = (f32[3,561]{1,0:T(4,128)S(1)}, f32[3,561]{1,0:T(4,128)}, u32[]{:S(2)}) copy-start(f32[3,561]{1,0:T(4,128)} %vertices_ref.1) | copy-start | bytes 20200
  2.5 7.4 %copy-start.4 = (s32[4,256]{1,0:T(4,128)S(1)}, s32[4,256]{1,0:T(4,128)}, u32[]{:S(2)}) copy-start(s32[4,256]{1,0:T(4,128)} %map_ref.1) | copy-start | bytes 12292
  2.5 14.6 %all-to-all-start = ((bf16[32,8,128]{2,1,0:T(8,128)(2,1)}), bf16[32,8,128]{2,1,0:T(8,128)(2,1)S(1)}, u32[]{:S(2)}, u32[]{:S(2)}) async-start(bf16[32,8,128]{2,1,0:T(8,128)(2,1)} %coeffs.1.after_ref), calls=%async_computation | async-start | bytes 131072 | tf_op jit(solution)/shard_map/all_to_all | solution.py:391
  9.8 4.0 %copy-start.6 = (bf16[16,1024]{1,0:T(8,128)(2,1)S(1)}, bf16[16,1024]{1,0:T(8,128)(2,1)}, u32[]{:S(2)}) copy-start(bf16[16,1024]{1,0:T(8,128)(2,1)} %param.16) | copy-start | bytes 98308
  10.1 3.9 %copy-start.5 = (s32[2,16]{1,0:T(2,128)S(1)}, s32[2,16]{1,0:T(2,128)}, u32[]{:S(2)}) copy-start(s32[2,16]{1,0:T(2,128)} %pairs_ref.1) | copy-start | bytes 388
  10.1 11.2 %collective-permute-start = (bf16[2,16,1024]{2,1,0:T(8,128)(2,1)S(1)}, bf16[2,16,1024]{2,1,0:T(8,128)(2,1)S(1)}, u32[]{:S(2)}, u32[]{:S(2)}) collective-permute-start(bf16[2,16,1024]{2,1,0:T(8,128)(2,1)S(1)} %get-tuple-element.17), channel_id=1, source_target_pairs={{0,1},{1,2},{2,3},{3,4},{4,5},{5,6},{6,7},{9,8},{10,9},{11,10},{12... | collective-permute-start | bytes 196616 | tf_op jit(solution)/shard_map/ppermute | solution.py:414
  18.7 10.3 %all-to-all-start.1 = ((bf16[32,16,128]{2,1,0:T(8,128)(2,1)}), bf16[32,16,128]{2,1,0:T(8,128)(2,1)S(1)}, u32[]{:S(2)}, u32[]{:S(2)}) async-start(bf16[32,16,128]{2,1,0:T(8,128)(2,1)} %get-tuple-element.24), calls=%async_computation.1 | async-start | bytes 262144 | tf_op jit(solution)/shard_map/all_to_all | solution.py:455
  21.4 7.7 %copy-start.1 = (bf16[4,32,768]{2,1,0:T(8,128)(2,1)S(1)}, bf16[4,32,768]{2,1,0:T(8,128)(2,1)}, u32[]{:S(2)}) copy-start(bf16[4,32,768]{2,1,0:T(8,128)(2,1)} %basis_ref.1) | copy-start | bytes 589828
  25.1 1.4 %collective-permute-start.1 = (f32[2,16,768]{2,1,0:T(8,128)S(1)}, f32[2,16,768]{2,1,0:T(8,128)S(1)}, u32[]{:S(2)}, u32[]{:S(2)}) collective-permute-start(f32[2,16,768]{2,1,0:T(8,128)S(1)} %near.1.own_ref), channel_id=1, source_target_pairs={{0,8},{8,0},{16,24},{24,16},{1,9},{9,1},{17,25},{25,17},{2,10},{10... | collective-permute-start | bytes 294920 | tf_op jit(solution)/shard_map/ppermute | solution.py:474

commit v14 on v13

--- a/solution.py
+++ b/solution.py
@@ -17,6 +17,25 @@
 SMEM = pl.BlockSpec(memory_space=pltpu.SMEM)
 HBM = pl.BlockSpec(memory_space=pltpu.HBM)
 ANY = pl.BlockSpec(memory_space=pl.ANY)
+SMALL = pl.CostEstimate(flops=1000, bytes_accessed=1000, transcendentals=0)
+
+
+def first_place(row_count, long_count):
+    return row_count // 2 * long_count // 2 + long_count // 2 - 1
+
+
+def same_core(row_count, long_count):
+    total = row_count // 2 * long_count
+    order = [(place + first_place(row_count, long_count)) % total for place in range(total)]
+    return [
+        [(2 * (at // long_count) + core) * long_count + at % long_count for at in order]
+        for core in range(2)
+    ]
+
+
+def place_in_core(row, owner, row_count, long_count):
+    total = row_count // 2 * long_count
+    return (row * long_count + owner + total - first_place(row_count, long_count)) % total
 
 
 def lane_gather(table, index):
@@ -45,34 +64,35 @@
     slip_hbm, basis_hbm, pairs_hbm, count_ref, pay_hbm, slip_ref, basis_ref, pairs_ref, sent_ref, sems, out_sems
 ):
     clusters = slip_hbm.shape[0]
-    rhs_count = slip_ref.shape[0]
-    rank_size = basis_ref.shape[0]
-    mine = lax.axis_index("row") % clusters
+    share, rhs_count, _ = slip_ref.shape
+    rank_size = basis_ref.shape[1]
+    begin = (lax.axis_index("row") // 2) % (clusters // share) * share
     copies = [
-        pltpu.make_async_copy(slip_hbm.at[mine], slip_ref, sems.at[0]),
-        pltpu.make_async_copy(basis_hbm.at[mine], basis_ref, sems.at[1]),
+        pltpu.make_async_copy(slip_hbm.at[pl.ds(begin, share)], slip_ref, sems.at[0]),
+        pltpu.make_async_copy(basis_hbm.at[pl.ds(begin, share)], basis_ref, sems.at[1]),
         pltpu.make_async_copy(pairs_hbm, pairs_ref, sems.at[2]),
     ]
     for copy in copies:
         copy.start()
-    half = rhs_count // 2
     copies[2].wait()
     first = pairs_ref[0:1, :]
     kind = (first - lax.axis_index("long") * clusters) * (NEARC + 1) + pairs_ref[1:2, :] - first
-    kinds = lax.broadcasted_iota(jnp.int32, (half, kind.shape[1]), 0)
+    kinds = lax.broadcasted_iota(jnp.int32, (rhs_count, kind.shape[1]), 0)
     live = lax.broadcasted_iota(jnp.int32, kinds.shape, 1) < count_ref[0]
-    low = jnp.sum(jnp.where(live & (kinds == kind), 1.0, 0.0), axis=1, keepdims=True)
-    high = jnp.sum(jnp.where(live & (kinds + half == kind), 1.0, 0.0), axis=1, keepdims=True)
+    counts = jnp.sum(jnp.where(live & (kinds == kind), 1.0, 0.0), axis=1, keepdims=True)
     copies[0].wait()
     copies[1].wait()
-    coeffs = lax.dot_general(
-        slip_ref[...].astype(jnp.bfloat16),
-        basis_ref[...],
-        (((1,), (1,)), ((), ())),
-        preferred_element_type=jnp.float32,
-    )
-    counts = [jnp.broadcast_to(value, (half, rank_size)) for value in (low, high)]
-    pay = jnp.concatenate([coeffs[0:half], coeffs[half:]] + counts, axis=1).astype(jnp.bfloat16)
+    coeffs = [
+        lax.dot_general(
+            slip_ref[turn].astype(jnp.bfloat16),
+            basis_ref[turn],
+            (((1,), (1,)), ((), ())),
+            preferred_element_type=jnp.float32,
+        )
+        for turn in range(share)
+    ]
+    counts = jnp.broadcast_to(counts, (rhs_count, LANES - share * rank_size))
+    pay = jnp.concatenate(coeffs + [counts], axis=1).astype(jnp.bfloat16)
     for target in range(sent_ref.shape[0]):
         sent_ref[target] = pay
     parts = pay_hbm.shape[0] // sent_ref.shape[0]
@@ -172,25 +192,27 @@
         )
 
 
+def totals_kernel(pay_ref, after_ref, out_ref, *, long_count):
+    row_count = 2 * pay_ref.shape[0] // long_count
+    long_index = lax.axis_index("long")
+    totals = [jnp.zeros(pay_ref.shape[1:], jnp.float32) for _ in range(2)]
+    for row in range(row_count // 2):
+        for source, owner in enumerate((long_index, jnp.maximum(long_index - 1, 0))):
+            at = place_in_core(row, owner, row_count, long_count)
+            totals[source] += pay_ref[at].astype(jnp.float32)
+    lane_id = lax.broadcasted_iota(jnp.int32, out_ref.shape, 1)
+    out_ref[...] = jnp.where(lane_id < 3 * LANES // 4, totals[0], totals[1])
+
+
 def near_kernel(
-    slip_ref, place_ref, pay_ref, after_ref, out_ref, cols_ref, even_ref, odd_ref, *, long_count, clusters
+    slip_ref, place_ref, mine_ref, theirs_ref, out_ref, cols_ref, even_ref, odd_ref, *, clusters
 ):
     slots, rhs_count, unknowns = slip_ref.shape
     size = place_ref.shape[2]
-    long_index = lax.axis_index("long")
-    before = jnp.maximum(long_index - 1, 0)
-    totals = [jnp.zeros(pay_ref.shape[1:], jnp.float32) for _ in range(2)]
-    for row in range(pay_ref.shape[0] // long_count):
-        for source, owner in enumerate((long_index, before)):
-            totals[source] += pay_ref[row * long_count + owner].astype(jnp.float32)
+    totals = mine_ref[...] + theirs_ref[...]
     even = lax.axis_index("row") % 2 == 0
-    half = pay_ref.shape[1]
-    rank_size = pay_ref.shape[2] // 4
-    group = lax.broadcasted_iota(jnp.int32, (half, LANES), 1) // rank_size
-    kinds = lax.broadcasted_iota(jnp.int32, (half, LANES), 0) + jnp.where(group == 3, half, 0)
-    kinds = jnp.where(group < 2, -1, kinds)
-    lane_id = lax.broadcasted_iota(jnp.int32, (half, LANES), 1)
-    kinds = jnp.where(lane_id % rank_size == 0, kinds, -1)
+    kinds = lax.broadcasted_iota(jnp.int32, totals.shape, 0)
+    lane_id = lax.broadcasted_iota(jnp.int32, totals.shape, 1)
 
     def count_of(place, u):
         both = []
@@ -199,8 +221,8 @@
             lower = cluster + jnp.minimum(reach, 0)
             inside = lower >= 0
             kind = jnp.where(inside, lower, lower + clusters) * (NEARC + 1) + jnp.abs(reach)
-            source = jnp.where(inside, totals[0], totals[1])
-            both.append(jnp.where(kinds == kind, source, 0.0))
+            lane = jnp.where(inside, LANES // 2, 3 * LANES // 4)
+            both.append(jnp.where((kinds == kind) & (lane_id == lane), totals, 0.0))
         picked = jnp.sum(jnp.where(even, both[0], both[1]), axis=0, keepdims=True)
         return jnp.sum(picked, axis=1, keepdims=True)
 
@@ -285,6 +307,7 @@
 ):
     done_ref[...] = jnp.zeros(done_ref.shape, jnp.float32)
     long_count, rhs_count, _ = total_refs[0].shape
+    row_count = out_hbm.shape[0] // long_count
     pair_count = pairs_ref.shape[1]
     rank_size = LANES // clusters
     group_id = lax.broadcasted_iota(jnp.int32, (rhs_count, LANES), 1) // rank_size
@@ -292,11 +315,10 @@
         total_ref[...] = jnp.zeros(total_ref.shape, jnp.float32)
 
     def coeff_of(cluster, group):
-        whole = coeff_ref[(cluster % clusters) * long_count + cluster // clusters]
-        whole = whole.astype(jnp.float32)
-        low = pltpu.roll(whole, rank_size * group, 1) if group else whole
-        high = pltpu.roll(whole, (rank_size * (group - 1)) % LANES, 1) if group != 1 else whole
-        both = jnp.concatenate([low, high], axis=0)
+        share = clusters // 2
+        at = place_in_core(cluster % clusters // share, cluster // clusters, row_count, long_count)
+        whole = coeff_ref[at].astype(jnp.float32)
+        both = pltpu.roll(whole, (LANES + rank_size * (group - cluster % share)) % LANES, 1)
         return jnp.where(group_id == group, both, 0.0)
 
     results = []
@@ -363,21 +385,22 @@
     row_count = lax.axis_size("row")
     long_count = lax.axis_size("long")
     devices = row_count * long_count
+    share = clusters // 2
     coupling = far_coef.reshape(-1, rank_size, rank_size)
     slots = clusters + NEARC
 
     pay = pl.pallas_call(
         coeffs_kernel,
-        out_shape=jax.ShapeDtypeStruct((devices, rhs_count // 2, LANES), jnp.bfloat16),
+        out_shape=jax.ShapeDtypeStruct((devices // 2, rhs_count, LANES), jnp.bfloat16),
         in_specs=[HBM] * 3 + [SMEM],
         out_specs=HBM,
         scratch_shapes=[
-            pltpu.VMEM(slip.shape[1:], slip.dtype),
-            pltpu.VMEM(basis.shape[1:], basis.dtype),
+            pltpu.VMEM((share,) + slip.shape[1:], slip.dtype),
+            pltpu.VMEM((share,) + basis.shape[1:], basis.dtype),
             pltpu.VMEM(near_pairs.shape, near_pairs.dtype),
-            pltpu.VMEM((long_count, rhs_count // 2, LANES), jnp.bfloat16),
+            pltpu.VMEM((long_count, rhs_count, LANES), jnp.bfloat16),
             pltpu.SemaphoreType.DMA((3,)),
-            pltpu.SemaphoreType.DMA((row_count,)),
+            pltpu.SemaphoreType.DMA((row_count // 2,)),
         ],
         compiler_params=pltpu.CompilerParams(vmem_limit_bytes=16 << 20),
         name="coeffs",
@@ -388,7 +411,9 @@
         ],
         near_count,
     )
-    everyone = lax.all_to_all(pay, ("row", "long"), 0, 0, tiled=True)
+    everyone = lax.all_to_all(
+        pay, ("row", "long"), 0, 0, axis_index_groups=same_core(row_count, long_count), tiled=True
+    )
 
     xs, to_neighbour, geometry = pl.pallas_call(
         geometry_kernel,
@@ -454,10 +479,22 @@
     )(pair_list, everyone, to_second, to_first)
     far_terms = lax.all_to_all(far, ("row", "long"), 0, 0, tiled=True)
 
+    totals = pl.pallas_call(
+        functools.partial(totals_kernel, long_count=long_count),
+        out_shape=jax.ShapeDtypeStruct((rhs_count, LANES), jnp.float32),
+        in_specs=[VMEM, ANY],
+        out_specs=VMEM,
+        compiler_params=pltpu.CompilerParams(vmem_limit_bytes=16 << 20),
+        cost_estimate=SMALL,
+        name="totals",
+    )(everyone, far_done)
+    partner = [(row, row ^ 1) for row in range(row_count)]
+    totals_other = lax.ppermute(totals, "row", partner)
+
     near = pl.pallas_call(
-        functools.partial(near_kernel, long_count=long_count, clusters=clusters),
+        functools.partial(near_kernel, clusters=clusters),
         out_shape=jax.ShapeDtypeStruct((NEARC, rhs_count, unknowns), jnp.float32),
-        in_specs=[VMEM] * 3 + [ANY],
+        in_specs=[VMEM] * 4,
         out_specs=VMEM,
         scratch_shapes=[
             pltpu.VMEM((slots, size, 8), jnp.float32),
@@ -465,12 +502,9 @@
             pltpu.VMEM((NEARC, 6, size, size), jnp.bfloat16),
         ],
         compiler_params=pltpu.CompilerParams(vmem_limit_bytes=24 << 20),
-        cost_estimate=pl.CostEstimate(
-            flops=1_000_000_000, bytes_accessed=1_000_000, transcendentals=660_000
-        ),
+        cost_estimate=SMALL,
         name="near",
-    )(window, places, everyone, far_done)
-    partner = [(row, row ^ 1) for row in range(row_count)]
+    )(window, places, totals, totals_other)
     other = lax.ppermute(near, "row", partner)
 
     return pl.pallas_call(

time: 30.3 us -> 34.7 us (1.15)
  starting transfers between devices: 13.7 us -> 16.2 us
  waiting for transfers between devices: 6.55 us -> 7.51 us
  local copies, waits for them, and re-layouts: 0.19 us -> 0.7 us
  Pallas kernels: 8.65 us -> 9.12 us
    all_to_all x1, waiting for transfers between devices: 2.65 us -> 0.01 us  [shards(): far_terms = lax.all_to_all(far, ('row', 'long'), 0, 0, tiled=True)]
    ppermute x1, waiting for transfers between devices: 0.01 us -> 2.65 us  [shards(): halo = lax.ppermute(to_neighbour, ('row', 'long'), route)]
    all_to_all x1, starting transfers between devices: 7.3 us -> 8.8 us  [shards(): lax.all_to_all(pay, ('row', 'long'), 0, 0, axis_index_groups=same_core(ro...]
    all_to_all x1, starting transfers between devices: 2.59 us -> 3.59 us  [shards(): far_terms = lax.all_to_all(far, ('row', 'long'), 0, 0, tiled=True)]
    all_to_all x1, waiting for transfers between devices: 2.71 us -> 3.56 us  [shards(): lax.all_to_all(pay, ('row', 'long'), 0, 0, axis_index_groups=same_core(ro...]
    unnamed x14, local copies, waits for them, and re-layouts: 0.04 us -> 0.55 us
    pallas_call x1, Pallas kernels: 1.66 us -> 2.01 us  [shards(): pl.pallas_call(functools.partial(far_kernel, clusters=clusters), out_shap...]
    pallas_call x2 -> x3, Pallas kernels: 5.42 us -> 5.56 us  [the longest x1 3.68 us: shards(): pl.pallas_call(functools.partial(near_kernel, clusters=clusters), out_sha...]
  transfers between devices with their start and end apart: 4 -> 5, of which waited for: 3 -> 3; matrix products, arithmetic and copies ran while one was open for 0% -> 0% of each run, Pallas kernels for 20% -> 13%
where the time goes in v14:
time: 34.7 us; the launch traced here: 34.4 us
  starting transfers between devices  16.2 us (47%)
  Pallas kernels  9.12 us (26%)
  waiting for transfers between devices  7.51 us (22%)
  between operations  0.83 us (2%)
  local copies, waits for them, and re-layouts  0.7 us (2%)
    all_to_all x1, starting transfers between devices, shards(): lax.all_to_all(pay, ('row', 'long'), 0, 0, axis_index_groups=same_core(ro...  8.8 us
    pallas_call x1, Pallas kernels, shards(): pl.pallas_call(functools.partial(near_kernel, clusters=clusters), out_sha...  3.68 us
    ppermute x1, starting transfers between devices, shards(): halo = lax.ppermute(to_neighbour, ('row', 'long'), route)  3.68 us
    all_to_all x1, starting transfers between devices, shards(): far_terms = lax.all_to_all(far, ('row', 'long'), 0, 0, tiled=True)  3.59 us
    all_to_all x1, waiting for transfers between devices, shards(): lax.all_to_all(pay, ('row', 'long'), 0, 0, axis_index_groups=same_core(ro...  3.56 us
    ppermute x1, waiting for transfers between devices, shards(): halo = lax.ppermute(to_neighbour, ('row', 'long'), route)  2.65 us
    pallas_call x1, Pallas kernels, shards(): pl.pallas_call(functools.partial(far_kernel, clusters=clusters), out_shap...  2.01 us
    pallas_call x1, Pallas kernels, shards(): pl.pallas_call(coeffs_kernel, out_shape=jax.ShapeDtypeStruct((devices //...  1.85 us
  transfers between devices with their start and end apart: 5, of which 3 were waited for; matrix products, arithmetic and copies ran while one was open for 0% of the time, Pallas kernels for 13%

profile of v14, /device:TPU:0, one launch (start us, length us, event | category | flops | bytes accessed | tf_op | source)
XLA Modules:
  0.0 34.4 jit_solution(5634242348612042827)
XLA Ops:
  0.7 1.9 %coeffs.1.after_ref = bf16[16,16,128]{2,1,0:T(8,128)(2,1)} custom-call(f32[4,16,768]{2,1,0:T(8,128)} %slip_ref.1, bf16[4,32,768]{2,1,0:T(8,128)(2,1)} %basis_ref.1, s32[2,20]{1,0:T(2,128)} %pairs_hbm.1, s32[1]{0:T(128)S(6)} %copy.10.count_ref), custom_call_target="tpu_custom_call" | custom-call | tf_op jit(solution)/shard_map/coeffs/pallas_call | solution.py:392
  2.5 0.0 copy-start.6
  2.5 8.8 %all-to-all-start = ((bf16[16,16,128]{2,1,0:T(8,128)(2,1)}), bf16[16,16,128]{2,1,0:T(8,128)(2,1)S(1)}, u32[]{:S(2)}, u32[]{:S(2)}) async-start(bf16[16,16,128]{2,1,0:T(8,128)(2,1)} %coeffs.1.after_ref), calls=%async_computation | async-start | bytes 131072 | tf_op jit(solution)/shard_map/all_to_all | solution.py:414
  11.3 0.0 copy-done.6
  11.3 0.0 copy-start.5
  11.3 0.1 reshape.3.coupling_ref
  11.5 0.5 %copy-done.5 = s32[2,16]{1,0:T(2,128)S(1)} copy-done((s32[2,16]{1,0:T(2,128)S(1)}, s32[2,16]{1,0:T(2,128)}, u32[]{:S(2)}) %copy-start.5) | copy-done | bytes 152
  12.0 0.4 %coupling.1 = (bf16[512,128]{1,0:T(8,128)(2,1)S(1)}, bf16[512,128]{1,0:T(8,128)(2,1)S(1)}, s32[2,16]{1,0:T(2,128)S(1)}) custom-call(bf16[16,32,32]{2,1,0:T(8,128)(2,1)S(1)} %reshape.3.coupling_ref, s32[2,16]{1,0:T(2,128)S(1)} %copy-done.5, bf16[16,16,128]{2,1,0:T(8,128)(2,1)} %coeffs.1.after_ref), custom_call_target="tpu_custom_call" | custom-call | flops 1000 | bytes 1000 | tf_op jit(solution)/shard_map/coupling/pallas_call | solution.py:454
  12.4 3.6 %all-to-all-done.coeff_ref.pay_ref = bf16[16,16,128]{2,1,0:T(8,128)(2,1)S(1)} async-done(((bf16[16,16,128]{2,1,0:T(8,128)(2,1)}), bf16[16,16,128]{2,1,0:T(8,128)(2,1)S(1)}, u32[]{:S(2)}, u32[]{:S(2)}) %all-to-all-start) | async-done | bytes 65568 | tf_op jit(solution)/shard_map/all_to_all | solution.py:414
  15.9 2.0 %far.1 = (bf16[32,16,128]{2,1,0:T(8,128)(2,1)}, f32[8,128]{1,0:T(8,128)S(1)}) custom-call(s32[2,16]{1,0:T(2,128)S(1)} %get-tuple-element.20.pairs_ref, bf16[16,16,128]{2,1,0:T(8,128)(2,1)S(1)} %all-to-all-done.coeff_ref.pay_ref, bf16[512,128]{1,0:T(8,128)(2,1)S(1)} %get-tuple-element.21.to_second_ref, bf16[512,128]{1,0:T(8,128)(2,1)S(1)} %get-tuple-element.22.to_first_ref), custom_call_target="tpu_custom_call" | custom-call | tf_op jit(solution)/shard_map/far/pallas_call | solution.py:464
  18.0 0.0 copy-start
  18.0 0.0 copy-start.2
  18.0 0.0 copy-start.3
  18.0 0.0 copy-start.4
  18.0 3.6 %all-to-all-start.1 = ((bf16[32,16,128]{2,1,0:T(8,128)(2,1)}), bf16[32,16,128]{2,1,0:T(8,128)(2,1)S(1)}, u32[]{:S(2)}, u32[]{:S(2)}) async-start(bf16[32,16,128]{2,1,0:T(8,128)(2,1)} %get-tuple-element.24), calls=%async_computation.1 | async-start | bytes 262144 | tf_op jit(solution)/shard_map/all_to_all | solution.py:480
  21.6 0.0 copy-done
  21.6 0.0 copy-done.2
  21.6 0.0 copy-done.3
  21.6 0.0 copy-done.4
  21.6 0.3 geometry.1
  21.9 3.7 %collective-permute-start = (bf16[2,16,1024]{2,1,0:T(8,128)(2,1)S(1)}, bf16[2,16,1024]{2,1,0:T(8,128)(2,1)S(1)}, u32[]{:S(2)}, u32[]{:S(2)}) collective-permute-start(bf16[2,16,1024]{2,1,0:T(8,128)(2,1)S(1)} %get-tuple-element.17), channel_id=1, source_target_pairs={{0,1},{1,2},{2,3},{3,4},{4,5},{5,6},{6,7},{9,8},{10,9},{11,10},{12... | collective-permute-start | bytes 196616 | tf_op jit(solution)/shard_map/ppermute | solution.py:439
  25.6 0.1 collective-permute-start.1
  25.7 2.7 %collective-permute-done.halo_ref = bf16[2,16,1024]{2,1,0:T(8,128)(2,1)S(1)} collective-permute-done((bf16[2,16,1024]{2,1,0:T(8,128)(2,1)S(1)}, bf16[2,16,1024]{2,1,0:T(8,128)(2,1)S(1)}, u32[]{:S(2)}, u32[]{:S(2)}) %collective-permute-start) | collective-permute-done | bytes 65568 | tf_op jit(solution)/shard_map/ppermute | solution.py:439
  28.4 0.0 copy-start.1
  28.4 0.0 collective-permute-done.1.theirs_ref
  28.4 3.7 %near.1.own_ref = f32[2,16,768]{2,1,0:T(8,128)S(1)} custom-call(bf16[6,16,768]{2,1,0:T(8,128)(2,1)S(1)} %get-tuple-element.18.slip_ref, f32[6,4,256]{2,1,0:T(4,128)S(1)} %get-tuple-element.19.place_ref, f32[16,128]{1,0:T(8,128)S(1)} %totals.1.mine_ref, f32[16,128]{1,0:T(8,128)S(1)} %collective-permute-done.1.theirs_ref), custom_call_target="tpu_custom_call" | custom-call | flops 1000 | bytes 1000 | tf_op jit(solution)/shard_map/near/pallas_call | solution.py:494
  32.1 0.1 collective-permute-start.2
  32.2 1.3 %collective-permute-done.2.other_ref = f32[2,16,768]{2,1,0:T(8,128)S(1)} collective-permute-done((f32[2,16,768]{2,1,0:T(8,128)S(1)}, f32[2,16,768]{2,1,0:T(8,128)S(1)}, u32[]{:S(2)}, u32[]{:S(2)}) %collective-permute-start.2) | collective-permute-done | bytes 98336 | tf_op jit(solution)/shard_map/ppermute | solution.py:508
  33.5 0.0 all-to-all-done.1.far_ref
  33.5 0.0 copy-done.1
  33.5 0.9 %finish.1 = f32[4,16,768]{2,1,0:T(8,128)} custom-call(f32[2,16,768]{2,1,0:T(8,128)S(1)} %near.1.own_ref, f32[2,16,768]{2,1,0:T(8,128)S(1)} %collective-permute-done.2.other_ref, bf16[32,16,128]{2,1,0:T(8,128)(2,1)S(1)} %all-to-all-done.1.far_ref, bf16[4,32,768]{2,1,0:T(8,128)(2,1)S(1)} %copy-done.1), custom_call_target="tpu_custom_call" | custom-call | tf_op jit(solution)/shard_map/finish/pallas_call | solution.py:510
  (2 shorter events, 0.1 us)
Async XLA Ops:
  2.5 8.8 %copy-start.6 = (bf16[16,1024]{1,0:T(8,128)(2,1)S(1)}, bf16[16,1024]{1,0:T(8,128)(2,1)}, u32[]{:S(2)}) copy-start(bf16[16,1024]{1,0:T(8,128)(2,1)} %param.16) | copy-start | bytes 98308
  2.5 13.4 %all-to-all-start = ((bf16[16,16,128]{2,1,0:T(8,128)(2,1)}), bf16[16,16,128]{2,1,0:T(8,128)(2,1)S(1)}, u32[]{:S(2)}, u32[]{:S(2)}) async-start(bf16[16,16,128]{2,1,0:T(8,128)(2,1)} %coeffs.1.after_ref), calls=%async_computation | async-start | bytes 131072 | tf_op jit(solution)/shard_map/all_to_all | solution.py:414
  11.3 0.7 %copy-start.5 = (s32[2,16]{1,0:T(2,128)S(1)}, s32[2,16]{1,0:T(2,128)}, u32[]{:S(2)}) copy-start(s32[2,16]{1,0:T(2,128)} %pairs_ref.1) | copy-start | bytes 388
  18.0 3.7 %copy-start = (f32[4,16,768]{2,1,0:T(8,128)S(1)}, f32[4,16,768]{2,1,0:T(8,128)}, u32[]{:S(2)}) copy-start(f32[4,16,768]{2,1,0:T(8,128)} %slip_ref.1) | copy-start | bytes 589828
  18.0 3.6 %copy-start.2 = (s32[3,1024]{1,0:T(4,128)S(1)}, s32[3,1024]{1,0:T(4,128)}, u32[]{:S(2)}) copy-start(s32[3,1024]{1,0:T(4,128)} %triangles_ref.1) | copy-start | bytes 36868
  18.0 3.6 %copy-start.3 = (f32[3,561]{1,0:T(4,128)S(1)}, f32[3,561]{1,0:T(4,128)}, u32[]{:S(2)}) copy-start(f32[3,561]{1,0:T(4,128)} %vertices_ref.1) | copy-start | bytes 20200
  18.0 3.6 %copy-start.4 = (s32[4,256]{1,0:T(4,128)S(1)}, s32[4,256]{1,0:T(4,128)}, u32[]{:S(2)}) copy-start(s32[4,256]{1,0:T(4,128)} %map_ref.1) | copy-start | bytes 12292
  18.0 15.4 %all-to-all-start.1 = ((bf16[32,16,128]{2,1,0:T(8,128)(2,1)}), bf16[32,16,128]{2,1,0:T(8,128)(2,1)S(1)}, u32[]{:S(2)}, u32[]{:S(2)}) async-start(bf16[32,16,128]{2,1,0:T(8,128)(2,1)} %get-tuple-element.24), calls=%async_computation.1 | async-start | bytes 262144 | tf_op jit(solution)/shard_map/all_to_all | solution.py:480
  21.9 6.4 %collective-permute-start = (bf16[2,16,1024]{2,1,0:T(8,128)(2,1)S(1)}, bf16[2,16,1024]{2,1,0:T(8,128)(2,1)S(1)}, u32[]{:S(2)}, u32[]{:S(2)}) collective-permute-start(bf16[2,16,1024]{2,1,0:T(8,128)(2,1)S(1)} %get-tuple-element.17), channel_id=1, source_target_pairs={{0,1},{1,2},{2,3},{3,4},{4,5},{5,6},{6,7},{9,8},{10,9},{11,10},{12... | collective-permute-start | bytes 196616 | tf_op jit(solution)/shard_map/ppermute | solution.py:439
  25.6 2.8 %collective-permute-start.1 = (f32[16,128]{1,0:T(8,128)S(1)}, f32[16,128]{1,0:T(8,128)S(1)}, u32[]{:S(2)}, u32[]{:S(2)}) collective-permute-start(f32[16,128]{1,0:T(8,128)S(1)} %totals.1.mine_ref), channel_id=1, source_target_pairs={{0,8},{8,0},{16,24},{24,16},{1,9},{9,1},{17,25},{25,17},{2,10},{10... | collective-permute-start | bytes 24584 | tf_op jit(solution)/shard_map/ppermute | solution.py:492
  28.4 5.1 %copy-start.1 = (bf16[4,32,768]{2,1,0:T(8,128)(2,1)S(1)}, bf16[4,32,768]{2,1,0:T(8,128)(2,1)}, u32[]{:S(2)}) copy-start(bf16[4,32,768]{2,1,0:T(8,128)(2,1)} %basis_ref.1) | copy-start | bytes 589828
  32.1 1.4 %collective-permute-start.2 = (f32[2,16,768]{2,1,0:T(8,128)S(1)}, f32[2,16,768]{2,1,0:T(8,128)S(1)}, u32[]{:S(2)}, u32[]{:S(2)}) collective-permute-start(f32[2,16,768]{2,1,0:T(8,128)S(1)} %near.1.own_ref), channel_id=1, source_target_pairs={{0,8},{8,0},{16,24},{24,16},{1,9},{9,1},{17,25},{25,17},{2,10},{10... | collective-permute-start | bytes 294920 | tf_op jit(solution)/shard_map/ppermute | solution.py:508

commit v15 on v14

--- a/solution.py
+++ b/solution.py
@@ -192,7 +192,7 @@
         )
 
 
-def totals_kernel(pay_ref, after_ref, out_ref, *, long_count):
+def totals_kernel(pay_ref, out_ref, *, long_count):
     row_count = 2 * pay_ref.shape[0] // long_count
     long_index = lax.axis_index("long")
     totals = [jnp.zeros(pay_ref.shape[1:], jnp.float32) for _ in range(2)]
@@ -205,7 +205,7 @@
 
 
 def near_kernel(
-    slip_ref, place_ref, mine_ref, theirs_ref, out_ref, cols_ref, even_ref, odd_ref, *, clusters
+    slip_ref, place_ref, mine_ref, theirs_ref, after_ref, out_ref, cols_ref, even_ref, odd_ref, *, clusters
 ):
     slots, rhs_count, unknowns = slip_ref.shape
     size = place_ref.shape[2]
@@ -303,22 +303,28 @@
 
 
 def far_kernel(
-    pairs_ref, coeff_ref, to_second_ref, to_first_ref, out_hbm, done_ref, sent_ref, sems, *total_refs, clusters
+    pairs_ref, coeff_ref, to_second_ref, to_first_ref, out_hbm, done_ref, sent_ref, sems, moved_ref, *total_refs, clusters, row_count
 ):
     done_ref[...] = jnp.zeros(done_ref.shape, jnp.float32)
     long_count, rhs_count, _ = total_refs[0].shape
-    row_count = out_hbm.shape[0] // long_count
     pair_count = pairs_ref.shape[1]
     rank_size = LANES // clusters
     group_id = lax.broadcasted_iota(jnp.int32, (rhs_count, LANES), 1) // rank_size
     for total_ref in total_refs:
         total_ref[...] = jnp.zeros(total_ref.shape, jnp.float32)
 
+    share = clusters // 2
+    for at in range(coeff_ref.shape[0]):
+        whole = coeff_ref[at].astype(jnp.float32)
+        for turn in range(share):
+            moved_ref[at * share + turn] = (
+                pltpu.roll(whole, LANES - rank_size * turn, 1) if turn else whole
+            )
+
     def coeff_of(cluster, group):
-        share = clusters // 2
         at = place_in_core(cluster % clusters // share, cluster // clusters, row_count, long_count)
-        whole = coeff_ref[at].astype(jnp.float32)
-        both = pltpu.roll(whole, (LANES + rank_size * (group - cluster % share)) % LANES, 1)
+        whole = moved_ref[at * share + cluster % share]
+        both = pltpu.roll(whole, rank_size * group, 1) if group else whole
         return jnp.where(group_id == group, both, 0.0)
 
     results = []
@@ -343,25 +349,36 @@
     total = total_refs[0][...]
     for total_ref in total_refs[1:]:
         total = total + total_ref[...]
-    sent_ref[...] = total.astype(jnp.bfloat16)
-    copies = [
-        pltpu.make_async_copy(
-            sent_ref, out_hbm.at[pl.ds(copy_id * long_count, long_count)], sems.at[copy_id]
-        )
-        for copy_id in range(out_hbm.shape[0] // long_count)
-    ]
+    sent_ref[...] = total
+    copies = []
+    for row in range(row_count // 2):
+        first = place_in_core(row, 0, row_count, long_count)
+        kept = min(long_count, out_hbm.shape[0] - first)
+        pieces = [(0, first, kept)]
+        if kept < long_count:
+            pieces.append((kept, 0, long_count - kept))
+        for source, target, length in pieces:
+            copies.append(
+                pltpu.make_async_copy(
+                    sent_ref.at[pl.ds(source, length)],
+                    out_hbm.at[pl.ds(target, length)],
+                    sems.at[len(copies)],
+                )
+            )
     for copy in copies:
         copy.start()
     for copy in copies:
         copy.wait()
 
 
-def finish_kernel(own_ref, other_ref, far_ref, basis_ref, out_hbm, sent_ref, sems):
+def finish_kernel(own_ref, other_ref, far_ref, far_other_ref, basis_ref, out_hbm, sent_ref, sems):
     clusters, rank_size, unknowns = basis_ref.shape
-    total = jnp.sum(far_ref[...].astype(jnp.float32), axis=0)
+    even = lax.axis_index("row") % 2 == 0
+    mine = jnp.sum(far_ref[...], axis=0)
+    theirs = jnp.sum(far_other_ref[...], axis=0)
+    total = jnp.where(even, mine, theirs) + jnp.where(even, theirs, mine)
     group_id = lax.broadcasted_iota(jnp.int32, total.shape, 1) // rank_size
     flat_basis = basis_ref[...].reshape(clusters * rank_size, unknowns)
-    even = lax.axis_index("row") % 2 == 0
     copies = []
     for cluster in range(clusters):
         u = cluster % NEARC
@@ -462,39 +479,43 @@
         name="coupling",
     )(coupling, far_pairs, pay)
     far, far_done = pl.pallas_call(
-        functools.partial(far_kernel, clusters=clusters),
+        functools.partial(far_kernel, clusters=clusters, row_count=row_count),
         out_shape=[
-            jax.ShapeDtypeStruct((devices, rhs_count, clusters * rank_size), jnp.bfloat16),
+            jax.ShapeDtypeStruct((devices // 2, rhs_count, clusters * rank_size), jnp.float32),
             jax.ShapeDtypeStruct((8, LANES), jnp.float32),
         ],
         in_specs=[SMEM, VMEM, VMEM, VMEM],
         out_specs=[HBM, VMEM],
         scratch_shapes=[
-            pltpu.VMEM((long_count, rhs_count, clusters * rank_size), jnp.bfloat16),
+            pltpu.VMEM((long_count, rhs_count, clusters * rank_size), jnp.float32),
             pltpu.SemaphoreType.DMA((row_count,)),
+            pltpu.VMEM((devices // 2 * share, rhs_count, LANES), jnp.float32),
         ]
         + [pltpu.VMEM((long_count, rhs_count, clusters * rank_size), jnp.float32)] * 4,
         compiler_params=pltpu.CompilerParams(vmem_limit_bytes=16 << 20),
         name="far",
     )(pair_list, everyone, to_second, to_first)
-    far_terms = lax.all_to_all(far, ("row", "long"), 0, 0, tiled=True)
+    far_terms = lax.all_to_all(
+        far, ("row", "long"), 0, 0, axis_index_groups=same_core(row_count, long_count), tiled=True
+    )
+    partner = [(row, row ^ 1) for row in range(row_count)]
+    far_other = lax.ppermute(far_terms, "row", partner)
 
     totals = pl.pallas_call(
         functools.partial(totals_kernel, long_count=long_count),
         out_shape=jax.ShapeDtypeStruct((rhs_count, LANES), jnp.float32),
-        in_specs=[VMEM, ANY],
+        in_specs=[VMEM],
         out_specs=VMEM,
         compiler_params=pltpu.CompilerParams(vmem_limit_bytes=16 << 20),
         cost_estimate=SMALL,
         name="totals",
-    )(everyone, far_done)
-    partner = [(row, row ^ 1) for row in range(row_count)]
+    )(everyone)
     totals_other = lax.ppermute(totals, "row", partner)
 
     near = pl.pallas_call(
         functools.partial(near_kernel, clusters=clusters),
         out_shape=jax.ShapeDtypeStruct((NEARC, rhs_count, unknowns), jnp.float32),
-        in_specs=[VMEM] * 4,
+        in_specs=[VMEM] * 4 + [ANY],
         out_specs=VMEM,
         scratch_shapes=[
             pltpu.VMEM((slots, size, 8), jnp.float32),
@@ -502,15 +523,17 @@
             pltpu.VMEM((NEARC, 6, size, size), jnp.bfloat16),
         ],
         compiler_params=pltpu.CompilerParams(vmem_limit_bytes=24 << 20),
-        cost_estimate=SMALL,
+        cost_estimate=pl.CostEstimate(
+            flops=1_000_000_000, bytes_accessed=1_000_000, transcendentals=660_000
+        ),
         name="near",
-    )(window, places, totals, totals_other)
+    )(window, places, totals, totals_other, far_done)
     other = lax.ppermute(near, "row", partner)
 
     return pl.pallas_call(
         finish_kernel,
         out_shape=jax.ShapeDtypeStruct(slip.shape, jnp.float32),
-        in_specs=[VMEM] * 4,
+        in_specs=[VMEM] * 5,
         out_specs=HBM,
         scratch_shapes=[
             pltpu.VMEM(slip.shape, jnp.float32),
@@ -518,7 +541,7 @@
         ],
         compiler_params=pltpu.CompilerParams(vmem_limit_bytes=16 << 20),
         name="finish",
-    )(near, other, far_terms, basis)
+    )(near, other, far_terms, far_other, basis)
 
 
 def solution(mesh):

time: 34.7 us -> 35.6 us (1.026)
  starting transfers between devices: 16.2 us -> 17.5 us
  waiting for transfers between devices: 7.51 us -> 7.12 us
    all_to_all x1, starting transfers between devices: 3.59 us -> 5.62 us  [shards(): lax.all_to_all(far, ('row', 'long'), 0, 0, axis_index_groups=same_core(ro...]
    ppermute x1, starting transfers between devices: 3.68 us -> 2.48 us  [shards(): halo = lax.ppermute(to_neighbour, ('row', 'long'), route)]
    ppermute x1, waiting for transfers between devices: 2.65 us -> 1.86 us  [shards(): halo = lax.ppermute(to_neighbour, ('row', 'long'), route)]
    all_to_all x1, waiting for transfers between devices: 0.01 us -> 0.74 us  [shards(): lax.all_to_all(far, ('row', 'long'), 0, 0, axis_index_groups=same_core(ro...]
    ppermute x1, starting transfers between devices: 0.06 us -> 0.55 us  [shards(): other = lax.ppermute(near, 'row', partner)]
  transfers between devices with their start and end apart: 5 -> 6, of which waited for: 3 -> 4; matrix products, arithmetic and copies ran while one was open for 0% -> 0% of each run, Pallas kernels for 13% -> 12%
where the time goes in v15:
time: 35.6 us; the launch traced here: 35.2 us
  starting transfers between devices  17.5 us (49%)
  Pallas kernels  9.01 us (25%)
  waiting for transfers between devices  7.12 us (20%)
  between operations  0.81 us (2%)
  local copies, waits for them, and re-layouts  0.7 us (2%)
    all_to_all x1, starting transfers between devices, shards(): lax.all_to_all(pay, ('row', 'long'), 0, 0, axis_index_groups=same_core(ro...  8.8 us
    all_to_all x1, starting transfers between devices, shards(): lax.all_to_all(far, ('row', 'long'), 0, 0, axis_index_groups=same_core(ro...  5.62 us
    pallas_call x1, Pallas kernels, shards(): pl.pallas_call(functools.partial(near_kernel, clusters=clusters), out_sha...  3.7 us
    all_to_all x1, waiting for transfers between devices, shards(): lax.all_to_all(pay, ('row', 'long'), 0, 0, axis_index_groups=same_core(ro...  3.56 us
    ppermute x1, starting transfers between devices, shards(): halo = lax.ppermute(to_neighbour, ('row', 'long'), route)  2.48 us
    pallas_call x1, Pallas kernels, shards(): pl.pallas_call(functools.partial(far_kernel, clusters=clusters, row_count...  1.88 us
    ppermute x1, waiting for transfers between devices, shards(): halo = lax.ppermute(to_neighbour, ('row', 'long'), route)  1.86 us
    pallas_call x1, Pallas kernels, shards(): pl.pallas_call(coeffs_kernel, out_shape=jax.ShapeDtypeStruct((devices //...  1.85 us
  transfers between devices with their start and end apart: 6, of which 4 were waited for; matrix products, arithmetic and copies ran while one was open for 0% of the time, Pallas kernels for 12%

profile of v15, /device:TPU:0, one launch (start us, length us, event | category | flops | bytes accessed | tf_op | source)
XLA Modules:
  0.0 35.2 jit_solution(12415510021616992154)
XLA Ops:
  0.7 1.9 %coeffs.1.after_ref = bf16[16,16,128]{2,1,0:T(8,128)(2,1)} custom-call(f32[4,16,768]{2,1,0:T(8,128)} %slip_ref.1, bf16[4,32,768]{2,1,0:T(8,128)(2,1)} %basis_ref.1, s32[2,20]{1,0:T(2,128)} %pairs_hbm.1, s32[1]{0:T(128)S(6)} %copy.10.count_ref), custom_call_target="tpu_custom_call" | custom-call | tf_op jit(solution)/shard_map/coeffs/pallas_call | solution.py:409
  2.5 0.0 copy-start.6
  2.5 8.8 %all-to-all-start = ((bf16[16,16,128]{2,1,0:T(8,128)(2,1)}), bf16[16,16,128]{2,1,0:T(8,128)(2,1)S(1)}, u32[]{:S(2)}, u32[]{:S(2)}) async-start(bf16[16,16,128]{2,1,0:T(8,128)(2,1)} %coeffs.1.after_ref), calls=%async_computation | async-start | bytes 131072 | tf_op jit(solution)/shard_map/all_to_all | solution.py:431
  11.3 0.0 copy-done.6
  11.3 0.0 copy-start.5
  11.3 0.1 reshape.3.coupling_ref
  11.5 0.5 %copy-done.5 = s32[2,16]{1,0:T(2,128)S(1)} copy-done((s32[2,16]{1,0:T(2,128)S(1)}, s32[2,16]{1,0:T(2,128)}, u32[]{:S(2)}) %copy-start.5) | copy-done | bytes 152
  12.0 0.4 %coupling.1 = (bf16[512,128]{1,0:T(8,128)(2,1)S(1)}, bf16[512,128]{1,0:T(8,128)(2,1)S(1)}, s32[2,16]{1,0:T(2,128)S(1)}) custom-call(bf16[16,32,32]{2,1,0:T(8,128)(2,1)S(1)} %reshape.3.coupling_ref, s32[2,16]{1,0:T(2,128)S(1)} %copy-done.5, bf16[16,16,128]{2,1,0:T(8,128)(2,1)} %coeffs.1.after_ref), custom_call_target="tpu_custom_call" | custom-call | flops 1000 | bytes 1000 | tf_op jit(solution)/shard_map/coupling/pallas_call | solution.py:471
  12.4 3.6 %all-to-all-done.pay_ref.coeff_ref = bf16[16,16,128]{2,1,0:T(8,128)(2,1)S(1)} async-done(((bf16[16,16,128]{2,1,0:T(8,128)(2,1)}), bf16[16,16,128]{2,1,0:T(8,128)(2,1)S(1)}, u32[]{:S(2)}, u32[]{:S(2)}) %all-to-all-start) | async-done | bytes 65568 | tf_op jit(solution)/shard_map/all_to_all | solution.py:431
  16.0 1.9 %far.1 = (f32[16,16,128]{2,1,0:T(8,128)}, f32[8,128]{1,0:T(8,128)S(1)}) custom-call(s32[2,16]{1,0:T(2,128)S(1)} %get-tuple-element.20.pairs_ref, bf16[16,16,128]{2,1,0:T(8,128)(2,1)S(1)} %all-to-all-done.pay_ref.coeff_ref, bf16[512,128]{1,0:T(8,128)(2,1)S(1)} %get-tuple-element.21.to_second_ref, bf16[512,128]{1,0:T(8,128)(2,1)S(1)} %get-tuple-element.22.to_first_ref), custom_call_target="tpu_custom_call" | custom-call | tf_op jit(solution)/shard_map/far/pallas_call | solution.py:481
  17.8 0.0 copy-start
  17.9 0.0 copy-start.2
  17.9 0.0 copy-start.3
  17.9 0.0 copy-start.4
  17.9 5.6 %all-to-all-start.1 = ((f32[16,16,128]{2,1,0:T(8,128)}), f32[16,16,128]{2,1,0:T(8,128)S(1)}, u32[]{:S(2)}, u32[]{:S(2)}) async-start(f32[16,16,128]{2,1,0:T(8,128)} %get-tuple-element.24), calls=%async_computation.1 | async-start | bytes 262144 | tf_op jit(solution)/shard_map/all_to_all | solution.py:498
  23.5 0.0 copy-done
  23.5 0.0 copy-done.2
  23.5 0.0 copy-done.3
  23.5 0.0 copy-done.4
  23.5 0.3 geometry.1
  23.8 2.5 %collective-permute-start = (bf16[2,16,1024]{2,1,0:T(8,128)(2,1)S(1)}, bf16[2,16,1024]{2,1,0:T(8,128)(2,1)S(1)}, u32[]{:S(2)}, u32[]{:S(2)}) collective-permute-start(bf16[2,16,1024]{2,1,0:T(8,128)(2,1)S(1)} %get-tuple-element.17), channel_id=1, source_target_pairs={{0,1},{1,2},{2,3},{3,4},{4,5},{5,6},{6,7},{9,8},{10,9},{11,10},{12... | collective-permute-start | bytes 196616 | tf_op jit(solution)/shard_map/ppermute | solution.py:456
  26.3 0.1 collective-permute-start.1
  26.4 1.9 %collective-permute-done.halo_ref = bf16[2,16,1024]{2,1,0:T(8,128)(2,1)S(1)} collective-permute-done((bf16[2,16,1024]{2,1,0:T(8,128)(2,1)S(1)}, bf16[2,16,1024]{2,1,0:T(8,128)(2,1)S(1)}, u32[]{:S(2)}, u32[]{:S(2)}) %collective-permute-start) | collective-permute-done | bytes 65568 | tf_op jit(solution)/shard_map/ppermute | solution.py:456
  28.3 0.7 %all-to-all-done.1.far_ref = f32[16,16,128]{2,1,0:T(8,128)S(1)} async-done(((f32[16,16,128]{2,1,0:T(8,128)}), f32[16,16,128]{2,1,0:T(8,128)S(1)}, u32[]{:S(2)}, u32[]{:S(2)}) %all-to-all-start.1) | async-done | bytes 131104 | tf_op jit(solution)/shard_map/all_to_all | solution.py:498
  29.1 0.0 collective-permute-start.3
  29.1 0.0 collective-permute-done.1.theirs_ref
  29.1 0.0 copy-start.1
  29.1 3.7 %near.1.own_ref = f32[2,16,768]{2,1,0:T(8,128)S(1)} custom-call(bf16[6,16,768]{2,1,0:T(8,128)(2,1)S(1)} %get-tuple-element.18.slip_ref, f32[6,4,256]{2,1,0:T(4,128)S(1)} %get-tuple-element.19.place_ref, f32[16,128]{1,0:T(8,128)S(1)} %totals.1.mine_ref, f32[16,128]{1,0:T(8,128)S(1)} %collective-permute-done.1.theirs_ref, f32[8,128]{1,0:T(8,128)S(1)} %get-tuple-element.23.after_ref), custom_call_target="tpu_custom_call" | custom-call | flops 1000000000 | bytes 1000000 | tf_op jit(solution)/shard_map/near/pallas_call | solution.py:515
  32.8 0.6 %collective-permute-start.2 = (f32[2,16,768]{2,1,0:T(8,128)S(1)}, f32[2,16,768]{2,1,0:T(8,128)S(1)}, u32[]{:S(2)}, u32[]{:S(2)}) collective-permute-start(f32[2,16,768]{2,1,0:T(8,128)S(1)} %near.1.own_ref), channel_id=1, source_target_pairs={{0,8},{8,0},{16,24},{24,16},{1,9},{9,1},{17,25},{25,17},{2,10},{10... | collective-permute-start | bytes 294920 | tf_op jit(solution)/shard_map/ppermute | solution.py:531
  33.3 0.9 %collective-permute-done.2.other_ref = f32[2,16,768]{2,1,0:T(8,128)S(1)} collective-permute-done((f32[2,16,768]{2,1,0:T(8,128)S(1)}, f32[2,16,768]{2,1,0:T(8,128)S(1)}, u32[]{:S(2)}, u32[]{:S(2)}) %collective-permute-start.2) | collective-permute-done | bytes 98336 | tf_op jit(solution)/shard_map/ppermute | solution.py:531
  34.3 0.0 collective-permute-done.3.far_other_ref
  34.3 0.0 copy-done.1
  34.3 0.9 %finish.1 = f32[4,16,768]{2,1,0:T(8,128)} custom-call(f32[2,16,768]{2,1,0:T(8,128)S(1)} %near.1.own_ref, f32[2,16,768]{2,1,0:T(8,128)S(1)} %collective-permute-done.2.other_ref, f32[16,16,128]{2,1,0:T(8,128)S(1)} %all-to-all-done.1.far_ref, f32[16,16,128]{2,1,0:T(8,128)S(1)} %collective-permute-done.3.far_other_ref, bf16[4,32,768]{2,1,0:T(8,128)(2,1)S(1)} %copy-done.1), custom_call_target="tpu_custom_call" | custom-call | tf_op jit(solution)/shard_map/finish/pallas_call | solution.py:533
  (2 shorter events, 0.1 us)
Async XLA Ops:
  2.5 8.8 %copy-start.6 = (bf16[16,1024]{1,0:T(8,128)(2,1)S(1)}, bf16[16,1024]{1,0:T(8,128)(2,1)}, u32[]{:S(2)}) copy-start(bf16[16,1024]{1,0:T(8,128)(2,1)} %param.16) | copy-start | bytes 98308
  2.5 13.4 %all-to-all-start = ((bf16[16,16,128]{2,1,0:T(8,128)(2,1)}), bf16[16,16,128]{2,1,0:T(8,128)(2,1)S(1)}, u32[]{:S(2)}, u32[]{:S(2)}) async-start(bf16[16,16,128]{2,1,0:T(8,128)(2,1)} %coeffs.1.after_ref), calls=%async_computation | async-start | bytes 131072 | tf_op jit(solution)/shard_map/all_to_all | solution.py:431
  11.3 0.7 %copy-start.5 = (s32[2,16]{1,0:T(2,128)S(1)}, s32[2,16]{1,0:T(2,128)}, u32[]{:S(2)}) copy-start(s32[2,16]{1,0:T(2,128)} %pairs_ref.1) | copy-start | bytes 388
  17.8 5.7 %copy-start = (f32[4,16,768]{2,1,0:T(8,128)S(1)}, f32[4,16,768]{2,1,0:T(8,128)}, u32[]{:S(2)}) copy-start(f32[4,16,768]{2,1,0:T(8,128)} %slip_ref.1) | copy-start | bytes 589828
  17.9 5.7 %copy-start.2 = (s32[3,1024]{1,0:T(4,128)S(1)}, s32[3,1024]{1,0:T(4,128)}, u32[]{:S(2)}) copy-start(s32[3,1024]{1,0:T(4,128)} %triangles_ref.1) | copy-start | bytes 36868
  17.9 5.7 %copy-start.3 = (f32[3,561]{1,0:T(4,128)S(1)}, f32[3,561]{1,0:T(4,128)}, u32[]{:S(2)}) copy-start(f32[3,561]{1,0:T(4,128)} %vertices_ref.1) | copy-start | bytes 20200
  17.9 5.7 %copy-start.4 = (s32[4,256]{1,0:T(4,128)S(1)}, s32[4,256]{1,0:T(4,128)}, u32[]{:S(2)}) copy-start(s32[4,256]{1,0:T(4,128)} %map_ref.1) | copy-start | bytes 12292
  17.9 11.2 %all-to-all-start.1 = ((f32[16,16,128]{2,1,0:T(8,128)}), f32[16,16,128]{2,1,0:T(8,128)S(1)}, u32[]{:S(2)}, u32[]{:S(2)}) async-start(f32[16,16,128]{2,1,0:T(8,128)} %get-tuple-element.24), calls=%async_computation.1 | async-start | bytes 262144 | tf_op jit(solution)/shard_map/all_to_all | solution.py:498
  23.8 4.5 %collective-permute-start = (bf16[2,16,1024]{2,1,0:T(8,128)(2,1)S(1)}, bf16[2,16,1024]{2,1,0:T(8,128)(2,1)S(1)}, u32[]{:S(2)}, u32[]{:S(2)}) collective-permute-start(bf16[2,16,1024]{2,1,0:T(8,128)(2,1)S(1)} %get-tuple-element.17), channel_id=1, source_target_pairs={{0,1},{1,2},{2,3},{3,4},{4,5},{5,6},{6,7},{9,8},{10,9},{11,10},{12... | collective-permute-start | bytes 196616 | tf_op jit(solution)/shard_map/ppermute | solution.py:456
  26.3 2.7 %collective-permute-start.1 = (f32[16,128]{1,0:T(8,128)S(1)}, f32[16,128]{1,0:T(8,128)S(1)}, u32[]{:S(2)}, u32[]{:S(2)}) collective-permute-start(f32[16,128]{1,0:T(8,128)S(1)} %totals.1.mine_ref), channel_id=1, source_target_pairs={{0,8},{8,0},{16,24},{24,16},{1,9},{9,1},{17,25},{25,17},{2,10},{10... | collective-permute-start | bytes 24584 | tf_op jit(solution)/shard_map/ppermute | solution.py:513
  29.1 5.2 %collective-permute-start.3 = (f32[16,16,128]{2,1,0:T(8,128)S(1)}, f32[16,16,128]{2,1,0:T(8,128)S(1)}, u32[]{:S(2)}, u32[]{:S(2)}) collective-permute-start(f32[16,16,128]{2,1,0:T(8,128)S(1)} %all-to-all-done.1.far_ref), channel_id=1, source_target_pairs={{0,8},{8,0},{16,24},{24,16},{1,9},{9,1},{17,25},{25,17},{2,10},{10... | collective-permute-start | bytes 393224 | tf_op jit(solution)/shard_map/ppermute | solution.py:502
  29.1 5.2 %copy-start.1 = (bf16[4,32,768]{2,1,0:T(8,128)(2,1)S(1)}, bf16[4,32,768]{2,1,0:T(8,128)(2,1)}, u32[]{:S(2)}) copy-start(bf16[4,32,768]{2,1,0:T(8,128)(2,1)} %basis_ref.1) | copy-start | bytes 589828
  32.8 1.5 %collective-permute-start.2 = (f32[2,16,768]{2,1,0:T(8,128)S(1)}, f32[2,16,768]{2,1,0:T(8,128)S(1)}, u32[]{:S(2)}, u32[]{:S(2)}) collective-permute-start(f32[2,16,768]{2,1,0:T(8,128)S(1)} %near.1.own_ref), channel_id=1, source_target_pairs={{0,8},{8,0},{16,24},{24,16},{1,9},{9,1},{17,25},{25,17},{2,10},{10... | collective-permute-start | bytes 294920 | tf_op jit(solution)/shard_map/ppermute | solution.py:531

commit v16 on v13

--- a/solution.py
+++ b/solution.py
@@ -9,6 +9,7 @@
 
 NEARC = 2
 LANES = 128
+AHEAD = 2
 ROWS = 16
 
 soften = 0.25
@@ -17,6 +18,26 @@
 SMEM = pl.BlockSpec(memory_space=pltpu.SMEM)
 HBM = pl.BlockSpec(memory_space=pltpu.HBM)
 ANY = pl.BlockSpec(memory_space=pl.ANY)
+
+
+def exchange_order(row_count, long_count):
+    order = list(range(0, AHEAD * long_count, long_count))
+    for owner in reversed(range(long_count)):
+        for row in range(row_count):
+            if owner or row >= AHEAD:
+                order.append(row * long_count + owner)
+    return order
+
+
+def place_of(row, owner, row_count, long_count):
+    place = AHEAD + (long_count - 1 - owner) * row_count + row
+    at_first = jnp.where(row < AHEAD, row, place - AHEAD)
+    return jnp.where(owner == 0, at_first, place)
+
+
+def everyone_sends(chunks, row_count, long_count):
+    order = [exchange_order(row_count, long_count)]
+    return lax.all_to_all(chunks, ("row", "long"), 0, 0, axis_index_groups=order, tiled=True)
 
 
 def lane_gather(table, index):
@@ -180,9 +201,11 @@
     long_index = lax.axis_index("long")
     before = jnp.maximum(long_index - 1, 0)
     totals = [jnp.zeros(pay_ref.shape[1:], jnp.float32) for _ in range(2)]
-    for row in range(pay_ref.shape[0] // long_count):
+    row_count = pay_ref.shape[0] // long_count
+    for row in range(row_count):
         for source, owner in enumerate((long_index, before)):
-            totals[source] += pay_ref[row * long_count + owner].astype(jnp.float32)
+            at = place_of(row, owner, row_count, long_count)
+            totals[source] += pay_ref[at].astype(jnp.float32)
     even = lax.axis_index("row") % 2 == 0
     half = pay_ref.shape[1]
     rank_size = pay_ref.shape[2] // 4
@@ -281,10 +304,11 @@
 
 
 def far_kernel(
-    pairs_ref, coeff_ref, to_second_ref, to_first_ref, out_hbm, done_ref, sent_ref, sems, *total_refs, clusters
+    pairs_ref, coeff_ref, to_second_ref, to_first_ref, out_ref, done_ref, *total_refs, clusters
 ):
     done_ref[...] = jnp.zeros(done_ref.shape, jnp.float32)
     long_count, rhs_count, _ = total_refs[0].shape
+    row_count = out_ref.shape[0] // long_count
     pair_count = pairs_ref.shape[1]
     rank_size = LANES // clusters
     group_id = lax.broadcasted_iota(jnp.int32, (rhs_count, LANES), 1) // rank_size
@@ -292,7 +316,7 @@
         total_ref[...] = jnp.zeros(total_ref.shape, jnp.float32)
 
     def coeff_of(cluster, group):
-        whole = coeff_ref[(cluster % clusters) * long_count + cluster // clusters]
+        whole = coeff_ref[place_of(cluster % clusters, cluster // clusters, row_count, long_count)]
         whole = whole.astype(jnp.float32)
         low = pltpu.roll(whole, rank_size * group, 1) if group else whole
         high = pltpu.roll(whole, (rank_size * (group - 1)) % LANES, 1) if group != 1 else whole
@@ -321,17 +345,9 @@
     total = total_refs[0][...]
     for total_ref in total_refs[1:]:
         total = total + total_ref[...]
-    sent_ref[...] = total.astype(jnp.bfloat16)
-    copies = [
-        pltpu.make_async_copy(
-            sent_ref, out_hbm.at[pl.ds(copy_id * long_count, long_count)], sems.at[copy_id]
-        )
-        for copy_id in range(out_hbm.shape[0] // long_count)
-    ]
-    for copy in copies:
-        copy.start()
-    for copy in copies:
-        copy.wait()
+    sent = total.astype(jnp.bfloat16)
+    for place, at in enumerate(exchange_order(row_count, long_count)):
+        out_ref[place] = sent[at % long_count]
 
 
 def finish_kernel(own_ref, other_ref, far_ref, basis_ref, out_hbm, sent_ref, sems):
@@ -388,7 +404,7 @@
         ],
         near_count,
     )
-    everyone = lax.all_to_all(pay, ("row", "long"), 0, 0, tiled=True)
+    everyone = everyone_sends(pay, row_count, long_count)
 
     xs, to_neighbour, geometry = pl.pallas_call(
         geometry_kernel,
@@ -443,16 +459,12 @@
             jax.ShapeDtypeStruct((8, LANES), jnp.float32),
         ],
         in_specs=[SMEM, VMEM, VMEM, VMEM],
-        out_specs=[HBM, VMEM],
-        scratch_shapes=[
-            pltpu.VMEM((long_count, rhs_count, clusters * rank_size), jnp.bfloat16),
-            pltpu.SemaphoreType.DMA((row_count,)),
-        ]
-        + [pltpu.VMEM((long_count, rhs_count, clusters * rank_size), jnp.float32)] * 4,
+        out_specs=[VMEM] * 2,
+        scratch_shapes=[pltpu.VMEM((long_count, rhs_count, clusters * rank_size), jnp.float32)] * 4,
         compiler_params=pltpu.CompilerParams(vmem_limit_bytes=16 << 20),
         name="far",
     )(pair_list, everyone, to_second, to_first)
-    far_terms = lax.all_to_all(far, ("row", "long"), 0, 0, tiled=True)
+    far_terms = everyone_sends(far, row_count, long_count)
 
     near = pl.pallas_call(
         functools.partial(near_kernel, long_count=long_count, clusters=clusters),

time: 30.3 us -> 31.1 us (1.026)
  waiting for transfers between devices: 6.55 us -> 7.3 us
    all_to_all x2, waiting for transfers between devices: 5.36 us -> 6.11 us  [everyone_sends(): lax.all_to_all(chunks, ('row', 'long'), 0, 0, axis_index_groups=order, ti...]
where the time goes in v16:
time: 31.1 us; the launch traced here: 30.7 us
  starting transfers between devices  13.7 us (44%)
  Pallas kernels  8.7 us (28%)
  waiting for transfers between devices  7.3 us (23%)
  between operations  0.83 us (3%)
    all_to_all x2, starting transfers between devices, everyone_sends(): lax.all_to_all(chunks, ('row', 'long'), 0, 0, axis_index_groups=order, ti...  9.88 us
    all_to_all x2, waiting for transfers between devices, everyone_sends(): lax.all_to_all(chunks, ('row', 'long'), 0, 0, axis_index_groups=order, ti...  6.11 us
    ppermute x1, starting transfers between devices, shards(): halo = lax.ppermute(to_neighbour, ('row', 'long'), route)  3.68 us
    pallas_call x1, Pallas kernels, shards(): pl.pallas_call(functools.partial(near_kernel, long_count=long_count, clus...  3.66 us
    pallas_call x1, Pallas kernels, shards(): pl.pallas_call(coeffs_kernel, out_shape=jax.ShapeDtypeStruct((devices, rh...  1.76 us
    pallas_call x1, Pallas kernels, shards(): pl.pallas_call(functools.partial(far_kernel, clusters=clusters), out_shap...  1.71 us
    ppermute x1, waiting for transfers between devices, shards(): other = lax.ppermute(near, 'row', partner)  1.19 us
    pallas_call x1, Pallas kernels, shards(): pl.pallas_call(finish_kernel, out_shape=jax.ShapeDtypeStruct(slip.shape,...  0.9 us
  transfers between devices with their start and end apart: 4, of which 3 were waited for; matrix products, arithmetic and copies ran while one was open for 0% of the time, Pallas kernels for 20%

profile of v16, /device:TPU:0, one launch (start us, length us, event | category | flops | bytes accessed | tf_op | source)
XLA Modules:
  0.0 30.7 jit_solution(9625935458862510855)
XLA Ops:
  0.7 0.0 copy-start
  0.7 1.8 %coeffs.1.after_ref = bf16[32,8,128]{2,1,0:T(8,128)(2,1)} custom-call(f32[4,16,768]{2,1,0:T(8,128)} %slip_ref.1, bf16[4,32,768]{2,1,0:T(8,128)(2,1)} %basis_ref.1, s32[2,20]{1,0:T(2,128)} %pairs_hbm.1, s32[1]{0:T(128)S(6)} %copy.10.count_ref), custom_call_target="tpu_custom_call" | custom-call | tf_op jit(solution)/shard_map/coeffs/pallas_call | solution.py:385
  2.4 0.0 copy-start.2
  2.4 0.0 copy-start.3
  2.5 0.0 copy-start.4
  2.5 7.3 %all-to-all-start = ((bf16[32,8,128]{2,1,0:T(8,128)(2,1)}), bf16[32,8,128]{2,1,0:T(8,128)(2,1)S(1)}, u32[]{:S(2)}, u32[]{:S(2)}) async-start(bf16[32,8,128]{2,1,0:T(8,128)(2,1)} %coeffs.1.after_ref), calls=%async_computation | async-start | bytes 131072 | tf_op jit(solution)/shard_map/all_to_all | solution.py:40
  9.8 0.0 copy-done
  9.8 0.0 copy-done.2
  9.8 0.0 copy-done.3
  9.8 0.0 copy-done.4
  9.8 0.0 copy-start.6
  9.8 0.3 geometry.1
  10.1 0.0 copy-start.5
  10.1 3.7 %collective-permute-start = (bf16[2,16,1024]{2,1,0:T(8,128)(2,1)S(1)}, bf16[2,16,1024]{2,1,0:T(8,128)(2,1)S(1)}, u32[]{:S(2)}, u32[]{:S(2)}) collective-permute-start(bf16[2,16,1024]{2,1,0:T(8,128)(2,1)S(1)} %get-tuple-element.17), channel_id=1, source_target_pairs={{0,1},{1,2},{2,3},{3,4},{4,5},{5,6},{6,7},{9,8},{10,9},{11,10},{12... | collective-permute-start | bytes 196616 | tf_op jit(solution)/shard_map/ppermute | solution.py:430
  13.8 0.0 copy-done.6
  13.8 0.1 reshape.3.coupling_ref
  14.0 0.0 copy-done.5
  14.0 0.4 %coupling.1 = (bf16[512,128]{1,0:T(8,128)(2,1)S(1)}, bf16[512,128]{1,0:T(8,128)(2,1)S(1)}, s32[2,16]{1,0:T(2,128)S(1)}) custom-call(bf16[16,32,32]{2,1,0:T(8,128)(2,1)S(1)} %reshape.3.coupling_ref, s32[2,16]{1,0:T(2,128)S(1)} %copy-done.5, bf16[32,8,128]{2,1,0:T(8,128)(2,1)} %coeffs.1.after_ref), custom_call_target="tpu_custom_call" | custom-call | flops 1000 | bytes 1000 | tf_op jit(solution)/shard_map/coupling/pallas_call | solution.py:445
  14.3 2.9 %all-to-all-done.coeff_ref.pay_ref = bf16[32,8,128]{2,1,0:T(8,128)(2,1)S(1)} async-done(((bf16[32,8,128]{2,1,0:T(8,128)(2,1)}), bf16[32,8,128]{2,1,0:T(8,128)(2,1)S(1)}, u32[]{:S(2)}, u32[]{:S(2)}) %all-to-all-start) | async-done | bytes 65568 | tf_op jit(solution)/shard_map/all_to_all | solution.py:40
  17.2 1.7 %far.1 = (bf16[32,16,128]{2,1,0:T(8,128)(2,1)}, f32[8,128]{1,0:T(8,128)S(1)}) custom-call(s32[2,16]{1,0:T(2,128)S(1)} %get-tuple-element.20.pairs_ref, bf16[32,8,128]{2,1,0:T(8,128)(2,1)S(1)} %all-to-all-done.coeff_ref.pay_ref, bf16[512,128]{1,0:T(8,128)(2,1)S(1)} %get-tuple-element.21.to_second_ref, bf16[512,128]{1,0:T(8,128)(2,1)S(1)} %get-tuple-element.22.to_first_ref), custom_call_target="tpu_custom_call" | custom-call | tf_op jit(solution)/shard_map/far/pallas_call | solution.py:455
  18.9 2.6 %all-to-all-start.1 = ((bf16[32,16,128]{2,1,0:T(8,128)(2,1)}), bf16[32,16,128]{2,1,0:T(8,128)(2,1)S(1)}, u32[]{:S(2)}, u32[]{:S(2)}) async-start(bf16[32,16,128]{2,1,0:T(8,128)(2,1)} %get-tuple-element.24), calls=%async_computation.1 | async-start | bytes 262144 | tf_op jit(solution)/shard_map/all_to_all | solution.py:40
  21.5 0.0 collective-permute-done.halo_ref
  21.6 0.0 copy-start.1
  21.6 3.7 %near.1.own_ref = f32[2,16,768]{2,1,0:T(8,128)S(1)} custom-call(bf16[6,16,768]{2,1,0:T(8,128)(2,1)S(1)} %get-tuple-element.18.slip_ref, f32[6,4,256]{2,1,0:T(4,128)S(1)} %get-tuple-element.19.place_ref, bf16[32,8,128]{2,1,0:T(8,128)(2,1)S(1)} %all-to-all-done.coeff_ref.pay_ref, f32[8,128]{1,0:T(8,128)S(1)} %get-tuple-element.23.after_ref), custom_call_target="tpu_custom_call" | custom-call | flops 1000000000 | bytes 1000000 | tf_op jit(solution)/shard_map/near/pallas_call | solution.py:469
  25.3 0.2 collective-permute-start.1
  25.4 1.2 %collective-permute-done.1.other_ref = f32[2,16,768]{2,1,0:T(8,128)S(1)} collective-permute-done((f32[2,16,768]{2,1,0:T(8,128)S(1)}, f32[2,16,768]{2,1,0:T(8,128)S(1)}, u32[]{:S(2)}, u32[]{:S(2)}) %collective-permute-start.1) | collective-permute-done | bytes 98336 | tf_op jit(solution)/shard_map/ppermute | solution.py:486
  26.6 3.2 %all-to-all-done.1.far_ref = bf16[32,16,128]{2,1,0:T(8,128)(2,1)S(1)} async-done(((bf16[32,16,128]{2,1,0:T(8,128)(2,1)}), bf16[32,16,128]{2,1,0:T(8,128)(2,1)S(1)}, u32[]{:S(2)}, u32[]{:S(2)}) %all-to-all-start.1) | async-done | bytes 131104 | tf_op jit(solution)/shard_map/all_to_all | solution.py:40
  29.8 0.0 copy-done.1
  29.8 0.9 %finish.1 = f32[4,16,768]{2,1,0:T(8,128)} custom-call(f32[2,16,768]{2,1,0:T(8,128)S(1)} %near.1.own_ref, f32[2,16,768]{2,1,0:T(8,128)S(1)} %collective-permute-done.1.other_ref, bf16[32,16,128]{2,1,0:T(8,128)(2,1)S(1)} %all-to-all-done.1.far_ref, bf16[4,32,768]{2,1,0:T(8,128)(2,1)S(1)} %copy-done.1), custom_call_target="tpu_custom_call" | custom-call | tf_op jit(solution)/shard_map/finish/pallas_call | solution.py:488
  (1 shorter events, 0.0 us)
Async XLA Ops:
  0.7 9.1 %copy-start = (f32[4,16,768]{2,1,0:T(8,128)S(1)}, f32[4,16,768]{2,1,0:T(8,128)}, u32[]{:S(2)}) copy-start(f32[4,16,768]{2,1,0:T(8,128)} %slip_ref.1) | copy-start | bytes 589828
  2.4 7.4 %copy-start.2 = (s32[3,1024]{1,0:T(4,128)S(1)}, s32[3,1024]{1,0:T(4,128)}, u32[]{:S(2)}) copy-start(s32[3,1024]{1,0:T(4,128)} %triangles_ref.1) | copy-start | bytes 36868
  2.4 7.4 %copy-start.3 = (f32[3,561]{1,0:T(4,128)S(1)}, f32[3,561]{1,0:T(4,128)}, u32[]{:S(2)}) copy-start(f32[3,561]{1,0:T(4,128)} %vertices_ref.1) | copy-start | bytes 20200
  2.5 7.4 %copy-start.4 = (s32[4,256]{1,0:T(4,128)S(1)}, s32[4,256]{1,0:T(4,128)}, u32[]{:S(2)}) copy-start(s32[4,256]{1,0:T(4,128)} %map_ref.1) | copy-start | bytes 12292
  2.5 14.8 %all-to-all-start = ((bf16[32,8,128]{2,1,0:T(8,128)(2,1)}), bf16[32,8,128]{2,1,0:T(8,128)(2,1)S(1)}, u32[]{:S(2)}, u32[]{:S(2)}) async-start(bf16[32,8,128]{2,1,0:T(8,128)(2,1)} %coeffs.1.after_ref), calls=%async_computation | async-start | bytes 131072 | tf_op jit(solution)/shard_map/all_to_all | solution.py:40
  9.8 4.0 %copy-start.6 = (bf16[16,1024]{1,0:T(8,128)(2,1)S(1)}, bf16[16,1024]{1,0:T(8,128)(2,1)}, u32[]{:S(2)}) copy-start(bf16[16,1024]{1,0:T(8,128)(2,1)} %param.16) | copy-start | bytes 98308
  10.1 3.9 %copy-start.5 = (s32[2,16]{1,0:T(2,128)S(1)}, s32[2,16]{1,0:T(2,128)}, u32[]{:S(2)}) copy-start(s32[2,16]{1,0:T(2,128)} %pairs_ref.1) | copy-start | bytes 388
  10.1 11.4 %collective-permute-start = (bf16[2,16,1024]{2,1,0:T(8,128)(2,1)S(1)}, bf16[2,16,1024]{2,1,0:T(8,128)(2,1)S(1)}, u32[]{:S(2)}, u32[]{:S(2)}) collective-permute-start(bf16[2,16,1024]{2,1,0:T(8,128)(2,1)S(1)} %get-tuple-element.17), channel_id=1, source_target_pairs={{0,1},{1,2},{2,3},{3,4},{4,5},{5,6},{6,7},{9,8},{10,9},{11,10},{12... | collective-permute-start | bytes 196616 | tf_op jit(solution)/shard_map/ppermute | solution.py:430
  18.9 10.9 %all-to-all-start.1 = ((bf16[32,16,128]{2,1,0:T(8,128)(2,1)}), bf16[32,16,128]{2,1,0:T(8,128)(2,1)S(1)}, u32[]{:S(2)}, u32[]{:S(2)}) async-start(bf16[32,16,128]{2,1,0:T(8,128)(2,1)} %get-tuple-element.24), calls=%async_computation.1 | async-start | bytes 262144 | tf_op jit(solution)/shard_map/all_to_all | solution.py:40
  21.6 8.3 %copy-start.1 = (bf16[4,32,768]{2,1,0:T(8,128)(2,1)S(1)}, bf16[4,32,768]{2,1,0:T(8,128)(2,1)}, u32[]{:S(2)}) copy-start(bf16[4,32,768]{2,1,0:T(8,128)(2,1)} %basis_ref.1) | copy-start | bytes 589828
  25.3 1.4 %collective-permute-start.1 = (f32[2,16,768]{2,1,0:T(8,128)S(1)}, f32[2,16,768]{2,1,0:T(8,128)S(1)}, u32[]{:S(2)}, u32[]{:S(2)}) collective-permute-start(f32[2,16,768]{2,1,0:T(8,128)S(1)} %near.1.own_ref), channel_id=1, source_target_pairs={{0,8},{8,0},{16,24},{24,16},{1,9},{9,1},{17,25},{25,17},{2,10},{10... | collective-permute-start | bytes 294920 | tf_op jit(solution)/shard_map/ppermute | solution.py:486

commit v17 on v14

--- a/solution.py
+++ b/solution.py
@@ -192,7 +192,7 @@
         )
 
 
-def totals_kernel(pay_ref, after_ref, out_ref, *, long_count):
+def totals_kernel(pay_ref, out_ref, *, long_count):
     row_count = 2 * pay_ref.shape[0] // long_count
     long_index = lax.axis_index("long")
     totals = [jnp.zeros(pay_ref.shape[1:], jnp.float32) for _ in range(2)]
@@ -205,7 +205,7 @@
 
 
 def near_kernel(
-    slip_ref, place_ref, mine_ref, theirs_ref, out_ref, cols_ref, even_ref, odd_ref, *, clusters
+    slip_ref, place_ref, mine_ref, theirs_ref, after_ref, out_ref, cols_ref, even_ref, odd_ref, *, clusters
 ):
     slots, rhs_count, unknowns = slip_ref.shape
     size = place_ref.shape[2]
@@ -303,7 +303,7 @@
 
 
 def far_kernel(
-    pairs_ref, coeff_ref, to_second_ref, to_first_ref, out_hbm, done_ref, sent_ref, sems, *total_refs, clusters
+    pairs_ref, coeff_ref, to_second_ref, to_first_ref, out_hbm, done_ref, sent_ref, sems, moved_ref, *total_refs, clusters
 ):
     done_ref[...] = jnp.zeros(done_ref.shape, jnp.float32)
     long_count, rhs_count, _ = total_refs[0].shape
@@ -314,11 +314,18 @@
     for total_ref in total_refs:
         total_ref[...] = jnp.zeros(total_ref.shape, jnp.float32)
 
+    share = clusters // 2
+    for at in range(coeff_ref.shape[0]):
+        whole = coeff_ref[at].astype(jnp.float32)
+        for turn in range(share):
+            moved_ref[at * share + turn] = (
+                pltpu.roll(whole, LANES - rank_size * turn, 1) if turn else whole
+            )
+
     def coeff_of(cluster, group):
-        share = clusters // 2
         at = place_in_core(cluster % clusters // share, cluster // clusters, row_count, long_count)
-        whole = coeff_ref[at].astype(jnp.float32)
-        both = pltpu.roll(whole, (LANES + rank_size * (group - cluster % share)) % LANES, 1)
+        whole = moved_ref[at * share + cluster % share]
+        both = pltpu.roll(whole, rank_size * group, 1) if group else whole
         return jnp.where(group_id == group, both, 0.0)
 
     results = []
@@ -472,6 +479,7 @@
         scratch_shapes=[
             pltpu.VMEM((long_count, rhs_count, clusters * rank_size), jnp.bfloat16),
             pltpu.SemaphoreType.DMA((row_count,)),
+            pltpu.VMEM((devices // 2 * share, rhs_count, LANES), jnp.float32),
         ]
         + [pltpu.VMEM((long_count, rhs_count, clusters * rank_size), jnp.float32)] * 4,
         compiler_params=pltpu.CompilerParams(vmem_limit_bytes=16 << 20),
@@ -482,19 +490,19 @@
     totals = pl.pallas_call(
         functools.partial(totals_kernel, long_count=long_count),
         out_shape=jax.ShapeDtypeStruct((rhs_count, LANES), jnp.float32),
-        in_specs=[VMEM, ANY],
+        in_specs=[VMEM],
         out_specs=VMEM,
         compiler_params=pltpu.CompilerParams(vmem_limit_bytes=16 << 20),
         cost_estimate=SMALL,
         name="totals",
-    )(everyone, far_done)
+    )(everyone)
     partner = [(row, row ^ 1) for row in range(row_count)]
     totals_other = lax.ppermute(totals, "row", partner)
 
     near = pl.pallas_call(
         functools.partial(near_kernel, clusters=clusters),
         out_shape=jax.ShapeDtypeStruct((NEARC, rhs_count, unknowns), jnp.float32),
-        in_specs=[VMEM] * 4,
+        in_specs=[VMEM] * 4 + [ANY],
         out_specs=VMEM,
         scratch_shapes=[
             pltpu.VMEM((slots, size, 8), jnp.float32),
@@ -502,9 +510,11 @@
             pltpu.VMEM((NEARC, 6, size, size), jnp.bfloat16),
         ],
         compiler_params=pltpu.CompilerParams(vmem_limit_bytes=24 << 20),
-        cost_estimate=SMALL,
+        cost_estimate=pl.CostEstimate(
+            flops=1_000_000_000, bytes_accessed=1_000_000, transcendentals=660_000
+        ),
         name="near",
-    )(window, places, totals, totals_other)
+    )(window, places, totals, totals_other, far_done)
     other = lax.ppermute(near, "row", partner)
 
     return pl.pallas_call(

time: 34.7 us -> 30.6 us (0.88)
  waiting for transfers between devices: 7.51 us -> 4.63 us
  starting transfers between devices: 16.2 us -> 15.6 us
  local copies, waits for them, and re-layouts: 0.7 us -> 0.19 us
    ppermute x1, waiting for transfers between devices: 2.65 us -> 0.01 us  [shards(): halo = lax.ppermute(to_neighbour, ('row', 'long'), route)]
    all_to_all x1, waiting for transfers between devices: 3.56 us -> 1.27 us  [shards(): lax.all_to_all(pay, ('row', 'long'), 0, 0, axis_index_groups=same_core(ro...]
    all_to_all x1, waiting for transfers between devices: 0.01 us -> 1.44 us  [shards(): far_terms = lax.all_to_all(far, ('row', 'long'), 0, 0, tiled=True)]
    ppermute x1, starting transfers between devices: 3.68 us -> 2.47 us  [shards(): halo = lax.ppermute(to_neighbour, ('row', 'long'), route)]
    ppermute x1, waiting for transfers between devices: 0.01 us -> 0.87 us  [shards(): totals_other = lax.ppermute(totals, 'row', partner)]
    unnamed x14, local copies, waits for them, and re-layouts: 0.55 us -> 0.04 us
  transfers between devices with their start and end apart: 5 -> 5, of which waited for: 3 -> 4; matrix products, arithmetic and copies ran while one was open for 0% -> 0% of each run, Pallas kernels for 13% -> 21%
where the time goes in v17:
time: 30.6 us; the launch traced here: 30.3 us
  starting transfers between devices  15.6 us (51%)
  Pallas kernels  9.03 us (30%)
  waiting for transfers between devices  4.63 us (15%)
  between operations  0.82 us (3%)
    all_to_all x1, starting transfers between devices, shards(): lax.all_to_all(pay, ('row', 'long'), 0, 0, axis_index_groups=same_core(ro...  8.93 us
    pallas_call x1, Pallas kernels, shards(): pl.pallas_call(functools.partial(near_kernel, clusters=clusters), out_sha...  3.68 us
    all_to_all x1, starting transfers between devices, shards(): far_terms = lax.all_to_all(far, ('row', 'long'), 0, 0, tiled=True)  3.58 us
    ppermute x1, starting transfers between devices, shards(): halo = lax.ppermute(to_neighbour, ('row', 'long'), route)  2.47 us
    pallas_call x1, Pallas kernels, shards(): pl.pallas_call(coeffs_kernel, out_shape=jax.ShapeDtypeStruct((devices //...  1.89 us
    pallas_call x1, Pallas kernels, shards(): pl.pallas_call(functools.partial(far_kernel, clusters=clusters), out_shap...  1.88 us
    all_to_all x1, waiting for transfers between devices, shards(): far_terms = lax.all_to_all(far, ('row', 'long'), 0, 0, tiled=True)  1.44 us
    all_to_all x1, waiting for transfers between devices, shards(): lax.all_to_all(pay, ('row', 'long'), 0, 0, axis_index_groups=same_core(ro...  1.27 us
  transfers between devices with their start and end apart: 5, of which 4 were waited for; matrix products, arithmetic and copies ran while one was open for 0% of the time, Pallas kernels for 21%

profile of v17, /device:TPU:0, one launch (start us, length us, event | category | flops | bytes accessed | tf_op | source)
XLA Modules:
  0.0 30.3 jit_solution(15969980518771057531)
XLA Ops:
  0.7 0.0 copy-start
  0.7 1.9 %coeffs.1.after_ref = bf16[16,16,128]{2,1,0:T(8,128)(2,1)} custom-call(f32[4,16,768]{2,1,0:T(8,128)} %slip_ref.1, bf16[4,32,768]{2,1,0:T(8,128)(2,1)} %basis_ref.1, s32[2,20]{1,0:T(2,128)} %pairs_hbm.1, s32[1]{0:T(128)S(6)} %copy.10.count_ref), custom_call_target="tpu_custom_call" | custom-call | tf_op jit(solution)/shard_map/coeffs/pallas_call | solution.py:399
  2.6 0.0 copy-start.2
  2.6 0.0 copy-start.3
  2.6 0.0 copy-start.4
  2.6 8.9 %all-to-all-start = ((bf16[16,16,128]{2,1,0:T(8,128)(2,1)}), bf16[16,16,128]{2,1,0:T(8,128)(2,1)S(1)}, u32[]{:S(2)}, u32[]{:S(2)}) async-start(bf16[16,16,128]{2,1,0:T(8,128)(2,1)} %coeffs.1.after_ref), calls=%async_computation | async-start | bytes 131072 | tf_op jit(solution)/shard_map/all_to_all | solution.py:421
  11.5 0.0 copy-done
  11.5 0.0 copy-done.2
  11.5 0.0 copy-done.3
  11.5 0.0 copy-done.4
  11.6 0.0 copy-start.6
  11.6 0.3 geometry.1
  11.8 0.0 copy-start.5
  11.9 2.5 %collective-permute-start = (bf16[2,16,1024]{2,1,0:T(8,128)(2,1)S(1)}, bf16[2,16,1024]{2,1,0:T(8,128)(2,1)S(1)}, u32[]{:S(2)}, u32[]{:S(2)}) collective-permute-start(bf16[2,16,1024]{2,1,0:T(8,128)(2,1)S(1)} %get-tuple-element.17), channel_id=1, source_target_pairs={{0,1},{1,2},{2,3},{3,4},{4,5},{5,6},{6,7},{9,8},{10,9},{11,10},{12... | collective-permute-start | bytes 196616 | tf_op jit(solution)/shard_map/ppermute | solution.py:446
  14.3 0.0 copy-done.6
  14.3 0.1 reshape.3.coupling_ref
  14.5 0.0 copy-done.5
  14.5 0.4 %coupling.1 = (bf16[512,128]{1,0:T(8,128)(2,1)S(1)}, bf16[512,128]{1,0:T(8,128)(2,1)S(1)}, s32[2,16]{1,0:T(2,128)S(1)}) custom-call(bf16[16,32,32]{2,1,0:T(8,128)(2,1)S(1)} %reshape.3.coupling_ref, s32[2,16]{1,0:T(2,128)S(1)} %copy-done.5, bf16[16,16,128]{2,1,0:T(8,128)(2,1)} %coeffs.1.after_ref), custom_call_target="tpu_custom_call" | custom-call | flops 1000 | bytes 1000 | tf_op jit(solution)/shard_map/coupling/pallas_call | solution.py:461
  14.9 1.3 %all-to-all-done.pay_ref.coeff_ref = bf16[16,16,128]{2,1,0:T(8,128)(2,1)S(1)} async-done(((bf16[16,16,128]{2,1,0:T(8,128)(2,1)}), bf16[16,16,128]{2,1,0:T(8,128)(2,1)S(1)}, u32[]{:S(2)}, u32[]{:S(2)}) %all-to-all-start) | async-done | bytes 65568 | tf_op jit(solution)/shard_map/all_to_all | solution.py:421
  16.2 1.9 %far.1 = (bf16[32,16,128]{2,1,0:T(8,128)(2,1)}, f32[8,128]{1,0:T(8,128)S(1)}) custom-call(s32[2,16]{1,0:T(2,128)S(1)} %get-tuple-element.20.pairs_ref, bf16[16,16,128]{2,1,0:T(8,128)(2,1)S(1)} %all-to-all-done.pay_ref.coeff_ref, bf16[512,128]{1,0:T(8,128)(2,1)S(1)} %get-tuple-element.21.to_second_ref, bf16[512,128]{1,0:T(8,128)(2,1)S(1)} %get-tuple-element.22.to_first_ref), custom_call_target="tpu_custom_call" | custom-call | tf_op jit(solution)/shard_map/far/pallas_call | solution.py:471
  18.0 3.6 %all-to-all-start.1 = ((bf16[32,16,128]{2,1,0:T(8,128)(2,1)}), bf16[32,16,128]{2,1,0:T(8,128)(2,1)S(1)}, u32[]{:S(2)}, u32[]{:S(2)}) async-start(bf16[32,16,128]{2,1,0:T(8,128)(2,1)} %get-tuple-element.24), calls=%async_computation.1 | async-start | bytes 262144 | tf_op jit(solution)/shard_map/all_to_all | solution.py:488
  21.7 0.3 %collective-permute-start.1 = (f32[16,128]{1,0:T(8,128)S(1)}, f32[16,128]{1,0:T(8,128)S(1)}, u32[]{:S(2)}, u32[]{:S(2)}) collective-permute-start(f32[16,128]{1,0:T(8,128)S(1)} %totals.1.mine_ref), channel_id=1, source_target_pairs={{0,8},{8,0},{16,24},{24,16},{1,9},{9,1},{17,25},{25,17},{2,10},{10... | collective-permute-start | bytes 24584 | tf_op jit(solution)/shard_map/ppermute | solution.py:500
  22.0 0.0 collective-permute-done.halo_ref
  22.0 0.9 %collective-permute-done.1.theirs_ref = f32[16,128]{1,0:T(8,128)S(1)} collective-permute-done((f32[16,128]{1,0:T(8,128)S(1)}, f32[16,128]{1,0:T(8,128)S(1)}, u32[]{:S(2)}, u32[]{:S(2)}) %collective-permute-start.1) | collective-permute-done | bytes 8224 | tf_op jit(solution)/shard_map/ppermute | solution.py:500
  22.9 0.0 copy-start.1
  22.9 3.7 %near.1.own_ref = f32[2,16,768]{2,1,0:T(8,128)S(1)} custom-call(bf16[6,16,768]{2,1,0:T(8,128)(2,1)S(1)} %get-tuple-element.18.slip_ref, f32[6,4,256]{2,1,0:T(4,128)S(1)} %get-tuple-element.19.place_ref, f32[16,128]{1,0:T(8,128)S(1)} %totals.1.mine_ref, f32[16,128]{1,0:T(8,128)S(1)} %collective-permute-done.1.theirs_ref, f32[8,128]{1,0:T(8,128)S(1)} %get-tuple-element.23.after_ref), custom_call_target="tpu_custom_call" | custom-call | flops 1000000000 | bytes 1000000 | tf_op jit(solution)/shard_map/near/pallas_call | solution.py:502
  26.6 0.3 collective-permute-start.2
  26.9 1.0 %collective-permute-done.2.other_ref = f32[2,16,768]{2,1,0:T(8,128)S(1)} collective-permute-done((f32[2,16,768]{2,1,0:T(8,128)S(1)}, f32[2,16,768]{2,1,0:T(8,128)S(1)}, u32[]{:S(2)}, u32[]{:S(2)}) %collective-permute-start.2) | collective-permute-done | bytes 98336 | tf_op jit(solution)/shard_map/ppermute | solution.py:518
  27.9 1.4 %all-to-all-done.1.far_ref = bf16[32,16,128]{2,1,0:T(8,128)(2,1)S(1)} async-done(((bf16[32,16,128]{2,1,0:T(8,128)(2,1)}), bf16[32,16,128]{2,1,0:T(8,128)(2,1)S(1)}, u32[]{:S(2)}, u32[]{:S(2)}) %all-to-all-start.1) | async-done | bytes 131104 | tf_op jit(solution)/shard_map/all_to_all | solution.py:488
  29.4 0.0 copy-done.1
  29.4 0.9 %finish.1 = f32[4,16,768]{2,1,0:T(8,128)} custom-call(f32[2,16,768]{2,1,0:T(8,128)S(1)} %near.1.own_ref, f32[2,16,768]{2,1,0:T(8,128)S(1)} %collective-permute-done.2.other_ref, bf16[32,16,128]{2,1,0:T(8,128)(2,1)S(1)} %all-to-all-done.1.far_ref, bf16[4,32,768]{2,1,0:T(8,128)(2,1)S(1)} %copy-done.1), custom_call_target="tpu_custom_call" | custom-call | tf_op jit(solution)/shard_map/finish/pallas_call | solution.py:520
  (2 shorter events, 0.1 us)
Async XLA Ops:
  0.7 10.9 %copy-start = (f32[4,16,768]{2,1,0:T(8,128)S(1)}, f32[4,16,768]{2,1,0:T(8,128)}, u32[]{:S(2)}) copy-start(f32[4,16,768]{2,1,0:T(8,128)} %slip_ref.1) | copy-start | bytes 589828
  2.6 9.0 %copy-start.2 = (s32[3,1024]{1,0:T(4,128)S(1)}, s32[3,1024]{1,0:T(4,128)}, u32[]{:S(2)}) copy-start(s32[3,1024]{1,0:T(4,128)} %triangles_ref.1) | copy-start | bytes 36868
  2.6 9.0 %copy-start.3 = (f32[3,561]{1,0:T(4,128)S(1)}, f32[3,561]{1,0:T(4,128)}, u32[]{:S(2)}) copy-start(f32[3,561]{1,0:T(4,128)} %vertices_ref.1) | copy-start | bytes 20200
  2.6 9.0 %copy-start.4 = (s32[4,256]{1,0:T(4,128)S(1)}, s32[4,256]{1,0:T(4,128)}, u32[]{:S(2)}) copy-start(s32[4,256]{1,0:T(4,128)} %map_ref.1) | copy-start | bytes 12292
  2.6 13.6 %all-to-all-start = ((bf16[16,16,128]{2,1,0:T(8,128)(2,1)}), bf16[16,16,128]{2,1,0:T(8,128)(2,1)S(1)}, u32[]{:S(2)}, u32[]{:S(2)}) async-start(bf16[16,16,128]{2,1,0:T(8,128)(2,1)} %coeffs.1.after_ref), calls=%async_computation | async-start | bytes 131072 | tf_op jit(solution)/shard_map/all_to_all | solution.py:421
  11.6 2.8 %copy-start.6 = (bf16[16,1024]{1,0:T(8,128)(2,1)S(1)}, bf16[16,1024]{1,0:T(8,128)(2,1)}, u32[]{:S(2)}) copy-start(bf16[16,1024]{1,0:T(8,128)(2,1)} %param.16) | copy-start | bytes 98308
  11.8 2.7 %copy-start.5 = (s32[2,16]{1,0:T(2,128)S(1)}, s32[2,16]{1,0:T(2,128)}, u32[]{:S(2)}) copy-start(s32[2,16]{1,0:T(2,128)} %pairs_ref.1) | copy-start | bytes 388
  11.9 10.1 %collective-permute-start = (bf16[2,16,1024]{2,1,0:T(8,128)(2,1)S(1)}, bf16[2,16,1024]{2,1,0:T(8,128)(2,1)S(1)}, u32[]{:S(2)}, u32[]{:S(2)}) collective-permute-start(bf16[2,16,1024]{2,1,0:T(8,128)(2,1)S(1)} %get-tuple-element.17), channel_id=1, source_target_pairs={{0,1},{1,2},{2,3},{3,4},{4,5},{5,6},{6,7},{9,8},{10,9},{11,10},{12... | collective-permute-start | bytes 196616 | tf_op jit(solution)/shard_map/ppermute | solution.py:446
  18.0 11.3 %all-to-all-start.1 = ((bf16[32,16,128]{2,1,0:T(8,128)(2,1)}), bf16[32,16,128]{2,1,0:T(8,128)(2,1)S(1)}, u32[]{:S(2)}, u32[]{:S(2)}) async-start(bf16[32,16,128]{2,1,0:T(8,128)(2,1)} %get-tuple-element.24), calls=%async_computation.1 | async-start | bytes 262144 | tf_op jit(solution)/shard_map/all_to_all | solution.py:488
  21.7 1.2 %collective-permute-start.1 = (f32[16,128]{1,0:T(8,128)S(1)}, f32[16,128]{1,0:T(8,128)S(1)}, u32[]{:S(2)}, u32[]{:S(2)}) collective-permute-start(f32[16,128]{1,0:T(8,128)S(1)} %totals.1.mine_ref), channel_id=1, source_target_pairs={{0,8},{8,0},{16,24},{24,16},{1,9},{9,1},{17,25},{25,17},{2,10},{10... | collective-permute-start | bytes 24584 | tf_op jit(solution)/shard_map/ppermute | solution.py:500
  22.9 6.5 %copy-start.1 = (bf16[4,32,768]{2,1,0:T(8,128)(2,1)S(1)}, bf16[4,32,768]{2,1,0:T(8,128)(2,1)}, u32[]{:S(2)}) copy-start(bf16[4,32,768]{2,1,0:T(8,128)(2,1)} %basis_ref.1) | copy-start | bytes 589828
  26.6 1.4 %collective-permute-start.2 = (f32[2,16,768]{2,1,0:T(8,128)S(1)}, f32[2,16,768]{2,1,0:T(8,128)S(1)}, u32[]{:S(2)}, u32[]{:S(2)}) collective-permute-start(f32[2,16,768]{2,1,0:T(8,128)S(1)} %near.1.own_ref), channel_id=1, source_target_pairs={{0,8},{8,0},{16,24},{24,16},{1,9},{9,1},{17,25},{25,17},{2,10},{10... | collective-permute-start | bytes 294920 | tf_op jit(solution)/shard_map/ppermute | solution.py:518

commit v18 on v13

--- a/solution.py
+++ b/solution.py
@@ -269,8 +269,11 @@
     apply(slots - 1, [NEARC - 1], odd_ref)
 
 
-def coupling_kernel(coupling_ref, pairs_ref, after_ref, to_second_ref, to_first_ref, list_ref):
-    list_ref[...] = pairs_ref[...]
+def coupling_kernel(
+    coupling_ref, pairs_ref, after_ref, to_second_ref, to_first_ref, list_ref, *, clusters, long_count
+):
+    owner, group = pairs_ref[...] // clusters, pairs_ref[...] % clusters
+    list_ref[...] = jnp.concatenate([group * long_count + owner, owner, group], axis=0)
     pair_count, rank_size, _ = coupling_ref.shape
     groups = LANES // rank_size
     for pair_id in range(pair_count):
@@ -291,8 +294,8 @@
     for total_ref in total_refs:
         total_ref[...] = jnp.zeros(total_ref.shape, jnp.float32)
 
-    def coeff_of(cluster, group):
-        whole = coeff_ref[(cluster % clusters) * long_count + cluster // clusters]
+    def coeff_of(at, group):
+        whole = coeff_ref[at]
         whole = whole.astype(jnp.float32)
         low = pltpu.roll(whole, rank_size * group, 1) if group else whole
         high = pltpu.roll(whole, (rank_size * (group - 1)) % LANES, 1) if group != 1 else whole
@@ -313,11 +316,12 @@
             )
             for turn, f in enumerate(pair_ids):
                 results.append(
-                    (pairs_ref[target, f], value[turn * rhs_count : (turn + 1) * rhs_count])
+                    (target, f, value[turn * rhs_count : (turn + 1) * rhs_count])
                 )
-    for turn, (cluster, value) in enumerate(results):
+    for turn, (target, f, value) in enumerate(results):
         total_ref = total_refs[turn % len(total_refs)]
-        total_ref[cluster // clusters] += jnp.where(group_id == cluster % clusters, value, 0.0)
+        owner, group = pairs_ref[2 + target, f], pairs_ref[4 + target, f]
+        total_ref[owner] += jnp.where(group_id == group, value, 0.0)
     total = total_refs[0][...]
     for total_ref in total_refs[1:]:
         total = total + total_ref[...]
@@ -427,9 +431,9 @@
     )(xs, geometry, halo)
 
     to_second, to_first, pair_list = pl.pallas_call(
-        coupling_kernel,
+        functools.partial(coupling_kernel, clusters=clusters, long_count=long_count),
         out_shape=[jax.ShapeDtypeStruct((coupling.shape[0] * rank_size, LANES), jnp.bfloat16)] * 2
-        + [jax.ShapeDtypeStruct(far_pairs.shape, far_pairs.dtype)],
+        + [jax.ShapeDtypeStruct((6,) + far_pairs.shape[1:], far_pairs.dtype)],
         in_specs=[VMEM, VMEM, ANY],
         out_specs=[VMEM] * 3,
         compiler_params=pltpu.CompilerParams(vmem_limit_bytes=16 << 20),

time: 30.3 us -> 30.2 us (level)
  no operation moved by 1% of the time
where the time goes in v18:
time: 30.2 us; the launch traced here: 29.9 us
  starting transfers between devices  13.7 us (45%)
  Pallas kernels  8.55 us (28%)
  waiting for transfers between devices  6.55 us (22%)
  between operations  0.84 us (3%)
    all_to_all x1, starting transfers between devices, shards(): everyone = lax.all_to_all(pay, ('row', 'long'), 0, 0, tiled=True)  7.3 us
    ppermute x1, starting transfers between devices, shards(): halo = lax.ppermute(to_neighbour, ('row', 'long'), route)  3.68 us
    pallas_call x1, Pallas kernels, shards(): pl.pallas_call(functools.partial(near_kernel, long_count=long_count, clus...  3.66 us
    all_to_all x1, waiting for transfers between devices, shards(): everyone = lax.all_to_all(pay, ('row', 'long'), 0, 0, tiled=True)  2.71 us
    all_to_all x1, waiting for transfers between devices, shards(): far_terms = lax.all_to_all(far, ('row', 'long'), 0, 0, tiled=True)  2.65 us
    all_to_all x1, starting transfers between devices, shards(): far_terms = lax.all_to_all(far, ('row', 'long'), 0, 0, tiled=True)  2.59 us
    pallas_call x1, Pallas kernels, shards(): pl.pallas_call(coeffs_kernel, out_shape=jax.ShapeDtypeStruct((devices, rh...  1.76 us
    pallas_call x1, Pallas kernels, shards(): pl.pallas_call(functools.partial(far_kernel, clusters=clusters), out_shap...  1.55 us
  transfers between devices with their start and end apart: 4, of which 3 were waited for; matrix products, arithmetic and copies ran while one was open for 0% of the time, Pallas kernels for 20%

profile of v18, /device:TPU:0, one launch (start us, length us, event | category | flops | bytes accessed | tf_op | source)
XLA Modules:
  0.0 29.9 jit_solution(763905233540760676)
XLA Ops:
  0.7 0.0 copy-start
  0.7 1.8 %coeffs.1.after_ref = bf16[32,8,128]{2,1,0:T(8,128)(2,1)} custom-call(f32[4,16,768]{2,1,0:T(8,128)} %slip_ref.1, bf16[4,32,768]{2,1,0:T(8,128)(2,1)} %basis_ref.1, s32[2,20]{1,0:T(2,128)} %pairs_hbm.1, s32[1]{0:T(128)S(6)} %copy.10.count_ref), custom_call_target="tpu_custom_call" | custom-call | tf_op jit(solution)/shard_map/coeffs/pallas_call | solution.py:373
  2.4 0.0 copy-start.2
  2.4 0.0 copy-start.3
  2.5 0.0 copy-start.4
  2.5 7.3 %all-to-all-start = ((bf16[32,8,128]{2,1,0:T(8,128)(2,1)}), bf16[32,8,128]{2,1,0:T(8,128)(2,1)S(1)}, u32[]{:S(2)}, u32[]{:S(2)}) async-start(bf16[32,8,128]{2,1,0:T(8,128)(2,1)} %coeffs.1.after_ref), calls=%async_computation | async-start | bytes 131072 | tf_op jit(solution)/shard_map/all_to_all | solution.py:395
  9.8 0.0 copy-done
  9.8 0.0 copy-done.2
  9.8 0.0 copy-done.3
  9.8 0.0 copy-done.4
  9.8 0.0 copy-start.6
  9.8 0.3 geometry.1
  10.1 0.0 copy-start.5
  10.1 3.7 %collective-permute-start = (bf16[2,16,1024]{2,1,0:T(8,128)(2,1)S(1)}, bf16[2,16,1024]{2,1,0:T(8,128)(2,1)S(1)}, u32[]{:S(2)}, u32[]{:S(2)}) collective-permute-start(bf16[2,16,1024]{2,1,0:T(8,128)(2,1)S(1)} %get-tuple-element.17), channel_id=1, source_target_pairs={{0,1},{1,2},{2,3},{3,4},{4,5},{5,6},{6,7},{9,8},{10,9},{11,10},{12... | collective-permute-start | bytes 196616 | tf_op jit(solution)/shard_map/ppermute | solution.py:418
  13.8 0.0 copy-done.6
  13.8 0.1 reshape.3.coupling_ref
  14.0 0.0 copy-done.5
  14.0 0.4 %coupling.1 = (bf16[512,128]{1,0:T(8,128)(2,1)S(1)}, bf16[512,128]{1,0:T(8,128)(2,1)S(1)}, s32[6,16]{1,0:T(8,128)S(1)}) custom-call(bf16[16,32,32]{2,1,0:T(8,128)(2,1)S(1)} %reshape.3.coupling_ref, s32[2,16]{1,0:T(2,128)S(1)} %copy-done.5, bf16[32,8,128]{2,1,0:T(8,128)(2,1)} %coeffs.1.after_ref), custom_call_target="tpu_custom_call" | custom-call | flops 1000 | bytes 1000 | tf_op jit(solution)/shard_map/coupling/pallas_call | solution.py:433
  14.3 2.7 %all-to-all-done.coeff_ref.pay_ref = bf16[32,8,128]{2,1,0:T(8,128)(2,1)S(1)} async-done(((bf16[32,8,128]{2,1,0:T(8,128)(2,1)}), bf16[32,8,128]{2,1,0:T(8,128)(2,1)S(1)}, u32[]{:S(2)}, u32[]{:S(2)}) %all-to-all-start) | async-done | bytes 65568 | tf_op jit(solution)/shard_map/all_to_all | solution.py:395
  17.1 1.6 %far.1 = (bf16[32,16,128]{2,1,0:T(8,128)(2,1)}, f32[8,128]{1,0:T(8,128)S(1)}) custom-call(s32[6,16]{1,0:T(8,128)S(1)} %get-tuple-element.20.pairs_ref, bf16[32,8,128]{2,1,0:T(8,128)(2,1)S(1)} %all-to-all-done.coeff_ref.pay_ref, bf16[512,128]{1,0:T(8,128)(2,1)S(1)} %get-tuple-element.21.to_second_ref, bf16[512,128]{1,0:T(8,128)(2,1)S(1)} %get-tuple-element.22.to_first_ref), custom_call_target="tpu_custom_call" | custom-call | tf_op jit(solution)/shard_map/far/pallas_call | solution.py:443
  18.6 2.6 %all-to-all-start.1 = ((bf16[32,16,128]{2,1,0:T(8,128)(2,1)}), bf16[32,16,128]{2,1,0:T(8,128)(2,1)S(1)}, u32[]{:S(2)}, u32[]{:S(2)}) async-start(bf16[32,16,128]{2,1,0:T(8,128)(2,1)} %get-tuple-element.24), calls=%async_computation.1 | async-start | bytes 262144 | tf_op jit(solution)/shard_map/all_to_all | solution.py:459
  21.2 0.0 collective-permute-done.halo_ref
  21.3 0.0 copy-start.1
  21.3 3.7 %near.1.own_ref = f32[2,16,768]{2,1,0:T(8,128)S(1)} custom-call(bf16[6,16,768]{2,1,0:T(8,128)(2,1)S(1)} %get-tuple-element.18.slip_ref, f32[6,4,256]{2,1,0:T(4,128)S(1)} %get-tuple-element.19.place_ref, bf16[32,8,128]{2,1,0:T(8,128)(2,1)S(1)} %all-to-all-done.coeff_ref.pay_ref, f32[8,128]{1,0:T(8,128)S(1)} %get-tuple-element.23.after_ref), custom_call_target="tpu_custom_call" | custom-call | flops 1000000000 | bytes 1000000 | tf_op jit(solution)/shard_map/near/pallas_call | solution.py:461
  25.0 0.2 collective-permute-start.1
  25.1 1.2 %collective-permute-done.1.other_ref = f32[2,16,768]{2,1,0:T(8,128)S(1)} collective-permute-done((f32[2,16,768]{2,1,0:T(8,128)S(1)}, f32[2,16,768]{2,1,0:T(8,128)S(1)}, u32[]{:S(2)}, u32[]{:S(2)}) %collective-permute-start.1) | collective-permute-done | bytes 98336 | tf_op jit(solution)/shard_map/ppermute | solution.py:478
  26.3 2.7 %all-to-all-done.1.far_ref = bf16[32,16,128]{2,1,0:T(8,128)(2,1)S(1)} async-done(((bf16[32,16,128]{2,1,0:T(8,128)(2,1)}), bf16[32,16,128]{2,1,0:T(8,128)(2,1)S(1)}, u32[]{:S(2)}, u32[]{:S(2)}) %all-to-all-start.1) | async-done | bytes 131104 | tf_op jit(solution)/shard_map/all_to_all | solution.py:459
  29.0 0.0 copy-done.1
  29.0 0.9 %finish.1 = f32[4,16,768]{2,1,0:T(8,128)} custom-call(f32[2,16,768]{2,1,0:T(8,128)S(1)} %near.1.own_ref, f32[2,16,768]{2,1,0:T(8,128)S(1)} %collective-permute-done.1.other_ref, bf16[32,16,128]{2,1,0:T(8,128)(2,1)S(1)} %all-to-all-done.1.far_ref, bf16[4,32,768]{2,1,0:T(8,128)(2,1)S(1)} %copy-done.1), custom_call_target="tpu_custom_call" | custom-call | tf_op jit(solution)/shard_map/finish/pallas_call | solution.py:480
  (1 shorter events, 0.0 us)
Async XLA Ops:
  0.7 9.1 %copy-start = (f32[4,16,768]{2,1,0:T(8,128)S(1)}, f32[4,16,768]{2,1,0:T(8,128)}, u32[]{:S(2)}) copy-start(f32[4,16,768]{2,1,0:T(8,128)} %slip_ref.1) | copy-start | bytes 589828
  2.4 7.4 %copy-start.2 = (s32[3,1024]{1,0:T(4,128)S(1)}, s32[3,1024]{1,0:T(4,128)}, u32[]{:S(2)}) copy-start(s32[3,1024]{1,0:T(4,128)} %triangles_ref.1) | copy-start | bytes 36868
  2.4 7.4 %copy-start.3 = (f32[3,561]{1,0:T(4,128)S(1)}, f32[3,561]{1,0:T(4,128)}, u32[]{:S(2)}) copy-start(f32[3,561]{1,0:T(4,128)} %vertices_ref.1) | copy-start | bytes 20200
  2.5 7.4 %copy-start.4 = (s32[4,256]{1,0:T(4,128)S(1)}, s32[4,256]{1,0:T(4,128)}, u32[]{:S(2)}) copy-start(s32[4,256]{1,0:T(4,128)} %map_ref.1) | copy-start | bytes 12292
  2.5 14.6 %all-to-all-start = ((bf16[32,8,128]{2,1,0:T(8,128)(2,1)}), bf16[32,8,128]{2,1,0:T(8,128)(2,1)S(1)}, u32[]{:S(2)}, u32[]{:S(2)}) async-start(bf16[32,8,128]{2,1,0:T(8,128)(2,1)} %coeffs.1.after_ref), calls=%async_computation | async-start | bytes 131072 | tf_op jit(solution)/shard_map/all_to_all | solution.py:395
  9.8 4.0 %copy-start.6 = (bf16[16,1024]{1,0:T(8,128)(2,1)S(1)}, bf16[16,1024]{1,0:T(8,128)(2,1)}, u32[]{:S(2)}) copy-start(bf16[16,1024]{1,0:T(8,128)(2,1)} %param.16) | copy-start | bytes 98308
  10.1 3.9 %copy-start.5 = (s32[2,16]{1,0:T(2,128)S(1)}, s32[2,16]{1,0:T(2,128)}, u32[]{:S(2)}) copy-start(s32[2,16]{1,0:T(2,128)} %pairs_ref.1) | copy-start | bytes 388
  10.1 11.1 %collective-permute-start = (bf16[2,16,1024]{2,1,0:T(8,128)(2,1)S(1)}, bf16[2,16,1024]{2,1,0:T(8,128)(2,1)S(1)}, u32[]{:S(2)}, u32[]{:S(2)}) collective-permute-start(bf16[2,16,1024]{2,1,0:T(8,128)(2,1)S(1)} %get-tuple-element.17), channel_id=1, source_target_pairs={{0,1},{1,2},{2,3},{3,4},{4,5},{5,6},{6,7},{9,8},{10,9},{11,10},{12... | collective-permute-start | bytes 196616 | tf_op jit(solution)/shard_map/ppermute | solution.py:418
  18.6 10.3 %all-to-all-start.1 = ((bf16[32,16,128]{2,1,0:T(8,128)(2,1)}), bf16[32,16,128]{2,1,0:T(8,128)(2,1)S(1)}, u32[]{:S(2)}, u32[]{:S(2)}) async-start(bf16[32,16,128]{2,1,0:T(8,128)(2,1)} %get-tuple-element.24), calls=%async_computation.1 | async-start | bytes 262144 | tf_op jit(solution)/shard_map/all_to_all | solution.py:459
  21.3 7.7 %copy-start.1 = (bf16[4,32,768]{2,1,0:T(8,128)(2,1)S(1)}, bf16[4,32,768]{2,1,0:T(8,128)(2,1)}, u32[]{:S(2)}) copy-start(bf16[4,32,768]{2,1,0:T(8,128)(2,1)} %basis_ref.1) | copy-start | bytes 589828
  25.0 1.4 %collective-permute-start.1 = (f32[2,16,768]{2,1,0:T(8,128)S(1)}, f32[2,16,768]{2,1,0:T(8,128)S(1)}, u32[]{:S(2)}, u32[]{:S(2)}) collective-permute-start(f32[2,16,768]{2,1,0:T(8,128)S(1)} %near.1.own_ref), channel_id=1, source_target_pairs={{0,8},{8,0},{16,24},{24,16},{1,9},{9,1},{17,25},{25,17},{2,10},{10... | collective-permute-start | bytes 294920 | tf_op jit(solution)/shard_map/ppermute | solution.py:478

commit v19 on v17

--- a/solution.py
+++ b/solution.py
@@ -21,7 +21,7 @@
 
 
 def first_place(row_count, long_count):
-    return row_count // 2 * long_count // 2 + long_count // 2 - 1
+    return row_count // 2 * long_count - 1
 
 
 def same_core(row_count, long_count):
@@ -291,8 +291,13 @@
     apply(slots - 1, [NEARC - 1], odd_ref)
 
 
-def coupling_kernel(coupling_ref, pairs_ref, after_ref, to_second_ref, to_first_ref, list_ref):
-    list_ref[...] = pairs_ref[...]
+def coupling_kernel(
+    coupling_ref, pairs_ref, after_ref, to_second_ref, to_first_ref, list_ref, *, clusters, long_count, row_count
+):
+    share = clusters // 2
+    owner, group = pairs_ref[...] // clusters, pairs_ref[...] % clusters
+    at = place_in_core(group // share, owner, row_count, long_count) * share + group % share
+    list_ref[...] = jnp.concatenate([at, owner, group], axis=0)
     pair_count, rank_size, _ = coupling_ref.shape
     groups = LANES // rank_size
     for pair_id in range(pair_count):
@@ -322,9 +327,8 @@
                 pltpu.roll(whole, LANES - rank_size * turn, 1) if turn else whole
             )
 
-    def coeff_of(cluster, group):
-        at = place_in_core(cluster % clusters // share, cluster // clusters, row_count, long_count)
-        whole = moved_ref[at * share + cluster % share]
+    def coeff_of(at, group):
+        whole = moved_ref[at]
         both = pltpu.roll(whole, rank_size * group, 1) if group else whole
         return jnp.where(group_id == group, both, 0.0)
 
@@ -342,11 +346,12 @@
             )
             for turn, f in enumerate(pair_ids):
                 results.append(
-                    (pairs_ref[target, f], value[turn * rhs_count : (turn + 1) * rhs_count])
+                    (target, f, value[turn * rhs_count : (turn + 1) * rhs_count])
                 )
-    for turn, (cluster, value) in enumerate(results):
+    for turn, (target, f, value) in enumerate(results):
         total_ref = total_refs[turn % len(total_refs)]
-        total_ref[cluster // clusters] += jnp.where(group_id == cluster % clusters, value, 0.0)
+        owner, group = pairs_ref[2 + target, f], pairs_ref[4 + target, f]
+        total_ref[owner] += jnp.where(group_id == group, value, 0.0)
     total = total_refs[0][...]
     for total_ref in total_refs[1:]:
         total = total + total_ref[...]
@@ -459,9 +464,11 @@
     )(xs, geometry, halo)
 
     to_second, to_first, pair_list = pl.pallas_call(
-        coupling_kernel,
+        functools.partial(
+            coupling_kernel, clusters=clusters, long_count=long_count, row_count=row_count
+        ),
         out_shape=[jax.ShapeDtypeStruct((coupling.shape[0] * rank_size, LANES), jnp.bfloat16)] * 2
-        + [jax.ShapeDtypeStruct(far_pairs.shape, far_pairs.dtype)],
+        + [jax.ShapeDtypeStruct((6,) + far_pairs.shape[1:], far_pairs.dtype)],
         in_specs=[VMEM, VMEM, ANY],
         out_specs=[VMEM] * 3,
         compiler_params=pltpu.CompilerParams(vmem_limit_bytes=16 << 20),

time: 30.6 us -> 31.8 us (1.039)
  starting transfers between devices: 15.6 us -> 18.3 us
  waiting for transfers between devices: 4.63 us -> 3.36 us
    all_to_all x1, starting transfers between devices: 8.93 us -> 10.4 us  [shards(): lax.all_to_all(pay, ('row', 'long'), 0, 0, axis_index_groups=same_core(ro...]
    all_to_all x1, waiting for transfers between devices: 1.27 us -> 0.01 us  [shards(): lax.all_to_all(pay, ('row', 'long'), 0, 0, axis_index_groups=same_core(ro...]
    all_to_all x1, starting transfers between devices: 3.58 us -> 4.84 us  [shards(): far_terms = lax.all_to_all(far, ('row', 'long'), 0, 0, tiled=True)]
  transfers between devices with their start and end apart: 5 -> 5, of which waited for: 4 -> 3; matrix products, arithmetic and copies ran while one was open for 0% -> 0% of each run, Pallas kernels for 21% -> 19%
where the time goes in v19:
time: 31.8 us; the launch traced here: 31.5 us
  starting transfers between devices  18.3 us (58%)
  Pallas kernels  8.8 us (28%)
  waiting for transfers between devices  3.36 us (11%)
  between operations  0.82 us (3%)
    all_to_all x1, starting transfers between devices, shards(): lax.all_to_all(pay, ('row', 'long'), 0, 0, axis_index_groups=same_core(ro...  10.4 us
    all_to_all x1, starting transfers between devices, shards(): far_terms = lax.all_to_all(far, ('row', 'long'), 0, 0, tiled=True)  4.84 us
    pallas_call x1, Pallas kernels, shards(): pl.pallas_call(functools.partial(near_kernel, clusters=clusters), out_sha...  3.68 us
    ppermute x1, starting transfers between devices, shards(): halo = lax.ppermute(to_neighbour, ('row', 'long'), route)  2.48 us
    pallas_call x1, Pallas kernels, shards(): pl.pallas_call(coeffs_kernel, out_shape=jax.ShapeDtypeStruct((devices //...  1.89 us
    pallas_call x1, Pallas kernels, shards(): pl.pallas_call(functools.partial(far_kernel, clusters=clusters), out_shap...  1.65 us
    all_to_all x1, waiting for transfers between devices, shards(): far_terms = lax.all_to_all(far, ('row', 'long'), 0, 0, tiled=True)  1.44 us
    ppermute x1, waiting for transfers between devices, shards(): other = lax.ppermute(near, 'row', partner)  1.05 us
  transfers between devices with their start and end apart: 5, of which 3 were waited for; matrix products, arithmetic and copies ran while one was open for 0% of the time, Pallas kernels for 19%

profile of v19, /device:TPU:0, one launch (start us, length us, event | category | flops | bytes accessed | tf_op | source)
XLA Modules:
  0.0 31.5 jit_solution(2347388490358115035)
XLA Ops:
  0.7 0.0 copy-start
  0.7 1.9 %coeffs.1.after_ref = bf16[16,16,128]{2,1,0:T(8,128)(2,1)} custom-call(f32[4,16,768]{2,1,0:T(8,128)} %slip_ref.1, bf16[4,32,768]{2,1,0:T(8,128)(2,1)} %basis_ref.1, s32[2,20]{1,0:T(2,128)} %pairs_hbm.1, s32[1]{0:T(128)S(6)} %copy.10.count_ref), custom_call_target="tpu_custom_call" | custom-call | tf_op jit(solution)/shard_map/coeffs/pallas_call | solution.py:404
  2.6 0.0 copy-start.2
  2.6 0.0 copy-start.3
  2.6 0.0 copy-start.4
  2.6 10.4 %all-to-all-start = ((bf16[16,16,128]{2,1,0:T(8,128)(2,1)}), bf16[16,16,128]{2,1,0:T(8,128)(2,1)S(1)}, u32[]{:S(2)}, u32[]{:S(2)}) async-start(bf16[16,16,128]{2,1,0:T(8,128)(2,1)} %coeffs.1.after_ref), calls=%async_computation | async-start | bytes 131072 | tf_op jit(solution)/shard_map/all_to_all | solution.py:426
  13.0 0.0 copy-done
  13.0 0.0 copy-done.2
  13.0 0.0 copy-done.3
  13.0 0.0 copy-done.4
  13.0 0.0 copy-start.6
  13.0 0.3 geometry.1
  13.3 0.0 copy-start.5
  13.3 2.5 %collective-permute-start = (bf16[2,16,1024]{2,1,0:T(8,128)(2,1)S(1)}, bf16[2,16,1024]{2,1,0:T(8,128)(2,1)S(1)}, u32[]{:S(2)}, u32[]{:S(2)}) collective-permute-start(bf16[2,16,1024]{2,1,0:T(8,128)(2,1)S(1)} %get-tuple-element.17), channel_id=1, source_target_pairs={{0,1},{1,2},{2,3},{3,4},{4,5},{5,6},{6,7},{9,8},{10,9},{11,10},{12... | collective-permute-start | bytes 196616 | tf_op jit(solution)/shard_map/ppermute | solution.py:451
  15.8 0.0 copy-done.6
  15.8 0.1 reshape.3.coupling_ref
  15.9 0.0 copy-done.5
  15.9 0.4 %coupling.1 = (bf16[512,128]{1,0:T(8,128)(2,1)S(1)}, bf16[512,128]{1,0:T(8,128)(2,1)S(1)}, s32[6,16]{1,0:T(8,128)S(1)}) custom-call(bf16[16,32,32]{2,1,0:T(8,128)(2,1)S(1)} %reshape.3.coupling_ref, s32[2,16]{1,0:T(2,128)S(1)} %copy-done.5, bf16[16,16,128]{2,1,0:T(8,128)(2,1)} %coeffs.1.after_ref), custom_call_target="tpu_custom_call" | custom-call | flops 1000 | bytes 1000 | tf_op jit(solution)/shard_map/coupling/pallas_call | solution.py:466
  16.3 0.0 all-to-all-done.pay_ref.coeff_ref
  16.3 1.6 %far.1 = (bf16[32,16,128]{2,1,0:T(8,128)(2,1)}, f32[8,128]{1,0:T(8,128)S(1)}) custom-call(s32[6,16]{1,0:T(8,128)S(1)} %get-tuple-element.20.pairs_ref, bf16[16,16,128]{2,1,0:T(8,128)(2,1)S(1)} %all-to-all-done.pay_ref.coeff_ref, bf16[512,128]{1,0:T(8,128)(2,1)S(1)} %get-tuple-element.21.to_second_ref, bf16[512,128]{1,0:T(8,128)(2,1)S(1)} %get-tuple-element.22.to_first_ref), custom_call_target="tpu_custom_call" | custom-call | tf_op jit(solution)/shard_map/far/pallas_call | solution.py:478
  18.0 4.8 %all-to-all-start.1 = ((bf16[32,16,128]{2,1,0:T(8,128)(2,1)}), bf16[32,16,128]{2,1,0:T(8,128)(2,1)S(1)}, u32[]{:S(2)}, u32[]{:S(2)}) async-start(bf16[32,16,128]{2,1,0:T(8,128)(2,1)} %get-tuple-element.24), calls=%async_computation.1 | async-start | bytes 262144 | tf_op jit(solution)/shard_map/all_to_all | solution.py:495
  22.9 0.3 %collective-permute-start.1 = (f32[16,128]{1,0:T(8,128)S(1)}, f32[16,128]{1,0:T(8,128)S(1)}, u32[]{:S(2)}, u32[]{:S(2)}) collective-permute-start(f32[16,128]{1,0:T(8,128)S(1)} %totals.1.mine_ref), channel_id=1, source_target_pairs={{0,8},{8,0},{16,24},{24,16},{1,9},{9,1},{17,25},{25,17},{2,10},{10... | collective-permute-start | bytes 24584 | tf_op jit(solution)/shard_map/ppermute | solution.py:507
  23.2 0.0 collective-permute-done.halo_ref
  23.2 0.9 %collective-permute-done.1.theirs_ref = f32[16,128]{1,0:T(8,128)S(1)} collective-permute-done((f32[16,128]{1,0:T(8,128)S(1)}, f32[16,128]{1,0:T(8,128)S(1)}, u32[]{:S(2)}, u32[]{:S(2)}) %collective-permute-start.1) | collective-permute-done | bytes 8224 | tf_op jit(solution)/shard_map/ppermute | solution.py:507
  24.1 0.0 copy-start.1
  24.1 3.7 %near.1.own_ref = f32[2,16,768]{2,1,0:T(8,128)S(1)} custom-call(bf16[6,16,768]{2,1,0:T(8,128)(2,1)S(1)} %get-tuple-element.18.slip_ref, f32[6,4,256]{2,1,0:T(4,128)S(1)} %get-tuple-element.19.place_ref, f32[16,128]{1,0:T(8,128)S(1)} %totals.1.mine_ref, f32[16,128]{1,0:T(8,128)S(1)} %collective-permute-done.1.theirs_ref, f32[8,128]{1,0:T(8,128)S(1)} %get-tuple-element.23.after_ref), custom_call_target="tpu_custom_call" | custom-call | flops 1000000000 | bytes 1000000 | tf_op jit(solution)/shard_map/near/pallas_call | solution.py:509
  27.8 0.3 collective-permute-start.2
  28.1 1.1 %collective-permute-done.2.other_ref = f32[2,16,768]{2,1,0:T(8,128)S(1)} collective-permute-done((f32[2,16,768]{2,1,0:T(8,128)S(1)}, f32[2,16,768]{2,1,0:T(8,128)S(1)}, u32[]{:S(2)}, u32[]{:S(2)}) %collective-permute-start.2) | collective-permute-done | bytes 98336 | tf_op jit(solution)/shard_map/ppermute | solution.py:525
  29.1 1.4 %all-to-all-done.1.far_ref = bf16[32,16,128]{2,1,0:T(8,128)(2,1)S(1)} async-done(((bf16[32,16,128]{2,1,0:T(8,128)(2,1)}), bf16[32,16,128]{2,1,0:T(8,128)(2,1)S(1)}, u32[]{:S(2)}, u32[]{:S(2)}) %all-to-all-start.1) | async-done | bytes 131104 | tf_op jit(solution)/shard_map/all_to_all | solution.py:495
  30.6 0.0 copy-done.1
  30.6 0.9 %finish.1 = f32[4,16,768]{2,1,0:T(8,128)} custom-call(f32[2,16,768]{2,1,0:T(8,128)S(1)} %near.1.own_ref, f32[2,16,768]{2,1,0:T(8,128)S(1)} %collective-permute-done.2.other_ref, bf16[32,16,128]{2,1,0:T(8,128)(2,1)S(1)} %all-to-all-done.1.far_ref, bf16[4,32,768]{2,1,0:T(8,128)(2,1)S(1)} %copy-done.1), custom_call_target="tpu_custom_call" | custom-call | tf_op jit(solution)/shard_map/finish/pallas_call | solution.py:527
  (2 shorter events, 0.1 us)
Async XLA Ops:
  0.7 12.3 %copy-start = (f32[4,16,768]{2,1,0:T(8,128)S(1)}, f32[4,16,768]{2,1,0:T(8,128)}, u32[]{:S(2)}) copy-start(f32[4,16,768]{2,1,0:T(8,128)} %slip_ref.1) | copy-start | bytes 589828
  2.6 10.4 %copy-start.2 = (s32[3,1024]{1,0:T(4,128)S(1)}, s32[3,1024]{1,0:T(4,128)}, u32[]{:S(2)}) copy-start(s32[3,1024]{1,0:T(4,128)} %triangles_ref.1) | copy-start | bytes 36868
  2.6 10.4 %copy-start.3 = (f32[3,561]{1,0:T(4,128)S(1)}, f32[3,561]{1,0:T(4,128)}, u32[]{:S(2)}) copy-start(f32[3,561]{1,0:T(4,128)} %vertices_ref.1) | copy-start | bytes 20200
  2.6 10.4 %copy-start.4 = (s32[4,256]{1,0:T(4,128)S(1)}, s32[4,256]{1,0:T(4,128)}, u32[]{:S(2)}) copy-start(s32[4,256]{1,0:T(4,128)} %map_ref.1) | copy-start | bytes 12292
  2.6 13.7 %all-to-all-start = ((bf16[16,16,128]{2,1,0:T(8,128)(2,1)}), bf16[16,16,128]{2,1,0:T(8,128)(2,1)S(1)}, u32[]{:S(2)}, u32[]{:S(2)}) async-start(bf16[16,16,128]{2,1,0:T(8,128)(2,1)} %coeffs.1.after_ref), calls=%async_computation | async-start | bytes 131072 | tf_op jit(solution)/shard_map/all_to_all | solution.py:426
  13.0 2.8 %copy-start.6 = (bf16[16,1024]{1,0:T(8,128)(2,1)S(1)}, bf16[16,1024]{1,0:T(8,128)(2,1)}, u32[]{:S(2)}) copy-start(bf16[16,1024]{1,0:T(8,128)(2,1)} %param.16) | copy-start | bytes 98308
  13.3 2.7 %copy-start.5 = (s32[2,16]{1,0:T(2,128)S(1)}, s32[2,16]{1,0:T(2,128)}, u32[]{:S(2)}) copy-start(s32[2,16]{1,0:T(2,128)} %pairs_ref.1) | copy-start | bytes 388
  13.3 9.9 %collective-permute-start = (bf16[2,16,1024]{2,1,0:T(8,128)(2,1)S(1)}, bf16[2,16,1024]{2,1,0:T(8,128)(2,1)S(1)}, u32[]{:S(2)}, u32[]{:S(2)}) collective-permute-start(bf16[2,16,1024]{2,1,0:T(8,128)(2,1)S(1)} %get-tuple-element.17), channel_id=1, source_target_pairs={{0,1},{1,2},{2,3},{3,4},{4,5},{5,6},{6,7},{9,8},{10,9},{11,10},{12... | collective-permute-start | bytes 196616 | tf_op jit(solution)/shard_map/ppermute | solution.py:451
  18.0 12.6 %all-to-all-start.1 = ((bf16[32,16,128]{2,1,0:T(8,128)(2,1)}), bf16[32,16,128]{2,1,0:T(8,128)(2,1)S(1)}, u32[]{:S(2)}, u32[]{:S(2)}) async-start(bf16[32,16,128]{2,1,0:T(8,128)(2,1)} %get-tuple-element.24), calls=%async_computation.1 | async-start | bytes 262144 | tf_op jit(solution)/shard_map/all_to_all | solution.py:495
  22.9 1.2 %collective-permute-start.1 = (f32[16,128]{1,0:T(8,128)S(1)}, f32[16,128]{1,0:T(8,128)S(1)}, u32[]{:S(2)}, u32[]{:S(2)}) collective-permute-start(f32[16,128]{1,0:T(8,128)S(1)} %totals.1.mine_ref), channel_id=1, source_target_pairs={{0,8},{8,0},{16,24},{24,16},{1,9},{9,1},{17,25},{25,17},{2,10},{10... | collective-permute-start | bytes 24584 | tf_op jit(solution)/shard_map/ppermute | solution.py:507
  24.1 6.5 %copy-start.1 = (bf16[4,32,768]{2,1,0:T(8,128)(2,1)S(1)}, bf16[4,32,768]{2,1,0:T(8,128)(2,1)}, u32[]{:S(2)}) copy-start(bf16[4,32,768]{2,1,0:T(8,128)(2,1)} %basis_ref.1) | copy-start | bytes 589828
  27.8 1.4 %collective-permute-start.2 = (f32[2,16,768]{2,1,0:T(8,128)S(1)}, f32[2,16,768]{2,1,0:T(8,128)S(1)}, u32[]{:S(2)}, u32[]{:S(2)}) collective-permute-start(f32[2,16,768]{2,1,0:T(8,128)S(1)} %near.1.own_ref), channel_id=1, source_target_pairs={{0,8},{8,0},{16,24},{24,16},{1,9},{9,1},{17,25},{25,17},{2,10},{10... | collective-permute-start | bytes 294920 | tf_op jit(solution)/shard_map/ppermute | solution.py:525

commit v20 on v18

--- a/solution.py
+++ b/solution.py
@@ -284,8 +284,11 @@
 
 
 def far_kernel(
-    pairs_ref, coeff_ref, to_second_ref, to_first_ref, out_hbm, done_ref, sent_ref, sems, *total_refs, clusters
+    list_ref, coeff_ref, to_second_ref, to_first_ref, out_hbm, done_ref, pairs_ref, moved_ref, sent_ref, sems,
+    *total_refs, clusters
 ):
+    fetch = pltpu.make_async_copy(list_ref, pairs_ref, sems.at[0])
+    fetch.start()
     done_ref[...] = jnp.zeros(done_ref.shape, jnp.float32)
     long_count, rhs_count, _ = total_refs[0].shape
     pair_count = pairs_ref.shape[1]
@@ -293,13 +296,14 @@
     group_id = lax.broadcasted_iota(jnp.int32, (rhs_count, LANES), 1) // rank_size
     for total_ref in total_refs:
         total_ref[...] = jnp.zeros(total_ref.shape, jnp.float32)
+    for at in range(coeff_ref.shape[0]):
+        whole = coeff_ref[at].astype(jnp.float32)
+        moved_ref[at] = jnp.concatenate([whole, pltpu.roll(whole, LANES - rank_size, 1)], axis=0)
+    fetch.wait()
 
     def coeff_of(at, group):
-        whole = coeff_ref[at]
-        whole = whole.astype(jnp.float32)
-        low = pltpu.roll(whole, rank_size * group, 1) if group else whole
-        high = pltpu.roll(whole, (rank_size * (group - 1)) % LANES, 1) if group != 1 else whole
-        both = jnp.concatenate([low, high], axis=0)
+        whole = moved_ref[at]
+        both = pltpu.roll(whole, rank_size * group, 1) if group else whole
         return jnp.where(group_id == group, both, 0.0)
 
     results = []
@@ -338,20 +342,30 @@
         copy.wait()
 
 
-def finish_kernel(own_ref, other_ref, far_ref, basis_ref, out_hbm, sent_ref, sems):
+def gather_near_kernel(own_ref, other_ref, out_ref):
+    even = lax.axis_index("row") % 2 == 0
+    for cluster in range(out_ref.shape[0]):
+        u = cluster % NEARC
+        here = even if cluster < NEARC else jnp.logical_not(even)
+        out_ref[cluster] = jnp.where(here, own_ref[u], other_ref[u])
+
+
+def finish_kernel(near_ref, far_ref, basis_ref, out_hbm, sent_ref, sems):
     clusters, rank_size, unknowns = basis_ref.shape
+    rhs_count = near_ref.shape[1]
     total = jnp.sum(far_ref[...].astype(jnp.float32), axis=0)
     group_id = lax.broadcasted_iota(jnp.int32, total.shape, 1) // rank_size
     flat_basis = basis_ref[...].reshape(clusters * rank_size, unknowns)
-    even = lax.axis_index("row") % 2 == 0
+    picked = [jnp.where(group_id == cluster, total, 0.0) for cluster in range(clusters)]
+    result = jnp.dot(
+        jnp.concatenate(picked, axis=0).astype(jnp.bfloat16),
+        flat_basis,
+        preferred_element_type=jnp.float32,
+    )
     copies = []
     for cluster in range(clusters):
-        u = cluster % NEARC
-        here = even if cluster < NEARC else jnp.logical_not(even)
-        near = jnp.where(here, own_ref[u], other_ref[u])
-        picked = jnp.where(group_id == cluster, total, 0.0).astype(jnp.bfloat16)
-        result = jnp.dot(picked, flat_basis, preferred_element_type=jnp.float32)
-        sent_ref[cluster] = result + near
+        far = result[cluster * rhs_count : (cluster + 1) * rhs_count]
+        sent_ref[cluster] = far + near_ref[cluster]
         copies.append(
             pltpu.make_async_copy(sent_ref.at[cluster], out_hbm.at[cluster], sems.at[cluster])
         )
@@ -446,9 +460,11 @@
             jax.ShapeDtypeStruct((devices, rhs_count, clusters * rank_size), jnp.bfloat16),
             jax.ShapeDtypeStruct((8, LANES), jnp.float32),
         ],
-        in_specs=[SMEM, VMEM, VMEM, VMEM],
+        in_specs=[VMEM] * 4,
         out_specs=[HBM, VMEM],
         scratch_shapes=[
+            pltpu.SMEM((6,) + far_pairs.shape[1:], far_pairs.dtype),
+            pltpu.VMEM((devices, rhs_count, LANES), jnp.float32),
             pltpu.VMEM((long_count, rhs_count, clusters * rank_size), jnp.bfloat16),
             pltpu.SemaphoreType.DMA((row_count,)),
         ]
@@ -477,10 +493,20 @@
     partner = [(row, row ^ 1) for row in range(row_count)]
     other = lax.ppermute(near, "row", partner)
 
+    near_field = pl.pallas_call(
+        gather_near_kernel,
+        out_shape=jax.ShapeDtypeStruct(slip.shape, jnp.float32),
+        in_specs=[VMEM] * 2,
+        out_specs=VMEM,
+        compiler_params=pltpu.CompilerParams(vmem_limit_bytes=16 << 20),
+        cost_estimate=pl.CostEstimate(flops=1000, bytes_accessed=1000, transcendentals=0),
+        name="gather_near",
+    )(near, other)
+
     return pl.pallas_call(
         finish_kernel,
         out_shape=jax.ShapeDtypeStruct(slip.shape, jnp.float32),
-        in_specs=[VMEM] * 4,
+        in_specs=[VMEM] * 3,
         out_specs=HBM,
         scratch_shapes=[
             pltpu.VMEM(slip.shape, jnp.float32),
@@ -488,7 +514,7 @@
         ],
         compiler_params=pltpu.CompilerParams(vmem_limit_bytes=16 << 20),
         name="finish",
-    )(near, other, far_terms, basis)
+    )(near_field, far_terms, basis)
 
 
 def solution(mesh):

time: 30.2 us -> 30.2 us (level)
  no operation moved by 1% of the time
where the time goes in v20:
time: 30.2 us; the launch traced here: 29.8 us
  starting transfers between devices  13.7 us (45%)
  Pallas kernels  8.57 us (28%)
  waiting for transfers between devices  6.5 us (22%)
  between operations  0.84 us (3%)
    all_to_all x1, starting transfers between devices, shards(): everyone = lax.all_to_all(pay, ('row', 'long'), 0, 0, tiled=True)  7.3 us
    pallas_call x1, Pallas kernels, shards(): pl.pallas_call(functools.partial(near_kernel, long_count=long_count, clus...  3.68 us
    ppermute x1, starting transfers between devices, shards(): halo = lax.ppermute(to_neighbour, ('row', 'long'), route)  3.68 us
    all_to_all x1, waiting for transfers between devices, shards(): everyone = lax.all_to_all(pay, ('row', 'long'), 0, 0, tiled=True)  2.71 us
    all_to_all x1, waiting for transfers between devices, shards(): far_terms = lax.all_to_all(far, ('row', 'long'), 0, 0, tiled=True)  2.6 us
    all_to_all x1, starting transfers between devices, shards(): far_terms = lax.all_to_all(far, ('row', 'long'), 0, 0, tiled=True)  2.59 us
    pallas_call x1, Pallas kernels, shards(): pl.pallas_call(coeffs_kernel, out_shape=jax.ShapeDtypeStruct((devices, rh...  1.76 us
    pallas_call x1, Pallas kernels, shards(): pl.pallas_call(functools.partial(far_kernel, clusters=clusters), out_shap...  1.54 us
  transfers between devices with their start and end apart: 4, of which 3 were waited for; matrix products, arithmetic and copies ran while one was open for 0% of the time, Pallas kernels for 20%

profile of v20, /device:TPU:0, one launch (start us, length us, event | category | flops | bytes accessed | tf_op | source)
XLA Modules:
  0.0 29.8 jit_solution(8835132653773989507)
XLA Ops:
  0.7 0.0 copy-start
  0.7 1.8 %coeffs.1.after_ref = bf16[32,8,128]{2,1,0:T(8,128)(2,1)} custom-call(f32[4,16,768]{2,1,0:T(8,128)} %slip_ref.1, bf16[4,32,768]{2,1,0:T(8,128)(2,1)} %basis_ref.1, s32[2,20]{1,0:T(2,128)} %pairs_hbm.1, s32[1]{0:T(128)S(6)} %copy.10.count_ref), custom_call_target="tpu_custom_call" | custom-call | tf_op jit(solution)/shard_map/coeffs/pallas_call | solution.py:387
  2.4 0.0 copy-start.2
  2.4 0.0 copy-start.3
  2.5 0.0 copy-start.4
  2.5 7.3 %all-to-all-start = ((bf16[32,8,128]{2,1,0:T(8,128)(2,1)}), bf16[32,8,128]{2,1,0:T(8,128)(2,1)S(1)}, u32[]{:S(2)}, u32[]{:S(2)}) async-start(bf16[32,8,128]{2,1,0:T(8,128)(2,1)} %coeffs.1.after_ref), calls=%async_computation | async-start | bytes 131072 | tf_op jit(solution)/shard_map/all_to_all | solution.py:409
  9.8 0.0 copy-done
  9.8 0.0 copy-done.2
  9.8 0.0 copy-done.3
  9.8 0.0 copy-done.4
  9.8 0.0 copy-start.6
  9.8 0.3 geometry.1
  10.1 0.0 copy-start.5
  10.1 3.7 %collective-permute-start = (bf16[2,16,1024]{2,1,0:T(8,128)(2,1)S(1)}, bf16[2,16,1024]{2,1,0:T(8,128)(2,1)S(1)}, u32[]{:S(2)}, u32[]{:S(2)}) collective-permute-start(bf16[2,16,1024]{2,1,0:T(8,128)(2,1)S(1)} %get-tuple-element.17), channel_id=1, source_target_pairs={{0,1},{1,2},{2,3},{3,4},{4,5},{5,6},{6,7},{9,8},{10,9},{11,10},{12... | collective-permute-start | bytes 196616 | tf_op jit(solution)/shard_map/ppermute | solution.py:432
  13.8 0.0 copy-done.6
  13.8 0.1 reshape.3.coupling_ref
  14.0 0.0 copy-done.5
  14.0 0.4 %coupling.1 = (bf16[512,128]{1,0:T(8,128)(2,1)S(1)}, bf16[512,128]{1,0:T(8,128)(2,1)S(1)}, s32[6,16]{1,0:T(8,128)S(1)}) custom-call(bf16[16,32,32]{2,1,0:T(8,128)(2,1)S(1)} %reshape.3.coupling_ref, s32[2,16]{1,0:T(2,128)S(1)} %copy-done.5, bf16[32,8,128]{2,1,0:T(8,128)(2,1)} %coeffs.1.after_ref), custom_call_target="tpu_custom_call" | custom-call | flops 1000 | bytes 1000 | tf_op jit(solution)/shard_map/coupling/pallas_call | solution.py:447
  14.3 2.7 %all-to-all-done.coeff_ref.pay_ref = bf16[32,8,128]{2,1,0:T(8,128)(2,1)S(1)} async-done(((bf16[32,8,128]{2,1,0:T(8,128)(2,1)}), bf16[32,8,128]{2,1,0:T(8,128)(2,1)S(1)}, u32[]{:S(2)}, u32[]{:S(2)}) %all-to-all-start) | async-done | bytes 65568 | tf_op jit(solution)/shard_map/all_to_all | solution.py:409
  17.1 1.5 %far.1 = (bf16[32,16,128]{2,1,0:T(8,128)(2,1)}, f32[8,128]{1,0:T(8,128)S(1)}) custom-call(s32[6,16]{1,0:T(8,128)S(1)} %get-tuple-element.20.list_ref, bf16[32,8,128]{2,1,0:T(8,128)(2,1)S(1)} %all-to-all-done.coeff_ref.pay_ref, bf16[512,128]{1,0:T(8,128)(2,1)S(1)} %get-tuple-element.21.to_second_ref, bf16[512,128]{1,0:T(8,128)(2,1)S(1)} %get-tuple-element.22.to_first_ref), custom_call_target="tpu_custom_call" | custom-call | tf_op jit(solution)/shard_map/far/pallas_call | solution.py:457
  18.6 2.6 %all-to-all-start.1 = ((bf16[32,16,128]{2,1,0:T(8,128)(2,1)}), bf16[32,16,128]{2,1,0:T(8,128)(2,1)S(1)}, u32[]{:S(2)}, u32[]{:S(2)}) async-start(bf16[32,16,128]{2,1,0:T(8,128)(2,1)} %get-tuple-element.24), calls=%async_computation.1 | async-start | bytes 262144 | tf_op jit(solution)/shard_map/all_to_all | solution.py:475
  21.2 0.0 collective-permute-done.halo_ref
  21.3 3.7 %near.1.own_ref = f32[2,16,768]{2,1,0:T(8,128)S(1)} custom-call(bf16[6,16,768]{2,1,0:T(8,128)(2,1)S(1)} %get-tuple-element.18.slip_ref, f32[6,4,256]{2,1,0:T(4,128)S(1)} %get-tuple-element.19.place_ref, bf16[32,8,128]{2,1,0:T(8,128)(2,1)S(1)} %all-to-all-done.coeff_ref.pay_ref, f32[8,128]{1,0:T(8,128)S(1)} %get-tuple-element.23.after_ref), custom_call_target="tpu_custom_call" | custom-call | flops 1000000000 | bytes 1000000 | tf_op jit(solution)/shard_map/near/pallas_call | solution.py:477
  24.9 0.0 copy-start.1
  24.9 0.2 collective-permute-start.1
  25.1 1.2 %collective-permute-done.1.other_ref = f32[2,16,768]{2,1,0:T(8,128)S(1)} collective-permute-done((f32[2,16,768]{2,1,0:T(8,128)S(1)}, f32[2,16,768]{2,1,0:T(8,128)S(1)}, u32[]{:S(2)}, u32[]{:S(2)}) %collective-permute-start.1) | collective-permute-done | bytes 98336 | tf_op jit(solution)/shard_map/ppermute | solution.py:494
  26.3 2.6 %all-to-all-done.1.far_ref = bf16[32,16,128]{2,1,0:T(8,128)(2,1)S(1)} async-done(((bf16[32,16,128]{2,1,0:T(8,128)(2,1)}), bf16[32,16,128]{2,1,0:T(8,128)(2,1)S(1)}, u32[]{:S(2)}, u32[]{:S(2)}) %all-to-all-start.1) | async-done | bytes 131104 | tf_op jit(solution)/shard_map/all_to_all | solution.py:475
  28.9 0.0 copy-done.1
  28.9 0.9 %finish.1 = f32[4,16,768]{2,1,0:T(8,128)} custom-call(f32[4,16,768]{2,1,0:T(8,128)S(1)} %gather_near.1.near_ref, bf16[32,16,128]{2,1,0:T(8,128)(2,1)S(1)} %all-to-all-done.1.far_ref, bf16[4,32,768]{2,1,0:T(8,128)(2,1)S(1)} %copy-done.1), custom_call_target="tpu_custom_call" | custom-call | tf_op jit(solution)/shard_map/finish/pallas_call | solution.py:506
  (2 shorter events, 0.1 us)
Async XLA Ops:
  0.7 9.1 %copy-start = (f32[4,16,768]{2,1,0:T(8,128)S(1)}, f32[4,16,768]{2,1,0:T(8,128)}, u32[]{:S(2)}) copy-start(f32[4,16,768]{2,1,0:T(8,128)} %slip_ref.1) | copy-start | bytes 589828
  2.4 7.4 %copy-start.2 = (s32[3,1024]{1,0:T(4,128)S(1)}, s32[3,1024]{1,0:T(4,128)}, u32[]{:S(2)}) copy-start(s32[3,1024]{1,0:T(4,128)} %triangles_ref.1) | copy-start | bytes 36868
  2.4 7.4 %copy-start.3 = (f32[3,561]{1,0:T(4,128)S(1)}, f32[3,561]{1,0:T(4,128)}, u32[]{:S(2)}) copy-start(f32[3,561]{1,0:T(4,128)} %vertices_ref.1) | copy-start | bytes 20200
  2.5 7.4 %copy-start.4 = (s32[4,256]{1,0:T(4,128)S(1)}, s32[4,256]{1,0:T(4,128)}, u32[]{:S(2)}) copy-start(s32[4,256]{1,0:T(4,128)} %map_ref.1) | copy-start | bytes 12292
  2.5 14.6 %all-to-all-start = ((bf16[32,8,128]{2,1,0:T(8,128)(2,1)}), bf16[32,8,128]{2,1,0:T(8,128)(2,1)S(1)}, u32[]{:S(2)}, u32[]{:S(2)}) async-start(bf16[32,8,128]{2,1,0:T(8,128)(2,1)} %coeffs.1.after_ref), calls=%async_computation | async-start | bytes 131072 | tf_op jit(solution)/shard_map/all_to_all | solution.py:409
  9.8 4.0 %copy-start.6 = (bf16[16,1024]{1,0:T(8,128)(2,1)S(1)}, bf16[16,1024]{1,0:T(8,128)(2,1)}, u32[]{:S(2)}) copy-start(bf16[16,1024]{1,0:T(8,128)(2,1)} %param.16) | copy-start | bytes 98308
  10.1 3.9 %copy-start.5 = (s32[2,16]{1,0:T(2,128)S(1)}, s32[2,16]{1,0:T(2,128)}, u32[]{:S(2)}) copy-start(s32[2,16]{1,0:T(2,128)} %pairs_ref.1) | copy-start | bytes 388
  10.1 11.1 %collective-permute-start = (bf16[2,16,1024]{2,1,0:T(8,128)(2,1)S(1)}, bf16[2,16,1024]{2,1,0:T(8,128)(2,1)S(1)}, u32[]{:S(2)}, u32[]{:S(2)}) collective-permute-start(bf16[2,16,1024]{2,1,0:T(8,128)(2,1)S(1)} %get-tuple-element.17), channel_id=1, source_target_pairs={{0,1},{1,2},{2,3},{3,4},{4,5},{5,6},{6,7},{9,8},{10,9},{11,10},{12... | collective-permute-start | bytes 196616 | tf_op jit(solution)/shard_map/ppermute | solution.py:432
  18.6 10.3 %all-to-all-start.1 = ((bf16[32,16,128]{2,1,0:T(8,128)(2,1)}), bf16[32,16,128]{2,1,0:T(8,128)(2,1)S(1)}, u32[]{:S(2)}, u32[]{:S(2)}) async-start(bf16[32,16,128]{2,1,0:T(8,128)(2,1)} %get-tuple-element.24), calls=%async_computation.1 | async-start | bytes 262144 | tf_op jit(solution)/shard_map/all_to_all | solution.py:475
  24.9 4.0 %copy-start.1 = (bf16[4,32,768]{2,1,0:T(8,128)(2,1)S(1)}, bf16[4,32,768]{2,1,0:T(8,128)(2,1)}, u32[]{:S(2)}) copy-start(bf16[4,32,768]{2,1,0:T(8,128)(2,1)} %basis_ref.1) | copy-start | bytes 589828
  24.9 1.4 %collective-permute-start.1 = (f32[2,16,768]{2,1,0:T(8,128)S(1)}, f32[2,16,768]{2,1,0:T(8,128)S(1)}, u32[]{:S(2)}, u32[]{:S(2)}) collective-permute-start(f32[2,16,768]{2,1,0:T(8,128)S(1)} %near.1.own_ref), channel_id=1, source_target_pairs={{0,8},{8,0},{16,24},{24,16},{1,9},{9,1},{17,25},{25,17},{2,10},{10... | collective-permute-start | bytes 294920 | tf_op jit(solution)/shard_map/ppermute | solution.py:494

commit v21 on v20

--- a/solution.py
+++ b/solution.py
@@ -42,7 +42,7 @@
 
 
 def coeffs_kernel(
-    slip_hbm, basis_hbm, pairs_hbm, count_ref, pay_hbm, slip_ref, basis_ref, pairs_ref, sent_ref, sems, out_sems
+    slip_hbm, basis_hbm, pairs_hbm, count_ref, room_ref, pay_ref, slip_ref, basis_ref, pairs_ref, sems
 ):
     clusters = slip_hbm.shape[0]
     rhs_count = slip_ref.shape[0]
@@ -73,19 +73,8 @@
     )
     counts = [jnp.broadcast_to(value, (half, rank_size)) for value in (low, high)]
     pay = jnp.concatenate([coeffs[0:half], coeffs[half:]] + counts, axis=1).astype(jnp.bfloat16)
-    for target in range(sent_ref.shape[0]):
-        sent_ref[target] = pay
-    parts = pay_hbm.shape[0] // sent_ref.shape[0]
-    sends = [
-        pltpu.make_async_copy(
-            sent_ref, pay_hbm.at[pl.ds(part * sent_ref.shape[0], sent_ref.shape[0])], out_sems.at[part]
-        )
-        for part in range(parts)
-    ]
-    for send in sends:
-        send.start()
-    for send in sends:
-        send.wait()
+    for target in range(pay_ref.shape[0]):
+        pay_ref[target] = pay
 
 
 def geometry_kernel(
@@ -270,8 +259,9 @@
 
 
 def coupling_kernel(
-    coupling_ref, pairs_ref, after_ref, to_second_ref, to_first_ref, list_ref, *, clusters, long_count
+    coupling_ref, pairs_ref, after_ref, to_second_ref, to_first_ref, list_ref, room_ref, *, clusters, long_count
 ):
+    room_ref[...] = jnp.zeros(room_ref.shape, room_ref.dtype)
     owner, group = pairs_ref[...] // clusters, pairs_ref[...] % clusters
     list_ref[...] = jnp.concatenate([group * long_count + owner, owner, group], axis=0)
     pair_count, rank_size, _ = coupling_ref.shape
@@ -284,7 +274,7 @@
 
 
 def far_kernel(
-    list_ref, coeff_ref, to_second_ref, to_first_ref, out_hbm, done_ref, pairs_ref, moved_ref, sent_ref, sems,
+    list_ref, coeff_ref, to_second_ref, to_first_ref, room_ref, out_ref, done_ref, pairs_ref, moved_ref, sems,
     *total_refs, clusters
 ):
     fetch = pltpu.make_async_copy(list_ref, pairs_ref, sems.at[0])
@@ -329,17 +319,9 @@
     total = total_refs[0][...]
     for total_ref in total_refs[1:]:
         total = total + total_ref[...]
-    sent_ref[...] = total.astype(jnp.bfloat16)
-    copies = [
-        pltpu.make_async_copy(
-            sent_ref, out_hbm.at[pl.ds(copy_id * long_count, long_count)], sems.at[copy_id]
-        )
-        for copy_id in range(out_hbm.shape[0] // long_count)
-    ]
-    for copy in copies:
-        copy.start()
-    for copy in copies:
-        copy.wait()
+    sent = total.astype(jnp.bfloat16)
+    for copy_id in range(out_ref.shape[0] // long_count):
+        out_ref[copy_id * long_count : (copy_id + 1) * long_count] = sent
 
 
 def gather_near_kernel(own_ref, other_ref, out_ref):
@@ -387,15 +369,14 @@
     pay = pl.pallas_call(
         coeffs_kernel,
         out_shape=jax.ShapeDtypeStruct((devices, rhs_count // 2, LANES), jnp.bfloat16),
-        in_specs=[HBM] * 3 + [SMEM],
-        out_specs=HBM,
+        in_specs=[HBM] * 3 + [SMEM, VMEM],
+        out_specs=VMEM,
+        input_output_aliases={4: 0},
         scratch_shapes=[
             pltpu.VMEM(slip.shape[1:], slip.dtype),
             pltpu.VMEM(basis.shape[1:], basis.dtype),
             pltpu.VMEM(near_pairs.shape, near_pairs.dtype),
-            pltpu.VMEM((long_count, rhs_count // 2, LANES), jnp.bfloat16),
             pltpu.SemaphoreType.DMA((3,)),
-            pltpu.SemaphoreType.DMA((row_count,)),
         ],
         compiler_params=pltpu.CompilerParams(vmem_limit_bytes=16 << 20),
         name="coeffs",
@@ -405,6 +386,9 @@
             for array in (slip, basis, near_pairs)
         ],
         near_count,
+        pltpu.with_memory_space_constraint(
+            jnp.zeros((devices, rhs_count // 2, LANES), jnp.bfloat16), pltpu.VMEM
+        ),
     )
     everyone = lax.all_to_all(pay, ("row", "long"), 0, 0, tiled=True)
 
@@ -444,12 +428,15 @@
         name="window",
     )(xs, geometry, halo)
 
-    to_second, to_first, pair_list = pl.pallas_call(
+    to_second, to_first, pair_list, room = pl.pallas_call(
         functools.partial(coupling_kernel, clusters=clusters, long_count=long_count),
         out_shape=[jax.ShapeDtypeStruct((coupling.shape[0] * rank_size, LANES), jnp.bfloat16)] * 2
-        + [jax.ShapeDtypeStruct((6,) + far_pairs.shape[1:], far_pairs.dtype)],
+        + [
+            jax.ShapeDtypeStruct((6,) + far_pairs.shape[1:], far_pairs.dtype),
+            jax.ShapeDtypeStruct((devices, rhs_count, clusters * rank_size), jnp.bfloat16),
+        ],
         in_specs=[VMEM, VMEM, ANY],
-        out_specs=[VMEM] * 3,
+        out_specs=[VMEM] * 4,
         compiler_params=pltpu.CompilerParams(vmem_limit_bytes=16 << 20),
         cost_estimate=pl.CostEstimate(flops=1000, bytes_accessed=1000, transcendentals=0),
         name="coupling",
@@ -460,18 +447,18 @@
             jax.ShapeDtypeStruct((devices, rhs_count, clusters * rank_size), jnp.bfloat16),
             jax.ShapeDtypeStruct((8, LANES), jnp.float32),
         ],
-        in_specs=[VMEM] * 4,
-        out_specs=[HBM, VMEM],
+        in_specs=[VMEM] * 5,
+        out_specs=[VMEM] * 2,
+        input_output_aliases={4: 0},
         scratch_shapes=[
             pltpu.SMEM((6,) + far_pairs.shape[1:], far_pairs.dtype),
             pltpu.VMEM((devices, rhs_count, LANES), jnp.float32),
-            pltpu.VMEM((long_count, rhs_count, clusters * rank_size), jnp.bfloat16),
-            pltpu.SemaphoreType.DMA((row_count,)),
+            pltpu.SemaphoreType.DMA((1,)),
         ]
         + [pltpu.VMEM((long_count, rhs_count, clusters * rank_size), jnp.float32)] * 4,
         compiler_params=pltpu.CompilerParams(vmem_limit_bytes=16 << 20),
         name="far",
-    )(pair_list, everyone, to_second, to_first)
+    )(pair_list, everyone, to_second, to_first, pltpu.with_memory_space_constraint(room, pltpu.VMEM))
     far_terms = lax.all_to_all(far, ("row", "long"), 0, 0, tiled=True)
 
     near = pl.pallas_call(

time: 30.2 us -> 32.5 us (1.076)
  Pallas kernels: 8.57 us -> 10.9 us
  waiting for transfers between devices: 6.5 us -> 5.84 us
  local copies, waits for them, and re-layouts: 0.19 us -> 0.82 us
    pallas_call x1, Pallas kernels: 1.54 us -> 2.44 us  [shards(): pl.pallas_call(functools.partial(far_kernel, clusters=clusters), out_shap...]
    pallas_call x1, Pallas kernels: 1.76 us -> 2.55 us  [shards(): pl.pallas_call(coeffs_kernel, out_shape=jax.ShapeDtypeStruct((devices, rh...]
    broadcast_in_dim x0 -> x1, local copies, waits for them, and re-layouts: none -> 0.63 us  [shards(): jnp.zeros((devices, rhs_count // 2, LANES), jnp.bfloat16)]
    pallas_call x1, Pallas kernels: 0.37 us -> 0.97 us  [shards(): pl.pallas_call(functools.partial(coupling_kernel, clusters=clusters, long...]
    all_to_all x1, waiting for transfers between devices: 2.71 us -> 2.11 us  [shards(): everyone = lax.all_to_all(pay, ('row', 'long'), 0, 0, tiled=True)]
  transfers between devices with their start and end apart: 4 -> 4, of which waited for: 3 -> 3; matrix products, arithmetic and copies ran while one was open for 0% -> 0% of each run, Pallas kernels for 20% -> 23%
where the time goes in v21:
time: 32.5 us; the launch traced here: 32.1 us
  starting transfers between devices  13.8 us (42%)
  Pallas kernels  10.9 us (34%)
  waiting for transfers between devices  5.84 us (18%)
  local copies, waits for them, and re-layouts  0.82 us (3%)
  between operations  0.82 us (3%)
    all_to_all x1, starting transfers between devices, shards(): everyone = lax.all_to_all(pay, ('row', 'long'), 0, 0, tiled=True)  7.3 us
    pallas_call x1, Pallas kernels, shards(): pl.pallas_call(functools.partial(near_kernel, long_count=long_count, clus...  3.68 us
    ppermute x1, starting transfers between devices, shards(): halo = lax.ppermute(to_neighbour, ('row', 'long'), route)  3.68 us
    all_to_all x1, waiting for transfers between devices, shards(): far_terms = lax.all_to_all(far, ('row', 'long'), 0, 0, tiled=True)  2.6 us
    all_to_all x1, starting transfers between devices, shards(): far_terms = lax.all_to_all(far, ('row', 'long'), 0, 0, tiled=True)  2.59 us
    pallas_call x1, Pallas kernels, shards(): pl.pallas_call(coeffs_kernel, out_shape=jax.ShapeDtypeStruct((devices, rh...  2.55 us
    pallas_call x1, Pallas kernels, shards(): pl.pallas_call(functools.partial(far_kernel, clusters=clusters), out_shap...  2.44 us
    all_to_all x1, waiting for transfers between devices, shards(): everyone = lax.all_to_all(pay, ('row', 'long'), 0, 0, tiled=True)  2.11 us
  transfers between devices with their start and end apart: 4, of which 3 were waited for; matrix products, arithmetic and copies ran while one was open for 0% of the time, Pallas kernels for 23%

profile of v21, /device:TPU:0, one launch (start us, length us, event | category | flops | bytes accessed | tf_op | source)
XLA Modules:
  0.0 32.1 jit_solution(10338804804347194256)
XLA Ops:
  0.7 0.6 %broadcast_in_dim.3.room_ref = bf16[32,8,128]{2,1,0:T(8,128)(2,1)} broadcast(bf16[]{:T(256)} %constant.0.clone.1), dimensions={} | broadcast | bytes 65538 | tf_op jit(solution)/shard_map/broadcast_in_dim | solution.py:390
  1.3 0.0 copy-start
  1.3 2.6 %coeffs.1.after_ref = bf16[32,8,128]{2,1,0:T(8,128)(2,1)} custom-call(f32[4,16,768]{2,1,0:T(8,128)} %slip_ref.1, bf16[4,32,768]{2,1,0:T(8,128)(2,1)} %basis_ref.1, s32[2,20]{1,0:T(2,128)} %pairs_hbm.1, s32[1]{0:T(128)S(6)} %copy.14.count_ref, bf16[32,8,128]{2,1,0:T(8,128)(2,1)} %broadcast_in_dim.3.room_ref), custom_call_target="tpu_custom_call", output_to_operand_aliasing={{}: (4, {})} | custom-call | tf_op jit(solution)/shard_map/coeffs/pallas_call | solution.py:369
  3.8 0.0 copy-start.2
  3.9 0.0 copy-start.3
  3.9 0.0 copy-start.4
  3.9 7.3 %all-to-all-start = ((bf16[32,8,128]{2,1,0:T(8,128)(2,1)}), bf16[32,8,128]{2,1,0:T(8,128)(2,1)S(1)}, u32[]{:S(2)}, u32[]{:S(2)}) async-start(bf16[32,8,128]{2,1,0:T(8,128)(2,1)} %coeffs.1.after_ref), calls=%async_computation | async-start | bytes 131072 | tf_op jit(solution)/shard_map/all_to_all | solution.py:393
  11.2 0.0 copy-done
  11.2 0.0 copy-done.2
  11.2 0.0 copy-done.3
  11.2 0.0 copy-done.4
  11.2 0.0 copy-start.6
  11.2 0.3 geometry.1
  11.5 0.0 copy-start.5
  11.5 3.7 %collective-permute-start = (bf16[2,16,1024]{2,1,0:T(8,128)(2,1)S(1)}, bf16[2,16,1024]{2,1,0:T(8,128)(2,1)S(1)}, u32[]{:S(2)}, u32[]{:S(2)}) collective-permute-start(bf16[2,16,1024]{2,1,0:T(8,128)(2,1)S(1)} %get-tuple-element.18), channel_id=1, source_target_pairs={{0,1},{1,2},{2,3},{3,4},{4,5},{5,6},{6,7},{9,8},{10,9},{11,10},{12... | collective-permute-start | bytes 196616 | tf_op jit(solution)/shard_map/ppermute | solution.py:416
  15.2 0.0 copy-done.6
  15.2 0.1 reshape.3.coupling_ref
  15.4 0.0 copy-done.5
  15.4 1.0 %coupling.1 = (bf16[512,128]{1,0:T(8,128)(2,1)S(1)}, bf16[512,128]{1,0:T(8,128)(2,1)S(1)}, s32[6,16]{1,0:T(8,128)S(1)}, bf16[32,16,128]{2,1,0:T(8,128)(2,1)}) custom-call(bf16[16,32,32]{2,1,0:T(8,128)(2,1)S(1)} %reshape.3.coupling_ref, s32[2,16]{1,0:T(2,128)S(1)} %copy-done.5, bf16[32,8,128]{2,1,0:T(8,128)(2,1)} %coeffs.1.after_ref), custom_call_target="tpu_custom_call" | custom-call | flops 1000 | bytes 1000 | tf_op jit(solution)/shard_map/coupling/pallas_call | solution.py:431
  16.4 2.1 %all-to-all-done.coeff_ref.pay_ref = bf16[32,8,128]{2,1,0:T(8,128)(2,1)S(1)} async-done(((bf16[32,8,128]{2,1,0:T(8,128)(2,1)}), bf16[32,8,128]{2,1,0:T(8,128)(2,1)S(1)}, u32[]{:S(2)}, u32[]{:S(2)}) %all-to-all-start) | async-done | bytes 65568 | tf_op jit(solution)/shard_map/all_to_all | solution.py:393
  18.5 2.4 %far.1 = (bf16[32,16,128]{2,1,0:T(8,128)(2,1)}, f32[8,128]{1,0:T(8,128)S(1)}) custom-call(s32[6,16]{1,0:T(8,128)S(1)} %get-tuple-element.21.list_ref, bf16[32,8,128]{2,1,0:T(8,128)(2,1)S(1)} %all-to-all-done.coeff_ref.pay_ref, bf16[512,128]{1,0:T(8,128)(2,1)S(1)} %get-tuple-element.22.to_second_ref, ...), custom_call_target="tpu_custom_call", output_to_operand_aliasing={{0}: (4, {})} | custom-call | tf_op jit(solution)/shard_map/far/pallas_call | solution.py:444
  20.9 2.6 %all-to-all-start.1 = ((bf16[32,16,128]{2,1,0:T(8,128)(2,1)}), bf16[32,16,128]{2,1,0:T(8,128)(2,1)S(1)}, u32[]{:S(2)}, u32[]{:S(2)}) async-start(bf16[32,16,128]{2,1,0:T(8,128)(2,1)} %get-tuple-element.26), calls=%async_computation.1 | async-start | bytes 262144 | tf_op jit(solution)/shard_map/all_to_all | solution.py:462
  23.5 0.0 collective-permute-done.halo_ref
  23.6 3.7 %near.1.own_ref = f32[2,16,768]{2,1,0:T(8,128)S(1)} custom-call(bf16[6,16,768]{2,1,0:T(8,128)(2,1)S(1)} %get-tuple-element.19.slip_ref, f32[6,4,256]{2,1,0:T(4,128)S(1)} %get-tuple-element.20.place_ref, bf16[32,8,128]{2,1,0:T(8,128)(2,1)S(1)} %all-to-all-done.coeff_ref.pay_ref, f32[8,128]{1,0:T(8,128)S(1)} %get-tuple-element.25.after_ref), custom_call_target="tpu_custom_call" | custom-call | flops 1000000000 | bytes 1000000 | tf_op jit(solution)/shard_map/near/pallas_call | solution.py:464
  27.3 0.0 copy-start.1
  27.3 0.2 collective-permute-start.1
  27.5 1.1 %collective-permute-done.1.other_ref = f32[2,16,768]{2,1,0:T(8,128)S(1)} collective-permute-done((f32[2,16,768]{2,1,0:T(8,128)S(1)}, f32[2,16,768]{2,1,0:T(8,128)S(1)}, u32[]{:S(2)}, u32[]{:S(2)}) %collective-permute-start.1) | collective-permute-done | bytes 98336 | tf_op jit(solution)/shard_map/ppermute | solution.py:481
  28.7 2.6 %all-to-all-done.1.far_ref = bf16[32,16,128]{2,1,0:T(8,128)(2,1)S(1)} async-done(((bf16[32,16,128]{2,1,0:T(8,128)(2,1)}), bf16[32,16,128]{2,1,0:T(8,128)(2,1)S(1)}, u32[]{:S(2)}, u32[]{:S(2)}) %all-to-all-start.1) | async-done | bytes 131104 | tf_op jit(solution)/shard_map/all_to_all | solution.py:462
  31.3 0.0 copy-done.1
  31.3 0.9 %finish.1 = f32[4,16,768]{2,1,0:T(8,128)} custom-call(f32[4,16,768]{2,1,0:T(8,128)S(1)} %gather_near.1.near_ref, bf16[32,16,128]{2,1,0:T(8,128)(2,1)S(1)} %all-to-all-done.1.far_ref, bf16[4,32,768]{2,1,0:T(8,128)(2,1)S(1)} %copy-done.1), custom_call_target="tpu_custom_call" | custom-call | tf_op jit(solution)/shard_map/finish/pallas_call | solution.py:493
  (2 shorter events, 0.1 us)
Async XLA Ops:
  1.3 9.9 %copy-start = (f32[4,16,768]{2,1,0:T(8,128)S(1)}, f32[4,16,768]{2,1,0:T(8,128)}, u32[]{:S(2)}) copy-start(f32[4,16,768]{2,1,0:T(8,128)} %slip_ref.1) | copy-start | bytes 589828
  3.8 7.4 %copy-start.2 = (s32[3,1024]{1,0:T(4,128)S(1)}, s32[3,1024]{1,0:T(4,128)}, u32[]{:S(2)}) copy-start(s32[3,1024]{1,0:T(4,128)} %triangles_ref.1) | copy-start | bytes 36868
  3.9 7.4 %copy-start.3 = (f32[3,561]{1,0:T(4,128)S(1)}, f32[3,561]{1,0:T(4,128)}, u32[]{:S(2)}) copy-start(f32[3,561]{1,0:T(4,128)} %vertices_ref.1) | copy-start | bytes 20200
  3.9 7.4 %copy-start.4 = (s32[4,256]{1,0:T(4,128)S(1)}, s32[4,256]{1,0:T(4,128)}, u32[]{:S(2)}) copy-start(s32[4,256]{1,0:T(4,128)} %map_ref.1) | copy-start | bytes 12292
  3.9 14.6 %all-to-all-start = ((bf16[32,8,128]{2,1,0:T(8,128)(2,1)}), bf16[32,8,128]{2,1,0:T(8,128)(2,1)S(1)}, u32[]{:S(2)}, u32[]{:S(2)}) async-start(bf16[32,8,128]{2,1,0:T(8,128)(2,1)} %coeffs.1.after_ref), calls=%async_computation | async-start | bytes 131072 | tf_op jit(solution)/shard_map/all_to_all | solution.py:393
  11.2 4.0 %copy-start.6 = (bf16[16,1024]{1,0:T(8,128)(2,1)S(1)}, bf16[16,1024]{1,0:T(8,128)(2,1)}, u32[]{:S(2)}) copy-start(bf16[16,1024]{1,0:T(8,128)(2,1)} %param.16) | copy-start | bytes 98308
  11.5 3.9 %copy-start.5 = (s32[2,16]{1,0:T(2,128)S(1)}, s32[2,16]{1,0:T(2,128)}, u32[]{:S(2)}) copy-start(s32[2,16]{1,0:T(2,128)} %pairs_ref.1) | copy-start | bytes 388
  11.5 12.0 %collective-permute-start = (bf16[2,16,1024]{2,1,0:T(8,128)(2,1)S(1)}, bf16[2,16,1024]{2,1,0:T(8,128)(2,1)S(1)}, u32[]{:S(2)}, u32[]{:S(2)}) collective-permute-start(bf16[2,16,1024]{2,1,0:T(8,128)(2,1)S(1)} %get-tuple-element.18), channel_id=1, source_target_pairs={{0,1},{1,2},{2,3},{3,4},{4,5},{5,6},{6,7},{9,8},{10,9},{11,10},{12... | collective-permute-start | bytes 196616 | tf_op jit(solution)/shard_map/ppermute | solution.py:416
  20.9 10.3 %all-to-all-start.1 = ((bf16[32,16,128]{2,1,0:T(8,128)(2,1)}), bf16[32,16,128]{2,1,0:T(8,128)(2,1)S(1)}, u32[]{:S(2)}, u32[]{:S(2)}) async-start(bf16[32,16,128]{2,1,0:T(8,128)(2,1)} %get-tuple-element.26), calls=%async_computation.1 | async-start | bytes 262144 | tf_op jit(solution)/shard_map/all_to_all | solution.py:462
  27.3 4.0 %copy-start.1 = (bf16[4,32,768]{2,1,0:T(8,128)(2,1)S(1)}, bf16[4,32,768]{2,1,0:T(8,128)(2,1)}, u32[]{:S(2)}) copy-start(bf16[4,32,768]{2,1,0:T(8,128)(2,1)} %basis_ref.1) | copy-start | bytes 589828
  27.3 1.4 %collective-permute-start.1 = (f32[2,16,768]{2,1,0:T(8,128)S(1)}, f32[2,16,768]{2,1,0:T(8,128)S(1)}, u32[]{:S(2)}, u32[]{:S(2)}) collective-permute-start(f32[2,16,768]{2,1,0:T(8,128)S(1)} %near.1.own_ref), channel_id=1, source_target_pairs={{0,8},{8,0},{16,24},{24,16},{1,9},{9,1},{17,25},{25,17},{2,10},{10... | collective-permute-start | bytes 294920 | tf_op jit(solution)/shard_map/ppermute | solution.py:481

commit v22 on v20

--- a/solution.py
+++ b/solution.py
@@ -472,7 +472,9 @@
         compiler_params=pltpu.CompilerParams(vmem_limit_bytes=16 << 20),
         name="far",
     )(pair_list, everyone, to_second, to_first)
-    far_terms = lax.all_to_all(far, ("row", "long"), 0, 0, tiled=True)
+    rows = list(range(0, row_count, 2)) + list(range(1, row_count, 2))
+    order = [[row * long_count + owner for row in rows for owner in range(long_count)]]
+    far_terms = lax.all_to_all(far, ("row", "long"), 0, 0, axis_index_groups=order, tiled=True)
 
     near = pl.pallas_call(
         functools.partial(near_kernel, long_count=long_count, clusters=clusters),

time: 30.2 us -> 30.4 us (level)
  no operation moved by 1% of the time
where the time goes in v22:
time: 30.4 us; the launch traced here: 30.1 us
  starting transfers between devices  13.7 us (45%)
  Pallas kernels  8.57 us (28%)
  waiting for transfers between devices  6.76 us (22%)
  between operations  0.84 us (3%)
    all_to_all x1, starting transfers between devices, shards(): everyone = lax.all_to_all(pay, ('row', 'long'), 0, 0, tiled=True)  7.3 us
    pallas_call x1, Pallas kernels, shards(): pl.pallas_call(functools.partial(near_kernel, long_count=long_count, clus...  3.68 us
    ppermute x1, starting transfers between devices, shards(): halo = lax.ppermute(to_neighbour, ('row', 'long'), route)  3.68 us
    all_to_all x1, waiting for transfers between devices, shards(): lax.all_to_all(far, ('row', 'long'), 0, 0, axis_index_groups=order, tiled...  2.86 us
    all_to_all x1, waiting for transfers between devices, shards(): everyone = lax.all_to_all(pay, ('row', 'long'), 0, 0, tiled=True)  2.71 us
    all_to_all x1, starting transfers between devices, shards(): lax.all_to_all(far, ('row', 'long'), 0, 0, axis_index_groups=order, tiled...  2.59 us
    pallas_call x1, Pallas kernels, shards(): pl.pallas_call(coeffs_kernel, out_shape=jax.ShapeDtypeStruct((devices, rh...  1.76 us
    pallas_call x1, Pallas kernels, shards(): pl.pallas_call(functools.partial(far_kernel, clusters=clusters), out_shap...  1.55 us
  transfers between devices with their start and end apart: 4, of which 3 were waited for; matrix products, arithmetic and copies ran while one was open for 0% of the time, Pallas kernels for 20%

profile of v22, /device:TPU:0, one launch (start us, length us, event | category | flops | bytes accessed | tf_op | source)
XLA Modules:
  0.0 30.1 jit_solution(6448633115651062105)
XLA Ops:
  0.7 0.0 copy-start
  0.7 1.8 %coeffs.1.after_ref = bf16[32,8,128]{2,1,0:T(8,128)(2,1)} custom-call(f32[4,16,768]{2,1,0:T(8,128)} %slip_ref.1, bf16[4,32,768]{2,1,0:T(8,128)(2,1)} %basis_ref.1, s32[2,20]{1,0:T(2,128)} %pairs_hbm.1, s32[1]{0:T(128)S(6)} %copy.10.count_ref), custom_call_target="tpu_custom_call" | custom-call | tf_op jit(solution)/shard_map/coeffs/pallas_call | solution.py:387
  2.4 0.0 copy-start.2
  2.4 0.0 copy-start.3
  2.5 0.0 copy-start.4
  2.5 7.3 %all-to-all-start = ((bf16[32,8,128]{2,1,0:T(8,128)(2,1)}), bf16[32,8,128]{2,1,0:T(8,128)(2,1)S(1)}, u32[]{:S(2)}, u32[]{:S(2)}) async-start(bf16[32,8,128]{2,1,0:T(8,128)(2,1)} %coeffs.1.after_ref), calls=%async_computation | async-start | bytes 131072 | tf_op jit(solution)/shard_map/all_to_all | solution.py:409
  9.8 0.0 copy-done
  9.8 0.0 copy-done.2
  9.8 0.0 copy-done.3
  9.8 0.0 copy-done.4
  9.8 0.0 copy-start.6
  9.8 0.3 geometry.1
  10.1 0.0 copy-start.5
  10.1 3.7 %collective-permute-start = (bf16[2,16,1024]{2,1,0:T(8,128)(2,1)S(1)}, bf16[2,16,1024]{2,1,0:T(8,128)(2,1)S(1)}, u32[]{:S(2)}, u32[]{:S(2)}) collective-permute-start(bf16[2,16,1024]{2,1,0:T(8,128)(2,1)S(1)} %get-tuple-element.17), channel_id=1, source_target_pairs={{0,1},{1,2},{2,3},{3,4},{4,5},{5,6},{6,7},{9,8},{10,9},{11,10},{12... | collective-permute-start | bytes 196616 | tf_op jit(solution)/shard_map/ppermute | solution.py:432
  13.8 0.0 copy-done.6
  13.8 0.1 reshape.3.coupling_ref
  14.0 0.0 copy-done.5
  14.0 0.4 %coupling.1 = (bf16[512,128]{1,0:T(8,128)(2,1)S(1)}, bf16[512,128]{1,0:T(8,128)(2,1)S(1)}, s32[6,16]{1,0:T(8,128)S(1)}) custom-call(bf16[16,32,32]{2,1,0:T(8,128)(2,1)S(1)} %reshape.3.coupling_ref, s32[2,16]{1,0:T(2,128)S(1)} %copy-done.5, bf16[32,8,128]{2,1,0:T(8,128)(2,1)} %coeffs.1.after_ref), custom_call_target="tpu_custom_call" | custom-call | flops 1000 | bytes 1000 | tf_op jit(solution)/shard_map/coupling/pallas_call | solution.py:447
  14.3 2.7 %all-to-all-done.coeff_ref.pay_ref = bf16[32,8,128]{2,1,0:T(8,128)(2,1)S(1)} async-done(((bf16[32,8,128]{2,1,0:T(8,128)(2,1)}), bf16[32,8,128]{2,1,0:T(8,128)(2,1)S(1)}, u32[]{:S(2)}, u32[]{:S(2)}) %all-to-all-start) | async-done | bytes 65568 | tf_op jit(solution)/shard_map/all_to_all | solution.py:409
  17.1 1.5 %far.1 = (bf16[32,16,128]{2,1,0:T(8,128)(2,1)}, f32[8,128]{1,0:T(8,128)S(1)}) custom-call(s32[6,16]{1,0:T(8,128)S(1)} %get-tuple-element.20.list_ref, bf16[32,8,128]{2,1,0:T(8,128)(2,1)S(1)} %all-to-all-done.coeff_ref.pay_ref, bf16[512,128]{1,0:T(8,128)(2,1)S(1)} %get-tuple-element.21.to_second_ref, bf16[512,128]{1,0:T(8,128)(2,1)S(1)} %get-tuple-element.22.to_first_ref), custom_call_target="tpu_custom_call" | custom-call | tf_op jit(solution)/shard_map/far/pallas_call | solution.py:457
  18.6 2.6 %all-to-all-start.1 = ((bf16[32,16,128]{2,1,0:T(8,128)(2,1)}), bf16[32,16,128]{2,1,0:T(8,128)(2,1)S(1)}, u32[]{:S(2)}, u32[]{:S(2)}) async-start(bf16[32,16,128]{2,1,0:T(8,128)(2,1)} %get-tuple-element.24), calls=%async_computation.1 | async-start | bytes 262144 | tf_op jit(solution)/shard_map/all_to_all | solution.py:477
  21.2 0.0 collective-permute-done.halo_ref
  21.3 3.7 %near.1.own_ref = f32[2,16,768]{2,1,0:T(8,128)S(1)} custom-call(bf16[6,16,768]{2,1,0:T(8,128)(2,1)S(1)} %get-tuple-element.18.slip_ref, f32[6,4,256]{2,1,0:T(4,128)S(1)} %get-tuple-element.19.place_ref, bf16[32,8,128]{2,1,0:T(8,128)(2,1)S(1)} %all-to-all-done.coeff_ref.pay_ref, f32[8,128]{1,0:T(8,128)S(1)} %get-tuple-element.23.after_ref), custom_call_target="tpu_custom_call" | custom-call | flops 1000000000 | bytes 1000000 | tf_op jit(solution)/shard_map/near/pallas_call | solution.py:479
  24.9 0.0 copy-start.1
  24.9 0.2 collective-permute-start.1
  25.1 1.2 %collective-permute-done.1.other_ref = f32[2,16,768]{2,1,0:T(8,128)S(1)} collective-permute-done((f32[2,16,768]{2,1,0:T(8,128)S(1)}, f32[2,16,768]{2,1,0:T(8,128)S(1)}, u32[]{:S(2)}, u32[]{:S(2)}) %collective-permute-start.1) | collective-permute-done | bytes 98336 | tf_op jit(solution)/shard_map/ppermute | solution.py:496
  26.3 2.9 %all-to-all-done.1.far_ref = bf16[32,16,128]{2,1,0:T(8,128)(2,1)S(1)} async-done(((bf16[32,16,128]{2,1,0:T(8,128)(2,1)}), bf16[32,16,128]{2,1,0:T(8,128)(2,1)S(1)}, u32[]{:S(2)}, u32[]{:S(2)}) %all-to-all-start.1) | async-done | bytes 131104 | tf_op jit(solution)/shard_map/all_to_all | solution.py:477
  29.2 0.0 copy-done.1
  29.2 0.9 %finish.1 = f32[4,16,768]{2,1,0:T(8,128)} custom-call(f32[4,16,768]{2,1,0:T(8,128)S(1)} %gather_near.1.near_ref, bf16[32,16,128]{2,1,0:T(8,128)(2,1)S(1)} %all-to-all-done.1.far_ref, bf16[4,32,768]{2,1,0:T(8,128)(2,1)S(1)} %copy-done.1), custom_call_target="tpu_custom_call" | custom-call | tf_op jit(solution)/shard_map/finish/pallas_call | solution.py:508
  (2 shorter events, 0.1 us)
Async XLA Ops:
  0.7 9.1 %copy-start = (f32[4,16,768]{2,1,0:T(8,128)S(1)}, f32[4,16,768]{2,1,0:T(8,128)}, u32[]{:S(2)}) copy-start(f32[4,16,768]{2,1,0:T(8,128)} %slip_ref.1) | copy-start | bytes 589828
  2.4 7.4 %copy-start.2 = (s32[3,1024]{1,0:T(4,128)S(1)}, s32[3,1024]{1,0:T(4,128)}, u32[]{:S(2)}) copy-start(s32[3,1024]{1,0:T(4,128)} %triangles_ref.1) | copy-start | bytes 36868
  2.4 7.4 %copy-start.3 = (f32[3,561]{1,0:T(4,128)S(1)}, f32[3,561]{1,0:T(4,128)}, u32[]{:S(2)}) copy-start(f32[3,561]{1,0:T(4,128)} %vertices_ref.1) | copy-start | bytes 20200
  2.5 7.4 %copy-start.4 = (s32[4,256]{1,0:T(4,128)S(1)}, s32[4,256]{1,0:T(4,128)}, u32[]{:S(2)}) copy-start(s32[4,256]{1,0:T(4,128)} %map_ref.1) | copy-start | bytes 12292
  2.5 14.6 %all-to-all-start = ((bf16[32,8,128]{2,1,0:T(8,128)(2,1)}), bf16[32,8,128]{2,1,0:T(8,128)(2,1)S(1)}, u32[]{:S(2)}, u32[]{:S(2)}) async-start(bf16[32,8,128]{2,1,0:T(8,128)(2,1)} %coeffs.1.after_ref), calls=%async_computation | async-start | bytes 131072 | tf_op jit(solution)/shard_map/all_to_all | solution.py:409
  9.8 4.0 %copy-start.6 = (bf16[16,1024]{1,0:T(8,128)(2,1)S(1)}, bf16[16,1024]{1,0:T(8,128)(2,1)}, u32[]{:S(2)}) copy-start(bf16[16,1024]{1,0:T(8,128)(2,1)} %param.16) | copy-start | bytes 98308
  10.1 3.9 %copy-start.5 = (s32[2,16]{1,0:T(2,128)S(1)}, s32[2,16]{1,0:T(2,128)}, u32[]{:S(2)}) copy-start(s32[2,16]{1,0:T(2,128)} %pairs_ref.1) | copy-start | bytes 388
  10.1 11.1 %collective-permute-start = (bf16[2,16,1024]{2,1,0:T(8,128)(2,1)S(1)}, bf16[2,16,1024]{2,1,0:T(8,128)(2,1)S(1)}, u32[]{:S(2)}, u32[]{:S(2)}) collective-permute-start(bf16[2,16,1024]{2,1,0:T(8,128)(2,1)S(1)} %get-tuple-element.17), channel_id=1, source_target_pairs={{0,1},{1,2},{2,3},{3,4},{4,5},{5,6},{6,7},{9,8},{10,9},{11,10},{12... | collective-permute-start | bytes 196616 | tf_op jit(solution)/shard_map/ppermute | solution.py:432
  18.6 10.6 %all-to-all-start.1 = ((bf16[32,16,128]{2,1,0:T(8,128)(2,1)}), bf16[32,16,128]{2,1,0:T(8,128)(2,1)S(1)}, u32[]{:S(2)}, u32[]{:S(2)}) async-start(bf16[32,16,128]{2,1,0:T(8,128)(2,1)} %get-tuple-element.24), calls=%async_computation.1 | async-start | bytes 262144 | tf_op jit(solution)/shard_map/all_to_all | solution.py:477
  24.9 4.3 %copy-start.1 = (bf16[4,32,768]{2,1,0:T(8,128)(2,1)S(1)}, bf16[4,32,768]{2,1,0:T(8,128)(2,1)}, u32[]{:S(2)}) copy-start(bf16[4,32,768]{2,1,0:T(8,128)(2,1)} %basis_ref.1) | copy-start | bytes 589828
  24.9 1.4 %collective-permute-start.1 = (f32[2,16,768]{2,1,0:T(8,128)S(1)}, f32[2,16,768]{2,1,0:T(8,128)S(1)}, u32[]{:S(2)}, u32[]{:S(2)}) collective-permute-start(f32[2,16,768]{2,1,0:T(8,128)S(1)} %near.1.own_ref), channel_id=1, source_target_pairs={{0,8},{8,0},{16,24},{24,16},{1,9},{9,1},{17,25},{25,17},{2,10},{10... | collective-permute-start | bytes 294920 | tf_op jit(solution)/shard_map/ppermute | solution.py:496

commit v23 on v22

--- a/solution.py
+++ b/solution.py
@@ -329,7 +329,8 @@
     total = total_refs[0][...]
     for total_ref in total_refs[1:]:
         total = total + total_ref[...]
-    sent_ref[...] = total.astype(jnp.bfloat16)
+    for owner in range(long_count):
+        sent_ref[long_count - 1 - owner] = total[owner].astype(jnp.bfloat16)
     copies = [
         pltpu.make_async_copy(
             sent_ref, out_hbm.at[pl.ds(copy_id * long_count, long_count)], sems.at[copy_id]
@@ -472,8 +473,7 @@
         compiler_params=pltpu.CompilerParams(vmem_limit_bytes=16 << 20),
         name="far",
     )(pair_list, everyone, to_second, to_first)
-    rows = list(range(0, row_count, 2)) + list(range(1, row_count, 2))
-    order = [[row * long_count + owner for row in rows for owner in range(long_count)]]
+    order = [list(reversed(range(devices)))]
     far_terms = lax.all_to_all(far, ("row", "long"), 0, 0, axis_index_groups=order, tiled=True)
 
     near = pl.pallas_call(

time: 30.4 us -> 30.8 us (1.013)
  waiting for transfers between devices: 6.76 us -> 7.12 us
    all_to_all x1, waiting for transfers between devices: 2.86 us -> 3.22 us  [shards(): lax.all_to_all(far, ('row', 'long'), 0, 0, axis_index_groups=order, tiled...]
  transfers between devices with their start and end apart: 4 -> 4, of which waited for: 3 -> 3; matrix products, arithmetic and copies ran while one was open for 0% -> 0% of each run, Pallas kernels for 20% -> 19%
where the time goes in v23:
time: 30.8 us; the launch traced here: 30.5 us
  starting transfers between devices  13.7 us (44%)
  Pallas kernels  8.56 us (28%)
  waiting for transfers between devices  7.12 us (23%)
  between operations  0.84 us (3%)
    all_to_all x1, starting transfers between devices, shards(): everyone = lax.all_to_all(pay, ('row', 'long'), 0, 0, tiled=True)  7.3 us
    pallas_call x1, Pallas kernels, shards(): pl.pallas_call(functools.partial(near_kernel, long_count=long_count, clus...  3.68 us
    ppermute x1, starting transfers between devices, shards(): halo = lax.ppermute(to_neighbour, ('row', 'long'), route)  3.68 us
    all_to_all x1, waiting for transfers between devices, shards(): lax.all_to_all(far, ('row', 'long'), 0, 0, axis_index_groups=order, tiled...  3.22 us
    all_to_all x1, waiting for transfers between devices, shards(): everyone = lax.all_to_all(pay, ('row', 'long'), 0, 0, tiled=True)  2.71 us
    all_to_all x1, starting transfers between devices, shards(): lax.all_to_all(far, ('row', 'long'), 0, 0, axis_index_groups=order, tiled...  2.59 us
    pallas_call x1, Pallas kernels, shards(): pl.pallas_call(coeffs_kernel, out_shape=jax.ShapeDtypeStruct((devices, rh...  1.76 us
    pallas_call x1, Pallas kernels, shards(): pl.pallas_call(functools.partial(far_kernel, clusters=clusters), out_shap...  1.54 us
  transfers between devices with their start and end apart: 4, of which 3 were waited for; matrix products, arithmetic and copies ran while one was open for 0% of the time, Pallas kernels for 19%

profile of v23, /device:TPU:0, one launch (start us, length us, event | category | flops | bytes accessed | tf_op | source)
XLA Modules:
  0.0 30.5 jit_solution(7411275753639743079)
XLA Ops:
  0.7 0.0 copy-start
  0.7 1.8 %coeffs.1.after_ref = bf16[32,8,128]{2,1,0:T(8,128)(2,1)} custom-call(f32[4,16,768]{2,1,0:T(8,128)} %slip_ref.1, bf16[4,32,768]{2,1,0:T(8,128)(2,1)} %basis_ref.1, s32[2,20]{1,0:T(2,128)} %pairs_hbm.1, s32[1]{0:T(128)S(6)} %copy.10.count_ref), custom_call_target="tpu_custom_call" | custom-call | tf_op jit(solution)/shard_map/coeffs/pallas_call | solution.py:388
  2.4 0.0 copy-start.2
  2.4 0.0 copy-start.3
  2.5 0.0 copy-start.4
  2.5 7.3 %all-to-all-start = ((bf16[32,8,128]{2,1,0:T(8,128)(2,1)}), bf16[32,8,128]{2,1,0:T(8,128)(2,1)S(1)}, u32[]{:S(2)}, u32[]{:S(2)}) async-start(bf16[32,8,128]{2,1,0:T(8,128)(2,1)} %coeffs.1.after_ref), calls=%async_computation | async-start | bytes 131072 | tf_op jit(solution)/shard_map/all_to_all | solution.py:410
  9.8 0.0 copy-done
  9.8 0.0 copy-done.2
  9.8 0.0 copy-done.3
  9.8 0.0 copy-done.4
  9.8 0.0 copy-start.6
  9.8 0.3 geometry.1
  10.1 0.0 copy-start.5
  10.1 3.7 %collective-permute-start = (bf16[2,16,1024]{2,1,0:T(8,128)(2,1)S(1)}, bf16[2,16,1024]{2,1,0:T(8,128)(2,1)S(1)}, u32[]{:S(2)}, u32[]{:S(2)}) collective-permute-start(bf16[2,16,1024]{2,1,0:T(8,128)(2,1)S(1)} %get-tuple-element.17), channel_id=1, source_target_pairs={{0,1},{1,2},{2,3},{3,4},{4,5},{5,6},{6,7},{9,8},{10,9},{11,10},{12... | collective-permute-start | bytes 196616 | tf_op jit(solution)/shard_map/ppermute | solution.py:433
  13.8 0.0 copy-done.6
  13.8 0.1 reshape.3.coupling_ref
  14.0 0.0 copy-done.5
  14.0 0.4 %coupling.1 = (bf16[512,128]{1,0:T(8,128)(2,1)S(1)}, bf16[512,128]{1,0:T(8,128)(2,1)S(1)}, s32[6,16]{1,0:T(8,128)S(1)}) custom-call(bf16[16,32,32]{2,1,0:T(8,128)(2,1)S(1)} %reshape.3.coupling_ref, s32[2,16]{1,0:T(2,128)S(1)} %copy-done.5, bf16[32,8,128]{2,1,0:T(8,128)(2,1)} %coeffs.1.after_ref), custom_call_target="tpu_custom_call" | custom-call | flops 1000 | bytes 1000 | tf_op jit(solution)/shard_map/coupling/pallas_call | solution.py:448
  14.3 2.7 %all-to-all-done.coeff_ref.pay_ref = bf16[32,8,128]{2,1,0:T(8,128)(2,1)S(1)} async-done(((bf16[32,8,128]{2,1,0:T(8,128)(2,1)}), bf16[32,8,128]{2,1,0:T(8,128)(2,1)S(1)}, u32[]{:S(2)}, u32[]{:S(2)}) %all-to-all-start) | async-done | bytes 65568 | tf_op jit(solution)/shard_map/all_to_all | solution.py:410
  17.1 1.5 %far.1 = (bf16[32,16,128]{2,1,0:T(8,128)(2,1)}, f32[8,128]{1,0:T(8,128)S(1)}) custom-call(s32[6,16]{1,0:T(8,128)S(1)} %get-tuple-element.20.list_ref, bf16[32,8,128]{2,1,0:T(8,128)(2,1)S(1)} %all-to-all-done.coeff_ref.pay_ref, bf16[512,128]{1,0:T(8,128)(2,1)S(1)} %get-tuple-element.21.to_second_ref, bf16[512,128]{1,0:T(8,128)(2,1)S(1)} %get-tuple-element.22.to_first_ref), custom_call_target="tpu_custom_call" | custom-call | tf_op jit(solution)/shard_map/far/pallas_call | solution.py:458
  18.6 2.6 %all-to-all-start.1 = ((bf16[32,16,128]{2,1,0:T(8,128)(2,1)}), bf16[32,16,128]{2,1,0:T(8,128)(2,1)S(1)}, u32[]{:S(2)}, u32[]{:S(2)}) async-start(bf16[32,16,128]{2,1,0:T(8,128)(2,1)} %get-tuple-element.24), calls=%async_computation.1 | async-start | bytes 262144 | tf_op jit(solution)/shard_map/all_to_all | solution.py:477
  21.2 0.0 collective-permute-done.halo_ref
  21.3 3.7 %near.1.own_ref = f32[2,16,768]{2,1,0:T(8,128)S(1)} custom-call(bf16[6,16,768]{2,1,0:T(8,128)(2,1)S(1)} %get-tuple-element.18.slip_ref, f32[6,4,256]{2,1,0:T(4,128)S(1)} %get-tuple-element.19.place_ref, bf16[32,8,128]{2,1,0:T(8,128)(2,1)S(1)} %all-to-all-done.coeff_ref.pay_ref, f32[8,128]{1,0:T(8,128)S(1)} %get-tuple-element.23.after_ref), custom_call_target="tpu_custom_call" | custom-call | flops 1000000000 | bytes 1000000 | tf_op jit(solution)/shard_map/near/pallas_call | solution.py:479
  24.9 0.0 copy-start.1
  24.9 0.2 collective-permute-start.1
  25.1 1.2 %collective-permute-done.1.other_ref = f32[2,16,768]{2,1,0:T(8,128)S(1)} collective-permute-done((f32[2,16,768]{2,1,0:T(8,128)S(1)}, f32[2,16,768]{2,1,0:T(8,128)S(1)}, u32[]{:S(2)}, u32[]{:S(2)}) %collective-permute-start.1) | collective-permute-done | bytes 98336 | tf_op jit(solution)/shard_map/ppermute | solution.py:496
  26.3 3.2 %all-to-all-done.1.far_ref = bf16[32,16,128]{2,1,0:T(8,128)(2,1)S(1)} async-done(((bf16[32,16,128]{2,1,0:T(8,128)(2,1)}), bf16[32,16,128]{2,1,0:T(8,128)(2,1)S(1)}, u32[]{:S(2)}, u32[]{:S(2)}) %all-to-all-start.1) | async-done | bytes 131104 | tf_op jit(solution)/shard_map/all_to_all | solution.py:477
  29.6 0.0 copy-done.1
  29.6 0.9 %finish.1 = f32[4,16,768]{2,1,0:T(8,128)} custom-call(f32[4,16,768]{2,1,0:T(8,128)S(1)} %gather_near.1.near_ref, bf16[32,16,128]{2,1,0:T(8,128)(2,1)S(1)} %all-to-all-done.1.far_ref, bf16[4,32,768]{2,1,0:T(8,128)(2,1)S(1)} %copy-done.1), custom_call_target="tpu_custom_call" | custom-call | tf_op jit(solution)/shard_map/finish/pallas_call | solution.py:508
  (2 shorter events, 0.1 us)
Async XLA Ops:
  0.7 9.1 %copy-start = (f32[4,16,768]{2,1,0:T(8,128)S(1)}, f32[4,16,768]{2,1,0:T(8,128)}, u32[]{:S(2)}) copy-start(f32[4,16,768]{2,1,0:T(8,128)} %slip_ref.1) | copy-start | bytes 589828
  2.4 7.4 %copy-start.2 = (s32[3,1024]{1,0:T(4,128)S(1)}, s32[3,1024]{1,0:T(4,128)}, u32[]{:S(2)}) copy-start(s32[3,1024]{1,0:T(4,128)} %triangles_ref.1) | copy-start | bytes 36868
  2.4 7.4 %copy-start.3 = (f32[3,561]{1,0:T(4,128)S(1)}, f32[3,561]{1,0:T(4,128)}, u32[]{:S(2)}) copy-start(f32[3,561]{1,0:T(4,128)} %vertices_ref.1) | copy-start | bytes 20200
  2.5 7.4 %copy-start.4 = (s32[4,256]{1,0:T(4,128)S(1)}, s32[4,256]{1,0:T(4,128)}, u32[]{:S(2)}) copy-start(s32[4,256]{1,0:T(4,128)} %map_ref.1) | copy-start | bytes 12292
  2.5 14.6 %all-to-all-start = ((bf16[32,8,128]{2,1,0:T(8,128)(2,1)}), bf16[32,8,128]{2,1,0:T(8,128)(2,1)S(1)}, u32[]{:S(2)}, u32[]{:S(2)}) async-start(bf16[32,8,128]{2,1,0:T(8,128)(2,1)} %coeffs.1.after_ref), calls=%async_computation | async-start | bytes 131072 | tf_op jit(solution)/shard_map/all_to_all | solution.py:410
  9.8 4.0 %copy-start.6 = (bf16[16,1024]{1,0:T(8,128)(2,1)S(1)}, bf16[16,1024]{1,0:T(8,128)(2,1)}, u32[]{:S(2)}) copy-start(bf16[16,1024]{1,0:T(8,128)(2,1)} %param.16) | copy-start | bytes 98308
  10.1 3.9 %copy-start.5 = (s32[2,16]{1,0:T(2,128)S(1)}, s32[2,16]{1,0:T(2,128)}, u32[]{:S(2)}) copy-start(s32[2,16]{1,0:T(2,128)} %pairs_ref.1) | copy-start | bytes 388
  10.1 11.1 %collective-permute-start = (bf16[2,16,1024]{2,1,0:T(8,128)(2,1)S(1)}, bf16[2,16,1024]{2,1,0:T(8,128)(2,1)S(1)}, u32[]{:S(2)}, u32[]{:S(2)}) collective-permute-start(bf16[2,16,1024]{2,1,0:T(8,128)(2,1)S(1)} %get-tuple-element.17), channel_id=1, source_target_pairs={{0,1},{1,2},{2,3},{3,4},{4,5},{5,6},{6,7},{9,8},{10,9},{11,10},{12... | collective-permute-start | bytes 196616 | tf_op jit(solution)/shard_map/ppermute | solution.py:433
  18.6 11.0 %all-to-all-start.1 = ((bf16[32,16,128]{2,1,0:T(8,128)(2,1)}), bf16[32,16,128]{2,1,0:T(8,128)(2,1)S(1)}, u32[]{:S(2)}, u32[]{:S(2)}) async-start(bf16[32,16,128]{2,1,0:T(8,128)(2,1)} %get-tuple-element.24), calls=%async_computation.1 | async-start | bytes 262144 | tf_op jit(solution)/shard_map/all_to_all | solution.py:477
  24.9 4.6 %copy-start.1 = (bf16[4,32,768]{2,1,0:T(8,128)(2,1)S(1)}, bf16[4,32,768]{2,1,0:T(8,128)(2,1)}, u32[]{:S(2)}) copy-start(bf16[4,32,768]{2,1,0:T(8,128)(2,1)} %basis_ref.1) | copy-start | bytes 589828
  24.9 1.4 %collective-permute-start.1 = (f32[2,16,768]{2,1,0:T(8,128)S(1)}, f32[2,16,768]{2,1,0:T(8,128)S(1)}, u32[]{:S(2)}, u32[]{:S(2)}) collective-permute-start(f32[2,16,768]{2,1,0:T(8,128)S(1)} %near.1.own_ref), channel_id=1, source_target_pairs={{0,8},{8,0},{16,24},{24,16},{1,9},{9,1},{17,25},{25,17},{2,10},{10... | collective-permute-start | bytes 294920 | tf_op jit(solution)/shard_map/ppermute | solution.py:496

commit v24 on v20

--- a/solution.py
+++ b/solution.py
@@ -17,6 +17,12 @@
 SMEM = pl.BlockSpec(memory_space=pltpu.SMEM)
 HBM = pl.BlockSpec(memory_space=pltpu.HBM)
 ANY = pl.BlockSpec(memory_space=pl.ANY)
+
+
+def everyone_sends(chunks, row_count, long_count):
+    rows = [(row + row_count // 2) % row_count for row in range(row_count)]
+    order = [[row * long_count + owner for row in rows for owner in range(long_count)]]
+    return lax.all_to_all(chunks, ("row", "long"), 0, 0, axis_index_groups=order, tiled=True)
 
 
 def lane_gather(table, index):
@@ -270,10 +276,11 @@
 
 
 def coupling_kernel(
-    coupling_ref, pairs_ref, after_ref, to_second_ref, to_first_ref, list_ref, *, clusters, long_count
+    coupling_ref, pairs_ref, after_ref, to_second_ref, to_first_ref, list_ref, *, clusters, long_count, row_count
 ):
     owner, group = pairs_ref[...] // clusters, pairs_ref[...] % clusters
-    list_ref[...] = jnp.concatenate([group * long_count + owner, owner, group], axis=0)
+    at = (group + row_count // 2) % row_count * long_count + owner
+    list_ref[...] = jnp.concatenate([at, owner, group], axis=0)
     pair_count, rank_size, _ = coupling_ref.shape
     groups = LANES // rank_size
     for pair_id in range(pair_count):
@@ -406,7 +413,7 @@
         ],
         near_count,
     )
-    everyone = lax.all_to_all(pay, ("row", "long"), 0, 0, tiled=True)
+    everyone = everyone_sends(pay, row_count, long_count)
 
     xs, to_neighbour, geometry = pl.pallas_call(
         geometry_kernel,
@@ -445,7 +452,9 @@
     )(xs, geometry, halo)
 
     to_second, to_first, pair_list = pl.pallas_call(
-        functools.partial(coupling_kernel, clusters=clusters, long_count=long_count),
+        functools.partial(
+            coupling_kernel, clusters=clusters, long_count=long_count, row_count=row_count
+        ),
         out_shape=[jax.ShapeDtypeStruct((coupling.shape[0] * rank_size, LANES), jnp.bfloat16)] * 2
         + [jax.ShapeDtypeStruct((6,) + far_pairs.shape[1:], far_pairs.dtype)],
         in_specs=[VMEM, VMEM, ANY],
@@ -472,7 +481,7 @@
         compiler_params=pltpu.CompilerParams(vmem_limit_bytes=16 << 20),
         name="far",
     )(pair_list, everyone, to_second, to_first)
-    far_terms = lax.all_to_all(far, ("row", "long"), 0, 0, tiled=True)
+    far_terms = everyone_sends(far, row_count, long_count)
 
     near = pl.pallas_call(
         functools.partial(near_kernel, long_count=long_count, clusters=clusters),

time: 30.2 us -> 30.2 us (level)
  no operation moved by 1% of the time
where the time goes in v24:
time: 30.2 us; the launch traced here: 29.8 us
  starting transfers between devices  13.7 us (45%)
  Pallas kernels  8.57 us (28%)
  waiting for transfers between devices  6.5 us (22%)
  between operations  0.84 us (3%)
    all_to_all x2, starting transfers between devices, everyone_sends(): lax.all_to_all(chunks, ('row', 'long'), 0, 0, axis_index_groups=order, ti...  9.9 us
    all_to_all x2, waiting for transfers between devices, everyone_sends(): lax.all_to_all(chunks, ('row', 'long'), 0, 0, axis_index_groups=order, ti...  5.31 us
    pallas_call x1, Pallas kernels, shards(): pl.pallas_call(functools.partial(near_kernel, long_count=long_count, clus...  3.68 us
    ppermute x1, starting transfers between devices, shards(): halo = lax.ppermute(to_neighbour, ('row', 'long'), route)  3.68 us
    pallas_call x1, Pallas kernels, shards(): pl.pallas_call(coeffs_kernel, out_shape=jax.ShapeDtypeStruct((devices, rh...  1.76 us
    pallas_call x1, Pallas kernels, shards(): pl.pallas_call(functools.partial(far_kernel, clusters=clusters), out_shap...  1.54 us
    ppermute x1, waiting for transfers between devices, shards(): other = lax.ppermute(near, 'row', partner)  1.19 us
    pallas_call x1, Pallas kernels, shards(): pl.pallas_call(finish_kernel, out_shape=jax.ShapeDtypeStruct(slip.shape,...  0.89 us
  transfers between devices with their start and end apart: 4, of which 3 were waited for; matrix products, arithmetic and copies ran while one was open for 0% of the time, Pallas kernels for 20%

profile of v24, /device:TPU:0, one launch (start us, length us, event | category | flops | bytes accessed | tf_op | source)
XLA Modules:
  0.0 29.8 jit_solution(5620135948744076980)
XLA Ops:
  0.7 0.0 copy-start
  0.7 1.8 %coeffs.1.after_ref = bf16[32,8,128]{2,1,0:T(8,128)(2,1)} custom-call(f32[4,16,768]{2,1,0:T(8,128)} %slip_ref.1, bf16[4,32,768]{2,1,0:T(8,128)(2,1)} %basis_ref.1, s32[2,20]{1,0:T(2,128)} %pairs_hbm.1, s32[1]{0:T(128)S(6)} %copy.10.count_ref), custom_call_target="tpu_custom_call" | custom-call | tf_op jit(solution)/shard_map/coeffs/pallas_call | solution.py:394
  2.4 0.0 copy-start.2
  2.4 0.0 copy-start.3
  2.5 0.0 copy-start.4
  2.5 7.3 %all-to-all-start = ((bf16[32,8,128]{2,1,0:T(8,128)(2,1)}), bf16[32,8,128]{2,1,0:T(8,128)(2,1)S(1)}, u32[]{:S(2)}, u32[]{:S(2)}) async-start(bf16[32,8,128]{2,1,0:T(8,128)(2,1)} %coeffs.1.after_ref), calls=%async_computation | async-start | bytes 131072 | tf_op jit(solution)/shard_map/all_to_all | solution.py:25
  9.8 0.0 copy-done
  9.8 0.0 copy-done.2
  9.8 0.0 copy-done.3
  9.8 0.0 copy-done.4
  9.8 0.0 copy-start.6
  9.8 0.3 geometry.1
  10.1 0.0 copy-start.5
  10.1 3.7 %collective-permute-start = (bf16[2,16,1024]{2,1,0:T(8,128)(2,1)S(1)}, bf16[2,16,1024]{2,1,0:T(8,128)(2,1)S(1)}, u32[]{:S(2)}, u32[]{:S(2)}) collective-permute-start(bf16[2,16,1024]{2,1,0:T(8,128)(2,1)S(1)} %get-tuple-element.17), channel_id=1, source_target_pairs={{0,1},{1,2},{2,3},{3,4},{4,5},{5,6},{6,7},{9,8},{10,9},{11,10},{12... | collective-permute-start | bytes 196616 | tf_op jit(solution)/shard_map/ppermute | solution.py:439
  13.8 0.0 copy-done.6
  13.8 0.1 reshape.3.coupling_ref
  14.0 0.0 copy-done.5
  14.0 0.4 %coupling.1 = (bf16[512,128]{1,0:T(8,128)(2,1)S(1)}, bf16[512,128]{1,0:T(8,128)(2,1)S(1)}, s32[6,16]{1,0:T(8,128)S(1)}) custom-call(bf16[16,32,32]{2,1,0:T(8,128)(2,1)S(1)} %reshape.3.coupling_ref, s32[2,16]{1,0:T(2,128)S(1)} %copy-done.5, bf16[32,8,128]{2,1,0:T(8,128)(2,1)} %coeffs.1.after_ref), custom_call_target="tpu_custom_call" | custom-call | flops 1000 | bytes 1000 | tf_op jit(solution)/shard_map/coupling/pallas_call | solution.py:454
  14.3 2.7 %all-to-all-done.coeff_ref.pay_ref = bf16[32,8,128]{2,1,0:T(8,128)(2,1)S(1)} async-done(((bf16[32,8,128]{2,1,0:T(8,128)(2,1)}), bf16[32,8,128]{2,1,0:T(8,128)(2,1)S(1)}, u32[]{:S(2)}, u32[]{:S(2)}) %all-to-all-start) | async-done | bytes 65568 | tf_op jit(solution)/shard_map/all_to_all | solution.py:25
  17.1 1.5 %far.1 = (bf16[32,16,128]{2,1,0:T(8,128)(2,1)}, f32[8,128]{1,0:T(8,128)S(1)}) custom-call(s32[6,16]{1,0:T(8,128)S(1)} %get-tuple-element.20.list_ref, bf16[32,8,128]{2,1,0:T(8,128)(2,1)S(1)} %all-to-all-done.coeff_ref.pay_ref, bf16[512,128]{1,0:T(8,128)(2,1)S(1)} %get-tuple-element.21.to_second_ref, bf16[512,128]{1,0:T(8,128)(2,1)S(1)} %get-tuple-element.22.to_first_ref), custom_call_target="tpu_custom_call" | custom-call | tf_op jit(solution)/shard_map/far/pallas_call | solution.py:466
  18.6 2.6 %all-to-all-start.1 = ((bf16[32,16,128]{2,1,0:T(8,128)(2,1)}), bf16[32,16,128]{2,1,0:T(8,128)(2,1)S(1)}, u32[]{:S(2)}, u32[]{:S(2)}) async-start(bf16[32,16,128]{2,1,0:T(8,128)(2,1)} %get-tuple-element.24), calls=%async_computation.1 | async-start | bytes 262144 | tf_op jit(solution)/shard_map/all_to_all | solution.py:25
  21.2 0.0 collective-permute-done.halo_ref
  21.3 3.7 %near.1.own_ref = f32[2,16,768]{2,1,0:T(8,128)S(1)} custom-call(bf16[6,16,768]{2,1,0:T(8,128)(2,1)S(1)} %get-tuple-element.18.slip_ref, f32[6,4,256]{2,1,0:T(4,128)S(1)} %get-tuple-element.19.place_ref, bf16[32,8,128]{2,1,0:T(8,128)(2,1)S(1)} %all-to-all-done.coeff_ref.pay_ref, f32[8,128]{1,0:T(8,128)S(1)} %get-tuple-element.23.after_ref), custom_call_target="tpu_custom_call" | custom-call | flops 1000000000 | bytes 1000000 | tf_op jit(solution)/shard_map/near/pallas_call | solution.py:486
  24.9 0.0 copy-start.1
  24.9 0.2 collective-permute-start.1
  25.1 1.2 %collective-permute-done.1.other_ref = f32[2,16,768]{2,1,0:T(8,128)S(1)} collective-permute-done((f32[2,16,768]{2,1,0:T(8,128)S(1)}, f32[2,16,768]{2,1,0:T(8,128)S(1)}, u32[]{:S(2)}, u32[]{:S(2)}) %collective-permute-start.1) | collective-permute-done | bytes 98336 | tf_op jit(solution)/shard_map/ppermute | solution.py:503
  26.3 2.6 %all-to-all-done.1.far_ref = bf16[32,16,128]{2,1,0:T(8,128)(2,1)S(1)} async-done(((bf16[32,16,128]{2,1,0:T(8,128)(2,1)}), bf16[32,16,128]{2,1,0:T(8,128)(2,1)S(1)}, u32[]{:S(2)}, u32[]{:S(2)}) %all-to-all-start.1) | async-done | bytes 131104 | tf_op jit(solution)/shard_map/all_to_all | solution.py:25
  28.9 0.0 copy-done.1
  28.9 0.9 %finish.1 = f32[4,16,768]{2,1,0:T(8,128)} custom-call(f32[4,16,768]{2,1,0:T(8,128)S(1)} %gather_near.1.near_ref, bf16[32,16,128]{2,1,0:T(8,128)(2,1)S(1)} %all-to-all-done.1.far_ref, bf16[4,32,768]{2,1,0:T(8,128)(2,1)S(1)} %copy-done.1), custom_call_target="tpu_custom_call" | custom-call | tf_op jit(solution)/shard_map/finish/pallas_call | solution.py:515
  (2 shorter events, 0.1 us)
Async XLA Ops:
  0.7 9.1 %copy-start = (f32[4,16,768]{2,1,0:T(8,128)S(1)}, f32[4,16,768]{2,1,0:T(8,128)}, u32[]{:S(2)}) copy-start(f32[4,16,768]{2,1,0:T(8,128)} %slip_ref.1) | copy-start | bytes 589828
  2.4 7.4 %copy-start.2 = (s32[3,1024]{1,0:T(4,128)S(1)}, s32[3,1024]{1,0:T(4,128)}, u32[]{:S(2)}) copy-start(s32[3,1024]{1,0:T(4,128)} %triangles_ref.1) | copy-start | bytes 36868
  2.4 7.4 %copy-start.3 = (f32[3,561]{1,0:T(4,128)S(1)}, f32[3,561]{1,0:T(4,128)}, u32[]{:S(2)}) copy-start(f32[3,561]{1,0:T(4,128)} %vertices_ref.1) | copy-start | bytes 20200
  2.5 7.4 %copy-start.4 = (s32[4,256]{1,0:T(4,128)S(1)}, s32[4,256]{1,0:T(4,128)}, u32[]{:S(2)}) copy-start(s32[4,256]{1,0:T(4,128)} %map_ref.1) | copy-start | bytes 12292
  2.5 14.6 %all-to-all-start = ((bf16[32,8,128]{2,1,0:T(8,128)(2,1)}), bf16[32,8,128]{2,1,0:T(8,128)(2,1)S(1)}, u32[]{:S(2)}, u32[]{:S(2)}) async-start(bf16[32,8,128]{2,1,0:T(8,128)(2,1)} %coeffs.1.after_ref), calls=%async_computation | async-start | bytes 131072 | tf_op jit(solution)/shard_map/all_to_all | solution.py:25
  9.8 4.0 %copy-start.6 = (bf16[16,1024]{1,0:T(8,128)(2,1)S(1)}, bf16[16,1024]{1,0:T(8,128)(2,1)}, u32[]{:S(2)}) copy-start(bf16[16,1024]{1,0:T(8,128)(2,1)} %param.16) | copy-start | bytes 98308
  10.1 3.9 %copy-start.5 = (s32[2,16]{1,0:T(2,128)S(1)}, s32[2,16]{1,0:T(2,128)}, u32[]{:S(2)}) copy-start(s32[2,16]{1,0:T(2,128)} %pairs_ref.1) | copy-start | bytes 388
  10.1 11.1 %collective-permute-start = (bf16[2,16,1024]{2,1,0:T(8,128)(2,1)S(1)}, bf16[2,16,1024]{2,1,0:T(8,128)(2,1)S(1)}, u32[]{:S(2)}, u32[]{:S(2)}) collective-permute-start(bf16[2,16,1024]{2,1,0:T(8,128)(2,1)S(1)} %get-tuple-element.17), channel_id=1, source_target_pairs={{0,1},{1,2},{2,3},{3,4},{4,5},{5,6},{6,7},{9,8},{10,9},{11,10},{12... | collective-permute-start | bytes 196616 | tf_op jit(solution)/shard_map/ppermute | solution.py:439
  18.6 10.3 %all-to-all-start.1 = ((bf16[32,16,128]{2,1,0:T(8,128)(2,1)}), bf16[32,16,128]{2,1,0:T(8,128)(2,1)S(1)}, u32[]{:S(2)}, u32[]{:S(2)}) async-start(bf16[32,16,128]{2,1,0:T(8,128)(2,1)} %get-tuple-element.24), calls=%async_computation.1 | async-start | bytes 262144 | tf_op jit(solution)/shard_map/all_to_all | solution.py:25
  24.9 4.0 %copy-start.1 = (bf16[4,32,768]{2,1,0:T(8,128)(2,1)S(1)}, bf16[4,32,768]{2,1,0:T(8,128)(2,1)}, u32[]{:S(2)}) copy-start(bf16[4,32,768]{2,1,0:T(8,128)(2,1)} %basis_ref.1) | copy-start | bytes 589828
  24.9 1.4 %collective-permute-start.1 = (f32[2,16,768]{2,1,0:T(8,128)S(1)}, f32[2,16,768]{2,1,0:T(8,128)S(1)}, u32[]{:S(2)}, u32[]{:S(2)}) collective-permute-start(f32[2,16,768]{2,1,0:T(8,128)S(1)} %near.1.own_ref), channel_id=1, source_target_pairs={{0,8},{8,0},{16,24},{24,16},{1,9},{9,1},{17,25},{25,17},{2,10},{10... | collective-permute-start | bytes 294920 | tf_op jit(solution)/shard_map/ppermute | solution.py:503

commit v25 on v20

--- a/solution.py
+++ b/solution.py
@@ -408,6 +408,7 @@
     )
     everyone = lax.all_to_all(pay, ("row", "long"), 0, 0, tiled=True)
 
+    slip_later, pay = lax.optimization_barrier((slip, pay))
     xs, to_neighbour, geometry = pl.pallas_call(
         geometry_kernel,
         out_shape=[
@@ -422,7 +423,7 @@
             flops=2_000_000, bytes_accessed=1_000_000, transcendentals=1_000
         ),
         name="geometry",
-    )(slip, vertices, triangles, elem_map, pay)
+    )(slip_later, vertices, triangles, elem_map, pay)
     route = []
     for row in range(row_count):
         step = 1 if row % 2 == 0 else -1

time: 30.2 us -> 30.2 us (level)
  no operation moved by 1% of the time
where the time goes in v25:
time: 30.2 us; the launch traced here: 29.8 us
  starting transfers between devices  13.7 us (45%)
  Pallas kernels  8.56 us (28%)
  waiting for transfers between devices  6.5 us (22%)
  between operations  0.84 us (3%)
    all_to_all x1, starting transfers between devices, shards(): everyone = lax.all_to_all(pay, ('row', 'long'), 0, 0, tiled=True)  7.3 us
    pallas_call x1, Pallas kernels, shards(): pl.pallas_call(functools.partial(near_kernel, long_count=long_count, clus...  3.68 us
    ppermute x1, starting transfers between devices, shards(): halo = lax.ppermute(to_neighbour, ('row', 'long'), route)  3.68 us
    all_to_all x1, waiting for transfers between devices, shards(): everyone = lax.all_to_all(pay, ('row', 'long'), 0, 0, tiled=True)  2.71 us
    all_to_all x1, waiting for transfers between devices, shards(): far_terms = lax.all_to_all(far, ('row', 'long'), 0, 0, tiled=True)  2.6 us
    all_to_all x1, starting transfers between devices, shards(): far_terms = lax.all_to_all(far, ('row', 'long'), 0, 0, tiled=True)  2.59 us
    pallas_call x1, Pallas kernels, shards(): pl.pallas_call(coeffs_kernel, out_shape=jax.ShapeDtypeStruct((devices, rh...  1.76 us
    pallas_call x1, Pallas kernels, shards(): pl.pallas_call(functools.partial(far_kernel, clusters=clusters), out_shap...  1.54 us
  transfers between devices with their start and end apart: 4, of which 3 were waited for; matrix products, arithmetic and copies ran while one was open for 0% of the time, Pallas kernels for 20%

profile of v25, /device:TPU:0, one launch (start us, length us, event | category | flops | bytes accessed | tf_op | source)
XLA Modules:
  0.0 29.8 jit_solution(8835132653773989507)
XLA Ops:
  0.7 0.0 copy-start
  0.7 1.8 %coeffs.1.after_ref = bf16[32,8,128]{2,1,0:T(8,128)(2,1)} custom-call(f32[4,16,768]{2,1,0:T(8,128)} %slip_ref, bf16[4,32,768]{2,1,0:T(8,128)(2,1)} %basis_ref.1, s32[2,20]{1,0:T(2,128)} %pairs_hbm.1, s32[1]{0:T(128)S(6)} %copy.10.count_ref), custom_call_target="tpu_custom_call" | custom-call | tf_op jit(solution)/shard_map/coeffs/pallas_call | solution.py:387
  2.4 0.0 copy-start.2
  2.4 0.0 copy-start.3
  2.5 0.0 copy-start.4
  2.5 7.3 %all-to-all-start = ((bf16[32,8,128]{2,1,0:T(8,128)(2,1)}), bf16[32,8,128]{2,1,0:T(8,128)(2,1)S(1)}, u32[]{:S(2)}, u32[]{:S(2)}) async-start(bf16[32,8,128]{2,1,0:T(8,128)(2,1)} %coeffs.1.after_ref), calls=%async_computation | async-start | bytes 131072 | tf_op jit(solution)/shard_map/all_to_all | solution.py:409
  9.8 0.0 copy-done
  9.8 0.0 copy-done.2
  9.8 0.0 copy-done.3
  9.8 0.0 copy-done.4
  9.8 0.0 copy-start.6
  9.8 0.3 geometry.1
  10.1 0.0 copy-start.5
  10.1 3.7 %collective-permute-start = (bf16[2,16,1024]{2,1,0:T(8,128)(2,1)S(1)}, bf16[2,16,1024]{2,1,0:T(8,128)(2,1)S(1)}, u32[]{:S(2)}, u32[]{:S(2)}) collective-permute-start(bf16[2,16,1024]{2,1,0:T(8,128)(2,1)S(1)} %get-tuple-element.21), channel_id=1, source_target_pairs={{0,1},{1,2},{2,3},{3,4},{4,5},{5,6},{6,7},{9,8},{10,9},{11,10},{12... | collective-permute-start | bytes 196616 | tf_op jit(solution)/shard_map/ppermute | solution.py:433
  13.8 0.0 copy-done.6
  13.8 0.1 reshape.3.coupling_ref
  14.0 0.0 copy-done.5
  14.0 0.4 %coupling.1 = (bf16[512,128]{1,0:T(8,128)(2,1)S(1)}, bf16[512,128]{1,0:T(8,128)(2,1)S(1)}, s32[6,16]{1,0:T(8,128)S(1)}) custom-call(bf16[16,32,32]{2,1,0:T(8,128)(2,1)S(1)} %reshape.3.coupling_ref, s32[2,16]{1,0:T(2,128)S(1)} %copy-done.5, bf16[32,8,128]{2,1,0:T(8,128)(2,1)} %coeffs.1.after_ref), custom_call_target="tpu_custom_call" | custom-call | flops 1000 | bytes 1000 | tf_op jit(solution)/shard_map/coupling/pallas_call | solution.py:448
  14.3 2.7 %all-to-all-done.coeff_ref.pay_ref = bf16[32,8,128]{2,1,0:T(8,128)(2,1)S(1)} async-done(((bf16[32,8,128]{2,1,0:T(8,128)(2,1)}), bf16[32,8,128]{2,1,0:T(8,128)(2,1)S(1)}, u32[]{:S(2)}, u32[]{:S(2)}) %all-to-all-start) | async-done | bytes 65568 | tf_op jit(solution)/shard_map/all_to_all | solution.py:409
  17.1 1.5 %far.1 = (bf16[32,16,128]{2,1,0:T(8,128)(2,1)}, f32[8,128]{1,0:T(8,128)S(1)}) custom-call(s32[6,16]{1,0:T(8,128)S(1)} %get-tuple-element.24.list_ref, bf16[32,8,128]{2,1,0:T(8,128)(2,1)S(1)} %all-to-all-done.coeff_ref.pay_ref, bf16[512,128]{1,0:T(8,128)(2,1)S(1)} %get-tuple-element.25.to_second_ref, bf16[512,128]{1,0:T(8,128)(2,1)S(1)} %get-tuple-element.26.to_first_ref), custom_call_target="tpu_custom_call" | custom-call | tf_op jit(solution)/shard_map/far/pallas_call | solution.py:458
  18.6 2.6 %all-to-all-start.1 = ((bf16[32,16,128]{2,1,0:T(8,128)(2,1)}), bf16[32,16,128]{2,1,0:T(8,128)(2,1)S(1)}, u32[]{:S(2)}, u32[]{:S(2)}) async-start(bf16[32,16,128]{2,1,0:T(8,128)(2,1)} %get-tuple-element.28), calls=%async_computation.1 | async-start | bytes 262144 | tf_op jit(solution)/shard_map/all_to_all | solution.py:476
  21.2 0.0 collective-permute-done.halo_ref
  21.3 3.7 %near.1.own_ref = f32[2,16,768]{2,1,0:T(8,128)S(1)} custom-call(bf16[6,16,768]{2,1,0:T(8,128)(2,1)S(1)} %get-tuple-element.22.slip_ref, f32[6,4,256]{2,1,0:T(4,128)S(1)} %get-tuple-element.23.place_ref, bf16[32,8,128]{2,1,0:T(8,128)(2,1)S(1)} %all-to-all-done.coeff_ref.pay_ref, f32[8,128]{1,0:T(8,128)S(1)} %get-tuple-element.27.after_ref), custom_call_target="tpu_custom_call" | custom-call | flops 1000000000 | bytes 1000000 | tf_op jit(solution)/shard_map/near/pallas_call | solution.py:478
  24.9 0.0 copy-start.1
  24.9 0.2 collective-permute-start.1
  25.1 1.2 %collective-permute-done.1.other_ref = f32[2,16,768]{2,1,0:T(8,128)S(1)} collective-permute-done((f32[2,16,768]{2,1,0:T(8,128)S(1)}, f32[2,16,768]{2,1,0:T(8,128)S(1)}, u32[]{:S(2)}, u32[]{:S(2)}) %collective-permute-start.1) | collective-permute-done | bytes 98336 | tf_op jit(solution)/shard_map/ppermute | solution.py:495
  26.3 2.6 %all-to-all-done.1.far_ref = bf16[32,16,128]{2,1,0:T(8,128)(2,1)S(1)} async-done(((bf16[32,16,128]{2,1,0:T(8,128)(2,1)}), bf16[32,16,128]{2,1,0:T(8,128)(2,1)S(1)}, u32[]{:S(2)}, u32[]{:S(2)}) %all-to-all-start.1) | async-done | bytes 131104 | tf_op jit(solution)/shard_map/all_to_all | solution.py:476
  28.9 0.0 copy-done.1
  28.9 0.9 %finish.1 = f32[4,16,768]{2,1,0:T(8,128)} custom-call(f32[4,16,768]{2,1,0:T(8,128)S(1)} %gather_near.1.near_ref, bf16[32,16,128]{2,1,0:T(8,128)(2,1)S(1)} %all-to-all-done.1.far_ref, bf16[4,32,768]{2,1,0:T(8,128)(2,1)S(1)} %copy-done.1), custom_call_target="tpu_custom_call" | custom-call | tf_op jit(solution)/shard_map/finish/pallas_call | solution.py:507
  (2 shorter events, 0.1 us)
Async XLA Ops:
  0.7 9.1 %copy-start = (f32[4,16,768]{2,1,0:T(8,128)S(1)}, f32[4,16,768]{2,1,0:T(8,128)}, u32[]{:S(2)}) copy-start(f32[4,16,768]{2,1,0:T(8,128)} %slip_ref) | copy-start | bytes 589828
  2.4 7.4 %copy-start.2 = (s32[3,1024]{1,0:T(4,128)S(1)}, s32[3,1024]{1,0:T(4,128)}, u32[]{:S(2)}) copy-start(s32[3,1024]{1,0:T(4,128)} %triangles_ref.1) | copy-start | bytes 36868
  2.4 7.4 %copy-start.3 = (f32[3,561]{1,0:T(4,128)S(1)}, f32[3,561]{1,0:T(4,128)}, u32[]{:S(2)}) copy-start(f32[3,561]{1,0:T(4,128)} %vertices_ref.1) | copy-start | bytes 20200
  2.5 7.4 %copy-start.4 = (s32[4,256]{1,0:T(4,128)S(1)}, s32[4,256]{1,0:T(4,128)}, u32[]{:S(2)}) copy-start(s32[4,256]{1,0:T(4,128)} %map_ref.1) | copy-start | bytes 12292
  2.5 14.6 %all-to-all-start = ((bf16[32,8,128]{2,1,0:T(8,128)(2,1)}), bf16[32,8,128]{2,1,0:T(8,128)(2,1)S(1)}, u32[]{:S(2)}, u32[]{:S(2)}) async-start(bf16[32,8,128]{2,1,0:T(8,128)(2,1)} %coeffs.1.after_ref), calls=%async_computation | async-start | bytes 131072 | tf_op jit(solution)/shard_map/all_to_all | solution.py:409
  9.8 4.0 %copy-start.6 = (bf16[16,1024]{1,0:T(8,128)(2,1)S(1)}, bf16[16,1024]{1,0:T(8,128)(2,1)}, u32[]{:S(2)}) copy-start(bf16[16,1024]{1,0:T(8,128)(2,1)} %param.16) | copy-start | bytes 98308
  10.1 3.9 %copy-start.5 = (s32[2,16]{1,0:T(2,128)S(1)}, s32[2,16]{1,0:T(2,128)}, u32[]{:S(2)}) copy-start(s32[2,16]{1,0:T(2,128)} %pairs_ref.1) | copy-start | bytes 388
  10.1 11.1 %collective-permute-start = (bf16[2,16,1024]{2,1,0:T(8,128)(2,1)S(1)}, bf16[2,16,1024]{2,1,0:T(8,128)(2,1)S(1)}, u32[]{:S(2)}, u32[]{:S(2)}) collective-permute-start(bf16[2,16,1024]{2,1,0:T(8,128)(2,1)S(1)} %get-tuple-element.21), channel_id=1, source_target_pairs={{0,1},{1,2},{2,3},{3,4},{4,5},{5,6},{6,7},{9,8},{10,9},{11,10},{12... | collective-permute-start | bytes 196616 | tf_op jit(solution)/shard_map/ppermute | solution.py:433
  18.6 10.3 %all-to-all-start.1 = ((bf16[32,16,128]{2,1,0:T(8,128)(2,1)}), bf16[32,16,128]{2,1,0:T(8,128)(2,1)S(1)}, u32[]{:S(2)}, u32[]{:S(2)}) async-start(bf16[32,16,128]{2,1,0:T(8,128)(2,1)} %get-tuple-element.28), calls=%async_computation.1 | async-start | bytes 262144 | tf_op jit(solution)/shard_map/all_to_all | solution.py:476
  24.9 4.0 %copy-start.1 = (bf16[4,32,768]{2,1,0:T(8,128)(2,1)S(1)}, bf16[4,32,768]{2,1,0:T(8,128)(2,1)}, u32[]{:S(2)}) copy-start(bf16[4,32,768]{2,1,0:T(8,128)(2,1)} %basis_ref.1) | copy-start | bytes 589828
  24.9 1.4 %collective-permute-start.1 = (f32[2,16,768]{2,1,0:T(8,128)S(1)}, f32[2,16,768]{2,1,0:T(8,128)S(1)}, u32[]{:S(2)}, u32[]{:S(2)}) collective-permute-start(f32[2,16,768]{2,1,0:T(8,128)S(1)} %near.1.own_ref), channel_id=1, source_target_pairs={{0,8},{8,0},{16,24},{24,16},{1,9},{9,1},{17,25},{25,17},{2,10},{10... | collective-permute-start | bytes 294920 | tf_op jit(solution)/shard_map/ppermute | solution.py:495

commit v26 on v20

--- a/solution.py
+++ b/solution.py
@@ -89,10 +89,11 @@
 
 
 def geometry_kernel(
-    slip_ref, vertices_ref, triangles_ref, map_ref, after_ref, xs_ref, halo_ref, geom_ref
+    slip_hbm, vertices_ref, triangles_ref, map_ref, after_ref, xs_ref, halo_ref, geom_ref, slip_ref, sem
 ):
-    clusters, rhs_count, unknowns = slip_ref.shape
-    xs_ref[...] = slip_ref[...].astype(jnp.bfloat16)
+    clusters, rhs_count, unknowns = slip_hbm.shape
+    fetch = pltpu.make_async_copy(slip_hbm, slip_ref, sem)
+    fetch.start()
     long_index = lax.axis_index("long")
 
     size = map_ref.shape[1]
@@ -130,6 +131,8 @@
             [whole[cluster : cluster + 1, :] for whole in geometry], axis=0
         )
 
+    fetch.wait()
+    xs_ref[...] = slip_ref[...].astype(jnp.bfloat16)
     upward = lax.axis_index("row") % 2 == 0
     start = jnp.where(upward, clusters - NEARC, 0)
     pieces = [piece for whole in geometry for piece in split_three(whole)]
@@ -415,14 +418,17 @@
             jax.ShapeDtypeStruct((NEARC, rhs_count, unknowns + size), jnp.bfloat16),
             jax.ShapeDtypeStruct((clusters, 4, size), jnp.float32),
         ],
-        in_specs=[VMEM] * 4 + [ANY],
+        in_specs=[HBM] + [VMEM] * 3 + [ANY],
         out_specs=[VMEM] * 3,
+        scratch_shapes=[pltpu.VMEM(slip.shape, slip.dtype), pltpu.SemaphoreType.DMA],
         compiler_params=pltpu.CompilerParams(vmem_limit_bytes=16 << 20),
         cost_estimate=pl.CostEstimate(
             flops=2_000_000, bytes_accessed=1_000_000, transcendentals=1_000
         ),
         name="geometry",
-    )(slip, vertices, triangles, elem_map, pay)
+    )(
+        pltpu.with_memory_space_constraint(slip, pltpu.HBM), vertices, triangles, elem_map, pay
+    )
     route = []
     for row in range(row_count):
         step = 1 if row % 2 == 0 else -1

time: 30.2 us -> 30.3 us (level)
  waiting for transfers between devices: 6.5 us -> 5.59 us
  Pallas kernels: 8.57 us -> 9.31 us
    pallas_call x1, Pallas kernels: 0.26 us -> 1.05 us  [shards(): pl.pallas_call(geometry_kernel, out_shape=[jax.ShapeDtypeStruct(slip.shap...]
    all_to_all x1, waiting for transfers between devices: 2.71 us -> 1.93 us  [shards(): everyone = lax.all_to_all(pay, ('row', 'long'), 0, 0, tiled=True)]
  transfers between devices with their start and end apart: 4 -> 4, of which waited for: 3 -> 3; matrix products, arithmetic and copies ran while one was open for 0% -> 0% of each run, Pallas kernels for 20% -> 22%
where the time goes in v26:
time: 30.3 us; the launch traced here: 29.9 us
  starting transfers between devices  14 us (46%)
  Pallas kernels  9.31 us (31%)
  waiting for transfers between devices  5.59 us (18%)
  between operations  0.82 us (3%)
    all_to_all x1, starting transfers between devices, shards(): everyone = lax.all_to_all(pay, ('row', 'long'), 0, 0, tiled=True)  7.3 us
    ppermute x1, starting transfers between devices, shards(): halo = lax.ppermute(to_neighbour, ('row', 'long'), route)  3.68 us
    pallas_call x1, Pallas kernels, shards(): pl.pallas_call(functools.partial(near_kernel, long_count=long_count, clus...  3.68 us
    all_to_all x1, starting transfers between devices, shards(): far_terms = lax.all_to_all(far, ('row', 'long'), 0, 0, tiled=True)  2.71 us
    all_to_all x1, waiting for transfers between devices, shards(): far_terms = lax.all_to_all(far, ('row', 'long'), 0, 0, tiled=True)  2.6 us
    all_to_all x1, waiting for transfers between devices, shards(): everyone = lax.all_to_all(pay, ('row', 'long'), 0, 0, tiled=True)  1.93 us
    pallas_call x1, Pallas kernels, shards(): pl.pallas_call(coeffs_kernel, out_shape=jax.ShapeDtypeStruct((devices, rh...  1.72 us
    pallas_call x1, Pallas kernels, shards(): pl.pallas_call(functools.partial(far_kernel, clusters=clusters), out_shap...  1.55 us
  transfers between devices with their start and end apart: 4, of which 3 were waited for; matrix products, arithmetic and copies ran while one was open for 0% of the time, Pallas kernels for 22%

profile of v26, /device:TPU:0, one launch (start us, length us, event | category | flops | bytes accessed | tf_op | source)
XLA Modules:
  0.0 29.9 jit_solution(6948895026782082627)
XLA Ops:
  0.7 1.7 %coeffs.1.after_ref = bf16[32,8,128]{2,1,0:T(8,128)(2,1)} custom-call(f32[4,16,768]{2,1,0:T(8,128)} %slip_hbm.3, bf16[4,32,768]{2,1,0:T(8,128)(2,1)} %basis_ref.1, s32[2,20]{1,0:T(2,128)} %pairs_hbm.1, s32[1]{0:T(128)S(6)} %copy.10.count_ref), custom_call_target="tpu_custom_call" | custom-call | tf_op jit(solution)/shard_map/coeffs/pallas_call | solution.py:390
  2.4 0.0 copy-start.1
  2.4 0.0 copy-start.2
  2.4 0.0 copy-start.3
  2.4 7.3 %all-to-all-start = ((bf16[32,8,128]{2,1,0:T(8,128)(2,1)}), bf16[32,8,128]{2,1,0:T(8,128)(2,1)S(1)}, u32[]{:S(2)}, u32[]{:S(2)}) async-start(bf16[32,8,128]{2,1,0:T(8,128)(2,1)} %coeffs.1.after_ref), calls=%async_computation | async-start | bytes 131072 | tf_op jit(solution)/shard_map/all_to_all | solution.py:412
  9.7 0.0 copy-done.1
  9.7 0.0 copy-done.2
  9.7 0.0 copy-done.3
  9.8 0.0 copy-start.5
  9.8 1.0 %geometry.1 = (bf16[4,16,768]{2,1,0:T(8,128)(2,1)S(1)}, bf16[2,16,1024]{2,1,0:T(8,128)(2,1)S(1)}, f32[4,4,256]{2,1,0:T(4,128)S(1)}) custom-call(f32[4,16,768]{2,1,0:T(8,128)} %slip_hbm.3, f32[3,561]{1,0:T(4,128)S(1)} %copy-done.2, s32[3,1024]{1,0:T(4,128)S(1)} %copy-done.1, s32[4,256]{1,0:T(4,128)S(1)} %copy-done.3, bf16[32,8,128]{2,1,0:T(8,128)(2,1)} %coeffs.1.after_ref), custom_call_target="tpu_custom_call" | custom-call | flops 2000000 | bytes 1000000 | tf_op jit(solution)/shard_map/geometry/pallas_call | solution.py:414
  10.8 0.0 copy-start.4
  10.8 3.7 %collective-permute-start = (bf16[2,16,1024]{2,1,0:T(8,128)(2,1)S(1)}, bf16[2,16,1024]{2,1,0:T(8,128)(2,1)S(1)}, u32[]{:S(2)}, u32[]{:S(2)}) collective-permute-start(bf16[2,16,1024]{2,1,0:T(8,128)(2,1)S(1)} %get-tuple-element.17), channel_id=1, source_target_pairs={{0,1},{1,2},{2,3},{3,4},{4,5},{5,6},{6,7},{9,8},{10,9},{11,10},{12... | collective-permute-start | bytes 196616 | tf_op jit(solution)/shard_map/ppermute | solution.py:438
  14.5 0.0 copy-done.5
  14.5 0.1 reshape.3.coupling_ref
  14.7 0.0 copy-done.4
  14.7 0.4 %coupling.1 = (bf16[512,128]{1,0:T(8,128)(2,1)S(1)}, bf16[512,128]{1,0:T(8,128)(2,1)S(1)}, s32[6,16]{1,0:T(8,128)S(1)}) custom-call(bf16[16,32,32]{2,1,0:T(8,128)(2,1)S(1)} %reshape.3.coupling_ref, s32[2,16]{1,0:T(2,128)S(1)} %copy-done.4, bf16[32,8,128]{2,1,0:T(8,128)(2,1)} %coeffs.1.after_ref), custom_call_target="tpu_custom_call" | custom-call | flops 1000 | bytes 1000 | tf_op jit(solution)/shard_map/coupling/pallas_call | solution.py:453
  15.1 1.9 %all-to-all-done.coeff_ref.pay_ref = bf16[32,8,128]{2,1,0:T(8,128)(2,1)S(1)} async-done(((bf16[32,8,128]{2,1,0:T(8,128)(2,1)}), bf16[32,8,128]{2,1,0:T(8,128)(2,1)S(1)}, u32[]{:S(2)}, u32[]{:S(2)}) %all-to-all-start) | async-done | bytes 65568 | tf_op jit(solution)/shard_map/all_to_all | solution.py:412
  17.0 1.5 %far.1 = (bf16[32,16,128]{2,1,0:T(8,128)(2,1)}, f32[8,128]{1,0:T(8,128)S(1)}) custom-call(s32[6,16]{1,0:T(8,128)S(1)} %get-tuple-element.20.list_ref, bf16[32,8,128]{2,1,0:T(8,128)(2,1)S(1)} %all-to-all-done.coeff_ref.pay_ref, bf16[512,128]{1,0:T(8,128)(2,1)S(1)} %get-tuple-element.21.to_second_ref, bf16[512,128]{1,0:T(8,128)(2,1)S(1)} %get-tuple-element.22.to_first_ref), custom_call_target="tpu_custom_call" | custom-call | tf_op jit(solution)/shard_map/far/pallas_call | solution.py:463
  18.6 2.7 %all-to-all-start.1 = ((bf16[32,16,128]{2,1,0:T(8,128)(2,1)}), bf16[32,16,128]{2,1,0:T(8,128)(2,1)S(1)}, u32[]{:S(2)}, u32[]{:S(2)}) async-start(bf16[32,16,128]{2,1,0:T(8,128)(2,1)} %get-tuple-element.24), calls=%async_computation.1 | async-start | bytes 262144 | tf_op jit(solution)/shard_map/all_to_all | solution.py:481
  21.3 0.0 collective-permute-done.halo_ref
  21.3 3.7 %near.1.own_ref = f32[2,16,768]{2,1,0:T(8,128)S(1)} custom-call(bf16[6,16,768]{2,1,0:T(8,128)(2,1)S(1)} %get-tuple-element.18.slip_ref, f32[6,4,256]{2,1,0:T(4,128)S(1)} %get-tuple-element.19.place_ref, bf16[32,8,128]{2,1,0:T(8,128)(2,1)S(1)} %all-to-all-done.coeff_ref.pay_ref, f32[8,128]{1,0:T(8,128)S(1)} %get-tuple-element.23.after_ref), custom_call_target="tpu_custom_call" | custom-call | flops 1000000000 | bytes 1000000 | tf_op jit(solution)/shard_map/near/pallas_call | solution.py:483
  25.0 0.0 copy-start
  25.0 0.3 %collective-permute-start.1 = (f32[2,16,768]{2,1,0:T(8,128)S(1)}, f32[2,16,768]{2,1,0:T(8,128)S(1)}, u32[]{:S(2)}, u32[]{:S(2)}) collective-permute-start(f32[2,16,768]{2,1,0:T(8,128)S(1)} %near.1.own_ref), channel_id=1, source_target_pairs={{0,8},{8,0},{16,24},{24,16},{1,9},{9,1},{17,25},{25,17},{2,10},{10... | collective-permute-start | bytes 294920 | tf_op jit(solution)/shard_map/ppermute | solution.py:500
  25.3 1.0 %collective-permute-done.1.other_ref = f32[2,16,768]{2,1,0:T(8,128)S(1)} collective-permute-done((f32[2,16,768]{2,1,0:T(8,128)S(1)}, f32[2,16,768]{2,1,0:T(8,128)S(1)}, u32[]{:S(2)}, u32[]{:S(2)}) %collective-permute-start.1) | collective-permute-done | bytes 98336 | tf_op jit(solution)/shard_map/ppermute | solution.py:500
  26.4 2.6 %all-to-all-done.1.far_ref = bf16[32,16,128]{2,1,0:T(8,128)(2,1)S(1)} async-done(((bf16[32,16,128]{2,1,0:T(8,128)(2,1)}), bf16[32,16,128]{2,1,0:T(8,128)(2,1)S(1)}, u32[]{:S(2)}, u32[]{:S(2)}) %all-to-all-start.1) | async-done | bytes 131104 | tf_op jit(solution)/shard_map/all_to_all | solution.py:481
  29.0 0.0 copy-done
  29.0 0.9 %finish.1 = f32[4,16,768]{2,1,0:T(8,128)} custom-call(f32[4,16,768]{2,1,0:T(8,128)S(1)} %gather_near.1.near_ref, bf16[32,16,128]{2,1,0:T(8,128)(2,1)S(1)} %all-to-all-done.1.far_ref, bf16[4,32,768]{2,1,0:T(8,128)(2,1)S(1)} %copy-done), custom_call_target="tpu_custom_call" | custom-call | tf_op jit(solution)/shard_map/finish/pallas_call | solution.py:512
  (2 shorter events, 0.1 us)
Async XLA Ops:
  2.4 7.3 %copy-start.1 = (s32[3,1024]{1,0:T(4,128)S(1)}, s32[3,1024]{1,0:T(4,128)}, u32[]{:S(2)}) copy-start(s32[3,1024]{1,0:T(4,128)} %triangles_ref.1) | copy-start | bytes 36868
  2.4 7.3 %copy-start.2 = (f32[3,561]{1,0:T(4,128)S(1)}, f32[3,561]{1,0:T(4,128)}, u32[]{:S(2)}) copy-start(f32[3,561]{1,0:T(4,128)} %vertices_ref.1) | copy-start | bytes 20200
  2.4 7.3 %copy-start.3 = (s32[4,256]{1,0:T(4,128)S(1)}, s32[4,256]{1,0:T(4,128)}, u32[]{:S(2)}) copy-start(s32[4,256]{1,0:T(4,128)} %map_ref.1) | copy-start | bytes 12292
  2.4 14.6 %all-to-all-start = ((bf16[32,8,128]{2,1,0:T(8,128)(2,1)}), bf16[32,8,128]{2,1,0:T(8,128)(2,1)S(1)}, u32[]{:S(2)}, u32[]{:S(2)}) async-start(bf16[32,8,128]{2,1,0:T(8,128)(2,1)} %coeffs.1.after_ref), calls=%async_computation | async-start | bytes 131072 | tf_op jit(solution)/shard_map/all_to_all | solution.py:412
  9.8 4.8 %copy-start.5 = (bf16[16,1024]{1,0:T(8,128)(2,1)S(1)}, bf16[16,1024]{1,0:T(8,128)(2,1)}, u32[]{:S(2)}) copy-start(bf16[16,1024]{1,0:T(8,128)(2,1)} %param.16) | copy-start | bytes 98308
  10.8 3.9 %copy-start.4 = (s32[2,16]{1,0:T(2,128)S(1)}, s32[2,16]{1,0:T(2,128)}, u32[]{:S(2)}) copy-start(s32[2,16]{1,0:T(2,128)} %pairs_ref.1) | copy-start | bytes 388
  10.8 10.4 %collective-permute-start = (bf16[2,16,1024]{2,1,0:T(8,128)(2,1)S(1)}, bf16[2,16,1024]{2,1,0:T(8,128)(2,1)S(1)}, u32[]{:S(2)}, u32[]{:S(2)}) collective-permute-start(bf16[2,16,1024]{2,1,0:T(8,128)(2,1)S(1)} %get-tuple-element.17), channel_id=1, source_target_pairs={{0,1},{1,2},{2,3},{3,4},{4,5},{5,6},{6,7},{9,8},{10,9},{11,10},{12... | collective-permute-start | bytes 196616 | tf_op jit(solution)/shard_map/ppermute | solution.py:438
  18.6 10.5 %all-to-all-start.1 = ((bf16[32,16,128]{2,1,0:T(8,128)(2,1)}), bf16[32,16,128]{2,1,0:T(8,128)(2,1)S(1)}, u32[]{:S(2)}, u32[]{:S(2)}) async-start(bf16[32,16,128]{2,1,0:T(8,128)(2,1)} %get-tuple-element.24), calls=%async_computation.1 | async-start | bytes 262144 | tf_op jit(solution)/shard_map/all_to_all | solution.py:481
  25.0 4.0 %copy-start = (bf16[4,32,768]{2,1,0:T(8,128)(2,1)S(1)}, bf16[4,32,768]{2,1,0:T(8,128)(2,1)}, u32[]{:S(2)}) copy-start(bf16[4,32,768]{2,1,0:T(8,128)(2,1)} %basis_ref.1) | copy-start | bytes 589828
  25.0 1.4 %collective-permute-start.1 = (f32[2,16,768]{2,1,0:T(8,128)S(1)}, f32[2,16,768]{2,1,0:T(8,128)S(1)}, u32[]{:S(2)}, u32[]{:S(2)}) collective-permute-start(f32[2,16,768]{2,1,0:T(8,128)S(1)} %near.1.own_ref), channel_id=1, source_target_pairs={{0,8},{8,0},{16,24},{24,16},{1,9},{9,1},{17,25},{25,17},{2,10},{10... | collective-permute-start | bytes 294920 | tf_op jit(solution)/shard_map/ppermute | solution.py:500

commit v27 on v20

--- a/solution.py
+++ b/solution.py
@@ -42,7 +42,7 @@
 
 
 def coeffs_kernel(
-    slip_hbm, basis_hbm, pairs_hbm, count_ref, pay_hbm, slip_ref, basis_ref, pairs_ref, sent_ref, sems, out_sems
+    slip_hbm, basis_hbm, pairs_ref, count_ref, pay_hbm, slip_ref, basis_ref, sent_ref, sems, out_sems
 ):
     clusters = slip_hbm.shape[0]
     rhs_count = slip_ref.shape[0]
@@ -51,12 +51,10 @@
     copies = [
         pltpu.make_async_copy(slip_hbm.at[mine], slip_ref, sems.at[0]),
         pltpu.make_async_copy(basis_hbm.at[mine], basis_ref, sems.at[1]),
-        pltpu.make_async_copy(pairs_hbm, pairs_ref, sems.at[2]),
     ]
     for copy in copies:
         copy.start()
     half = rhs_count // 2
-    copies[2].wait()
     first = pairs_ref[0:1, :]
     kind = (first - lax.axis_index("long") * clusters) * (NEARC + 1) + pairs_ref[1:2, :] - first
     kinds = lax.broadcasted_iota(jnp.int32, (half, kind.shape[1]), 0)
@@ -387,14 +385,13 @@
     pay = pl.pallas_call(
         coeffs_kernel,
         out_shape=jax.ShapeDtypeStruct((devices, rhs_count // 2, LANES), jnp.bfloat16),
-        in_specs=[HBM] * 3 + [SMEM],
+        in_specs=[HBM] * 2 + [VMEM, SMEM],
         out_specs=HBM,
         scratch_shapes=[
             pltpu.VMEM(slip.shape[1:], slip.dtype),
             pltpu.VMEM(basis.shape[1:], basis.dtype),
-            pltpu.VMEM(near_pairs.shape, near_pairs.dtype),
             pltpu.VMEM((long_count, rhs_count // 2, LANES), jnp.bfloat16),
-            pltpu.SemaphoreType.DMA((3,)),
+            pltpu.SemaphoreType.DMA((2,)),
             pltpu.SemaphoreType.DMA((row_count,)),
         ],
         compiler_params=pltpu.CompilerParams(vmem_limit_bytes=16 << 20),
@@ -402,8 +399,9 @@
     )(
         *[
             pltpu.with_memory_space_constraint(array, pltpu.HBM)
-            for array in (slip, basis, near_pairs)
-        ],
+            for array in (slip, basis)
+        ],
+        near_pairs,
         near_count,
     )
     everyone = lax.all_to_all(pay, ("row", "long"), 0, 0, tiled=True)

time: 30.2 us -> 30.2 us (level)
  no operation moved by 1% of the time
where the time goes in v27:
time: 30.2 us; the launch traced here: 29.9 us
  starting transfers between devices  13.7 us (45%)
  Pallas kernels  8.56 us (28%)
  waiting for transfers between devices  6.5 us (22%)
  between operations  0.85 us (3%)
    all_to_all x1, starting transfers between devices, shards(): everyone = lax.all_to_all(pay, ('row', 'long'), 0, 0, tiled=True)  7.3 us
    pallas_call x1, Pallas kernels, shards(): pl.pallas_call(functools.partial(near_kernel, long_count=long_count, clus...  3.68 us
    ppermute x1, starting transfers between devices, shards(): halo = lax.ppermute(to_neighbour, ('row', 'long'), route)  3.68 us
    all_to_all x1, waiting for transfers between devices, shards(): everyone = lax.all_to_all(pay, ('row', 'long'), 0, 0, tiled=True)  2.71 us
    all_to_all x1, waiting for transfers between devices, shards(): far_terms = lax.all_to_all(far, ('row', 'long'), 0, 0, tiled=True)  2.6 us
    all_to_all x1, starting transfers between devices, shards(): far_terms = lax.all_to_all(far, ('row', 'long'), 0, 0, tiled=True)  2.59 us
    pallas_call x1, Pallas kernels, shards(): pl.pallas_call(coeffs_kernel, out_shape=jax.ShapeDtypeStruct((devices, rh...  1.75 us
    pallas_call x1, Pallas kernels, shards(): pl.pallas_call(functools.partial(far_kernel, clusters=clusters), out_shap...  1.54 us
  transfers between devices with their start and end apart: 4, of which 3 were waited for; matrix products, arithmetic and copies ran while one was open for 0% of the time, Pallas kernels for 20%

profile of v27, /device:TPU:0, one launch (start us, length us, event | category | flops | bytes accessed | tf_op | source)
XLA Modules:
  0.0 29.9 jit_solution(878073997291562557)
XLA Ops:
  0.0 0.0 copy-start.5
  0.7 0.0 copy-done.5
  0.7 0.0 copy-start
  0.7 1.8 %coeffs.1.after_ref = bf16[32,8,128]{2,1,0:T(8,128)(2,1)} custom-call(f32[4,16,768]{2,1,0:T(8,128)} %slip_ref.1, bf16[4,32,768]{2,1,0:T(8,128)(2,1)} %basis_ref.1, s32[2,20]{1,0:T(2,128)S(1)} %copy-done.5, s32[1]{0:T(128)S(6)} %copy.10.count_ref), custom_call_target="tpu_custom_call" | custom-call | tf_op jit(solution)/shard_map/coeffs/pallas_call | solution.py:385
  2.4 0.0 copy-start.2
  2.5 0.0 copy-start.3
  2.5 0.0 copy-start.4
  2.5 7.3 %all-to-all-start = ((bf16[32,8,128]{2,1,0:T(8,128)(2,1)}), bf16[32,8,128]{2,1,0:T(8,128)(2,1)S(1)}, u32[]{:S(2)}, u32[]{:S(2)}) async-start(bf16[32,8,128]{2,1,0:T(8,128)(2,1)} %coeffs.1.after_ref), calls=%async_computation | async-start | bytes 131072 | tf_op jit(solution)/shard_map/all_to_all | solution.py:407
  9.8 0.0 copy-done
  9.8 0.0 copy-done.2
  9.8 0.0 copy-done.3
  9.8 0.0 copy-done.4
  9.8 0.0 copy-start.7
  9.8 0.3 geometry.1
  10.1 0.0 copy-start.6
  10.1 3.7 %collective-permute-start = (bf16[2,16,1024]{2,1,0:T(8,128)(2,1)S(1)}, bf16[2,16,1024]{2,1,0:T(8,128)(2,1)S(1)}, u32[]{:S(2)}, u32[]{:S(2)}) collective-permute-start(bf16[2,16,1024]{2,1,0:T(8,128)(2,1)S(1)} %get-tuple-element.17), channel_id=1, source_target_pairs={{0,1},{1,2},{2,3},{3,4},{4,5},{5,6},{6,7},{9,8},{10,9},{11,10},{12... | collective-permute-start | bytes 196616 | tf_op jit(solution)/shard_map/ppermute | solution.py:430
  13.8 0.0 copy-done.7
  13.8 0.1 reshape.3.coupling_ref
  14.0 0.0 copy-done.6
  14.0 0.4 %coupling.1 = (bf16[512,128]{1,0:T(8,128)(2,1)S(1)}, bf16[512,128]{1,0:T(8,128)(2,1)S(1)}, s32[6,16]{1,0:T(8,128)S(1)}) custom-call(bf16[16,32,32]{2,1,0:T(8,128)(2,1)S(1)} %reshape.3.coupling_ref, s32[2,16]{1,0:T(2,128)S(1)} %copy-done.6, bf16[32,8,128]{2,1,0:T(8,128)(2,1)} %coeffs.1.after_ref), custom_call_target="tpu_custom_call" | custom-call | flops 1000 | bytes 1000 | tf_op jit(solution)/shard_map/coupling/pallas_call | solution.py:445
  14.4 2.7 %all-to-all-done.coeff_ref.pay_ref = bf16[32,8,128]{2,1,0:T(8,128)(2,1)S(1)} async-done(((bf16[32,8,128]{2,1,0:T(8,128)(2,1)}), bf16[32,8,128]{2,1,0:T(8,128)(2,1)S(1)}, u32[]{:S(2)}, u32[]{:S(2)}) %all-to-all-start) | async-done | bytes 65568 | tf_op jit(solution)/shard_map/all_to_all | solution.py:407
  17.1 1.5 %far.1 = (bf16[32,16,128]{2,1,0:T(8,128)(2,1)}, f32[8,128]{1,0:T(8,128)S(1)}) custom-call(s32[6,16]{1,0:T(8,128)S(1)} %get-tuple-element.20.list_ref, bf16[32,8,128]{2,1,0:T(8,128)(2,1)S(1)} %all-to-all-done.coeff_ref.pay_ref, bf16[512,128]{1,0:T(8,128)(2,1)S(1)} %get-tuple-element.21.to_second_ref, bf16[512,128]{1,0:T(8,128)(2,1)S(1)} %get-tuple-element.22.to_first_ref), custom_call_target="tpu_custom_call" | custom-call | tf_op jit(solution)/shard_map/far/pallas_call | solution.py:455
  18.6 2.6 %all-to-all-start.1 = ((bf16[32,16,128]{2,1,0:T(8,128)(2,1)}), bf16[32,16,128]{2,1,0:T(8,128)(2,1)S(1)}, u32[]{:S(2)}, u32[]{:S(2)}) async-start(bf16[32,16,128]{2,1,0:T(8,128)(2,1)} %get-tuple-element.24), calls=%async_computation.1 | async-start | bytes 262144 | tf_op jit(solution)/shard_map/all_to_all | solution.py:473
  21.2 0.0 collective-permute-done.halo_ref
  21.3 3.7 %near.1.own_ref = f32[2,16,768]{2,1,0:T(8,128)S(1)} custom-call(bf16[6,16,768]{2,1,0:T(8,128)(2,1)S(1)} %get-tuple-element.18.slip_ref, f32[6,4,256]{2,1,0:T(4,128)S(1)} %get-tuple-element.19.place_ref, bf16[32,8,128]{2,1,0:T(8,128)(2,1)S(1)} %all-to-all-done.coeff_ref.pay_ref, f32[8,128]{1,0:T(8,128)S(1)} %get-tuple-element.23.after_ref), custom_call_target="tpu_custom_call" | custom-call | flops 1000000000 | bytes 1000000 | tf_op jit(solution)/shard_map/near/pallas_call | solution.py:475
  25.0 0.0 copy-start.1
  25.0 0.2 collective-permute-start.1
  25.1 1.2 %collective-permute-done.1.other_ref = f32[2,16,768]{2,1,0:T(8,128)S(1)} collective-permute-done((f32[2,16,768]{2,1,0:T(8,128)S(1)}, f32[2,16,768]{2,1,0:T(8,128)S(1)}, u32[]{:S(2)}, u32[]{:S(2)}) %collective-permute-start.1) | collective-permute-done | bytes 98336 | tf_op jit(solution)/shard_map/ppermute | solution.py:492
  26.4 2.6 %all-to-all-done.1.far_ref = bf16[32,16,128]{2,1,0:T(8,128)(2,1)S(1)} async-done(((bf16[32,16,128]{2,1,0:T(8,128)(2,1)}), bf16[32,16,128]{2,1,0:T(8,128)(2,1)S(1)}, u32[]{:S(2)}, u32[]{:S(2)}) %all-to-all-start.1) | async-done | bytes 131104 | tf_op jit(solution)/shard_map/all_to_all | solution.py:473
  29.0 0.0 copy-done.1
  29.0 0.9 %finish.1 = f32[4,16,768]{2,1,0:T(8,128)} custom-call(f32[4,16,768]{2,1,0:T(8,128)S(1)} %gather_near.1.near_ref, bf16[32,16,128]{2,1,0:T(8,128)(2,1)S(1)} %all-to-all-done.1.far_ref, bf16[4,32,768]{2,1,0:T(8,128)(2,1)S(1)} %copy-done.1), custom_call_target="tpu_custom_call" | custom-call | tf_op jit(solution)/shard_map/finish/pallas_call | solution.py:504
  (2 shorter events, 0.1 us)
Async XLA Ops:
  0.0 0.7 %copy-start.5 = (s32[2,20]{1,0:T(2,128)S(1)}, s32[2,20]{1,0:T(2,128)}, u32[]{:S(2)}) copy-start(s32[2,20]{1,0:T(2,128)} %pairs_ref.2) | copy-start | bytes 484
  0.7 9.1 %copy-start = (f32[4,16,768]{2,1,0:T(8,128)S(1)}, f32[4,16,768]{2,1,0:T(8,128)}, u32[]{:S(2)}) copy-start(f32[4,16,768]{2,1,0:T(8,128)} %slip_ref.1) | copy-start | bytes 589828
  2.4 7.4 %copy-start.2 = (s32[3,1024]{1,0:T(4,128)S(1)}, s32[3,1024]{1,0:T(4,128)}, u32[]{:S(2)}) copy-start(s32[3,1024]{1,0:T(4,128)} %triangles_ref.1) | copy-start | bytes 36868
  2.5 7.4 %copy-start.3 = (f32[3,561]{1,0:T(4,128)S(1)}, f32[3,561]{1,0:T(4,128)}, u32[]{:S(2)}) copy-start(f32[3,561]{1,0:T(4,128)} %vertices_ref.1) | copy-start | bytes 20200
  2.5 7.4 %copy-start.4 = (s32[4,256]{1,0:T(4,128)S(1)}, s32[4,256]{1,0:T(4,128)}, u32[]{:S(2)}) copy-start(s32[4,256]{1,0:T(4,128)} %map_ref.1) | copy-start | bytes 12292
  2.5 14.6 %all-to-all-start = ((bf16[32,8,128]{2,1,0:T(8,128)(2,1)}), bf16[32,8,128]{2,1,0:T(8,128)(2,1)S(1)}, u32[]{:S(2)}, u32[]{:S(2)}) async-start(bf16[32,8,128]{2,1,0:T(8,128)(2,1)} %coeffs.1.after_ref), calls=%async_computation | async-start | bytes 131072 | tf_op jit(solution)/shard_map/all_to_all | solution.py:407
  9.8 4.0 %copy-start.7 = (bf16[16,1024]{1,0:T(8,128)(2,1)S(1)}, bf16[16,1024]{1,0:T(8,128)(2,1)}, u32[]{:S(2)}) copy-start(bf16[16,1024]{1,0:T(8,128)(2,1)} %param.16) | copy-start | bytes 98308
  10.1 3.9 %copy-start.6 = (s32[2,16]{1,0:T(2,128)S(1)}, s32[2,16]{1,0:T(2,128)}, u32[]{:S(2)}) copy-start(s32[2,16]{1,0:T(2,128)} %pairs_ref.3) | copy-start | bytes 388
  10.1 11.1 %collective-permute-start = (bf16[2,16,1024]{2,1,0:T(8,128)(2,1)S(1)}, bf16[2,16,1024]{2,1,0:T(8,128)(2,1)S(1)}, u32[]{:S(2)}, u32[]{:S(2)}) collective-permute-start(bf16[2,16,1024]{2,1,0:T(8,128)(2,1)S(1)} %get-tuple-element.17), channel_id=1, source_target_pairs={{0,1},{1,2},{2,3},{3,4},{4,5},{5,6},{6,7},{9,8},{10,9},{11,10},{12... | collective-permute-start | bytes 196616 | tf_op jit(solution)/shard_map/ppermute | solution.py:430
  18.6 10.3 %all-to-all-start.1 = ((bf16[32,16,128]{2,1,0:T(8,128)(2,1)}), bf16[32,16,128]{2,1,0:T(8,128)(2,1)S(1)}, u32[]{:S(2)}, u32[]{:S(2)}) async-start(bf16[32,16,128]{2,1,0:T(8,128)(2,1)} %get-tuple-element.24), calls=%async_computation.1 | async-start | bytes 262144 | tf_op jit(solution)/shard_map/all_to_all | solution.py:473
  25.0 4.0 %copy-start.1 = (bf16[4,32,768]{2,1,0:T(8,128)(2,1)S(1)}, bf16[4,32,768]{2,1,0:T(8,128)(2,1)}, u32[]{:S(2)}) copy-start(bf16[4,32,768]{2,1,0:T(8,128)(2,1)} %basis_ref.1) | copy-start | bytes 589828
  25.0 1.4 %collective-permute-start.1 = (f32[2,16,768]{2,1,0:T(8,128)S(1)}, f32[2,16,768]{2,1,0:T(8,128)S(1)}, u32[]{:S(2)}, u32[]{:S(2)}) collective-permute-start(f32[2,16,768]{2,1,0:T(8,128)S(1)} %near.1.own_ref), channel_id=1, source_target_pairs={{0,8},{8,0},{16,24},{24,16},{1,9},{9,1},{17,25},{25,17},{2,10},{10... | collective-permute-start | bytes 294920 | tf_op jit(solution)/shard_map/ppermute | solution.py:492
